TPU v7x, 32 devices: a whole 2x2x4 slice. The times are simulated.
32 devices in a mesh: dom: 16 (over z, y, x), cell: 2 (over core).
Axes of the slice: x: 2, y: 2, z: 4, core: 2. Of those that a mesh axis runs over, the one named last changes fastest.
Arguments:
- features: bfloat16 [8192, 128], P(('cell', 'dom')), parts along dimension 0, may hold values from -6 to 6
- positions: float32 [3, 8192], P(None, ('cell', 'dom')), parts along dimension 1, may hold values from 0 to 80, as said below
- neighbours: int32 [8192, 64], P(('cell', 'dom')), parts along dimension 0, may hold values from 0 to 767, as said below
- neighbour_count: int32 [8192], P(('cell', 'dom')), parts along dimension 0, may hold values from 16 to 64, as said below
- ghost_sends: int32 [2, 8192], P(None, ('cell', 'dom')), parts along dimension 1, may hold values from 0 to 255, as said below
- species: int32 [8192], P(('cell', 'dom')), parts along dimension 0, may hold values from 0 to 5
- wave_index: int32 [3, 1024], replicated, may hold values from -8 to 8, as said below
- force_ref: float32 [3, 8192], P(None, ('cell', 'dom')), parts along dimension 1, may hold values from -6 to 6
- radial_weight: bfloat16 [16, 128], replicated, may hold values from -1.5 to 1.5
- mix_weight: bfloat16 [128, 128], replicated, may hold values from -0.5 to 0.5
- charge_weight: bfloat16 [128, 64], replicated, may hold values from -0.5 to 0.5
- species_charge: float32 [6, 64], replicated, may hold values from -4 to 4
Outputs:
- forces: float32 [3, 8192], P(None, ('cell', 'dom')), parts along dimension 1
- radial_step: float32 [32, 128], P('cell'), parts along dimension 0
- mix_step: float32 [256, 128], P('cell'), parts along dimension 0
- charge_step: float32 [256, 64], P('cell'), parts along dimension 0
- species_step: float32 [12, 64], P('cell'), parts along dimension 0
There are 2 independent parts, one for each index of `cell`. A program takes and returns all parts, laid end to end along the dimension named above; an argument that names none is the same for every part. Nothing has to cross between parts.
Inputs may be any that keep to these rules, and one draw needn't show every extreme that they name: `neighbours`: in the shard of domain d, an entry e below 256 names the domain's own atom e; 256 + g names the atom at position g of row 1 of ghost_sends of domain d - 1; 512 + g names the atom at position g of row 0 of ghost_sends of domain d + 1 (domains cyclic). Entries of a row are distinct and never the atom itself. `neighbour_count`: slots below the count are live; in every domain some atom has all 64 slots live. `ghost_sends`: positions within the domain's shard; the entries of one row of one domain are distinct. `wave_index`: columns are distinct and their first component is 1 or more. `positions`: coordinates in a periodic box of 80 along the first axis and 20 along the other two.
All inputs are finite; a program needn't handle non-finite values.
Results may differ from a plain program's by a relative error of at most 0.0051.
Values may be sent and summed in bfloat16 or wider, within the bound.
No kernel may reach another device: no remote copies, remote signals or barrier semaphores. Data moves between devices by JAX's collectives and lax.ppermute only.
A program may use at most 64 MiB of HBM per device.

v0:
```python
import jax
import jax.numpy as jnp
from jax import lax
from jax.sharding import PartitionSpec as P

cutoff_radius = 5.0
kernel_width = 1.0
basis_width = 0.5
box_side = 20.0
two_pi = 6.283185307179586
highest = lax.Precision.HIGHEST


def extended(shard, sides, width):
    for axis, dim in sides:
        devices, length = (lax.axis_size(axis), shard.shape[dim])
        up = [(i, (i + 1) % devices) for i in range(devices)]
        down = [(j, i) for i, j in up]
        last = lax.slice_in_dim(shard, length - width, length, axis=dim)
        initial = lax.slice_in_dim(shard, 0, width, axis=dim)
        before = lax.ppermute(last, axis, up)
        after = lax.ppermute(initial, axis, down)
        shard = jnp.concatenate([before, shard, after], axis=dim)
    return shard


def contract_first(left, right):
    return lax.dot_general(
        left, right, (((0,), (0,)), ((), ())), precision=highest, preferred_element_type=jnp.float32
    )


def contract_last(left, right):
    return lax.dot_general(
        left, right, (((1,), (1,)), ((), ())), precision=highest, preferred_element_type=jnp.float32
    )


def product(left, right):
    return jnp.dot(left, right, precision=highest, preferred_element_type=jnp.float32)


def edge_terms(own_coords, other_coords, live_count, box_lengths, basis_count):
    slots_count = other_coords.shape[2]
    displacement = other_coords - own_coords[:, :, None]
    displacement = displacement - box_lengths[:, None, None] * jnp.floor(
        displacement / box_lengths[:, None, None] + 0.5
    )
    distance = jnp.sqrt(jnp.sum(displacement * displacement, axis=0))
    is_live = (jnp.arange(slots_count, dtype=jnp.int32)[None, :] < live_count[:, None]).astype(
        jnp.float32
    )
    cutoff_fade = 0.5 * (
        jnp.cos(jnp.pi * jnp.minimum(distance, cutoff_radius) / cutoff_radius) + 1.0
    )
    centers = 0.5 + (cutoff_radius - 0.5) * jnp.arange(basis_count, dtype=jnp.float32) / (
        basis_count - 1
    )
    basis_rows = jnp.exp(-jnp.square((distance[..., None] - centers) / basis_width)).astype(
        jnp.bfloat16
    )
    return (basis_rows, is_live * cutoff_fade)


def silu_slope(value):
    sigmoid = jax.nn.sigmoid(value)
    return sigmoid * (1.0 + value * (1.0 - sigmoid))


def normalized(gradient):
    return gradient / jnp.sqrt(jnp.mean(gradient * gradient) + 1e-06)


def on_device(
    features,
    positions,
    neighbours,
    neighbour_count,
    ghost_sends,
    species,
    wave_index,
    force_ref,
    radial_weight,
    mix_weight,
    charge_weight,
    species_charge,
):
    atoms, width = features.shape
    slots_count = neighbours.shape[1]
    basis_count = radial_weight.shape[0]
    charges_width = charge_weight.shape[1]
    wave_count = wave_index.shape[1]
    domains = lax.axis_size("dom")
    total_atoms = atoms * domains
    box_lengths = jnp.array([1.25 * total_atoms / 64, box_side, box_side], dtype=jnp.float32)
    outgoing = features[ghost_sends]
    arrived = extended(outgoing, (("dom", 0),), 1)
    feature_table = jnp.concatenate([features, arrived[0], arrived[3]], axis=0)
    outgoing_coords = jnp.stack(
        [positions[:, ghost_sends[0]], positions[:, ghost_sends[1]]], axis=0
    )
    arrived_coords = extended(outgoing_coords, (("dom", 0),), 1)
    coords_all = jnp.concatenate([positions, arrived_coords[0], arrived_coords[3]], axis=1)
    edge_rows = 64
    blocks = atoms // edge_rows
    slot_blocks = neighbours.reshape(blocks, edge_rows, slots_count)
    own_blocks = positions.reshape(3, blocks, edge_rows).transpose(1, 0, 2)
    count_blocks = neighbour_count.reshape(blocks, edge_rows)

    def message_block(block_args):
        slot_rows, own_coords, live_count = block_args
        basis_rows, edge_weight = edge_terms(
            own_coords, coords_all[:, slot_rows], live_count, box_lengths, basis_count
        )
        filters = jnp.dot(
            basis_rows.reshape(-1, basis_count), radial_weight, preferred_element_type=jnp.float32
        )
        filters = filters.reshape(edge_rows, slots_count, width)
        return jnp.sum(
            edge_weight[..., None] * filters * feature_table[slot_rows].astype(jnp.float32), axis=1
        )

    messages = (
        lax.map(message_block, (slot_blocks, own_blocks, count_blocks))
        .reshape(atoms, width)
        .astype(jnp.bfloat16)
    )
    before = jnp.dot(messages, mix_weight, preferred_element_type=jnp.float32)
    hidden = (features.astype(jnp.float32) + jax.nn.silu(before)).astype(jnp.bfloat16)
    one_hot = (
        species[:, None] == jnp.arange(species_charge.shape[0], dtype=jnp.int32)[None, :]
    ).astype(jnp.float32)
    charges = jnp.dot(hidden, charge_weight, preferred_element_type=jnp.float32) + product(
        one_hot, species_charge
    )
    wave_vectors = two_pi * wave_index.astype(jnp.float32) / box_lengths[:, None]
    damping = (
        jnp.exp(-0.5 * kernel_width * kernel_width * jnp.sum(wave_vectors * wave_vectors, axis=0))
        / total_atoms
    )

    def phases_of():
        phases = contract_first(positions, wave_vectors)
        return (jnp.cos(phases), jnp.sin(phases), wave_vectors)

    share_rows = wave_count // domains
    own_first = lax.axis_index("dom") * share_rows
    own_damping = lax.dynamic_slice_in_dim(damping, own_first, share_rows, 0)
    cosines, sines, wave_piece = phases_of()
    structure_part = lax.psum_scatter(
        jnp.concatenate([contract_first(cosines, charges), contract_first(sines, charges)], axis=1),
        "dom",
        scatter_dimension=0,
        tiled=True,
    )
    coeff_part = own_damping[:, None] * structure_part
    coeff_piece = lax.all_gather(coeff_part, "dom", axis=0, tiled=True)
    cosines, sines, wave_piece = phases_of()
    along_cos = contract_last(charges, coeff_piece[:, :charges_width])
    along_sin = contract_last(charges, coeff_piece[:, charges_width:])
    mixture = sines * along_cos - cosines * along_sin
    forces = contract_last(wave_piece, mixture)
    errors = 2.0 * (forces - force_ref)
    cosines, sines, wave_piece = phases_of()
    slopes = contract_first(errors, wave_piece)
    gradient_part = lax.psum_scatter(
        jnp.concatenate(
            [contract_first(slopes * sines, charges), -contract_first(slopes * cosines, charges)],
            axis=1,
        ),
        "dom",
        scatter_dimension=0,
        tiled=True,
    )
    back_part = own_damping[:, None] * gradient_part
    coeff_piece = lax.all_gather(coeff_part, "dom", axis=0, tiled=True)
    back_piece = lax.all_gather(back_part, "dom", axis=0, tiled=True)
    cosines, sines, wave_piece = phases_of()
    slopes = contract_first(errors, wave_piece)
    direct = product(slopes * sines, coeff_piece[:, :charges_width]) - product(
        slopes * cosines, coeff_piece[:, charges_width:]
    )
    indirect = product(cosines, back_piece[:, :charges_width]) + product(
        sines, back_piece[:, charges_width:]
    )
    charge_grad = direct + indirect
    charge_rounded = charge_grad.astype(jnp.bfloat16)
    charge_sum = contract_first(hidden, charge_rounded)
    species_sum = contract_first(one_hot, charge_grad)
    upstream = contract_last(charge_rounded, charge_weight)
    before_grad = (upstream * silu_slope(before)).astype(jnp.bfloat16)
    mix_sum = contract_first(messages, before_grad)
    message_grad = contract_last(before_grad, mix_weight).astype(jnp.bfloat16)

    def radial_block(running, block_args):
        slot_rows, own_coords, live_count, rows_grad = block_args
        basis_rows, edge_weight = edge_terms(
            own_coords, coords_all[:, slot_rows], live_count, box_lengths, basis_count
        )
        edge_term = (
            edge_weight[..., None]
            * rows_grad.astype(jnp.float32)[:, None, :]
            * feature_table[slot_rows].astype(jnp.float32)
        ).astype(jnp.bfloat16)
        return (
            running
            + contract_first(basis_rows.reshape(-1, basis_count), edge_term.reshape(-1, width)),
            None,
        )

    radial_sum, _ = lax.scan(
        radial_block,
        jnp.zeros((basis_count, width), jnp.float32),
        (slot_blocks, own_blocks, count_blocks, message_grad.reshape(blocks, edge_rows, width)),
    )
    radial_total, mix_total, charge_total, species_total = lax.psum(
        (radial_sum, mix_sum, charge_sum, species_sum), "dom"
    )
    return (
        forces,
        normalized(radial_total),
        normalized(mix_total),
        normalized(charge_total),
        normalized(species_total),
    )


def solution(mesh):
    placed = (
        P(("cell", "dom"), None),
        P(None, ("cell", "dom")),
        P(("cell", "dom"), None),
        P(("cell", "dom")),
        P(None, ("cell", "dom")),
        P(("cell", "dom")),
        P(),
        P(None, ("cell", "dom")),
        P(),
        P(),
        P(),
        P(),
    )
    return jax.shard_map(
        on_device,
        mesh=mesh,
        in_specs=placed,
        out_specs=(
            P(None, ("cell", "dom")),
            P("cell", None),
            P("cell", None),
            P("cell", None),
            P("cell", None),
        ),
        check_vma=False,
    )
```

profile of v0, /device:TPU:0, one launch (start us, length us, event | category | flops | bytes accessed | tf_op | source)
XLA Modules:
  0.0 701.0 jit_solution(9652773030858824743)
XLA Ops:
  10.0 3.0 collective-permute-start.2
  13.0 4.1 collective-permute-start.3
  22.2 6.5 fusion.57
  31.1 116.3 %while.27 = (s32[]{:T(128)}, bf16[4,64,128]{2,1,0:T(8,128)(2,1)S(1)}, s32[4,64]{1,0:T(4,128)S(1)}, s32[4,64,64]{2,1,0:T(8,128)S(1)}, f32[3,768]{0,1:T(8,128)S(1)...) while((s32[]{:T(128)}, ...), condition=%wide.region_3.4_spmd.clone, body=%wide.region_0.3_spmd.sunk.clone.sunk | while | flops 19329056 | bytes 3677469 | solution.py:124
  31.3 14.9 %gather_fusion = bf16[4096,128]{1,0:T(8,128)(2,1)} fusion(bf16[768,128]{1,0:T(8,128)(2,1)S(1)} %get-tuple-element.547, s32[4096]{0:T(1024)S(1)} %broadcast_clamp_fusion.4), kind=kCustom, calls=%fused_computation.1.clone.1 | custom fusion | bytes 2113536 | tf_op jit(solution)/shard_map/while/body/eval_jaxpr/gather | solution.py:120
  46.2 10.8 %gather_fusion.1 = f32[4096,3]{1,0:T(8,128)S(1)} fusion(f32[3,768]{0,1:T(8,128)S(1)} %get-tuple-element.544, s32[4096]{0:T(1024)S(1)} %broadcast_clamp_fusion.4), kind=kCustom, calls=%fused_computation.clone.1 | custom fusion | bytes 114688 | tf_op jit(solution)/shard_map/while/body/eval_jaxpr/gather | solution.py:113
  57.9 2.2 fusion.100
  60.4 14.9 %gather_fusion = bf16[4096,128]{1,0:T(8,128)(2,1)} fusion(bf16[768,128]{1,0:T(8,128)(2,1)S(1)} %get-tuple-element.547, s32[4096]{0:T(1024)S(1)} %broadcast_clamp_fusion.4), kind=kCustom, calls=%fused_computation.1.clone.1 | custom fusion | bytes 2113536 | tf_op jit(solution)/shard_map/while/body/eval_jaxpr/gather | solution.py:120
  75.3 10.8 %gather_fusion.1 = f32[4096,3]{1,0:T(8,128)S(1)} fusion(f32[3,768]{0,1:T(8,128)S(1)} %get-tuple-element.544, s32[4096]{0:T(1024)S(1)} %broadcast_clamp_fusion.4), kind=kCustom, calls=%fused_computation.clone.1 | custom fusion | bytes 114688 | tf_op jit(solution)/shard_map/while/body/eval_jaxpr/gather | solution.py:113
  87.0 2.2 fusion.100
  89.4 14.9 %gather_fusion = bf16[4096,128]{1,0:T(8,128)(2,1)} fusion(bf16[768,128]{1,0:T(8,128)(2,1)S(1)} %get-tuple-element.547, s32[4096]{0:T(1024)S(1)} %broadcast_clamp_fusion.4), kind=kCustom, calls=%fused_computation.1.clone.1 | custom fusion | bytes 2113536 | tf_op jit(solution)/shard_map/while/body/eval_jaxpr/gather | solution.py:120
  104.3 10.8 %gather_fusion.1 = f32[4096,3]{1,0:T(8,128)S(1)} fusion(f32[3,768]{0,1:T(8,128)S(1)} %get-tuple-element.544, s32[4096]{0:T(1024)S(1)} %broadcast_clamp_fusion.4), kind=kCustom, calls=%fused_computation.clone.1 | custom fusion | bytes 114688 | tf_op jit(solution)/shard_map/while/body/eval_jaxpr/gather | solution.py:113
  118.5 14.9 %gather_fusion = bf16[4096,128]{1,0:T(8,128)(2,1)} fusion(bf16[768,128]{1,0:T(8,128)(2,1)S(1)} %get-tuple-element.547, s32[4096]{0:T(1024)S(1)} %broadcast_clamp_fusion.4), kind=kCustom, calls=%fused_computation.1.clone.1 | custom fusion | bytes 2113536 | tf_op jit(solution)/shard_map/while/body/eval_jaxpr/gather | solution.py:120
  133.4 10.8 %gather_fusion.1 = f32[4096,3]{1,0:T(8,128)S(1)} fusion(f32[3,768]{0,1:T(8,128)S(1)} %get-tuple-element.544, s32[4096]{0:T(1024)S(1)} %broadcast_clamp_fusion.4), kind=kCustom, calls=%fused_computation.clone.1 | custom fusion | bytes 114688 | tf_op jit(solution)/shard_map/while/body/eval_jaxpr/gather | solution.py:113
  145.2 2.2 fusion.100
  149.3 2.4 fusion.59
  154.1 76.4 %reduce-scatter.7.cloned.1.call-done = f32[64,128]{1,0:T(8,128)} async-done(((f32[1024,128]{1,0:T(8,128)}), f32[64,128]{1,0:T(8,128)}) %reduce-scatter.7.cloned.1.call-update) | async-done | bytes 32784 | tf_op jit(solution)/shard_map/reduce_scatter | solution.py:150
  231.3 39.0 %all_gather.7 = f32[1024,128]{1,0:T(8,128)S(1)} all-gather(f32[64,128]{1,0:T(8,128)S(1)} %broadcast_multiply_fusion.1), channel_id=1, replica_groups=mesh['dom'=16,'cell'=2] {'dom'}, dimensions={0}, use_global_device_ids=true | all-gather | bytes 557056 | tf_op jit(solution)/shard_map/all_gather | solution.py:157
  279.4 2.4 fusion.35
  283.0 70.4 %reduce-scatter.9.cloned.1.call-done = f32[64,128]{1,0:T(8,128)} async-done(((f32[1024,128]{1,0:T(8,128)}), f32[64,128]{1,0:T(8,128)}) %reduce-scatter.9.cloned.1.call-update) | async-done | bytes 32784 | tf_op jit(solution)/shard_map/reduce_scatter | solution.py:166
  354.2 38.9 %all_gather.8 = f32[1024,128]{1,0:T(8,128)S(1)} all-gather(f32[64,128]{1,0:T(8,128)S(1)} %broadcast_multiply_fusion), channel_id=1, replica_groups=mesh['dom'=16,'cell'=2] {'dom'}, dimensions={0}, use_global_device_ids=true | all-gather | bytes 557056 | tf_op jit(solution)/shard_map/all_gather | solution.py:177
  397.0 118.1 %while.28 = (s32[]{:T(128)}, f32[16,128]{1,0:T(8,128)S(1)}, s32[4,64,64]{2,1,0:T(8,128)S(1)}, f32[3,768]{0,1:T(8,128)S(1)}, f32[4,3,64]{2,1,0:T(4,128)S(1)}, /*i...) while((s32[]{:T(128)}, f32[16,128]{1,0:T(8,128)S(1)}, ...), condition=%wide.region_9.10_spmd.clone.clone, body=%wide.region_7.9_spmd.sunk.clone.clone.sunk | while | flops 19349540 | bytes 3722543 | solution.py:211
  397.8 14.9 %gather_fusion.2 = bf16[4096,128]{1,0:T(8,128)(2,1)} fusion(bf16[768,128]{1,0:T(8,128)(2,1)S(1)} %get-tuple-element.582, s32[4096]{0:T(1024)S(1)} %broadcast_clamp_fusion.5), kind=kCustom, calls=%fused_computation.3.clone.clone.1 | custom fusion | bytes 2113536 | tf_op jit(solution)/shard_map/while/body/eval_jaxpr/gather | solution.py:203
  412.7 10.8 %gather_fusion.3 = f32[4096,3]{1,0:T(8,128)S(1)} fusion(f32[3,768]{0,1:T(8,128)S(1)} %get-tuple-element.578, s32[4096]{0:T(1024)S(1)} %broadcast_clamp_fusion.5), kind=kCustom, calls=%fused_computation.2.clone.clone.1 | custom fusion | bytes 114688 | tf_op jit(solution)/shard_map/while/body/eval_jaxpr/gather | solution.py:198
  427.3 14.9 %gather_fusion.2 = bf16[4096,128]{1,0:T(8,128)(2,1)} fusion(bf16[768,128]{1,0:T(8,128)(2,1)S(1)} %get-tuple-element.582, s32[4096]{0:T(1024)S(1)} %broadcast_clamp_fusion.5), kind=kCustom, calls=%fused_computation.3.clone.clone.1 | custom fusion | bytes 2113536 | tf_op jit(solution)/shard_map/while/body/eval_jaxpr/gather | solution.py:203
  442.2 10.8 %gather_fusion.3 = f32[4096,3]{1,0:T(8,128)S(1)} fusion(f32[3,768]{0,1:T(8,128)S(1)} %get-tuple-element.578, s32[4096]{0:T(1024)S(1)} %broadcast_clamp_fusion.5), kind=kCustom, calls=%fused_computation.2.clone.clone.1 | custom fusion | bytes 114688 | tf_op jit(solution)/shard_map/while/body/eval_jaxpr/gather | solution.py:198
  456.9 14.9 %gather_fusion.2 = bf16[4096,128]{1,0:T(8,128)(2,1)} fusion(bf16[768,128]{1,0:T(8,128)(2,1)S(1)} %get-tuple-element.582, s32[4096]{0:T(1024)S(1)} %broadcast_clamp_fusion.5), kind=kCustom, calls=%fused_computation.3.clone.clone.1 | custom fusion | bytes 2113536 | tf_op jit(solution)/shard_map/while/body/eval_jaxpr/gather | solution.py:203
  471.8 10.8 %gather_fusion.3 = f32[4096,3]{1,0:T(8,128)S(1)} fusion(f32[3,768]{0,1:T(8,128)S(1)} %get-tuple-element.578, s32[4096]{0:T(1024)S(1)} %broadcast_clamp_fusion.5), kind=kCustom, calls=%fused_computation.2.clone.clone.1 | custom fusion | bytes 114688 | tf_op jit(solution)/shard_map/while/body/eval_jaxpr/gather | solution.py:198
  486.4 14.9 %gather_fusion.2 = bf16[4096,128]{1,0:T(8,128)(2,1)} fusion(bf16[768,128]{1,0:T(8,128)(2,1)S(1)} %get-tuple-element.582, s32[4096]{0:T(1024)S(1)} %broadcast_clamp_fusion.5), kind=kCustom, calls=%fused_computation.3.clone.clone.1 | custom fusion | bytes 2113536 | tf_op jit(solution)/shard_map/while/body/eval_jaxpr/gather | solution.py:203
  501.3 10.8 %gather_fusion.3 = f32[4096,3]{1,0:T(8,128)S(1)} fusion(f32[3,768]{0,1:T(8,128)S(1)} %get-tuple-element.578, s32[4096]{0:T(1024)S(1)} %broadcast_clamp_fusion.5), kind=kCustom, calls=%fused_computation.2.clone.clone.1 | custom fusion | bytes 114688 | tf_op jit(solution)/shard_map/while/body/eval_jaxpr/gather | solution.py:198
  515.1 73.2 %all-reduce = (f32[16,128]{1,0:T(8,128)S(1)}, f32[128,64]{0,1:T(8,128)S(1)}, f32[6,64]{1,0:T(8,128)S(1)}) all-reduce(f32[16,128]{1,0:T(8,128)S(1)} %get-tuple-element.234, f32[128,64]{0,1:T(8,128)S(1)} %fusion.44, f32[6,64]{1,0:T(8,128)S(1)} %fusion.40), channel_id=1, replica_groups=mesh['dom'=16,'cell'=2] {'dom'}, use_global_device_ids=true, to_apply=%region_10.11 | all-reduce | flops 10624 | bytes 84992 | tf_op jit(solution)/shard_map/psum | solution.py:216
  594.0 96.8 %all-reduce.3.cloned.1.call-done = f32[128,128]{1,0:T(8,128)} async-done(((f32[128,128]{1,0:T(8,128)}), f32[128,128]{1,0:T(8,128)}) %all-reduce.3.cloned.1.call-update) | async-done | bytes 65552 | tf_op jit(solution)/shard_map/psum | solution.py:216
  (200 shorter events, 58.4 us)
Async XLA Ops:
  7.2 140.8 %copy-start = (bf16[128,128]{1,0:T(8,128)(2,1)S(1)}, bf16[128,128]{1,0:T(8,128)(2,1)}, u32[]{:S(2)}) copy-start(bf16[128,128]{1,0:T(8,128)(2,1)} %param.26) | copy-start | bytes 98308
  7.2 21.6 %copy-start.8 = (f32[3,256]{1,0:T(4,128)S(1)}, f32[3,256]{1,0:T(4,128)}, u32[]{:S(2)}) copy-start(f32[3,256]{1,0:T(4,128)} %param.18) | copy-start | bytes 9220
  7.2 21.7 %copy-start.20 = (s32[256]{0:T(256)S(1)}, s32[256]{0:T(256)}, u32[]{:S(2)}) copy-start(s32[256]{0:T(256)} %param.20) | copy-start | bytes 3076
  7.2 21.8 %copy-start.9 = (s32[256,64]{0,1:T(8,128)S(1)}, s32[256,64]{0,1:T(8,128)}, u32[]{:S(2)}) copy-start(s32[256,64]{0,1:T(8,128)} %param.19) | copy-start | bytes 196612
  7.2 223.3 %reduce-scatter.7.cloned.1.call-start = ((), (), s32[]{:S(2)}) async-start(), calls=%async_computation.3 | async-start | bytes 557056 | tf_op jit(solution)/shard_map/reduce_scatter | solution.py:150
  8.0 23.1 %copy-start.5 = (bf16[256,128]{1,0:T(8,128)(2,1)S(1)}, bf16[256,128]{1,0:T(8,128)(2,1)}, u32[]{:S(2)}) copy-start(bf16[256,128]{1,0:T(8,128)(2,1)} %param.17) | copy-start | bytes 196612
  9.9 21.1 %copy-start.7 = (f32[3]{0:T(128)S(1)}, f32[3]{0:T(128)}, u32[]{:S(2)}) copy-start(f32[3]{0:T(128)} %constant.198) | copy-start | bytes 40
  10.0 21.1 %copy-start.12 = (f32[3]{0:T(128)S(1)}, f32[3]{0:T(128)}, u32[]{:S(2)}) copy-start(f32[3]{0:T(128)} %constant.197.clone..sunk.5) | copy-start | bytes 40
  10.0 21.1 %copy-start.21 = (bf16[16,128]{1,0:T(8,128)(2,1)S(1)}, bf16[16,128]{1,0:T(8,128)(2,1)}, u32[]{:S(2)}) copy-start(bf16[16,128]{1,0:T(8,128)(2,1)} %param.25) | copy-start | bytes 12292
  10.0 21.0 %collective-permute-start.2 = (bf16[1,256,128]{2,1,0:T(8,128)(2,1)S(1)}, bf16[1,256,128]{2,1,0:T(8,128)(2,1)S(1)}, u32[]{:S(2)}, u32[]{:S(2)}) collective-permute-start(bf16[1,256,128]{2,1,0:T(8,128)(2,1)S(1)} %get-tuple-element.405), channel_id=1, source_target_pairs={{0,2},{2,4},{4,6},{6,8},{8,10},{10,12},{12,14},{14,16},{16,18},{18... | collective-permute-start | bytes 196616 | tf_op jit(solution)/shard_map/ppermute | solution.py:21
  13.0 18.0 %collective-permute-start.3 = (bf16[1,256,128]{2,1,0:T(8,128)(2,1)S(1)}, bf16[1,256,128]{2,1,0:T(8,128)(2,1)S(1)}, u32[]{:S(2)}, u32[]{:S(2)}) collective-permute-start(bf16[1,256,128]{2,1,0:T(8,128)(2,1)S(1)} %get-tuple-element.406), channel_id=1, source_target_pairs={{2,0},{4,2},{6,4},{8,6},{10,8},{12,10},{14,12},{16,14},{18,16},{20... | collective-permute-start | bytes 196616 | tf_op jit(solution)/shard_map/ppermute | solution.py:22
  19.4 9.7 %collective-permute-start.1 = (f32[1,3,256]{1,2,0:T(8,128)S(1)}, f32[1,3,256]{1,2,0:T(8,128)S(1)}, u32[]{:S(2)}, u32[]{:S(2)}) collective-permute-start(f32[1,3,256]{1,2,0:T(8,128)S(1)} %bitcast.153), channel_id=1, source_target_pairs={{2,0},{4,2},{6,4},{8,6},{10,8},{12,10},{14,12},{16,14},{18,16},{20... | collective-permute-start | bytes 9224 | tf_op jit(solution)/shard_map/ppermute | solution.py:22
  22.1 8.6 %collective-permute-start = (f32[1,3,256]{1,2,0:T(8,128)S(1)}, f32[1,3,256]{1,2,0:T(8,128)S(1)}, u32[]{:S(2)}, u32[]{:S(2)}) collective-permute-start(f32[1,3,256]{1,2,0:T(8,128)S(1)} %bitcast.154), channel_id=1, source_target_pairs={{0,2},{2,4},{4,6},{6,8},{8,10},{10,12},{12,14},{14,16},{16,18},{18... | collective-permute-start | bytes 9224 | tf_op jit(solution)/shard_map/ppermute | solution.py:21
  31.1 117.7 %copy-start.14 = (bf16[128,64]{0,1:T(8,128)(2,1)S(1)}, bf16[128,64]{0,1:T(8,128)(2,1)}, u32[]{:S(2)}) copy-start(bf16[128,64]{0,1:T(8,128)(2,1)} %param.27) | copy-start | bytes 49156
  31.1 117.8 %copy-start.17 = (s32[256]{0:T(256)S(1)}, s32[256]{0:T(256)}, u32[]{:S(2)}) copy-start(s32[256]{0:T(256)} %param.22) | copy-start | bytes 3076
  31.1 117.8 %copy-start.18 = (f32[6,64]{1,0:T(8,128)S(1)}, f32[6,64]{1,0:T(8,128)}, u32[]{:S(2)}) copy-start(f32[6,64]{1,0:T(8,128)} %param.28) | copy-start | bytes 4612
  147.4 0.6 copy-start.19
  147.4 5.4 copy-start.10
  147.4 4.2 copy-start.2
  151.6 2.3 copy-start.6
  153.9 117.5 %copy-start.1 = (f32[1024,256]{1,0:T(8,128)S(1)}, f32[1024,256]{1,0:T(8,128)}, u32[]{:S(2)}) copy-start(f32[1024,256]{1,0:T(8,128)} %get-tuple-element.403) | copy-start | bytes 3145732
  153.9 199.5 %reduce-scatter.9.cloned.1.call-start = ((), (), s32[]{:S(2)}) async-start(), calls=%async_computation.4 | async-start | bytes 557056 | tf_op jit(solution)/shard_map/reduce_scatter | solution.py:166
  271.3 1.6 copy-start.16
  273.0 3.5 copy-start.13
  274.1 2.4 copy-start.3
  279.4 411.5 %all-reduce.3.cloned.1.call-start = ((), (), s32[]{:S(2)}) async-start(), calls=%async_computation.2 | async-start | bytes 131072 | tf_op jit(solution)/shard_map/psum | solution.py:216
  279.4 2.4 copy-start.4
  354.2 41.5 %copy-start.15 = (bf16[128,64]{0,1:T(8,128)(2,1)S(1)}, bf16[128,64]{0,1:T(8,128)(2,1)}, u32[]{:S(2)}) copy-start(bf16[128,64]{0,1:T(8,128)(2,1)} %param.27) | copy-start | bytes 49156
  354.2 41.5 %copy-start.22 = (f32[256,128]{1,0:T(8,128)S(1)}, f32[256,128]{1,0:T(8,128)}, u32[]{:S(2)}) copy-start(f32[256,128]{1,0:T(8,128)} %get-tuple-element.410) | copy-start | bytes 393220
  393.1 2.8 copy-start.11
Sparse Core Ops, SparseCore 0:
  154.0 76.4 reduce-scatter.6
  279.5 73.8 reduce-scatter.8
  592.9 97.8 all-reduce.2
where the time goes:
time: 702 us; the launch traced here: 701 us
  waiting for transfers between devices  245 us (35%)
  local copies, waits for them, and re-layouts  223 us (32%)
  blocking collectives  151 us (22%)
  matrix products  41.7 us (6%)
  between operations  17 us (2%)
  other arithmetic  13.1 us (2%)
  starting transfers between devices  9.29 us (1%)
    psum x1, waiting for transfers between devices, on_device(): lax.psum((radial_sum, mix_sum, charge_sum, species_sum), 'dom')  96.8 us
    reduce_scatter x1, waiting for transfers between devices, on_device(): lax.psum_scatter(jnp.concatenate([contract_first(cosines, charges), contr...  76.4 us
    psum x1, blocking collectives, on_device(): lax.psum((radial_sum, mix_sum, charge_sum, species_sum), 'dom')  73.2 us
    reduce_scatter x1, waiting for transfers between devices, on_device(): lax.psum_scatter(jnp.concatenate([contract_first(slopes * sines, charges)...  70.4 us
    gather x4, local copies, waits for them, and re-layouts, radial_block(): feature_table[slot_rows].astype(jnp.float32)  59.7 us
    gather x4, local copies, waits for them, and re-layouts, message_block(): feature_table[slot_rows].astype(jnp.float32)  59.6 us
    gather x8, local copies, waits for them, and re-layouts, radial_block(): coords_all[:, slot_rows]  45.8 us
    gather x8, local copies, waits for them, and re-layouts, message_block(): coords_all[:, slot_rows]  45.8 us
  transfers between devices with their start and end apart: 7, of which 4 were waited for; matrix products, arithmetic and copies ran while one was open for 2% of the time, Pallas kernels for 0%

commit v1 on v0

v1 whole, which is shorter than its diff:
```python
import math

import jax
import jax.numpy as jnp
import numpy as np
from jax import lax
from jax.experimental import pallas as pl
from jax.experimental.pallas import tpu as pltpu
from jax.sharding import PartitionSpec as P

cutoff_radius = 5.0
kernel_width = 1.0
basis_width = 0.5
box_side = 20.0
two_pi = 6.283185307179586
highest = lax.Precision.HIGHEST
f32 = jnp.float32
bf16 = jnp.bfloat16
vmem_limit = 56 * 1024 * 1024


def fitted(function, degrees, reach):
    nodes = reach * np.cos((np.arange(400) + 0.5) * np.pi / 400)
    powers = np.stack([nodes**d for d in degrees], axis=1)
    return [float(c) for c in np.linalg.lstsq(powers, function(nodes), rcond=None)[0]]


sine_terms = fitted(lambda x: np.sin(np.pi * x), (1, 3, 5, 7, 9), 0.5)
cosine_terms = fitted(lambda x: np.cos(np.pi * x), (0, 2, 4, 6, 8), 0.5)


def horner(terms, square):
    value = terms[-1]
    for term in terms[-2::-1]:
        value = value * square + term
    return value


def matmul(left, right, precision=None):
    return lax.dot_general(
        left, right, (((1,), (0,)), ((), ())), precision=precision, preferred_element_type=f32
    )


def matmul_nt(left, right, precision=None):
    return lax.dot_general(
        left, right, (((1,), (1,)), ((), ())), precision=precision, preferred_element_type=f32
    )


def turned(value):
    return jnp.transpose(value.astype(f32)).astype(value.dtype)


def sigmoid(value):
    return 1.0 / (1.0 + jnp.exp(-value))


def edge_kernel(
    where_ref,
    feat_ref,
    low_ref,
    up_ref,
    small_ref,
    slots_ref,
    count_ref,
    species_ref,
    radial_ref,
    mix_ref,
    charge_ref,
    offset_ref,
    filtered_ref,
    messages_ref,
    before_ref,
    hidden_ref,
    charges_ref,
    words_ref,
    coords_ref,
    table_ref,
    pair_ref,
    *,
    box_x,
):
    atoms, width = feat_ref.shape
    slots = slots_ref.shape[1]
    basis_count = radial_ref.shape[0]
    low, own, up = where_ref[0], where_ref[1], where_ref[2]
    ghosts = atoms
    entries = atoms + 2 * ghosts
    own_rows = small_ref[own]
    site = lax.broadcasted_iota(jnp.int32, (atoms, ghosts), 0)

    own_feat = turned(feat_ref[...])
    table_ref[:, 0:atoms] = own_feat
    coords_ref[0:atoms, :] = jnp.transpose(own_rows)
    for place, ref, side, row in ((0, low_ref, low, 7), (1, up_ref, up, 6)):
        rows = small_ref[side]
        chosen = (site.astype(f32) == rows[row : row + 1, :]).astype(bf16)
        first = atoms + place * ghosts
        table_ref[:, first : first + ghosts] = matmul(turned(ref[...]), chosen).astype(bf16)
        part = rows.astype(bf16)
        rest = rows - part.astype(f32)
        second = rest.astype(bf16)
        third = (rest - second.astype(f32)).astype(bf16)
        moved = matmul(part, chosen) + (matmul(second, chosen) + matmul(third, chosen))
        coords_ref[first : first + ghosts, :] = jnp.transpose(moved)

    listed = jnp.transpose(slots_ref[...])
    live = lax.broadcasted_iota(jnp.int32, (slots, atoms), 0) < count_ref[...]
    word_of = jnp.where(live, listed >> 5, -1)
    bit = jnp.left_shift(jnp.ones_like(listed), listed & 31)
    for word in range(entries // 32):
        value = jnp.where(word_of == word, bit, 0)
        rows = slots
        while rows > 1:
            rows //= 2
            value = value[:rows] | value[rows:]
        words_ref[word : word + 1, :] = value

    centers = [
        0.5 + (cutoff_radius - 0.5) * float(b) / (basis_count - 1) for b in range(basis_count)
    ]
    scale = -math.log2(math.e) / (basis_width * basis_width)
    own_x, own_y, own_z = own_rows[0:1, :], own_rows[1:2, :], own_rows[2:3, :]
    step = 32

    def block(index, carry):
        first = pl.multiple_of(index * step, step)
        coords = coords_ref[pl.ds(first, step), :]
        total = jnp.zeros((step, atoms), f32)
        for axis, (mine, length) in enumerate(
            ((own_x, box_x), (own_y, box_side), (own_z, box_side))
        ):
            away = coords[:, axis : axis + 1] - mine
            away = away - length * jnp.floor(away * (1.0 / length) + 0.5)
            total = total + away * away
        distance = jnp.sqrt(total)
        word = words_ref[pl.ds(index, 1), :]
        sublane = lax.broadcasted_iota(jnp.int32, (step, atoms), 0)
        is_live = (jnp.right_shift(jnp.broadcast_to(word, (step, atoms)), sublane) & 1) != 0
        half = jnp.minimum(distance, cutoff_radius) * (1.0 / cutoff_radius) - 0.5
        fade = 0.5 - 0.5 * (half * horner(sine_terms, half * half))
        weight = jnp.where(is_live, fade, 0.0)
        for b in range(basis_count):
            offset = distance - centers[b]
            basis = jnp.exp2(offset * offset * scale).astype(bf16).astype(f32)
            pair_ref[b, pl.ds(first, step), :] = (weight * basis).astype(bf16)
        return carry

    lax.fori_loop(0, entries // step, block, 0)

    radial = jnp.transpose(radial_ref[...].astype(f32))
    messages = jnp.zeros((width, atoms), f32)
    for b in range(basis_count):
        filtered = matmul(table_ref[...], pair_ref[b])
        filtered_ref[b] = filtered
        messages = messages + radial[:, b : b + 1] * filtered
    messages = messages.astype(bf16)
    messages_ref[...] = messages
    before = matmul(turned(mix_ref[...]), messages)
    before_ref[...] = before
    hidden = (own_feat.astype(f32) + before * sigmoid(before)).astype(bf16)
    hidden_ref[...] = hidden
    kinds = offset_ref.shape[0]
    one_hot = (
        lax.broadcasted_iota(jnp.int32, (kinds, atoms), 0) == species_ref[...]
    ).astype(f32)
    charges = matmul(turned(charge_ref[...]), hidden) + matmul(
        jnp.transpose(offset_ref[...]), one_hot, highest
    )
    rounded = charges.astype(bf16)
    for copy in range(charges_ref.shape[0]):
        charges_ref[copy] = rounded


def wave_rows(wave_ref, first, count, box_x, total_atoms):
    index = wave_ref[:, pl.ds(first, count)].astype(f32)
    scales = (two_pi / box_x, two_pi / box_side, two_pi / box_side)
    waves = [index[a : a + 1, :] * scales[a] for a in range(3)]
    squares = waves[0] * waves[0] + waves[1] * waves[1] + waves[2] * waves[2]
    damping = jnp.exp(-0.5 * kernel_width * kernel_width * squares) * (1.0 / total_atoms)
    return index, waves, damping


def structure_kernel(
    where_ref,
    small_ref,
    charges_ref,
    wave_ref,
    cos_ref,
    sin_ref,
    field_ref,
    forces_ref,
    *,
    box_x,
):
    domains, charge_count, atoms = charges_ref.shape
    share = cos_ref.shape[1]
    group = forces_ref.shape[0]
    first = pl.multiple_of(where_ref[3] * share, share)
    index, waves, damping = wave_rows(wave_ref, first, share, box_x, domains * atoms)
    columns = jnp.transpose(jnp.concatenate([index, jnp.zeros((5, share), f32)], axis=0))
    lengths = (box_x, box_side, box_side)

    def gather(d, carry):
        rows = small_ref[d]
        turns = jnp.zeros((share, atoms), f32)
        for a in range(3):
            turns = turns + columns[:, a : a + 1] * (rows[a : a + 1, :] * (1.0 / lengths[a]))
        turns = turns - jnp.floor(turns + 0.5)
        square = turns * turns
        half_sine = turns * horner(sine_terms, square)
        half_cosine = horner(cosine_terms, square)
        cosine = (1.0 - 2.0 * half_sine * half_sine).astype(bf16)
        sine = (2.0 * half_sine * half_cosine).astype(bf16)
        cos_ref[d] = cosine
        sin_ref[d] = sine
        charges = charges_ref[d]
        return carry[0] + matmul_nt(charges, cosine), carry[1] + matmul_nt(charges, sine)

    zero = jnp.zeros((charge_count, share), f32)
    along_cos, along_sin = lax.fori_loop(0, domains, gather, (zero, zero))
    along_cos = along_cos * damping
    along_sin = along_sin * damping
    to_sine = jnp.concatenate([along_cos * waves[a] for a in range(3)], axis=0).astype(bf16)
    to_cosine = jnp.concatenate([-along_sin * waves[a] for a in range(3)], axis=0).astype(bf16)
    quad_first = where_ref[4]

    def force(d, carry):
        field = matmul(to_sine, sin_ref[d]) + matmul(to_cosine, cos_ref[d])
        charges = charges_ref[d].astype(f32)
        inside = jnp.logical_and(d >= quad_first, d < quad_first + group)

        @pl.when(inside)
        def _():
            field_ref[d - quad_first] = field

        for a in range(3):
            row = jnp.sum(
                field[a * charge_count : (a + 1) * charge_count, :] * charges,
                axis=0,
                keepdims=True,
            )
            for copy in range(group):
                forces_ref[copy, a, pl.ds(d, 1), :] = row
        return carry

    lax.fori_loop(0, domains, force, 0)


def gradient_kernel(
    where_ref,
    small_ref,
    charges_ref,
    wave_ref,
    cos_ref,
    sin_ref,
    field_ref,
    parts_ref,
    forces_ref,
    grad_ref,
    total_ref,
    *,
    box_x,
):
    domains, charge_count, atoms = charges_ref.shape
    share = cos_ref.shape[1]
    group = parts_ref.shape[0]
    first = pl.multiple_of(where_ref[3] * share, share)
    _, waves, damping = wave_rows(wave_ref, first, share, box_x, domains * atoms)
    total = parts_ref[0]
    for part in range(1, group):
        total = total + parts_ref[part]
    total_ref[...] = total
    own = where_ref[1]
    for a in range(3):
        forces_ref[a : a + 1, :] = total_ref[a, pl.ds(own, 1), :]

    def errors_of(d):
        rows = small_ref[d]
        return [2.0 * (total_ref[a, pl.ds(d, 1), :] - rows[3 + a : 4 + a, :]) for a in range(3)]

    def gather(d, carry):
        charges = charges_ref[d].astype(f32)
        errors = errors_of(d)
        scaled = jnp.concatenate([errors[a] * charges for a in range(3)], axis=0).astype(bf16)
        return carry[0] + matmul_nt(scaled, sin_ref[d]), carry[1] + matmul_nt(scaled, cos_ref[d])

    zero = jnp.zeros((3 * charge_count, share), f32)
    by_sine, by_cosine = lax.fori_loop(0, domains, gather, (zero, zero))

    def along(value):
        return sum(
            waves[a] * value[a * charge_count : (a + 1) * charge_count, :] for a in range(3)
        )

    back_cos = (damping * along(by_sine)).astype(bf16)
    back_sin = (-damping * along(by_cosine)).astype(bf16)
    quad_first = where_ref[4]
    for member in range(group):
        d = quad_first + member
        errors = errors_of(d)
        grad = matmul(back_cos, cos_ref[d]) + matmul(back_sin, sin_ref[d])
        for a in range(3):
            grad = grad + errors[a] * field_ref[
                member, a * charge_count : (a + 1) * charge_count, :
            ]
        grad_ref[member] = grad


def weights_kernel(
    parts_ref,
    filtered_ref,
    messages_ref,
    before_ref,
    hidden_ref,
    species_ref,
    mix_ref,
    charge_ref,
    packed_ref,
    *,
    kinds,
):
    group, charge_count, atoms = parts_ref.shape
    basis_count, width, _ = filtered_ref.shape
    grad = parts_ref[0]
    for part in range(1, group):
        grad = grad + parts_ref[part]
    rounded = grad.astype(bf16)
    before = before_ref[...]
    gate = sigmoid(before)
    upstream = matmul(charge_ref[...], rounded)
    before_grad = (upstream * (gate * (1.0 + before * (1.0 - gate)))).astype(bf16)
    message_grad = matmul(mix_ref[...], before_grad).astype(bf16).astype(f32)
    packed_ref[...] = jnp.zeros_like(packed_ref)
    columns = [
        jnp.sum(message_grad * filtered_ref[b], axis=1, keepdims=True) for b in range(basis_count)
    ]
    radial = jnp.concatenate(columns, axis=1)
    row = 0
    packed_ref[row : row + basis_count, :] = jnp.transpose(radial)
    row += basis_count
    packed_ref[row : row + width, :] = matmul_nt(messages_ref[...], before_grad)
    row += width
    packed_ref[row : row + charge_count, :] = matmul_nt(rounded, hidden_ref[...])
    row += charge_count
    one_hot = (
        lax.broadcasted_iota(jnp.int32, (kinds, atoms), 0) == species_ref[...]
    ).astype(f32)
    packed_ref[row : row + kinds, 0:charge_count] = matmul_nt(one_hot, grad, highest)


def step_kernel(total_ref, radial_ref, mix_ref, charge_ref, species_ref):
    basis_count, width = radial_ref.shape
    charge_count = charge_ref.shape[1]
    kinds = species_ref.shape[0]

    def normalized(gradient):
        mean = jnp.sum(gradient * gradient, keepdims=True) * (1.0 / gradient.size)
        return gradient * lax.rsqrt(mean + 1e-06)

    row = 0
    radial_ref[...] = normalized(total_ref[row : row + basis_count, :])
    row += basis_count
    mix_ref[...] = normalized(total_ref[row : row + width, :])
    row += width
    charge_ref[...] = normalized(jnp.transpose(total_ref[row : row + charge_count, :]))
    row += charge_count
    species_ref[...] = normalized(total_ref[row : row + kinds, 0:charge_count])


def in_smem():
    return pl.BlockSpec(memory_space=pltpu.SMEM)


def in_vmem(count):
    return [pl.BlockSpec(memory_space=pltpu.VMEM) for _ in range(count)]


def shaped(*dims, kind=f32):
    return jax.ShapeDtypeStruct(dims, kind)


def on_device(
    features,
    positions,
    neighbours,
    neighbour_count,
    ghost_sends,
    species,
    wave_index,
    force_ref,
    radial_weight,
    mix_weight,
    charge_weight,
    species_charge,
):
    atoms, width = features.shape
    basis_count = radial_weight.shape[0]
    charge_count = charge_weight.shape[1]
    kinds = species_charge.shape[0]
    wave_count = wave_index.shape[1]
    domains = lax.axis_size("dom")
    box_x = 1.25 * (atoms * domains) / 64
    group = 4 if domains % 4 == 0 else 1
    share = wave_count // group
    quads = [[group * q + m for m in range(group)] for q in range(domains // group)]
    entries = atoms + 2 * ghost_sends.shape[1]
    params = pltpu.CompilerParams(vmem_limit_bytes=vmem_limit)

    me = lax.axis_index("dom")
    where = jnp.stack(
        [
            (me + domains - 1) % domains,
            me,
            (me + 1) % domains,
            me % group,
            me // group * group,
        ]
    ).astype(jnp.int32)
    small = jnp.concatenate([positions, force_ref, ghost_sends.astype(f32)], axis=0)
    upward = [(i, (i + 1) % domains) for i in range(domains)]
    downward = [(j, i) for i, j in upward]
    from_low = lax.ppermute(features, "dom", upward)
    from_up = lax.ppermute(features, "dom", downward)
    small_all = lax.all_to_all(
        jnp.broadcast_to(small[None], (domains,) + small.shape), "dom", 0, 0
    )
    species_row = species[None, :]

    filtered, messages, before, hidden, charges = pl.pallas_call(
        lambda *refs: edge_kernel(*refs, box_x=box_x),
        out_shape=(
            shaped(basis_count, width, atoms),
            shaped(width, atoms, kind=bf16),
            shaped(width, atoms),
            shaped(width, atoms, kind=bf16),
            shaped(domains, charge_count, atoms, kind=bf16),
        ),
        in_specs=[in_smem()] + in_vmem(11),
        out_specs=tuple(in_vmem(5)),
        scratch_shapes=[
            pltpu.VMEM((entries // 32, atoms), jnp.int32),
            pltpu.VMEM((entries, small.shape[0]), f32),
            pltpu.VMEM((width, entries), bf16),
            pltpu.VMEM((basis_count, entries, atoms), bf16),
        ],
        compiler_params=params,
        name="edges",
    )(
        where,
        features,
        from_low,
        from_up,
        small_all,
        neighbours,
        neighbour_count[None, :],
        species_row,
        radial_weight,
        mix_weight,
        charge_weight,
        species_charge,
    )
    charges_all = lax.all_to_all(charges, "dom", 0, 0)

    cosines, sines, field, force_parts = pl.pallas_call(
        lambda *refs: structure_kernel(*refs, box_x=box_x),
        out_shape=(
            shaped(domains, share, atoms, kind=bf16),
            shaped(domains, share, atoms, kind=bf16),
            shaped(group, 3 * charge_count, atoms),
            shaped(group, 3, domains, atoms),
        ),
        in_specs=[in_smem()] + in_vmem(3),
        out_specs=tuple(in_vmem(4)),
        compiler_params=params,
        name="structure",
    )(where, small_all, charges_all, wave_index)
    force_parts = lax.all_to_all(force_parts, "dom", 0, 0, axis_index_groups=quads)

    forces, grad_parts = pl.pallas_call(
        lambda *refs: gradient_kernel(*refs, box_x=box_x),
        out_shape=(shaped(3, atoms), shaped(group, charge_count, atoms)),
        in_specs=[in_smem()] + in_vmem(7),
        out_specs=tuple(in_vmem(2)),
        scratch_shapes=[pltpu.VMEM((3, domains, atoms), f32)],
        compiler_params=params,
        name="gradient",
    )(where, small_all, charges_all, wave_index, cosines, sines, field, force_parts)
    grad_parts = lax.all_to_all(grad_parts, "dom", 0, 0, axis_index_groups=quads)

    rows = basis_count + width + charge_count + kinds
    rows = -(-rows // (8 * domains)) * (8 * domains)
    packed = pl.pallas_call(
        lambda *refs: weights_kernel(*refs, kinds=kinds),
        out_shape=shaped(rows, width),
        in_specs=in_vmem(8),
        out_specs=in_vmem(1)[0],
        compiler_params=params,
        name="weights",
    )(
        grad_parts,
        filtered,
        messages,
        before,
        hidden,
        species_row,
        mix_weight,
        charge_weight,
    )
    pieces = lax.all_to_all(packed.reshape(domains, rows // domains, width), "dom", 0, 0)
    piece = jnp.sum(pieces, axis=0)
    total = lax.all_to_all(jnp.broadcast_to(piece[None], pieces.shape), "dom", 0, 0)
    steps = pl.pallas_call(
        step_kernel,
        out_shape=(
            shaped(basis_count, width),
            shaped(width, width),
            shaped(width, charge_count),
            shaped(kinds, charge_count),
        ),
        in_specs=in_vmem(1),
        out_specs=tuple(in_vmem(4)),
        compiler_params=params,
        name="steps",
    )(total.reshape(rows, width))
    return (forces, *steps)


def solution(mesh):
    placed = (
        P(("cell", "dom"), None),
        P(None, ("cell", "dom")),
        P(("cell", "dom"), None),
        P(("cell", "dom")),
        P(None, ("cell", "dom")),
        P(("cell", "dom")),
        P(),
        P(None, ("cell", "dom")),
        P(),
        P(),
        P(),
        P(),
    )
    return jax.shard_map(
        on_device,
        mesh=mesh,
        in_specs=placed,
        out_specs=(
            P(None, ("cell", "dom")),
            P("cell", None),
            P("cell", None),
            P("cell", None),
            P("cell", None),
        ),
        check_vma=False,
    )
```

time: 702 us -> 123 us (0.18)
  waiting for transfers between devices: 245 us -> 0.01 us
  local copies, waits for them, and re-layouts: 223 us -> 6.58 us
  blocking collectives: 151 us -> 61.1 us
  matrix products: 41.7 us -> 0 us
  Pallas kernels: 0 us -> 38.7 us
  between operations: 17 us -> 0.69 us
  other arithmetic: 13.1 us -> 1.42 us
    gather x27 -> x0, local copies, waits for them, and re-layouts: 214 us -> none  [the longest x4 59.7 us: radial_block(): feature_table[slot_rows].astype(jnp.float32)]
    reduce_scatter x2 -> x0, waiting for transfers between devices: 147 us -> none  [the longest x1 76.4 us: on_device(): lax.psum_scatter(jnp.concatenate([contract_first(cosines, charges), contr...]
    psum x1 -> x0, waiting for transfers between devices: 96.8 us -> none  [on_device(): lax.psum((radial_sum, mix_sum, charge_sum, species_sum), 'dom')]
    all_gather x2 -> x0, blocking collectives: 77.9 us -> none  [the longest x1 39 us: on_device(): coeff_piece = lax.all_gather(coeff_part, 'dom', axis=0, tiled=True)]
    psum x1 -> x0, blocking collectives: 73.2 us -> none  [on_device(): lax.psum((radial_sum, mix_sum, charge_sum, species_sum), 'dom')]
    all_to_all x0 -> x5, blocking collectives: none -> 61.1 us  [the longest x1 19.3 us: on_device(): charges_all = lax.all_to_all(charges, 'dom', 0, 0)]
    dot_general x29 -> x0, matrix products: 41.7 us -> none  [the longest x13 22.8 us: contract_first(): lax.dot_general(left, right, (((0,), (0,)), ((), ())), precision=highest,...]
    pallas_call x0 -> x5, Pallas kernels: none -> 38.7 us  [the longest x1 15.3 us: on_device(): pl.pallas_call(lambda *refs: structure_kernel(*refs, box_x=box_x), out_sh...]
  transfers between devices with their start and end apart: 7 -> 3, of which waited for: 4 -> 0; matrix products, arithmetic and copies ran while one was open for 2% -> 3% of each run, Pallas kernels for 0% -> 0%
where the time goes in v1:
time: 123 us
  blocking collectives  61.1 us (50%)
  Pallas kernels  38.7 us (31%)
  starting transfers between devices  14 us (11%)
  local copies, waits for them, and re-layouts  6.58 us (5%)
  other arithmetic  1.42 us (1%)
    all_to_all x1, blocking collectives, on_device(): charges_all = lax.all_to_all(charges, 'dom', 0, 0)  19.3 us
    pallas_call x1, Pallas kernels, on_device(): pl.pallas_call(lambda *refs: structure_kernel(*refs, box_x=box_x), out_sh...  15.3 us
    all_to_all x1, blocking collectives, on_device(): lax.all_to_all(packed.reshape(domains, rows // domains, width), 'dom', 0, 0)  11.3 us
    all_to_all x1, blocking collectives, on_device(): lax.all_to_all(jnp.broadcast_to(piece[None], pieces.shape), 'dom', 0, 0)  11.1 us
    pallas_call x1, Pallas kernels, on_device(): pl.pallas_call(lambda *refs: edge_kernel(*refs, box_x=box_x), out_shape=(...  10.5 us
    all_to_all x1, blocking collectives, on_device(): lax.all_to_all(grad_parts, 'dom', 0, 0, axis_index_groups=quads)  9.83 us
    all_to_all x1, blocking collectives, on_device(): lax.all_to_all(force_parts, 'dom', 0, 0, axis_index_groups=quads)  9.6 us
    all_to_all x1, starting transfers between devices, on_device(): lax.all_to_all(jnp.broadcast_to(small[None], (domains,) + small.shape), '...  8.31 us
  transfers between devices with their start and end apart: 3, of which 0 were waited for; matrix products, arithmetic and copies ran while one was open for 3% of the time, Pallas kernels for 0%

profile of v1, /device:TPU:0, one launch (start us, length us, event | category | flops | bytes accessed | tf_op | source)
XLA Modules:
  0.0 122.5 jit_solution(15384665677371414963)
XLA Ops:
  0.6 0.7 convert_element_type.3
  1.3 0.7 pad_maximum_fusion
  2.0 0.7 broadcast_in_dim.8
  2.7 8.3 %all-to-all-start = ((f32[16,8,256]{2,1,0:T(8,128)}), f32[16,8,256]{2,1,0:T(8,128)S(1)}, u32[]{:S(2)}, u32[]{:S(2)}) async-start(f32[16,8,256]{2,1,0:T(8,128)} %broadcast_in_dim.8), calls=%async_computation | async-start | bytes 262144 | tf_op jit(solution)/shard_map/all_to_all | solution.py:426
  11.0 1.9 %collective-permute-start = (bf16[256,128]{1,0:T(8,128)(2,1)}, bf16[256,128]{1,0:T(8,128)(2,1)S(1)}, u32[]{:S(2)}, u32[]{:S(2)}) collective-permute-start(bf16[256,128]{1,0:T(8,128)(2,1)} %refs_1_.1), channel_id=1, source_target_pairs={{0,2},{2,4},{4,6},{6,8},{8,10},{10,12},{12,14},{14,16},{16,18},{18... | collective-permute-start | bytes 196616 | tf_op jit(solution)/shard_map/ppermute | solution.py:424
  12.9 3.7 %collective-permute-start.1 = (bf16[256,128]{1,0:T(8,128)(2,1)}, bf16[256,128]{1,0:T(8,128)(2,1)S(1)}, u32[]{:S(2)}, u32[]{:S(2)}) collective-permute-start(bf16[256,128]{1,0:T(8,128)(2,1)} %refs_1_.1), channel_id=1, source_target_pairs={{2,0},{4,2},{6,4},{8,6},{10,8},{12,10},{14,12},{16,14},{18,16},{20... | collective-permute-start | bytes 196616 | tf_op jit(solution)/shard_map/ppermute | solution.py:425
  16.7 1.4 %copy.18.refs_10_.refs_7_ = bf16[128,64]{1,0:T(8,128)(2,1)} copy(bf16[128,64]{0,1:T(8,128)(2,1)} %param.22) | data formatting | bytes 32768 | tf_op args[10]
  18.1 1.6 %copy.17.refs_5_ = s32[256,64]{1,0:T(8,128)} copy(s32[256,64]{0,1:T(8,128)} %param.14) | data formatting | bytes 131072 | tf_op args[2]
  19.7 0.7 stack.23.refs_0_
  20.4 0.0 collective-permute-done.refs_2_
  20.4 0.0 copy-start.1
  20.4 0.0 collective-permute-done.1.refs_3_
  20.4 0.0 copy-start.2
  20.4 0.0 all-to-all-done.refs_4_.refs_1_
  20.4 0.0 copy-start
  20.4 0.6 copy-done.1
  21.0 0.0 copy-done.2
  21.0 0.1 copy-done
  21.1 10.5 %edges.1 = (f32[16,128,256]{2,1,0:T(8,128)}, bf16[128,256]{1,0:T(8,128)(2,1)}, f32[128,256]{1,0:T(8,128)}, bf16[128,256]{1,0:T(8,128)(2,1)}, bf16[16,64,256]{2,1,0:T(8,128)(2,1)}) custom-call(s32[5]{0:T(128)} %stack.23.refs_0_, bf16[256,128]{1,0:T(8,128)(2,1)} %refs_1_.1, bf16[256,128]{1,0:T(8,128)(2,1)} %copy-done.1, bf16[256,128]{1,0:T(8,128)(2,1)} %copy-done.2, ...), custom_call_target="tpu_custom_call" | custom-call | tf_op jit(solution)/shard_map/edges/pallas_call | solution.py:431
  31.6 19.3 %all_to_all.30.refs_2_ = bf16[16,64,256]{2,1,0:T(8,128)(2,1)} all-to-all(bf16[16,64,256]{2,1,0:T(8,128)(2,1)} %get-tuple-element.20), channel_id=1, replica_groups=mesh['dom'=16,'cell'=2] {'dom'}, dimensions={0} | all-to-all | bytes 1048576 | tf_op jit(solution)/shard_map/all_to_all | solution.py:464
  50.9 15.3 %structure.1 = (bf16[16,256,256]{2,1,0:T(8,128)(2,1)}, bf16[16,256,256]{2,1,0:T(8,128)(2,1)}, f32[4,192,256]{2,1,0:T(8,128)}, f32[4,3,16,256]{3,2,1,0:T(8,128)}) custom-call(s32[5]{0:T(128)} %stack.23.refs_0_, f32[16,8,256]{2,1,0:T(8,128)} %copy-done, bf16[16,64,256]{2,1,0:T(8,128)(2,1)} %all_to_all.30.refs_2_, s32[3,1024]{1,0:T(4,128)} %refs_3_.3), custom_call_target="tpu_custom_call" | custom-call | tf_op jit(solution)/shard_map/structure/pallas_call | solution.py:466
  66.2 9.6 %all_to_all.31.refs_7_ = f32[4,3,16,256]{3,2,1,0:T(8,128)} all-to-all(f32[4,3,16,256]{3,2,1,0:T(8,128)} %get-tuple-element.24), channel_id=1, replica_groups={{0,2,4,6},{8,10,12,14},{16,18,20,22},{24,26,28,30},{1,3,5,7},{9,11,13,1..., dimensions={0} | all-to-all | bytes 393216 | tf_op jit(solution)/shard_map/all_to_all | solution.py:479
  75.8 8.2 %gradient.1 = (f32[3,256]{1,0:T(4,128)}, f32[4,64,256]{2,1,0:T(8,128)}) custom-call(s32[5]{0:T(128)} %stack.23.refs_0_, f32[16,8,256]{2,1,0:T(8,128)} %copy-done, bf16[16,64,256]{2,1,0:T(8,128)(2,1)} %all_to_all.30.refs_2_, s32[3,1024]{1,0:T(4,128)} %refs_3_.3, bf16[16,256,256]{2,1,0:T(8,128)(2,1)} %get-tuple-element.21.refs_4_, ...), custom_call_target="tpu_custom_call" | custom-call | tf_op jit(solution)/shard_map/gradient/pallas_call | solution.py:481
  84.0 9.8 %all_to_all.32.refs_0_ = f32[4,64,256]{2,1,0:T(8,128)} all-to-all(f32[4,64,256]{2,1,0:T(8,128)} %get-tuple-element.26), channel_id=1, replica_groups={{0,2,4,6},{8,10,12,14},{16,18,20,22},{24,26,28,30},{1,3,5,7},{9,11,13,1..., dimensions={0} | all-to-all | bytes 524288 | tf_op jit(solution)/shard_map/all_to_all | solution.py:490
  93.8 3.0 %weights.1 = f32[256,128]{1,0:T(8,128)} custom-call(f32[4,64,256]{2,1,0:T(8,128)} %all_to_all.32.refs_0_, f32[16,128,256]{2,1,0:T(8,128)} %get-tuple-element.27.refs_1_, bf16[128,256]{1,0:T(8,128)(2,1)} %get-tuple-element.28.refs_2_, f32[128,256]{1,0:T(8,128)} %get-tuple-element.29.refs_3_, bf16[128,256]{1,0:T(8,128)(2,1)} %get-tuple-element.30.refs_4_, ...), custom_call_target="tpu_custom_call" | custom-call | tf_op jit(solution)/shard_map/weights/pallas_call | solution.py:494
  96.8 11.3 %all_to_all.33 = f32[16,16,128]{2,1,0:T(8,128)S(1)} all-to-all(f32[16,16,128]{2,1,0:T(8,128)} %bitcast.9), channel_id=1, replica_groups=mesh['dom'=16,'cell'=2] {'dom'}, dimensions={0} | all-to-all | bytes 262144 | tf_op jit(solution)/shard_map/all_to_all | solution.py:511
  108.2 11.1 %all_to_all.34 = f32[16,16,128]{2,1,0:T(8,128)} all-to-all(f32[16,16,128]{2,1,0:T(8,128)S(1)} %broadcast_in_dim.21), channel_id=1, replica_groups=mesh['dom'=16,'cell'=2] {'dom'}, dimensions={0} | all-to-all | bytes 262144 | tf_op jit(solution)/shard_map/all_to_all | solution.py:513
  119.2 1.8 %steps.1 = (f32[16,128]{1,0:T(8,128)}, f32[128,128]{1,0:T(8,128)}, f32[128,64]{1,0:T(8,128)}, f32[6,64]{1,0:T(8,128)}) custom-call(f32[256,128]{1,0:T(8,128)} %bitcast.10), custom_call_target="tpu_custom_call" | custom-call | tf_op jit(solution)/shard_map/steps/pallas_call | solution.py:514
  121.0 1.5 %copy.20 = f32[128,64]{0,1:T(8,128)} copy(f32[128,64]{1,0:T(8,128)} %get-tuple-element.38) | data formatting | bytes 65536
  (2 shorter events, 0.0 us)
Async XLA Ops:
  2.7 17.7 %all-to-all-start = ((f32[16,8,256]{2,1,0:T(8,128)}), f32[16,8,256]{2,1,0:T(8,128)S(1)}, u32[]{:S(2)}, u32[]{:S(2)}) async-start(f32[16,8,256]{2,1,0:T(8,128)} %broadcast_in_dim.8), calls=%async_computation | async-start | bytes 262144 | tf_op jit(solution)/shard_map/all_to_all | solution.py:426
  11.0 9.4 %collective-permute-start = (bf16[256,128]{1,0:T(8,128)(2,1)}, bf16[256,128]{1,0:T(8,128)(2,1)S(1)}, u32[]{:S(2)}, u32[]{:S(2)}) collective-permute-start(bf16[256,128]{1,0:T(8,128)(2,1)} %refs_1_.1), channel_id=1, source_target_pairs={{0,2},{2,4},{4,6},{6,8},{8,10},{10,12},{12,14},{14,16},{16,18},{18... | collective-permute-start | bytes 196616 | tf_op jit(solution)/shard_map/ppermute | solution.py:424
  12.9 7.5 %collective-permute-start.1 = (bf16[256,128]{1,0:T(8,128)(2,1)}, bf16[256,128]{1,0:T(8,128)(2,1)S(1)}, u32[]{:S(2)}, u32[]{:S(2)}) collective-permute-start(bf16[256,128]{1,0:T(8,128)(2,1)} %refs_1_.1), channel_id=1, source_target_pairs={{2,0},{4,2},{6,4},{8,6},{10,8},{12,10},{14,12},{16,14},{18,16},{20... | collective-permute-start | bytes 196616 | tf_op jit(solution)/shard_map/ppermute | solution.py:425
  20.4 0.6 copy-start.1
  20.4 0.6 copy-start.2
  20.4 0.7 copy-start

commit v2 on v1

--- a/solution.py
+++ b/solution.py
@@ -16,7 +16,7 @@
 highest = lax.Precision.HIGHEST
 f32 = jnp.float32
 bf16 = jnp.bfloat16
-vmem_limit = 56 * 1024 * 1024
+spare_vmem = 8 * 1024 * 1024
 
 
 def fitted(function, degrees, reach):
@@ -82,7 +82,7 @@
     box_x,
 ):
     atoms, width = feat_ref.shape
-    slots = slots_ref.shape[1]
+    slots = slots_ref.shape[0]
     basis_count = radial_ref.shape[0]
     low, own, up = where_ref[0], where_ref[1], where_ref[2]
     ghosts = atoms
@@ -105,7 +105,7 @@
         moved = matmul(part, chosen) + (matmul(second, chosen) + matmul(third, chosen))
         coords_ref[first : first + ghosts, :] = jnp.transpose(moved)
 
-    listed = jnp.transpose(slots_ref[...])
+    listed = slots_ref[...]
     live = lax.broadcasted_iota(jnp.int32, (slots, atoms), 0) < count_ref[...]
     word_of = jnp.where(live, listed >> 5, -1)
     bit = jnp.left_shift(jnp.ones_like(listed), listed & 31)
@@ -155,9 +155,8 @@
         filtered = matmul(table_ref[...], pair_ref[b])
         filtered_ref[b] = filtered
         messages = messages + radial[:, b : b + 1] * filtered
-    messages = messages.astype(bf16)
     messages_ref[...] = messages
-    before = matmul(turned(mix_ref[...]), messages)
+    before = matmul(jnp.transpose(mix_ref[...].astype(f32)), messages, highest)
     before_ref[...] = before
     hidden = (own_feat.astype(f32) + before * sigmoid(before)).astype(bf16)
     hidden_ref[...] = hidden
@@ -165,7 +164,7 @@
     one_hot = (
         lax.broadcasted_iota(jnp.int32, (kinds, atoms), 0) == species_ref[...]
     ).astype(f32)
-    charges = matmul(turned(charge_ref[...]), hidden) + matmul(
+    charges = matmul(charge_ref[...], hidden) + matmul(
         jnp.transpose(offset_ref[...]), one_hot, highest
     )
     rounded = charges.astype(bf16)
@@ -182,70 +181,82 @@
     return index, waves, damping
 
 
+def pieces_of(value):
+    first = value.astype(bf16).astype(f32)
+    rest = value - first
+    second = rest.astype(bf16).astype(f32)
+    return first, second, rest - second
+
+
+def phase_kernel(where_ref, small_ref, wave_ref, waves_ref, *, box_x):
+    domains, _, atoms = small_ref.shape
+    share = waves_ref.shape[0] // 2
+    first = pl.multiple_of(where_ref[3] * share, share)
+    index = wave_ref[:, pl.ds(first, share)].astype(f32)
+    columns = jnp.transpose(
+        jnp.concatenate([index] * 3 + [jnp.zeros((7, share), f32)], axis=0)
+    ).astype(bf16)
+    lengths = (box_x, box_side, box_side)
+    shift = 12582912.0
+
+    def block(d, carry):
+        rows = small_ref[d]
+        turns = jnp.concatenate(
+            [rows[a : a + 1, :] * (1.0 / lengths[a]) for a in range(3)], axis=0
+        )
+        parts = jnp.concatenate(pieces_of(turns) + (jnp.zeros((7, atoms), f32),), axis=0)
+        turns = matmul(columns, parts.astype(bf16))
+        turns = turns - ((turns + shift) - shift)
+        square = turns * turns
+        half_sine = turns * horner(sine_terms, square)
+        half_cosine = horner(cosine_terms, square)
+        place = pl.ds(pl.multiple_of(d * atoms, atoms), atoms)
+        waves_ref[0:share, place] = (2.0 * half_sine * half_cosine).astype(bf16)
+        waves_ref[share : 2 * share, place] = (1.0 - 2.0 * half_sine * half_sine).astype(bf16)
+        return carry
+
+    lax.fori_loop(0, domains, block, 0, unroll=4)
+
+
 def structure_kernel(
     where_ref,
-    small_ref,
     charges_ref,
     wave_ref,
-    cos_ref,
-    sin_ref,
-    field_ref,
+    waves_ref,
+    weights_ref,
     forces_ref,
+    rows_ref,
     *,
     box_x,
 ):
     domains, charge_count, atoms = charges_ref.shape
-    share = cos_ref.shape[1]
+    share = waves_ref.shape[0] // 2
     group = forces_ref.shape[0]
     first = pl.multiple_of(where_ref[3] * share, share)
-    index, waves, damping = wave_rows(wave_ref, first, share, box_x, domains * atoms)
-    columns = jnp.transpose(jnp.concatenate([index, jnp.zeros((5, share), f32)], axis=0))
-    lengths = (box_x, box_side, box_side)
-
-    def gather(d, carry):
-        rows = small_ref[d]
-        turns = jnp.zeros((share, atoms), f32)
+    _, waves, damping = wave_rows(wave_ref, first, share, box_x, domains * atoms)
+    structure = jnp.zeros((charge_count, 2 * share), f32)
+    for d in range(domains):
+        structure = structure + matmul_nt(
+            charges_ref[d], waves_ref[:, d * atoms : (d + 1) * atoms]
+        )
+    along_sin = structure[:, :share] * damping
+    along_cos = structure[:, share:] * damping
+    to_sine = jnp.concatenate([along_cos * waves[a] for a in range(3)], axis=0)
+    to_cosine = jnp.concatenate([-along_sin * waves[a] for a in range(3)], axis=0)
+    weights = jnp.concatenate([to_sine, to_cosine], axis=1)
+    weights_ref[...] = weights
+    weights = weights.astype(bf16)
+    for d in range(domains):
+        field = matmul(weights, waves_ref[:, d * atoms : (d + 1) * atoms])
+        charges = charges_ref[d].astype(f32)
         for a in range(3):
-            turns = turns + columns[:, a : a + 1] * (rows[a : a + 1, :] * (1.0 / lengths[a]))
-        turns = turns - jnp.floor(turns + 0.5)
-        square = turns * turns
-        half_sine = turns * horner(sine_terms, square)
-        half_cosine = horner(cosine_terms, square)
-        cosine = (1.0 - 2.0 * half_sine * half_sine).astype(bf16)
-        sine = (2.0 * half_sine * half_cosine).astype(bf16)
-        cos_ref[d] = cosine
-        sin_ref[d] = sine
-        charges = charges_ref[d]
-        return carry[0] + matmul_nt(charges, cosine), carry[1] + matmul_nt(charges, sine)
-
-    zero = jnp.zeros((charge_count, share), f32)
-    along_cos, along_sin = lax.fori_loop(0, domains, gather, (zero, zero))
-    along_cos = along_cos * damping
-    along_sin = along_sin * damping
-    to_sine = jnp.concatenate([along_cos * waves[a] for a in range(3)], axis=0).astype(bf16)
-    to_cosine = jnp.concatenate([-along_sin * waves[a] for a in range(3)], axis=0).astype(bf16)
-    quad_first = where_ref[4]
-
-    def force(d, carry):
-        field = matmul(to_sine, sin_ref[d]) + matmul(to_cosine, cos_ref[d])
-        charges = charges_ref[d].astype(f32)
-        inside = jnp.logical_and(d >= quad_first, d < quad_first + group)
-
-        @pl.when(inside)
-        def _():
-            field_ref[d - quad_first] = field
-
-        for a in range(3):
-            row = jnp.sum(
+            rows_ref[a, d : d + 1, :] = jnp.sum(
                 field[a * charge_count : (a + 1) * charge_count, :] * charges,
                 axis=0,
                 keepdims=True,
             )
-            for copy in range(group):
-                forces_ref[copy, a, pl.ds(d, 1), :] = row
-        return carry
-
-    lax.fori_loop(0, domains, force, 0)
+    for copy in range(group):
+        forces_ref[copy] = rows_ref[...]
 
 
 def gradient_kernel(
@@ -253,9 +264,8 @@
     small_ref,
     charges_ref,
     wave_ref,
-    cos_ref,
-    sin_ref,
-    field_ref,
+    waves_ref,
+    weights_ref,
     parts_ref,
     forces_ref,
     grad_ref,
@@ -264,7 +274,7 @@
     box_x,
 ):
     domains, charge_count, atoms = charges_ref.shape
-    share = cos_ref.shape[1]
+    share = waves_ref.shape[0] // 2
     group = parts_ref.shape[0]
     first = pl.multiple_of(where_ref[3] * share, share)
     _, waves, damping = wave_rows(wave_ref, first, share, box_x, domains * atoms)
@@ -280,32 +290,36 @@
         rows = small_ref[d]
         return [2.0 * (total_ref[a, pl.ds(d, 1), :] - rows[3 + a : 4 + a, :]) for a in range(3)]
 
-    def gather(d, carry):
+    summed = jnp.zeros((3 * charge_count, 2 * share), f32)
+    for d in range(domains):
         charges = charges_ref[d].astype(f32)
         errors = errors_of(d)
         scaled = jnp.concatenate([errors[a] * charges for a in range(3)], axis=0).astype(bf16)
-        return carry[0] + matmul_nt(scaled, sin_ref[d]), carry[1] + matmul_nt(scaled, cos_ref[d])
-
-    zero = jnp.zeros((3 * charge_count, share), f32)
-    by_sine, by_cosine = lax.fori_loop(0, domains, gather, (zero, zero))
+        summed = summed + matmul_nt(scaled, waves_ref[:, d * atoms : (d + 1) * atoms])
 
     def along(value):
         return sum(
             waves[a] * value[a * charge_count : (a + 1) * charge_count, :] for a in range(3)
         )
 
-    back_cos = (damping * along(by_sine)).astype(bf16)
-    back_sin = (-damping * along(by_cosine)).astype(bf16)
+    back_cos = damping * along(summed[:, :share])
+    back_sin = -damping * along(summed[:, share:])
+    back = jnp.concatenate([back_sin, back_cos], axis=1)
+    back_high = back.astype(bf16)
+    back_low = (back - back_high.astype(f32)).astype(bf16)
+    weights = weights_ref[...]
+    weights_high = weights.astype(bf16)
+    weights_low = (weights - weights_high.astype(f32)).astype(bf16)
     quad_first = where_ref[4]
     for member in range(group):
         d = quad_first + member
         errors = errors_of(d)
-        grad = matmul(back_cos, cos_ref[d]) + matmul(back_sin, sin_ref[d])
+        block = waves_ref[:, pl.ds(pl.multiple_of(d * atoms, atoms), atoms)]
+        grad = matmul(back_high, block) + matmul(back_low, block)
+        field = matmul(weights_high, block) + matmul(weights_low, block)
         for a in range(3):
-            grad = grad + errors[a] * field_ref[
-                member, a * charge_count : (a + 1) * charge_count, :
-            ]
-        grad_ref[member] = grad
+            grad = grad + errors[a] * field[a * charge_count : (a + 1) * charge_count, :]
+        grad_ref[member] = grad.astype(grad_ref.dtype)
 
 
 def weights_kernel(
@@ -323,16 +337,14 @@
 ):
     group, charge_count, atoms = parts_ref.shape
     basis_count, width, _ = filtered_ref.shape
-    grad = parts_ref[0]
+    grad = parts_ref[0].astype(f32)
     for part in range(1, group):
-        grad = grad + parts_ref[part]
-    rounded = grad.astype(bf16)
+        grad = grad + parts_ref[part].astype(f32)
     before = before_ref[...]
     gate = sigmoid(before)
-    upstream = matmul(charge_ref[...], rounded)
-    before_grad = (upstream * (gate * (1.0 + before * (1.0 - gate)))).astype(bf16)
-    message_grad = matmul(mix_ref[...], before_grad).astype(bf16).astype(f32)
-    packed_ref[...] = jnp.zeros_like(packed_ref)
+    upstream = matmul(jnp.transpose(charge_ref[...].astype(f32)), grad, highest)
+    before_grad = upstream * (gate * (1.0 + before * (1.0 - gate)))
+    message_grad = matmul(mix_ref[...].astype(f32), before_grad, highest)
     columns = [
         jnp.sum(message_grad * filtered_ref[b], axis=1, keepdims=True) for b in range(basis_count)
     ]
@@ -340,10 +352,13 @@
     row = 0
     packed_ref[row : row + basis_count, :] = jnp.transpose(radial)
     row += basis_count
-    packed_ref[row : row + width, :] = matmul_nt(messages_ref[...], before_grad)
+    packed_ref[row : row + width, :] = matmul_nt(messages_ref[...], before_grad, highest)
     row += width
-    packed_ref[row : row + charge_count, :] = matmul_nt(rounded, hidden_ref[...])
+    packed_ref[row : row + charge_count, :] = matmul_nt(
+        grad, hidden_ref[...].astype(f32), highest
+    )
     row += charge_count
+    packed_ref[row:, :] = jnp.zeros((packed_ref.shape[0] - row, width), f32)
     one_hot = (
         lax.broadcasted_iota(jnp.int32, (kinds, atoms), 0) == species_ref[...]
     ).astype(f32)
@@ -352,7 +367,7 @@
 
 def step_kernel(total_ref, radial_ref, mix_ref, charge_ref, species_ref):
     basis_count, width = radial_ref.shape
-    charge_count = charge_ref.shape[1]
+    charge_count = charge_ref.shape[0]
     kinds = species_ref.shape[0]
 
     def normalized(gradient):
@@ -364,21 +379,31 @@
     row += basis_count
     mix_ref[...] = normalized(total_ref[row : row + width, :])
     row += width
-    charge_ref[...] = normalized(jnp.transpose(total_ref[row : row + charge_count, :]))
+    charge_ref[...] = normalized(total_ref[row : row + charge_count, :])
     row += charge_count
     species_ref[...] = normalized(total_ref[row : row + kinds, 0:charge_count])
 
 
-def in_smem():
-    return pl.BlockSpec(memory_space=pltpu.SMEM)
-
-
-def in_vmem(count):
-    return [pl.BlockSpec(memory_space=pltpu.VMEM) for _ in range(count)]
-
-
 def shaped(*dims, kind=f32):
     return jax.ShapeDtypeStruct(dims, kind)
+
+
+def kernel(body, name, out_shape, scratch, nanoseconds, where, *operands):
+    outs = out_shape if isinstance(out_shape, tuple) else (out_shape,)
+    held = sum(math.prod(x.shape) * x.dtype.itemsize for x in (*outs, *scratch, *operands))
+    in_vmem = pl.BlockSpec(memory_space=pltpu.VMEM)
+    return pl.pallas_call(
+        body,
+        out_shape=out_shape,
+        in_specs=[pl.BlockSpec(memory_space=pltpu.SMEM)] + [in_vmem] * len(operands),
+        out_specs=tuple(in_vmem for _ in outs) if isinstance(out_shape, tuple) else in_vmem,
+        scratch_shapes=[pltpu.VMEM(x.shape, x.dtype) for x in scratch],
+        compiler_params=pltpu.CompilerParams(vmem_limit_bytes=2 * held + spare_vmem),
+        cost_estimate=pl.CostEstimate(
+            flops=nanoseconds * 1_000_000, bytes_accessed=held, transcendentals=0
+        ),
+        name=name,
+    )(where, *operands)
 
 
 def on_device(
@@ -406,7 +431,6 @@
     share = wave_count // group
     quads = [[group * q + m for m in range(group)] for q in range(domains // group)]
     entries = atoms + 2 * ghost_sends.shape[1]
-    params = pltpu.CompilerParams(vmem_limit_bytes=vmem_limit)
 
     me = lax.axis_index("dom")
     where = jnp.stack(
@@ -427,78 +451,90 @@
         jnp.broadcast_to(small[None], (domains,) + small.shape), "dom", 0, 0
     )
     species_row = species[None, :]
-
-    filtered, messages, before, hidden, charges = pl.pallas_call(
+    slots = neighbours.T
+    charge_rows = charge_weight.T
+
+    filtered, messages, before, hidden, charges = kernel(
         lambda *refs: edge_kernel(*refs, box_x=box_x),
-        out_shape=(
+        "edges",
+        (
             shaped(basis_count, width, atoms),
-            shaped(width, atoms, kind=bf16),
+            shaped(width, atoms),
             shaped(width, atoms),
             shaped(width, atoms, kind=bf16),
             shaped(domains, charge_count, atoms, kind=bf16),
         ),
-        in_specs=[in_smem()] + in_vmem(11),
-        out_specs=tuple(in_vmem(5)),
-        scratch_shapes=[
-            pltpu.VMEM((entries // 32, atoms), jnp.int32),
-            pltpu.VMEM((entries, small.shape[0]), f32),
-            pltpu.VMEM((width, entries), bf16),
-            pltpu.VMEM((basis_count, entries, atoms), bf16),
-        ],
-        compiler_params=params,
-        name="edges",
-    )(
+        (
+            shaped(entries // 32, atoms, kind=jnp.int32),
+            shaped(entries, small.shape[0]),
+            shaped(width, entries, kind=bf16),
+            shaped(basis_count, entries, atoms, kind=bf16),
+        ),
+        12_000,
         where,
         features,
         from_low,
         from_up,
         small_all,
-        neighbours,
+        slots,
         neighbour_count[None, :],
         species_row,
         radial_weight,
         mix_weight,
-        charge_weight,
+        charge_rows,
         species_charge,
     )
     charges_all = lax.all_to_all(charges, "dom", 0, 0)
-
-    cosines, sines, field, force_parts = pl.pallas_call(
+    waves = kernel(
+        lambda *refs: phase_kernel(*refs, box_x=box_x),
+        "phases",
+        shaped(2 * share, domains * atoms, kind=bf16),
+        (),
+        8_000,
+        where,
+        small_all,
+        wave_index,
+    )
+    weights, force_parts = kernel(
         lambda *refs: structure_kernel(*refs, box_x=box_x),
-        out_shape=(
-            shaped(domains, share, atoms, kind=bf16),
-            shaped(domains, share, atoms, kind=bf16),
-            shaped(group, 3 * charge_count, atoms),
+        "structure",
+        (
+            shaped(3 * charge_count, 2 * share),
             shaped(group, 3, domains, atoms),
         ),
-        in_specs=[in_smem()] + in_vmem(3),
-        out_specs=tuple(in_vmem(4)),
-        compiler_params=params,
-        name="structure",
-    )(where, small_all, charges_all, wave_index)
+        (shaped(3, domains, atoms),),
+        5_000,
+        where,
+        charges_all,
+        wave_index,
+        waves,
+    )
     force_parts = lax.all_to_all(force_parts, "dom", 0, 0, axis_index_groups=quads)
-
-    forces, grad_parts = pl.pallas_call(
+    forces, grad_parts = kernel(
         lambda *refs: gradient_kernel(*refs, box_x=box_x),
-        out_shape=(shaped(3, atoms), shaped(group, charge_count, atoms)),
-        in_specs=[in_smem()] + in_vmem(7),
-        out_specs=tuple(in_vmem(2)),
-        scratch_shapes=[pltpu.VMEM((3, domains, atoms), f32)],
-        compiler_params=params,
-        name="gradient",
-    )(where, small_all, charges_all, wave_index, cosines, sines, field, force_parts)
+        "gradient",
+        (shaped(3, atoms), shaped(group, charge_count, atoms, kind=bf16)),
+        (shaped(3, domains, atoms),),
+        5_000,
+        where,
+        small_all,
+        charges_all,
+        wave_index,
+        waves,
+        weights,
+        force_parts,
+    )
     grad_parts = lax.all_to_all(grad_parts, "dom", 0, 0, axis_index_groups=quads)
 
     rows = basis_count + width + charge_count + kinds
     rows = -(-rows // (8 * domains)) * (8 * domains)
-    packed = pl.pallas_call(
-        lambda *refs: weights_kernel(*refs, kinds=kinds),
-        out_shape=shaped(rows, width),
-        in_specs=in_vmem(8),
-        out_specs=in_vmem(1)[0],
-        compiler_params=params,
-        name="weights",
-    )(
+    packed = kernel(
+        lambda _, *refs: weights_kernel(*refs, kinds=kinds),
+        "weights",
+        shaped(rows, width),
+        (),
+        3_000,
+        where,
         grad_parts,
         filtered,
         messages,
@@ -506,25 +542,26 @@
         hidden,
         species_row,
         mix_weight,
-        charge_weight,
+        charge_rows,
     )
     pieces = lax.all_to_all(packed.reshape(domains, rows // domains, width), "dom", 0, 0)
     piece = jnp.sum(pieces, axis=0)
     total = lax.all_to_all(jnp.broadcast_to(piece[None], pieces.shape), "dom", 0, 0)
-    steps = pl.pallas_call(
-        step_kernel,
-        out_shape=(
+    radial_step, mix_step, charge_step, species_step = kernel(
+        lambda _, *refs: step_kernel(*refs),
+        "steps",
+        (
             shaped(basis_count, width),
             shaped(width, width),
-            shaped(width, charge_count),
+            shaped(charge_count, width),
             shaped(kinds, charge_count),
         ),
-        in_specs=in_vmem(1),
-        out_specs=tuple(in_vmem(4)),
-        compiler_params=params,
-        name="steps",
-    )(total.reshape(rows, width))
-    return (forces, *steps)
+        (),
+        2_000,
+        where,
+        total.reshape(rows, width),
+    )
+    return forces, radial_step, mix_step, charge_step.T, species_step
 
 
 def solution(mesh):

time: 123 us -> 105 us (0.85)
  blocking collectives: 61.1 us -> 36.8 us
  Pallas kernels: 38.7 us -> 24.1 us
  waiting for transfers between devices: 0.01 us -> 10.1 us
  starting transfers between devices: 14 us -> 19.7 us
  local copies, waits for them, and re-layouts: 6.58 us -> 10.8 us
    all_to_all x1 -> x0, blocking collectives: 19.3 us -> none  [on_device(): charges_all = lax.all_to_all(charges, 'dom', 0, 0)]
    pallas_call x5 -> x6, Pallas kernels: 38.7 us -> 24.1 us  [kernel(): pl.pallas_call(body, out_shape=out_shape, in_specs=[pl.BlockSpec(memory_s...]
    all_to_all x0 -> x1, waiting for transfers between devices: none -> 6.49 us  [on_device(): charges_all = lax.all_to_all(charges, 'dom', 0, 0)]
    all_to_all x0 -> x1, starting transfers between devices: none -> 5.76 us  [on_device(): charges_all = lax.all_to_all(charges, 'dom', 0, 0)]
    unnamed x9 -> x30, local copies, waits for them, and re-layouts: 5.24 us -> 10 us
    ppermute x1, waiting for transfers between devices: 0.01 us -> 3.61 us  [on_device(): from_low = lax.ppermute(features, 'dom', upward)]
    all_to_all x1, blocking collectives: 9.83 us -> 7.4 us  [on_device(): lax.all_to_all(grad_parts, 'dom', 0, 0, axis_index_groups=quads)]
    all_to_all x1, blocking collectives: 9.6 us -> 7.92 us  [on_device(): lax.all_to_all(force_parts, 'dom', 0, 0, axis_index_groups=quads)]
  transfers between devices with their start and end apart: 3 -> 4, of which waited for: 0 -> 2; matrix products, arithmetic and copies ran while one was open for 3% -> 0% of each run, Pallas kernels for 0% -> 5%
where the time goes in v2:
time: 105 us; the launch traced here: 104 us
  blocking collectives  36.8 us (35%)
  Pallas kernels  24.1 us (23%)
  starting transfers between devices  19.7 us (19%)
  local copies, waits for them, and re-layouts  10.8 us (10%)
  waiting for transfers between devices  10.1 us (10%)
  other arithmetic  1.42 us (1%)
    pallas_call x6, Pallas kernels, kernel(): pl.pallas_call(body, out_shape=out_shape, in_specs=[pl.BlockSpec(memory_s...  24.1 us
    all_to_all x1, blocking collectives, on_device(): lax.all_to_all(packed.reshape(domains, rows // domains, width), 'dom', 0, 0)  11.1 us
    all_to_all x1, blocking collectives, on_device(): lax.all_to_all(jnp.broadcast_to(piece[None], pieces.shape), 'dom', 0, 0)  10.4 us
    unnamed x30, local copies, waits for them, and re-layouts  10 us
    all_to_all x1, starting transfers between devices, on_device(): lax.all_to_all(jnp.broadcast_to(small[None], (domains,) + small.shape), '...  8.31 us
    all_to_all x1, blocking collectives, on_device(): lax.all_to_all(force_parts, 'dom', 0, 0, axis_index_groups=quads)  7.92 us
    all_to_all x1, blocking collectives, on_device(): lax.all_to_all(grad_parts, 'dom', 0, 0, axis_index_groups=quads)  7.4 us
    all_to_all x1, waiting for transfers between devices, on_device(): charges_all = lax.all_to_all(charges, 'dom', 0, 0)  6.49 us
  transfers between devices with their start and end apart: 4, of which 2 were waited for; matrix products, arithmetic and copies ran while one was open for 0% of the time, Pallas kernels for 5%

profile of v2, /device:TPU:0, one launch (start us, length us, event | category | flops | bytes accessed | tf_op | source)
XLA Modules:
  0.0 103.8 jit_solution(536973365363655937)
XLA Ops:
  0.6 0.7 convert_element_type.3
  1.3 0.7 pad_maximum_fusion
  2.0 0.7 broadcast_in_dim.8
  2.7 8.3 %all-to-all-start = ((f32[16,8,256]{2,1,0:T(8,128)}), f32[16,8,256]{2,1,0:T(8,128)S(1)}, u32[]{:S(2)}, u32[]{:S(2)}) async-start(f32[16,8,256]{2,1,0:T(8,128)} %broadcast_in_dim.8), calls=%async_computation | async-start | bytes 262144 | tf_op jit(solution)/shard_map/all_to_all | solution.py:450
  11.0 1.9 %collective-permute-start = (bf16[256,128]{1,0:T(8,128)(2,1)}, bf16[256,128]{1,0:T(8,128)(2,1)S(1)}, u32[]{:S(2)}, u32[]{:S(2)}) collective-permute-start(bf16[256,128]{1,0:T(8,128)(2,1)} %refs_1_.1), channel_id=1, source_target_pairs={{0,2},{2,4},{4,6},{6,8},{8,10},{10,12},{12,14},{14,16},{16,18},{18... | collective-permute-start | bytes 196616 | tf_op jit(solution)/shard_map/ppermute | solution.py:448
  12.9 3.7 %collective-permute-start.1 = (bf16[256,128]{1,0:T(8,128)(2,1)}, bf16[256,128]{1,0:T(8,128)(2,1)S(1)}, u32[]{:S(2)}, u32[]{:S(2)}) collective-permute-start(bf16[256,128]{1,0:T(8,128)(2,1)} %refs_1_.1), channel_id=1, source_target_pairs={{2,0},{4,2},{6,4},{8,6},{10,8},{12,10},{14,12},{16,14},{18,16},{20... | collective-permute-start | bytes 196616 | tf_op jit(solution)/shard_map/ppermute | solution.py:449
  16.7 0.1 stack.23.refs_0_._
  16.8 3.6 %collective-permute-done.refs_2_ = bf16[256,128]{1,0:T(8,128)(2,1)S(1)} collective-permute-done((bf16[256,128]{1,0:T(8,128)(2,1)}, bf16[256,128]{1,0:T(8,128)(2,1)S(1)}, u32[]{:S(2)}, u32[]{:S(2)}) %collective-permute-start) | collective-permute-done | bytes 65568 | tf_op jit(solution)/shard_map/ppermute | solution.py:448
  20.4 0.0 collective-permute-done.1.refs_3_
  20.4 0.0 all-to-all-done.refs_4_.refs_1_
  20.4 0.8 copy-done
  21.2 0.8 copy-done.1
  22.1 0.8 copy-done.2
  22.8 0.7 copy-done.5
  23.5 0.7 copy-done.7
  24.2 0.7 copy-done.8
  24.9 0.7 copy-done.9
  25.6 0.7 copy-done.10
  26.3 9.7 %edges.1 = (f32[16,128,256]{2,1,0:T(8,128)S(1)}, f32[128,256]{1,0:T(8,128)S(1)}, f32[128,256]{1,0:T(8,128)S(1)}, bf16[128,256]{1,0:T(8,128)(2,1)S(1)}, bf16[16,64,256]{2,1,0:T(8,128)(2,1)}) custom-call(s32[5]{0:T(128)S(1)} %stack.23.refs_0_._, bf16[256,128]{1,0:T(8,128)(2,1)S(1)} %copy-done, bf16[256,128]{1,0:T(8,128)(2,1)S(1)} %collective-permute-done.refs_2_, ...), custom_call_target="tpu_custom_call" | custom-call | flops 12000000000 | bytes 9936384 | tf_op jit(solution)/shard_map/edges/pallas_call | solution.py:395
  36.0 5.8 %all-to-all-start.1 = ((bf16[16,64,256]{2,1,0:T(8,128)(2,1)}), bf16[16,64,256]{2,1,0:T(8,128)(2,1)S(1)}, u32[]{:S(2)}, u32[]{:S(2)}) async-start(bf16[16,64,256]{2,1,0:T(8,128)(2,1)} %get-tuple-element.18), calls=%async_computation.1 | async-start | bytes 1048576 | tf_op jit(solution)/shard_map/all_to_all | solution.py:487
  41.8 5.0 %phases.1.refs_3_.refs_4_ = bf16[512,4096]{1,0:T(8,128)(2,1)S(1)} custom-call(s32[5]{0:T(128)S(1)} %stack.23.refs_0_._, f32[16,8,256]{2,1,0:T(8,128)S(1)} %all-to-all-done.refs_4_.refs_1_, s32[3,1024]{1,0:T(4,128)S(1)} %copy-done.4), custom_call_target="tpu_custom_call" | custom-call | flops 8000000000 | bytes 4337664 | tf_op jit(solution)/shard_map/phases/pallas_call | solution.py:395
  46.8 1.9 %copy-done.12 = bf16[512,4096]{1,0:T(8,128)(2,1)} copy-done((bf16[512,4096]{1,0:T(8,128)(2,1)}, bf16[512,4096]{1,0:T(8,128)(2,1)S(1)}, u32[]{:S(2)}) %copy-start.12) | copy-done | bytes 4194328
  48.7 6.5 %all-to-all-done.1.refs_1_.refs_2_ = bf16[16,64,256]{2,1,0:T(8,128)(2,1)S(1)} async-done(((bf16[16,64,256]{2,1,0:T(8,128)(2,1)}), bf16[16,64,256]{2,1,0:T(8,128)(2,1)S(1)}, u32[]{:S(2)}, u32[]{:S(2)}) %all-to-all-start.1) | async-done | bytes 524320 | tf_op jit(solution)/shard_map/all_to_all | solution.py:487
  55.2 2.2 %copy-done.13 = bf16[512,4096]{1,0:T(8,128)(2,1)S(1)} copy-done((bf16[512,4096]{1,0:T(8,128)(2,1)S(1)}, bf16[512,4096]{1,0:T(8,128)(2,1)}, u32[]{:S(2)}) %copy-start.13) | copy-done | bytes 4194328
  57.4 2.9 %structure.1 = (f32[192,512]{1,0:T(8,128)S(1)}, f32[4,3,16,256]{3,2,1,0:T(8,128)S(1)}) custom-call(s32[5]{0:T(128)S(1)} %stack.23.refs_0_._, bf16[16,64,256]{2,1,0:T(8,128)(2,1)S(1)} %all-to-all-done.1.refs_1_.refs_2_, s32[3,1024]{1,0:T(4,128)S(1)} %copy-done.4, bf16[512,4096]{1,0:T(8,128)(2,1)S(1)} %copy-done.13), custom_call_target="tpu_custom_call" | custom-call | flops 5000000000 | bytes 5369856 | tf_op jit(solution)/shard_map/structure/pallas_call | solution.py:395
  60.4 7.9 %all_to_all.30.refs_6_ = f32[4,3,16,256]{3,2,1,0:T(8,128)S(1)} all-to-all(f32[4,3,16,256]{3,2,1,0:T(8,128)S(1)} %get-tuple-element.20), channel_id=1, replica_groups={{0,2,4,6},{8,10,12,14},{16,18,20,22},{24,26,28,30},{1,3,5,7},{9,11,13,1..., dimensions={0} | all-to-all | bytes 393216 | tf_op jit(solution)/shard_map/all_to_all | solution.py:512
  68.3 3.5 %gradient.1 = (f32[3,256]{1,0:T(4,128)}, bf16[4,64,256]{2,1,0:T(8,128)(2,1)S(1)}) custom-call(s32[5]{0:T(128)S(1)} %stack.23.refs_0_._, f32[16,8,256]{2,1,0:T(8,128)S(1)} %all-to-all-done.refs_4_.refs_1_, bf16[16,64,256]{2,1,0:T(8,128)(2,1)S(1)} %all-to-all-done.1.refs_1_.refs_2_, s32[3,1024]{1,0:T(4,128)S(1)} %copy-done.4, ...), custom_call_target="tpu_custom_call" | custom-call | flops 5000000000 | bytes 5635072 | tf_op jit(solution)/shard_map/gradient/pallas_call | solution.py:395
  71.8 7.4 %all_to_all.31.refs_0_ = bf16[4,64,256]{2,1,0:T(8,128)(2,1)S(1)} all-to-all(bf16[4,64,256]{2,1,0:T(8,128)(2,1)S(1)} %get-tuple-element.22), channel_id=1, replica_groups={{0,2,4,6},{8,10,12,14},{16,18,20,22},{24,26,28,30},{1,3,5,7},{9,11,13,1..., dimensions={0} | all-to-all | bytes 262144 | tf_op jit(solution)/shard_map/all_to_all | solution.py:527
  79.2 1.7 %weights.1 = f32[256,128]{1,0:T(8,128)S(1)} custom-call(s32[5]{0:T(128)S(1)} %stack.23.refs_0_._, bf16[4,64,256]{2,1,0:T(8,128)(2,1)S(1)} %all_to_all.31.refs_0_, f32[16,128,256]{2,1,0:T(8,128)S(1)} %get-tuple-element.23.refs_1_, f32[128,256]{1,0:T(8,128)S(1)} %get-tuple-element.24.refs_2_, f32[128,256]{1,0:T(8,128)S(1)} %get-tuple-element.25.refs_3_, ...), custom_call_target="tpu_custom_call" | custom-call | flops 3000000000 | bytes 2737152 | tf_op jit(solution)/shard_map/weights/pallas_call | solution.py:395
  80.8 11.1 %all_to_all.32 = f32[16,16,128]{2,1,0:T(8,128)S(1)} all-to-all(f32[16,16,128]{2,1,0:T(8,128)S(1)} %bitcast.13), channel_id=1, replica_groups=mesh['dom'=16,'cell'=2] {'dom'}, dimensions={0} | all-to-all | bytes 262144 | tf_op jit(solution)/shard_map/all_to_all | solution.py:547
  92.0 10.4 %all_to_all.33 = f32[16,16,128]{2,1,0:T(8,128)S(1)} all-to-all(f32[16,16,128]{2,1,0:T(8,128)S(1)} %broadcast_in_dim.21), channel_id=1, replica_groups=mesh['dom'=16,'cell'=2] {'dom'}, dimensions={0} | all-to-all | bytes 262144 | tf_op jit(solution)/shard_map/all_to_all | solution.py:549
  102.4 1.3 %steps.1 = (f32[16,128]{1,0:T(8,128)}, f32[128,128]{1,0:T(8,128)}, f32[64,128]{1,0:T(8,128)}, f32[6,64]{1,0:T(8,128)}) custom-call(s32[5]{0:T(128)S(1)} %stack.23.refs_0_._, f32[256,128]{1,0:T(8,128)S(1)} %bitcast.12), custom_call_target="tpu_custom_call" | custom-call | flops 2000000000 | bytes 239104 | tf_op jit(solution)/shard_map/steps/pallas_call | solution.py:395
  (22 shorter events, 0.1 us)
Async XLA Ops:
  2.7 17.7 %all-to-all-start = ((f32[16,8,256]{2,1,0:T(8,128)}), f32[16,8,256]{2,1,0:T(8,128)S(1)}, u32[]{:S(2)}, u32[]{:S(2)}) async-start(f32[16,8,256]{2,1,0:T(8,128)} %broadcast_in_dim.8), calls=%async_computation | async-start | bytes 262144 | tf_op jit(solution)/shard_map/all_to_all | solution.py:450
  11.0 9.4 %collective-permute-start = (bf16[256,128]{1,0:T(8,128)(2,1)}, bf16[256,128]{1,0:T(8,128)(2,1)S(1)}, u32[]{:S(2)}, u32[]{:S(2)}) collective-permute-start(bf16[256,128]{1,0:T(8,128)(2,1)} %refs_1_.1), channel_id=1, source_target_pairs={{0,2},{2,4},{4,6},{6,8},{8,10},{10,12},{12,14},{14,16},{16,18},{18... | collective-permute-start | bytes 196616 | tf_op jit(solution)/shard_map/ppermute | solution.py:448
  12.9 7.4 %collective-permute-start.1 = (bf16[256,128]{1,0:T(8,128)(2,1)}, bf16[256,128]{1,0:T(8,128)(2,1)S(1)}, u32[]{:S(2)}, u32[]{:S(2)}) collective-permute-start(bf16[256,128]{1,0:T(8,128)(2,1)} %refs_1_.1), channel_id=1, source_target_pairs={{2,0},{4,2},{6,4},{8,6},{10,8},{12,10},{14,12},{16,14},{18,16},{20... | collective-permute-start | bytes 196616 | tf_op jit(solution)/shard_map/ppermute | solution.py:449
  20.4 0.8 copy-start
  21.2 0.8 copy-start.1
  22.1 0.8 copy-start.2
  22.8 0.7 copy-start.5
  23.5 0.7 copy-start.7
  24.2 0.7 copy-start.8
  24.9 0.7 copy-start.9
  25.6 0.7 copy-start.10
  26.3 15.5 %copy-start.4 = (s32[3,1024]{1,0:T(4,128)S(1)}, s32[3,1024]{1,0:T(4,128)}, u32[]{:S(2)}) copy-start(s32[3,1024]{1,0:T(4,128)} %refs_3_.1) | copy-start | bytes 36868
  36.0 19.2 %all-to-all-start.1 = ((bf16[16,64,256]{2,1,0:T(8,128)(2,1)}), bf16[16,64,256]{2,1,0:T(8,128)(2,1)S(1)}, u32[]{:S(2)}, u32[]{:S(2)}) async-start(bf16[16,64,256]{2,1,0:T(8,128)(2,1)} %get-tuple-element.18), calls=%async_computation.1 | async-start | bytes 1048576 | tf_op jit(solution)/shard_map/all_to_all | solution.py:487
  46.8 1.9 %copy-start.12 = (bf16[512,4096]{1,0:T(8,128)(2,1)}, bf16[512,4096]{1,0:T(8,128)(2,1)S(1)}, u32[]{:S(2)}) copy-start(bf16[512,4096]{1,0:T(8,128)(2,1)S(1)} %phases.1.refs_3_.refs_4_) | copy-start | bytes 12582916
  55.2 2.2 %copy-start.13 = (bf16[512,4096]{1,0:T(8,128)(2,1)S(1)}, bf16[512,4096]{1,0:T(8,128)(2,1)}, u32[]{:S(2)}) copy-start(bf16[512,4096]{1,0:T(8,128)(2,1)} %copy-done.12) | copy-start | bytes 12582916
  57.4 10.9 %copy-start.14 = (bf16[512,4096]{1,0:T(8,128)(2,1)S(1)}, bf16[512,4096]{1,0:T(8,128)(2,1)}, u32[]{:S(2)}) copy-start(bf16[512,4096]{1,0:T(8,128)(2,1)} %copy-done.12) | copy-start | bytes 12582916
  68.3 10.9 %copy-start.3 = (bf16[128,128]{1,0:T(8,128)(2,1)S(1)}, bf16[128,128]{1,0:T(8,128)(2,1)}, u32[]{:S(2)}) copy-start(bf16[128,128]{1,0:T(8,128)(2,1)} %refs_6_.1) | copy-start | bytes 98308
  68.3 10.9 %copy-start.6 = (bf16[128,64]{0,1:T(8,128)(2,1)S(1)}, bf16[128,64]{0,1:T(8,128)(2,1)}, u32[]{:S(2)}) copy-start(bf16[128,64]{0,1:T(8,128)(2,1)} %param.22) | copy-start | bytes 49156
  68.3 10.9 %copy-start.11 = (s32[256]{0:T(256)S(1)}, s32[256]{0:T(256)}, u32[]{:S(2)}) copy-start(s32[256]{0:T(256)} %param.17) | copy-start | bytes 3076

commit v3 on v2

v3 whole, which is shorter than its diff:
```python
import math

import jax
import jax.numpy as jnp
import numpy as np
from jax import lax
from jax.experimental import pallas as pl
from jax.experimental.pallas import tpu as pltpu
from jax.sharding import PartitionSpec as P

cutoff_radius = 5.0
kernel_width = 1.0
basis_width = 0.5
box_side = 20.0
two_pi = 6.283185307179586
highest = lax.Precision.HIGHEST
f32 = jnp.float32
bf16 = jnp.bfloat16
spare_vmem = 4 * 1024 * 1024
waves_bytes = 8 * 1024 * 1024


def fitted(function, degrees, reach):
    nodes = reach * np.cos((np.arange(400) + 0.5) * np.pi / 400)
    powers = np.stack([nodes**d for d in degrees], axis=1)
    return [float(c) for c in np.linalg.lstsq(powers, function(nodes), rcond=None)[0]]


sine_terms = fitted(lambda x: np.sin(np.pi * x), (1, 3, 5, 7, 9), 0.5)
cosine_terms = fitted(lambda x: np.cos(np.pi * x), (0, 2, 4, 6, 8), 0.5)


def horner(terms, square):
    value = terms[-1]
    for term in terms[-2::-1]:
        value = value * square + term
    return value


def matmul(left, right, precision=None):
    return lax.dot_general(
        left, right, (((1,), (0,)), ((), ())), precision=precision, preferred_element_type=f32
    )


def matmul_nt(left, right, precision=None):
    return lax.dot_general(
        left, right, (((1,), (1,)), ((), ())), precision=precision, preferred_element_type=f32
    )


def turned(value):
    return jnp.transpose(value.astype(f32)).astype(value.dtype)


def sigmoid(value):
    return 1.0 / (1.0 + jnp.exp(-value))


def pieces_of(value):
    first = value.astype(bf16).astype(f32)
    rest = value - first
    second = rest.astype(bf16).astype(f32)
    return first, second, rest - second


def pack_kernel(feat_ref, positions_ref, ghost_ref, packed_ref):
    atoms, width = feat_ref.shape
    packed_ref[0:atoms, :] = feat_ref[...]
    extra = jnp.concatenate(
        pieces_of(positions_ref[...])
        + (ghost_ref[...].astype(f32), jnp.zeros((5, atoms), f32)),
        axis=0,
    ).astype(bf16)
    for part in range(atoms // width):
        first = atoms + part * 16
        packed_ref[first : first + 16, :] = extra[:, part * width : (part + 1) * width]


def edge_kernel(
    where_ref,
    feat_ref,
    positions_ref,
    force_ref,
    near_ref,
    far_ref,
    slots_ref,
    count_ref,
    species_ref,
    radial_ref,
    mix_ref,
    charge_ref,
    offset_ref,
    filtered_ref,
    messages_ref,
    before_ref,
    hidden_ref,
    shared_ref,
    words_ref,
    coords_ref,
    table_ref,
    pair_ref,
    *,
    box_x,
):
    atoms, width = feat_ref.shape
    slots = slots_ref.shape[0]
    basis_count = radial_ref.shape[0]
    ghosts = atoms
    entries = atoms + 2 * ghosts
    own_rows = positions_ref[...]
    site = lax.broadcasted_iota(jnp.int32, (atoms, ghosts), 0).astype(f32)

    own_feat = turned(feat_ref[...])
    table_ref[:, 0:atoms] = own_feat
    padding = jnp.zeros((5, atoms), f32)
    coords_ref[0:atoms, :] = jnp.transpose(jnp.concatenate([own_rows, padding], axis=0))
    for ref, is_low in ((near_ref, where_ref[0] == 1), (far_ref, where_ref[0] == 0)):
        extra = jnp.concatenate(
            [ref[atoms + part * 16 : atoms + part * 16 + 16, :] for part in range(atoms // width)],
            axis=1,
        )
        sends = extra[8:16, :].astype(f32)
        sends = jnp.where(is_low, sends[2:3, :], sends[1:2, :])
        chosen = (site == sends).astype(bf16)
        first = pl.multiple_of(jnp.where(is_low, atoms, atoms + ghosts), ghosts)
        places = pl.ds(first, ghosts)
        table_ref[:, places] = matmul(turned(ref[0:atoms, :]), chosen).astype(bf16)
        moved = matmul(extra, chosen)
        moved = moved[0:3, :] + (moved[3:6, :] + moved[6:9, :])
        coords_ref[places, :] = jnp.transpose(jnp.concatenate([moved, padding], axis=0))

    listed = slots_ref[...]
    live = lax.broadcasted_iota(jnp.int32, (slots, atoms), 0) < count_ref[...]
    word_of = jnp.where(live, listed >> 5, -1)
    bit = jnp.left_shift(jnp.ones_like(listed), listed & 31)
    for word in range(entries // 32):
        value = jnp.where(word_of == word, bit, 0)
        rows = slots
        while rows > 1:
            rows //= 2
            value = value[:rows] | value[rows:]
        words_ref[word : word + 1, :] = value

    centers = [
        0.5 + (cutoff_radius - 0.5) * float(b) / (basis_count - 1) for b in range(basis_count)
    ]
    scale = -math.log2(math.e) / (basis_width * basis_width)
    own_x, own_y, own_z = own_rows[0:1, :], own_rows[1:2, :], own_rows[2:3, :]
    step = 32

    def block(index, carry):
        first = pl.multiple_of(index * step, step)
        coords = coords_ref[pl.ds(first, step), :]
        total = jnp.zeros((step, atoms), f32)
        for axis, (mine, length) in enumerate(
            ((own_x, box_x), (own_y, box_side), (own_z, box_side))
        ):
            away = coords[:, axis : axis + 1] - mine
            away = away - length * jnp.floor(away * (1.0 / length) + 0.5)
            total = total + away * away
        distance = jnp.sqrt(total)
        word = words_ref[pl.ds(index, 1), :]
        sublane = lax.broadcasted_iota(jnp.int32, (step, atoms), 0)
        is_live = (jnp.right_shift(jnp.broadcast_to(word, (step, atoms)), sublane) & 1) != 0
        half = jnp.minimum(distance, cutoff_radius) * (1.0 / cutoff_radius) - 0.5
        fade = 0.5 - 0.5 * (half * horner(sine_terms, half * half))
        weight = jnp.where(is_live, fade, 0.0)
        for b in range(basis_count):
            offset = distance - centers[b]
            basis = jnp.exp2(offset * offset * scale).astype(bf16).astype(f32)
            pair_ref[b, pl.ds(first, step), :] = (weight * basis).astype(bf16)
        return carry

    lax.fori_loop(0, entries // step, block, 0)

    radial = jnp.transpose(radial_ref[...].astype(f32))
    messages = jnp.zeros((width, atoms), f32)
    for b in range(basis_count):
        filtered = matmul(table_ref[...], pair_ref[b])
        filtered_ref[b] = filtered
        messages = messages + radial[:, b : b + 1] * filtered
    messages_ref[...] = messages
    before = matmul(jnp.transpose(mix_ref[...].astype(f32)), messages, highest)
    before_ref[...] = before
    hidden = (own_feat.astype(f32) + before * sigmoid(before)).astype(bf16)
    hidden_ref[...] = hidden
    kinds = offset_ref.shape[0]
    one_hot = (
        lax.broadcasted_iota(jnp.int32, (kinds, atoms), 0) == species_ref[...]
    ).astype(f32)
    charges = matmul(charge_ref[...], hidden) + matmul(
        jnp.transpose(offset_ref[...]), one_hot, highest
    )
    lengths = (box_x, box_side, box_side)
    turns = jnp.concatenate([own_rows[a : a + 1, :] * (1.0 / lengths[a]) for a in range(3)], axis=0)
    target = force_ref[...]
    high = target.astype(bf16).astype(f32)
    rows = jnp.concatenate(
        (charges,) + pieces_of(turns) + (high, target - high, jnp.zeros((1, atoms), f32)), axis=0
    ).astype(bf16)
    shared_ref[0] = rows


def wave_rows(wave_ref, first, count, box_x, total_atoms):
    index = wave_ref[:, pl.ds(first, count)].astype(f32)
    scales = (two_pi / box_x, two_pi / box_side, two_pi / box_side)
    waves = [index[a : a + 1, :] * scales[a] for a in range(3)]
    squares = waves[0] * waves[0] + waves[1] * waves[1] + waves[2] * waves[2]
    damping = jnp.exp(-0.5 * kernel_width * kernel_width * squares) * (1.0 / total_atoms)
    return index, waves, damping


def structure_kernel(
    where_ref, *refs, group, blocks, charge_count, box_x
):
    shared_refs, (wave_ref, waves_ref, weights_ref, *force_refs) = refs[:blocks], refs[blocks:]
    columns_count, _, atoms = shared_refs[0].shape
    share = waves_ref.shape[1] // 2
    first = pl.multiple_of(where_ref[1] * share, share)
    index, waves, damping = wave_rows(
        wave_ref, first, share, box_x, blocks * columns_count * atoms
    )
    columns = jnp.transpose(
        jnp.concatenate([index] * 3 + [jnp.zeros((7, share), f32)], axis=0)
    ).astype(bf16)
    shift = 12582912.0

    def block(j, carry):
        for r in range(blocks):
            turns = matmul(columns, shared_refs[r][j, charge_count : charge_count + 16, :])
            turns = turns - ((turns + shift) - shift)
            square = turns * turns
            half_sine = turns * horner(sine_terms, square)
            half_cosine = horner(cosine_terms, square)
            d = j * blocks + r
            waves_ref[d, 0:share, :] = (2.0 * half_sine * half_cosine).astype(bf16)
            waves_ref[d, share : 2 * share, :] = (1.0 - 2.0 * half_sine * half_sine).astype(bf16)
        return carry

    lax.fori_loop(0, columns_count, block, 0)
    structure = jnp.zeros((charge_count, 2 * share), f32)
    for d in range(blocks * columns_count):
        j, r = divmod(d, blocks)
        structure = structure + matmul_nt(shared_refs[r][j, 0:charge_count, :], waves_ref[d])
    along_sin = structure[:, :share] * damping
    along_cos = structure[:, share:] * damping
    to_sine = jnp.concatenate([along_cos * waves[a] for a in range(3)], axis=0)
    to_cosine = jnp.concatenate([-along_sin * waves[a] for a in range(3)], axis=0)
    weights = jnp.concatenate([to_sine, to_cosine], axis=1)
    weights_ref[...] = weights
    weights = weights.astype(bf16)
    for d in range(blocks * columns_count):
        j, r = divmod(d, blocks)
        field = matmul(weights, waves_ref[d])
        charges = shared_refs[r][j, 0:charge_count, :].astype(f32)
        for a in range(3):
            row = jnp.sum(
                field[a * charge_count : (a + 1) * charge_count, :] * charges,
                axis=0,
                keepdims=True,
            )
            for m in range(group):
                force_refs[m][a, d ^ m : (d ^ m) + 1, :] = row


def gradient_kernel(where_ref, *refs, group, blocks, charge_count, box_x):
    shared_refs, part_refs = refs[:blocks], refs[blocks : blocks + group]
    wave_ref, waves_ref, weights_ref, forces_ref, *grad_refs, total_ref = refs[blocks + group :]
    columns_count, _, atoms = shared_refs[0].shape
    share = waves_ref.shape[1] // 2
    first = pl.multiple_of(where_ref[1] * share, share)
    _, waves, damping = wave_rows(wave_ref, first, share, box_x, blocks * columns_count * atoms)
    total = part_refs[0][...]
    for m in range(1, group):
        total = total + part_refs[m][...]
    total_ref[...] = total
    for a in range(3):
        forces_ref[a : a + 1, :] = total[a, 0:1, :]

    def errors_of(d):
        j, r = divmod(d, blocks)
        target = shared_refs[r][j, charge_count : charge_count + 16, :].astype(f32)
        target = target[9:12, :] + target[12:15, :]
        return [2.0 * (total_ref[a, d : d + 1, :] - target[a : a + 1, :]) for a in range(3)]

    summed = jnp.zeros((3 * charge_count, 2 * share), f32)
    for d in range(blocks * columns_count):
        j, r = divmod(d, blocks)
        charges = shared_refs[r][j, 0:charge_count, :].astype(f32)
        errors = errors_of(d)
        scaled = jnp.concatenate([errors[a] * charges for a in range(3)], axis=0).astype(bf16)
        summed = summed + matmul_nt(scaled, waves_ref[d])

    def along(value):
        return sum(
            waves[a] * value[a * charge_count : (a + 1) * charge_count, :] for a in range(3)
        )

    back_cos = damping * along(summed[:, :share])
    back_sin = -damping * along(summed[:, share:])
    back = jnp.concatenate([back_sin, back_cos], axis=1)
    back_high = back.astype(bf16)
    back_low = (back - back_high.astype(f32)).astype(bf16)
    weights = weights_ref[...]
    weights_high = weights.astype(bf16)
    weights_low = (weights - weights_high.astype(f32)).astype(bf16)
    for m in range(group):
        errors = errors_of(m)
        grad = matmul(back_high, waves_ref[m]) + matmul(back_low, waves_ref[m])
        field = matmul(weights_high, waves_ref[m]) + matmul(weights_low, waves_ref[m])
        for a in range(3):
            grad = grad + errors[a] * field[a * charge_count : (a + 1) * charge_count, :]
        grad_refs[m][...] = grad.astype(grad_refs[m].dtype)


def weights_kernel(*refs, group, kinds):
    part_refs = refs[:group]
    (
        filtered_ref,
        messages_ref,
        before_ref,
        hidden_ref,
        species_ref,
        mix_ref,
        charge_ref,
        packed_ref,
    ) = refs[group:]
    charge_count, atoms = part_refs[0].shape
    basis_count, width, _ = filtered_ref.shape
    grad = part_refs[0][...].astype(f32)
    for m in range(1, group):
        grad = grad + part_refs[m][...].astype(f32)
    before = before_ref[...]
    gate = sigmoid(before)
    upstream = matmul(jnp.transpose(charge_ref[...].astype(f32)), grad, highest)
    before_grad = upstream * (gate * (1.0 + before * (1.0 - gate)))
    message_grad = matmul(mix_ref[...].astype(f32), before_grad, highest)
    columns = [
        jnp.sum(message_grad * filtered_ref[b], axis=1, keepdims=True) for b in range(basis_count)
    ]
    radial = jnp.concatenate(columns, axis=1)
    row = 0
    packed_ref[row : row + basis_count, :] = jnp.transpose(radial)
    row += basis_count
    packed_ref[row : row + width, :] = matmul_nt(messages_ref[...], before_grad, highest)
    row += width
    packed_ref[row : row + charge_count, :] = matmul_nt(
        grad, hidden_ref[...].astype(f32), highest
    )
    row += charge_count
    packed_ref[row:, :] = jnp.zeros((packed_ref.shape[0] - row, width), f32)
    one_hot = (
        lax.broadcasted_iota(jnp.int32, (kinds, atoms), 0) == species_ref[...]
    ).astype(f32)
    packed_ref[row : row + kinds, 0:charge_count] = matmul_nt(one_hot, grad, highest)


def step_kernel(total_ref, radial_ref, mix_ref, charge_ref, species_ref):
    basis_count, width = radial_ref.shape
    charge_count = charge_ref.shape[0]
    kinds = species_ref.shape[0]

    def normalized(gradient):
        mean = jnp.sum(gradient * gradient, keepdims=True) * (1.0 / gradient.size)
        return gradient * lax.rsqrt(mean + 1e-06)

    row = 0
    radial_ref[...] = normalized(total_ref[row : row + basis_count, :])
    row += basis_count
    mix_ref[...] = normalized(total_ref[row : row + width, :])
    row += width
    charge_ref[...] = normalized(total_ref[row : row + charge_count, :])
    row += charge_count
    species_ref[...] = normalized(total_ref[row : row + kinds, 0:charge_count])


def shaped(*dims, kind=f32):
    return jax.ShapeDtypeStruct(dims, kind)


def kernel(body, name, out_shape, scratch, nanoseconds, *operands, scalars=(), wanted=0):
    outs = out_shape if isinstance(out_shape, tuple) else (out_shape,)
    held = sum(math.prod(x.shape) * x.dtype.itemsize for x in (*outs, *scratch, *operands))
    in_vmem = pl.BlockSpec(memory_space=pltpu.VMEM)
    in_smem = pl.BlockSpec(memory_space=pltpu.SMEM)
    return pl.pallas_call(
        body,
        out_shape=out_shape,
        in_specs=[in_smem] * len(scalars) + [in_vmem] * len(operands),
        out_specs=tuple(in_vmem for _ in outs) if isinstance(out_shape, tuple) else in_vmem,
        scratch_shapes=[pltpu.VMEM(x.shape, x.dtype) for x in scratch],
        compiler_params=pltpu.CompilerParams(vmem_limit_bytes=max(held + spare_vmem, wanted)),
        cost_estimate=pl.CostEstimate(
            flops=nanoseconds * 1_000_000, bytes_accessed=held, transcendentals=0
        ),
        name=name,
    )(*scalars, *operands)


def across(value, bits):
    domains = lax.axis_size("dom")
    return lax.ppermute(value, "dom", [(i, i ^ bits) for i in range(domains)])


def on_device(
    features,
    positions,
    neighbours,
    neighbour_count,
    ghost_sends,
    species,
    wave_index,
    force_ref,
    radial_weight,
    mix_weight,
    charge_weight,
    species_charge,
):
    atoms, width = features.shape
    basis_count = radial_weight.shape[0]
    charge_count = charge_weight.shape[1]
    kinds = species_charge.shape[0]
    wave_count = wave_index.shape[1]
    domains = lax.axis_size("dom")
    box_x = 1.25 * (atoms * domains) / 64
    group = 2 if domains % 2 == 0 else 1
    while group < domains and 4 * wave_count // group * atoms * domains > waves_bytes:
        group *= 2
    share = wave_count // group
    entries = atoms + 2 * ghost_sends.shape[1]

    me = lax.axis_index("dom")
    where = jnp.stack([me % 2, me % group]).astype(jnp.int32)
    packed = kernel(
        pack_kernel,
        "pack",
        shaped(atoms + 16 * (atoms // width), width, kind=bf16),
        (),
        1_000,
        features,
        positions,
        ghost_sends,
        wanted=60 * 1024 * 1024,
    )
    near = across(packed, 1)
    beyond = [(i, (i + 1 if i % 2 else i - 1) % domains) for i in range(domains)]
    far = lax.ppermute(packed, "dom", beyond)
    species_row = species[None, :]
    slots = neighbours.T
    charge_rows = charge_weight.T

    filtered, messages, before, hidden, shared = kernel(
        lambda *refs: edge_kernel(*refs, box_x=box_x),
        "edges",
        (
            shaped(basis_count, width, atoms),
            shaped(width, atoms),
            shaped(width, atoms),
            shaped(width, atoms, kind=bf16),
            shaped(1, charge_count + 16, atoms, kind=bf16),
        ),
        (
            shaped(entries // 32, atoms, kind=jnp.int32),
            shaped(entries, 8),
            shaped(width, entries, kind=bf16),
            shaped(basis_count, entries, atoms, kind=bf16),
        ),
        12_000,
        features,
        positions,
        force_ref,
        near,
        far,
        slots,
        neighbour_count[None, :],
        species_row,
        radial_weight,
        mix_weight,
        charge_rows,
        species_charge,
        scalars=(where,),
        wanted=60 * 1024 * 1024,
    )
    blocks = 4 if domains % 4 == 0 else 2
    column = jnp.concatenate(
        [shared] + [across(shared, bits) for bits in range(blocks, domains, blocks)], axis=0
    )
    columns = [column] + [across(column, bits) for bits in range(1, blocks)]
    waves, weights, *force_parts = kernel(
        lambda *refs: structure_kernel(
            *refs, group=group, blocks=blocks, charge_count=charge_count, box_x=box_x
        ),
        "structure",
        (
            shaped(domains, 2 * share, atoms, kind=bf16),
            shaped(3 * charge_count, 2 * share),
        )
        + (shaped(3, domains, atoms),) * group,
        (),
        10_000,
        *columns,
        wave_index,
        scalars=(where,),
    )
    force_parts = force_parts[:1] + [across(force_parts[m], m) for m in range(1, group)]
    forces, *grad_parts = kernel(
        lambda *refs: gradient_kernel(
            *refs, group=group, blocks=blocks, charge_count=charge_count, box_x=box_x
        ),
        "gradient",
        (shaped(3, atoms),) + (shaped(charge_count, atoms, kind=bf16),) * group,
        (shaped(3, domains, atoms),),
        5_000,
        *columns,
        *force_parts,
        wave_index,
        waves,
        weights,
        scalars=(where,),
    )
    grad_parts = grad_parts[:1] + [across(grad_parts[m], m) for m in range(1, group)]

    rows = basis_count + width + charge_count + kinds
    rows = -(-rows // (8 * domains)) * (8 * domains)
    packed = kernel(
        lambda *refs: weights_kernel(*refs, group=group, kinds=kinds),
        "weights",
        shaped(rows, width),
        (),
        3_000,
        *grad_parts,
        filtered,
        messages,
        before,
        hidden,
        species_row,
        mix_weight,
        charge_rows,
    )
    pieces = lax.all_to_all(packed.reshape(domains, rows // domains, width), "dom", 0, 0)
    piece = jnp.sum(pieces, axis=0)
    total = lax.all_to_all(jnp.broadcast_to(piece[None], pieces.shape), "dom", 0, 0)
    radial_step, mix_step, charge_step, species_step = kernel(
        step_kernel,
        "steps",
        (
            shaped(basis_count, width),
            shaped(width, width),
            shaped(charge_count, width),
            shaped(kinds, charge_count),
        ),
        (),
        2_000,
        total.reshape(rows, width),
    )
    return forces, radial_step, mix_step, charge_step.T, species_step


def solution(mesh):
    placed = (
        P(("cell", "dom"), None),
        P(None, ("cell", "dom")),
        P(("cell", "dom"), None),
        P(("cell", "dom")),
        P(None, ("cell", "dom")),
        P(("cell", "dom")),
        P(),
        P(None, ("cell", "dom")),
        P(),
        P(),
        P(),
        P(),
    )
    return jax.shard_map(
        on_device,
        mesh=mesh,
        in_specs=placed,
        out_specs=(
            P(None, ("cell", "dom")),
            P("cell", None),
            P("cell", None),
            P("cell", None),
            P("cell", None),
        ),
        check_vma=False,
    )
```

time: 105 us -> 90.3 us (0.86)
  blocking collectives: 36.8 us -> 22.1 us
  local copies, waits for them, and re-layouts: 10.8 us -> 1.51 us
  Pallas kernels: 24.1 us -> 31.2 us
  waiting for transfers between devices: 10.1 us -> 16.2 us
  starting transfers between devices: 19.7 us -> 17.5 us
    all_to_all x2 -> x0, blocking collectives: 15.3 us -> none  [the longest x1 7.92 us: on_device(): lax.all_to_all(force_parts, 'dom', 0, 0, axis_index_groups=quads)]
    all_to_all x2 -> x0, starting transfers between devices: 14.1 us -> none  [the longest x1 8.31 us: on_device(): lax.all_to_all(jnp.broadcast_to(small[None], (domains,) + small.shape), '...]
    ppermute x2 -> x10, waiting for transfers between devices: 3.61 us -> 16.2 us  [the longest x9 14.2 us: across(): return lax.ppermute(value, 'dom', [(i, i ^ bits) for i in range(domains)])]
    ppermute x2 -> x10, starting transfers between devices: 5.67 us -> 17.5 us  [the longest x9 10.6 us: across(): return lax.ppermute(value, 'dom', [(i, i ^ bits) for i in range(domains)])]
    unnamed x30 -> x25, local copies, waits for them, and re-layouts: 10 us -> 1.49 us
    pallas_call x6, Pallas kernels: 24.1 us -> 31.2 us  [kernel(): pl.pallas_call(body, out_shape=out_shape, in_specs=[in_smem] * len(scalar...]
    all_to_all x2 -> x0, waiting for transfers between devices: 6.49 us -> none  [the longest x1 6.49 us: on_device(): charges_all = lax.all_to_all(charges, 'dom', 0, 0)]
  transfers between devices with their start and end apart: 4 -> 10, of which waited for: 2 -> 7; matrix products, arithmetic and copies ran while one was open for 0% -> 2% of each run, Pallas kernels for 5% -> 0%
where the time goes in v3:
time: 90.3 us; the launch traced here: 89.9 us
  Pallas kernels  31.2 us (35%)
  blocking collectives  22.1 us (24%)
  starting transfers between devices  17.5 us (19%)
  waiting for transfers between devices  16.2 us (18%)
  local copies, waits for them, and re-layouts  1.51 us (2%)
    pallas_call x6, Pallas kernels, kernel(): pl.pallas_call(body, out_shape=out_shape, in_specs=[in_smem] * len(scalar...  31.2 us
    ppermute x9, waiting for transfers between devices, across(): return lax.ppermute(value, 'dom', [(i, i ^ bits) for i in range(domains)])  14.2 us
    all_to_all x1, blocking collectives, on_device(): lax.all_to_all(packed.reshape(domains, rows // domains, width), 'dom', 0, 0)  11.7 us
    ppermute x9, starting transfers between devices, across(): return lax.ppermute(value, 'dom', [(i, i ^ bits) for i in range(domains)])  10.6 us
    all_to_all x1, blocking collectives, on_device(): lax.all_to_all(jnp.broadcast_to(piece[None], pieces.shape), 'dom', 0, 0)  10.4 us
    ppermute x1, starting transfers between devices, on_device(): far = lax.ppermute(packed, 'dom', beyond)  6.93 us
    ppermute x1, waiting for transfers between devices, on_device(): far = lax.ppermute(packed, 'dom', beyond)  2.01 us
  transfers between devices with their start and end apart: 10, of which 7 were waited for; matrix products, arithmetic and copies ran while one was open for 2% of the time, Pallas kernels for 0%

profile of v3, /device:TPU:0, one launch (start us, length us, event | category | flops | bytes accessed | tf_op | source)
XLA Modules:
  0.0 89.9 jit_solution(14334406679036364523)
XLA Ops:
  0.6 1.5 %pack.1 = bf16[288,128]{1,0:T(8,128)(2,1)} custom-call(bf16[256,128]{1,0:T(8,128)(2,1)} %refs_1_.1, f32[3,256]{1,0:T(4,128)} %refs_2_.1, s32[2,256]{1,0:T(2,128)} %ghost_ref.1), custom_call_target="tpu_custom_call" | custom-call | flops 1000000000 | bytes 144384 | tf_op jit(solution)/shard_map/pack/pallas_call | solution.py:387
  2.1 6.9 %collective-permute-start.1 = (bf16[288,128]{1,0:T(8,128)(2,1)}, bf16[288,128]{1,0:T(8,128)(2,1)S(1)}, u32[]{:S(2)}, u32[]{:S(2)}) collective-permute-start(bf16[288,128]{1,0:T(8,128)(2,1)} %pack.1), channel_id=1, source_target_pairs={{0,30},{2,4},{4,2},{6,8},{8,6},{10,12},{12,10},{14,16},{16,14},{18... | collective-permute-start | bytes 221192 | tf_op jit(solution)/shard_map/ppermute | solution.py:448
  9.1 0.0 collective-permute-start
  9.1 0.6 pad_add_fusion.refs_0_
  9.7 2.0 %collective-permute-done.1.refs_5_ = bf16[288,128]{1,0:T(8,128)(2,1)S(1)} collective-permute-done((bf16[288,128]{1,0:T(8,128)(2,1)}, bf16[288,128]{1,0:T(8,128)(2,1)S(1)}, u32[]{:S(2)}, u32[]{:S(2)}) %collective-permute-start.1) | collective-permute-done | bytes 73760 | tf_op jit(solution)/shard_map/ppermute | solution.py:448
  11.7 2.0 %collective-permute-done.refs_4_ = bf16[288,128]{1,0:T(8,128)(2,1)S(1)} collective-permute-done((bf16[288,128]{1,0:T(8,128)(2,1)}, bf16[288,128]{1,0:T(8,128)(2,1)S(1)}, u32[]{:S(2)}, u32[]{:S(2)}) %collective-permute-start) | collective-permute-done | bytes 73760 | tf_op jit(solution)/shard_map/ppermute | solution.py:403
  13.6 0.6 copy-done.10
  14.3 10.3 %edges.1 = (f32[16,128,256]{2,1,0:T(8,128)}, f32[128,256]{1,0:T(8,128)}, f32[128,256]{1,0:T(8,128)}, bf16[128,256]{1,0:T(8,128)(2,1)}, bf16[1,80,256]{2,1,0:T(8,128)(2,1)}) custom-call(s32[2]{0:T(128)} %pad_add_fusion.refs_0_, bf16[256,128]{1,0:T(8,128)(2,1)} %refs_1_.1, f32[3,256]{1,0:T(4,128)} %refs_2_.1, f32[3,256]{1,0:T(4,128)} %refs_3_.1, ...), custom_call_target="tpu_custom_call" | custom-call | flops 12000000000 | bytes 9344512 | tf_op jit(solution)/shard_map/edges/pallas_call | solution.py:387
  24.5 0.6 collective-permute-start.4
  25.2 0.0 collective-permute-start.3
  25.2 3.8 %collective-permute-start.2 = (bf16[1,80,256]{2,1,0:T(8,128)(2,1)}, bf16[1,80,256]{2,1,0:T(8,128)(2,1)S(1)}, u32[]{:S(2)}, u32[]{:S(2)}) collective-permute-start(bf16[1,80,256]{2,1,0:T(8,128)(2,1)} %get-tuple-element.21), channel_id=1, source_target_pairs={{0,8},{2,10},{4,12},{6,14},{8,0},{10,2},{12,4},{14,6},{16,24},{18,... | collective-permute-start | bytes 122888 | tf_op jit(solution)/shard_map/ppermute | solution.py:403
  28.9 0.8 constant_dynamic-update-slice_fusion.3
  29.7 1.4 %collective-permute-done.2 = bf16[1,80,256]{2,1,0:T(8,128)(2,1)S(1)} collective-permute-done((bf16[1,80,256]{2,1,0:T(8,128)(2,1)}, bf16[1,80,256]{2,1,0:T(8,128)(2,1)S(1)}, u32[]{:S(2)}, u32[]{:S(2)}) %collective-permute-start.2) | collective-permute-done | bytes 40992 | tf_op jit(solution)/shard_map/ppermute | solution.py:403
  31.2 0.0 collective-permute-done.3
  31.2 0.0 collective-permute-done.4
  31.2 2.7 %collective-permute-start.7 = (bf16[4,80,256]{2,1,0:T(8,128)(2,1)S(1)}, bf16[4,80,256]{2,1,0:T(8,128)(2,1)S(1)}, u32[]{:S(2)}, u32[]{:S(2)}) collective-permute-start(bf16[4,80,256]{2,1,0:T(8,128)(2,1)S(1)} %constant_dynamic-update-slice_fusion.refs_1_), channel_id=1, source_target_pairs={{0,6},{2,4},{4,2},{6,0},{8,14},{10,12},{12,10},{14,8},{16,22},{18,... | collective-permute-start | bytes 491528 | tf_op jit(solution)/shard_map/ppermute | solution.py:403
  33.9 0.0 collective-permute-start.6
  33.9 0.8 collective-permute-start.5
  34.8 4.0 %collective-permute-done.7.refs_4_ = bf16[4,80,256]{2,1,0:T(8,128)(2,1)S(1)} collective-permute-done((bf16[4,80,256]{2,1,0:T(8,128)(2,1)S(1)}, bf16[4,80,256]{2,1,0:T(8,128)(2,1)S(1)}, u32[]{:S(2)}, u32[]{:S(2)}) %collective-permute-start.7) | collective-permute-done | bytes 163872 | tf_op jit(solution)/shard_map/ppermute | solution.py:403
  38.8 1.3 %collective-permute-done.6.refs_3_ = bf16[4,80,256]{2,1,0:T(8,128)(2,1)S(1)} collective-permute-done((bf16[4,80,256]{2,1,0:T(8,128)(2,1)S(1)}, bf16[4,80,256]{2,1,0:T(8,128)(2,1)S(1)}, u32[]{:S(2)}, u32[]{:S(2)}) %collective-permute-start.6) | collective-permute-done | bytes 163872 | tf_op jit(solution)/shard_map/ppermute | solution.py:403
  40.1 0.0 collective-permute-done.5.refs_2_
  40.1 12.8 %structure.1 = (bf16[16,1024,256]{2,1,0:T(8,128)(2,1)S(1)}, f32[192,1024]{1,0:T(8,128)S(1)}, f32[3,16,256]{2,1,0:T(8,128)S(1)}, f32[3,16,256]{2,1,0:T(8,128)S(1)}) custom-call(s32[2]{0:T(128)S(1)} %copy-done.4, bf16[4,80,256]{2,1,0:T(8,128)(2,1)S(1)} %constant_dynamic-update-slice_fusion.refs_1_, bf16[4,80,256]{2,1,0:T(8,128)(2,1)S(1)} %collective-permute-done.5.refs_2_, ...), custom_call_target="tpu_custom_call" | custom-call | flops 10000000000 | bytes 9940992 | tf_op jit(solution)/shard_map/structure/pallas_call | solution.py:387
  52.9 1.4 %collective-permute-start.8 = (f32[3,16,256]{2,1,0:T(8,128)S(1)}, f32[3,16,256]{2,1,0:T(8,128)S(1)}, u32[]{:S(2)}, u32[]{:S(2)}) collective-permute-start(f32[3,16,256]{2,1,0:T(8,128)S(1)} %get-tuple-element.23), channel_id=1, source_target_pairs={{0,2},{2,0},{4,6},{6,4},{8,10},{10,8},{12,14},{14,12},{16,18},{18,... | collective-permute-start | bytes 147464 | tf_op jit(solution)/shard_map/ppermute | solution.py:403
  54.2 2.8 %collective-permute-done.8.refs_6_ = f32[3,16,256]{2,1,0:T(8,128)S(1)} collective-permute-done((f32[3,16,256]{2,1,0:T(8,128)S(1)}, f32[3,16,256]{2,1,0:T(8,128)S(1)}, u32[]{:S(2)}, u32[]{:S(2)}) %collective-permute-start.8) | collective-permute-done | bytes 49184 | tf_op jit(solution)/shard_map/ppermute | solution.py:403
  57.1 0.0 copy-start.8
  57.1 4.8 %gradient.1 = (f32[3,256]{1,0:T(4,128)}, bf16[64,256]{1,0:T(8,128)(2,1)S(1)}, bf16[64,256]{1,0:T(8,128)(2,1)S(1)}) custom-call(s32[2]{0:T(128)S(1)} %copy-done.4, bf16[4,80,256]{2,1,0:T(8,128)(2,1)S(1)} %constant_dynamic-update-slice_fusion.refs_1_, bf16[4,80,256]{2,1,0:T(8,128)(2,1)S(1)} %collective-permute-done.5.refs_2_, ...), custom_call_target="tpu_custom_call" | custom-call | flops 5000000000 | bytes 10058752 | tf_op jit(solution)/shard_map/gradient/pallas_call | solution.py:387
  61.9 1.3 %collective-permute-start.9 = (bf16[64,256]{1,0:T(8,128)(2,1)S(1)}, bf16[64,256]{1,0:T(8,128)(2,1)S(1)}, u32[]{:S(2)}, u32[]{:S(2)}) collective-permute-start(bf16[64,256]{1,0:T(8,128)(2,1)S(1)} %get-tuple-element.28), channel_id=1, source_target_pairs={{0,2},{2,0},{4,6},{6,4},{8,10},{10,8},{12,14},{14,12},{16,18},{18,... | collective-permute-start | bytes 98312 | tf_op jit(solution)/shard_map/ppermute | solution.py:403
  63.2 2.6 %collective-permute-done.9.refs_1_ = bf16[64,256]{1,0:T(8,128)(2,1)S(1)} collective-permute-done((bf16[64,256]{1,0:T(8,128)(2,1)S(1)}, bf16[64,256]{1,0:T(8,128)(2,1)S(1)}, u32[]{:S(2)}, u32[]{:S(2)}) %collective-permute-start.9) | collective-permute-done | bytes 32800 | tf_op jit(solution)/shard_map/ppermute | solution.py:403
  65.8 1.1 %weights.1 = f32[256,128]{1,0:T(8,128)S(1)} custom-call(bf16[64,256]{1,0:T(8,128)(2,1)S(1)} %get-tuple-element.27.refs_0_, bf16[64,256]{1,0:T(8,128)(2,1)S(1)} %collective-permute-done.9.refs_1_, f32[16,128,256]{2,1,0:T(8,128)S(1)} %copy-done.5, f32[128,256]{1,0:T(8,128)S(1)} %copy-done.6, f32[128,256]{1,0:T(8,128)S(1)} %copy-done.7, ...), custom_call_target="tpu_custom_call" | custom-call | flops 3000000000 | bytes 2671616 | tf_op jit(solution)/shard_map/weights/pallas_call | solution.py:387
  66.9 11.7 %all_to_all.10 = f32[16,16,128]{2,1,0:T(8,128)S(1)} all-to-all(f32[16,16,128]{2,1,0:T(8,128)S(1)} %bitcast.8), channel_id=1, replica_groups=mesh['dom'=16,'cell'=2] {'dom'}, dimensions={0} | all-to-all | bytes 262144 | tf_op jit(solution)/shard_map/all_to_all | solution.py:541
  78.7 10.4 %all_to_all.11 = f32[16,16,128]{2,1,0:T(8,128)S(1)} all-to-all(f32[16,16,128]{2,1,0:T(8,128)S(1)} %broadcast_in_dim.14), channel_id=1, replica_groups=mesh['dom'=16,'cell'=2] {'dom'}, dimensions={0} | all-to-all | bytes 262144 | tf_op jit(solution)/shard_map/all_to_all | solution.py:543
  89.1 0.8 steps.1
  (25 shorter events, 0.1 us)
Async XLA Ops:
  2.1 9.5 %collective-permute-start.1 = (bf16[288,128]{1,0:T(8,128)(2,1)}, bf16[288,128]{1,0:T(8,128)(2,1)S(1)}, u32[]{:S(2)}, u32[]{:S(2)}) collective-permute-start(bf16[288,128]{1,0:T(8,128)(2,1)} %pack.1), channel_id=1, source_target_pairs={{0,30},{2,4},{4,2},{6,8},{8,6},{10,12},{12,10},{14,16},{16,14},{18... | collective-permute-start | bytes 221192 | tf_op jit(solution)/shard_map/ppermute | solution.py:448
  9.1 4.6 %collective-permute-start = (bf16[288,128]{1,0:T(8,128)(2,1)}, bf16[288,128]{1,0:T(8,128)(2,1)S(1)}, u32[]{:S(2)}, u32[]{:S(2)}) collective-permute-start(bf16[288,128]{1,0:T(8,128)(2,1)} %pack.1), channel_id=1, source_target_pairs={{0,2},{2,0},{4,6},{6,4},{8,10},{10,8},{12,14},{14,12},{16,18},{18,... | collective-permute-start | bytes 221192 | tf_op jit(solution)/shard_map/ppermute | solution.py:403
  11.7 2.0 %copy-start.9 = (bf16[288,128]{1,0:T(8,128)(2,1)}, bf16[288,128]{1,0:T(8,128)(2,1)S(1)}, u32[]{:S(2)}) copy-start(bf16[288,128]{1,0:T(8,128)(2,1)S(1)} %collective-permute-done.1.refs_5_) | copy-start | bytes 221188
  13.6 0.6 copy-start.10
  14.3 25.8 %copy-start.1 = (s32[3,1024]{1,0:T(4,128)S(1)}, s32[3,1024]{1,0:T(4,128)}, u32[]{:S(2)}) copy-start(s32[3,1024]{1,0:T(4,128)} %refs_7_.2) | copy-start | bytes 36868
  14.3 25.8 %copy-start.4 = (s32[2]{0:T(128)S(1)}, s32[2]{0:T(128)}, u32[]{:S(2)}) copy-start(s32[2]{0:T(128)} %pad_add_fusion.refs_0_) | copy-start | bytes 28
  24.5 6.7 %collective-permute-start.4 = (bf16[1,80,256]{2,1,0:T(8,128)(2,1)}, bf16[1,80,256]{2,1,0:T(8,128)(2,1)S(1)}, u32[]{:S(2)}, u32[]{:S(2)}) collective-permute-start(bf16[1,80,256]{2,1,0:T(8,128)(2,1)} %get-tuple-element.21), channel_id=1, source_target_pairs={{0,24},{2,26},{4,28},{6,30},{8,16},{10,18},{12,20},{14,22},{16,8},... | collective-permute-start | bytes 122888 | tf_op jit(solution)/shard_map/ppermute | solution.py:403
  25.2 6.0 %collective-permute-start.3 = (bf16[1,80,256]{2,1,0:T(8,128)(2,1)}, bf16[1,80,256]{2,1,0:T(8,128)(2,1)S(1)}, u32[]{:S(2)}, u32[]{:S(2)}) collective-permute-start(bf16[1,80,256]{2,1,0:T(8,128)(2,1)} %get-tuple-element.21), channel_id=1, source_target_pairs={{0,16},{2,18},{4,20},{6,22},{8,24},{10,26},{12,28},{14,30},{16,0},... | collective-permute-start | bytes 122888 | tf_op jit(solution)/shard_map/ppermute | solution.py:403
  25.2 6.0 %collective-permute-start.2 = (bf16[1,80,256]{2,1,0:T(8,128)(2,1)}, bf16[1,80,256]{2,1,0:T(8,128)(2,1)S(1)}, u32[]{:S(2)}, u32[]{:S(2)}) collective-permute-start(bf16[1,80,256]{2,1,0:T(8,128)(2,1)} %get-tuple-element.21), channel_id=1, source_target_pairs={{0,8},{2,10},{4,12},{6,14},{8,0},{10,2},{12,4},{14,6},{16,24},{18,... | collective-permute-start | bytes 122888 | tf_op jit(solution)/shard_map/ppermute | solution.py:403
  31.2 7.5 %collective-permute-start.7 = (bf16[4,80,256]{2,1,0:T(8,128)(2,1)S(1)}, bf16[4,80,256]{2,1,0:T(8,128)(2,1)S(1)}, u32[]{:S(2)}, u32[]{:S(2)}) collective-permute-start(bf16[4,80,256]{2,1,0:T(8,128)(2,1)S(1)} %constant_dynamic-update-slice_fusion.refs_1_), channel_id=1, source_target_pairs={{0,6},{2,4},{4,2},{6,0},{8,14},{10,12},{12,10},{14,8},{16,22},{18,... | collective-permute-start | bytes 491528 | tf_op jit(solution)/shard_map/ppermute | solution.py:403
  33.9 6.2 %collective-permute-start.6 = (bf16[4,80,256]{2,1,0:T(8,128)(2,1)S(1)}, bf16[4,80,256]{2,1,0:T(8,128)(2,1)S(1)}, u32[]{:S(2)}, u32[]{:S(2)}) collective-permute-start(bf16[4,80,256]{2,1,0:T(8,128)(2,1)S(1)} %constant_dynamic-update-slice_fusion.refs_1_), channel_id=1, source_target_pairs={{0,4},{2,6},{4,0},{6,2},{8,12},{10,14},{12,8},{14,10},{16,20},{18,... | collective-permute-start | bytes 491528 | tf_op jit(solution)/shard_map/ppermute | solution.py:403
  33.9 6.2 %collective-permute-start.5 = (bf16[4,80,256]{2,1,0:T(8,128)(2,1)S(1)}, bf16[4,80,256]{2,1,0:T(8,128)(2,1)S(1)}, u32[]{:S(2)}, u32[]{:S(2)}) collective-permute-start(bf16[4,80,256]{2,1,0:T(8,128)(2,1)S(1)} %constant_dynamic-update-slice_fusion.refs_1_), channel_id=1, source_target_pairs={{0,2},{2,0},{4,6},{6,4},{8,10},{10,8},{12,14},{14,12},{16,18},{18,... | collective-permute-start | bytes 491528 | tf_op jit(solution)/shard_map/ppermute | solution.py:403
  52.9 4.2 %collective-permute-start.8 = (f32[3,16,256]{2,1,0:T(8,128)S(1)}, f32[3,16,256]{2,1,0:T(8,128)S(1)}, u32[]{:S(2)}, u32[]{:S(2)}) collective-permute-start(f32[3,16,256]{2,1,0:T(8,128)S(1)} %get-tuple-element.23), channel_id=1, source_target_pairs={{0,2},{2,0},{4,6},{6,4},{8,10},{10,8},{12,14},{14,12},{16,18},{18,... | collective-permute-start | bytes 147464 | tf_op jit(solution)/shard_map/ppermute | solution.py:403
  57.0 8.7 %copy-start = (bf16[128,128]{1,0:T(8,128)(2,1)S(1)}, bf16[128,128]{1,0:T(8,128)(2,1)}, u32[]{:S(2)}) copy-start(bf16[128,128]{1,0:T(8,128)(2,1)} %refs_7_.3) | copy-start | bytes 98308
  57.0 8.7 %copy-start.2 = (bf16[128,64]{0,1:T(8,128)(2,1)S(1)}, bf16[128,64]{0,1:T(8,128)(2,1)}, u32[]{:S(2)}) copy-start(bf16[128,64]{0,1:T(8,128)(2,1)} %param.22) | copy-start | bytes 49156
  57.0 8.7 %copy-start.3 = (s32[256]{0:T(256)S(1)}, s32[256]{0:T(256)}, u32[]{:S(2)}) copy-start(s32[256]{0:T(256)} %param.17) | copy-start | bytes 3076
  57.0 8.7 %copy-start.5 = (f32[16,128,256]{2,1,0:T(8,128)S(1)}, f32[16,128,256]{2,1,0:T(8,128)}, u32[]{:S(2)}) copy-start(f32[16,128,256]{2,1,0:T(8,128)} %get-tuple-element.29.refs_2_) | copy-start | bytes 6291460
  57.0 8.8 %copy-start.6 = (f32[128,256]{1,0:T(8,128)S(1)}, f32[128,256]{1,0:T(8,128)}, u32[]{:S(2)}) copy-start(f32[128,256]{1,0:T(8,128)} %get-tuple-element.30.refs_3_) | copy-start | bytes 393220
  57.1 8.8 %copy-start.7 = (f32[128,256]{1,0:T(8,128)S(1)}, f32[128,256]{1,0:T(8,128)}, u32[]{:S(2)}) copy-start(f32[128,256]{1,0:T(8,128)} %get-tuple-element.31.refs_4_) | copy-start | bytes 393220
  57.1 8.8 %copy-start.8 = (bf16[128,256]{1,0:T(8,128)(2,1)S(1)}, bf16[128,256]{1,0:T(8,128)(2,1)}, u32[]{:S(2)}) copy-start(bf16[128,256]{1,0:T(8,128)(2,1)} %get-tuple-element.32.refs_5_) | copy-start | bytes 196612
  61.9 3.9 %collective-permute-start.9 = (bf16[64,256]{1,0:T(8,128)(2,1)S(1)}, bf16[64,256]{1,0:T(8,128)(2,1)S(1)}, u32[]{:S(2)}, u32[]{:S(2)}) collective-permute-start(bf16[64,256]{1,0:T(8,128)(2,1)S(1)} %get-tuple-element.28), channel_id=1, source_target_pairs={{0,2},{2,0},{4,6},{6,4},{8,10},{10,8},{12,14},{14,12},{16,18},{18,... | collective-permute-start | bytes 98312 | tf_op jit(solution)/shard_map/ppermute | solution.py:403

commit v4 on v3

--- a/solution.py
+++ b/solution.py
@@ -17,7 +17,7 @@
 f32 = jnp.float32
 bf16 = jnp.bfloat16
 spare_vmem = 4 * 1024 * 1024
-waves_bytes = 8 * 1024 * 1024
+waves_bytes = 4 * 1024 * 1024
 
 
 def fitted(function, degrees, reach):
@@ -27,7 +27,8 @@
 
 
 sine_terms = fitted(lambda x: np.sin(np.pi * x), (1, 3, 5, 7, 9), 0.5)
-cosine_terms = fitted(lambda x: np.cos(np.pi * x), (0, 2, 4, 6, 8), 0.5)
+short_sine = fitted(lambda x: np.sin(np.pi * x), (1, 3, 5, 7), 0.5)
+short_cosine = fitted(lambda x: np.cos(np.pi * x), (0, 2, 4, 6), 0.5)
 
 
 def horner(terms, square):
@@ -146,6 +147,8 @@
         0.5 + (cutoff_radius - 0.5) * float(b) / (basis_count - 1) for b in range(basis_count)
     ]
     scale = -math.log2(math.e) / (basis_width * basis_width)
+    middle = basis_count // 2
+    gap = centers[1] - centers[0]
     own_x, own_y, own_z = own_rows[0:1, :], own_rows[1:2, :], own_rows[2:3, :]
     step = 32
 
@@ -165,14 +168,21 @@
         is_live = (jnp.right_shift(jnp.broadcast_to(word, (step, atoms)), sublane) & 1) != 0
         half = jnp.minimum(distance, cutoff_radius) * (1.0 / cutoff_radius) - 0.5
         fade = 0.5 - 0.5 * (half * horner(sine_terms, half * half))
-        weight = jnp.where(is_live, fade, 0.0)
-        for b in range(basis_count):
-            offset = distance - centers[b]
-            basis = jnp.exp2(offset * offset * scale).astype(bf16).astype(f32)
-            pair_ref[b, pl.ds(first, step), :] = (weight * basis).astype(bf16)
+        weight = jnp.where(jnp.logical_and(is_live, distance < cutoff_radius), fade, 0.0)
+        offset = jnp.minimum(distance, cutoff_radius) - centers[middle]
+        value = jnp.exp2(offset * offset * scale)
+        for direction in (1, -1):
+            ratio = jnp.exp2(offset * (-2.0 * direction * gap * scale))
+            running = value
+            for b in range(middle, basis_count) if direction == 1 else range(middle - 1, -1, -1):
+                if b != middle:
+                    running = running * ratio
+                basis = running * math.exp(-(((b - middle) * gap / basis_width) ** 2))
+                basis = basis.astype(bf16).astype(f32)
+                pair_ref[b, pl.ds(first, step), :] = (weight * basis).astype(bf16)
         return carry
 
-    lax.fori_loop(0, entries // step, block, 0)
+    lax.fori_loop(0, entries // step, block, 0, unroll=8)
 
     radial = jnp.transpose(radial_ref[...].astype(f32))
     messages = jnp.zeros((width, atoms), f32)
@@ -231,14 +241,14 @@
             turns = matmul(columns, shared_refs[r][j, charge_count : charge_count + 16, :])
             turns = turns - ((turns + shift) - shift)
             square = turns * turns
-            half_sine = turns * horner(sine_terms, square)
-            half_cosine = horner(cosine_terms, square)
+            half_sine = turns * horner(short_sine, square)
+            half_cosine = horner(short_cosine, square)
             d = j * blocks + r
             waves_ref[d, 0:share, :] = (2.0 * half_sine * half_cosine).astype(bf16)
             waves_ref[d, share : 2 * share, :] = (1.0 - 2.0 * half_sine * half_sine).astype(bf16)
         return carry
 
-    lax.fori_loop(0, columns_count, block, 0)
+    lax.fori_loop(0, columns_count, block, 0, unroll=4)
     structure = jnp.zeros((charge_count, 2 * share), f32)
     for d in range(blocks * columns_count):
         j, r = divmod(d, blocks)
@@ -314,7 +324,7 @@
         grad_refs[m][...] = grad.astype(grad_refs[m].dtype)
 
 
-def weights_kernel(*refs, group, kinds):
+def weights_kernel(where_ref, *refs, group, kinds):
     part_refs = refs[:group]
     (
         filtered_ref,
@@ -324,6 +334,7 @@
         species_ref,
         mix_ref,
         charge_ref,
+        *piece_refs,
         packed_ref,
     ) = refs[group:]
     charge_count, atoms = part_refs[0].shape
@@ -354,12 +365,20 @@
         lax.broadcasted_iota(jnp.int32, (kinds, atoms), 0) == species_ref[...]
     ).astype(f32)
     packed_ref[row : row + kinds, 0:charge_count] = matmul_nt(one_hot, grad, highest)
-
-
-def step_kernel(total_ref, radial_ref, mix_ref, charge_ref, species_ref):
+    count = piece_refs[0].shape[0]
+    for r, ref in enumerate(piece_refs):
+        ref[...] = packed_ref[pl.ds(pl.multiple_of((where_ref[2] ^ r) * count, 8), count), :]
+
+
+def step_kernel(where_ref, *refs):
+    *piece_refs, radial_ref, mix_ref, charge_ref, species_ref, total_ref = refs
     basis_count, width = radial_ref.shape
     charge_count = charge_ref.shape[0]
     kinds = species_ref.shape[0]
+
+    count = piece_refs[0].shape[0]
+    for r, ref in enumerate(piece_refs):
+        total_ref[pl.ds(pl.multiple_of((where_ref[2] ^ r) * count, 8), count), :] = ref[...]
 
     def normalized(gradient):
         mean = jnp.sum(gradient * gradient, keepdims=True) * (1.0 / gradient.size)
@@ -401,6 +420,12 @@
 def across(value, bits):
     domains = lax.axis_size("dom")
     return lax.ppermute(value, "dom", [(i, i ^ bits) for i in range(domains)])
+
+
+def summed(values):
+    while len(values) > 1:
+        values = [values[i] + values[i + 1] for i in range(0, len(values), 2)]
+    return values[0]
 
 
 def on_device(
@@ -425,13 +450,18 @@
     domains = lax.axis_size("dom")
     box_x = 1.25 * (atoms * domains) / 64
     group = 2 if domains % 2 == 0 else 1
-    while group < domains and 4 * wave_count // group * atoms * domains > waves_bytes:
+    while (
+        group < domains
+        and 4 * wave_count // group * atoms * domains > waves_bytes
+        and wave_count % (256 * group) == 0
+    ):
         group *= 2
     share = wave_count // group
     entries = atoms + 2 * ghost_sends.shape[1]
 
     me = lax.axis_index("dom")
-    where = jnp.stack([me % 2, me % group]).astype(jnp.int32)
+    blocks = 4 if domains % 4 == 0 else 2
+    where = jnp.stack([me % 2, me % group, me % blocks]).astype(jnp.int32)
     packed = kernel(
         pack_kernel,
         "pack",
@@ -482,7 +512,6 @@
         scalars=(where,),
         wanted=60 * 1024 * 1024,
     )
-    blocks = 4 if domains % 4 == 0 else 2
     column = jnp.concatenate(
         [shared] + [across(shared, bits) for bits in range(blocks, domains, blocks)], axis=0
     )
@@ -522,12 +551,12 @@
     grad_parts = grad_parts[:1] + [across(grad_parts[m], m) for m in range(1, group)]
 
     rows = basis_count + width + charge_count + kinds
-    rows = -(-rows // (8 * domains)) * (8 * domains)
-    packed = kernel(
+    rows = -(-rows // (8 * blocks)) * 8
+    pieces = kernel(
         lambda *refs: weights_kernel(*refs, group=group, kinds=kinds),
         "weights",
-        shaped(rows, width),
-        (),
+        (shaped(rows, width),) * blocks,
+        (shaped(blocks * rows, width),),
         3_000,
         *grad_parts,
         filtered,
@@ -537,10 +566,11 @@
         species_row,
         mix_weight,
         charge_rows,
-    )
-    pieces = lax.all_to_all(packed.reshape(domains, rows // domains, width), "dom", 0, 0)
-    piece = jnp.sum(pieces, axis=0)
-    total = lax.all_to_all(jnp.broadcast_to(piece[None], pieces.shape), "dom", 0, 0)
+        scalars=(where,),
+    )
+    piece = summed([pieces[0]] + [across(pieces[r], r) for r in range(1, blocks)])
+    piece = summed([piece] + [across(piece, bits) for bits in range(blocks, domains, blocks)])
+    pieces = [piece] + [across(piece, r) for r in range(1, blocks)]
     radial_step, mix_step, charge_step, species_step = kernel(
         step_kernel,
         "steps",
@@ -550,9 +580,10 @@
             shaped(charge_count, width),
             shaped(kinds, charge_count),
         ),
-        (),
+        (shaped(blocks * rows, width),),
         2_000,
-        total.reshape(rows, width),
+        *pieces,
+        scalars=(where,),
     )
     return forces, radial_step, mix_step, charge_step.T, species_step
 

time: 90.3 us -> 84.5 us (0.936)
  blocking collectives: 22.1 us -> 0 us
  starting transfers between devices: 17.5 us -> 33.5 us
  waiting for transfers between devices: 16.2 us -> 26.1 us
  Pallas kernels: 31.2 us -> 21.8 us
    all_to_all x2 -> x0, blocking collectives: 22.1 us -> none  [the longest x1 11.7 us: on_device(): lax.all_to_all(packed.reshape(domains, rows // domains, width), 'dom', 0, 0)]
    ppermute x9 -> x22, starting transfers between devices: 10.6 us -> 26.5 us  [across(): return lax.ppermute(value, 'dom', [(i, i ^ bits) for i in range(domains)])]
    ppermute x9 -> x22, waiting for transfers between devices: 14.2 us -> 24.1 us  [across(): return lax.ppermute(value, 'dom', [(i, i ^ bits) for i in range(domains)])]
    pallas_call x6, Pallas kernels: 31.2 us -> 21.8 us  [kernel(): pl.pallas_call(body, out_shape=out_shape, in_specs=[in_smem] * len(scalar...]
  transfers between devices with their start and end apart: 10 -> 23, of which waited for: 7 -> 19; matrix products, arithmetic and copies ran while one was open for 2% -> 2% of each run, Pallas kernels for 0% -> 0%
where the time goes in v4:
time: 84.5 us; the launch traced here: 84.2 us
  starting transfers between devices  33.5 us (40%)
  waiting for transfers between devices  26.1 us (31%)
  Pallas kernels  21.8 us (26%)
  local copies, waits for them, and re-layouts  1.5 us (2%)
    ppermute x22, starting transfers between devices, across(): return lax.ppermute(value, 'dom', [(i, i ^ bits) for i in range(domains)])  26.5 us
    ppermute x22, waiting for transfers between devices, across(): return lax.ppermute(value, 'dom', [(i, i ^ bits) for i in range(domains)])  24.1 us
    pallas_call x6, Pallas kernels, kernel(): pl.pallas_call(body, out_shape=out_shape, in_specs=[in_smem] * len(scalar...  21.8 us
    ppermute x1, starting transfers between devices, on_device(): far = lax.ppermute(packed, 'dom', beyond)  6.93 us
    ppermute x1, waiting for transfers between devices, on_device(): far = lax.ppermute(packed, 'dom', beyond)  2.01 us
  transfers between devices with their start and end apart: 23, of which 19 were waited for; matrix products, arithmetic and copies ran while one was open for 2% of the time, Pallas kernels for 0%

profile of v4, /device:TPU:0, one launch (start us, length us, event | category | flops | bytes accessed | tf_op | source)
XLA Modules:
  0.0 84.2 jit_solution(15424692943158627522)
XLA Ops:
  0.6 1.5 %pack.1 = bf16[288,128]{1,0:T(8,128)(2,1)} custom-call(bf16[256,128]{1,0:T(8,128)(2,1)} %refs_1_.1, f32[3,256]{1,0:T(4,128)} %refs_2_.1, s32[2,256]{1,0:T(2,128)} %ghost_ref.1), custom_call_target="tpu_custom_call" | custom-call | flops 1000000000 | bytes 144384 | tf_op jit(solution)/shard_map/pack/pallas_call | solution.py:406
  2.1 6.9 %collective-permute-start.1 = (bf16[288,128]{1,0:T(8,128)(2,1)}, bf16[288,128]{1,0:T(8,128)(2,1)S(1)}, u32[]{:S(2)}, u32[]{:S(2)}) collective-permute-start(bf16[288,128]{1,0:T(8,128)(2,1)} %pack.1), channel_id=1, source_target_pairs={{0,30},{2,4},{4,2},{6,8},{8,6},{10,12},{12,10},{14,16},{16,14},{18... | collective-permute-start | bytes 221192 | tf_op jit(solution)/shard_map/ppermute | solution.py:478
  9.7 2.0 %collective-permute-done.1.refs_5_ = bf16[288,128]{1,0:T(8,128)(2,1)S(1)} collective-permute-done((bf16[288,128]{1,0:T(8,128)(2,1)}, bf16[288,128]{1,0:T(8,128)(2,1)S(1)}, u32[]{:S(2)}, u32[]{:S(2)}) %collective-permute-start.1) | collective-permute-done | bytes 73760 | tf_op jit(solution)/shard_map/ppermute | solution.py:478
  11.7 2.0 %collective-permute-done.refs_4_ = bf16[288,128]{1,0:T(8,128)(2,1)S(1)} collective-permute-done((bf16[288,128]{1,0:T(8,128)(2,1)}, bf16[288,128]{1,0:T(8,128)(2,1)S(1)}, u32[]{:S(2)}, u32[]{:S(2)}) %collective-permute-start) | collective-permute-done | bytes 73760 | tf_op jit(solution)/shard_map/ppermute | solution.py:422
  14.3 7.9 %edges.1 = (f32[16,128,256]{2,1,0:T(8,128)}, f32[128,256]{1,0:T(8,128)}, f32[128,256]{1,0:T(8,128)}, bf16[128,256]{1,0:T(8,128)(2,1)}, bf16[1,80,256]{2,1,0:T(8,128)(2,1)}) custom-call(s32[3]{0:T(128)} %pad_add_fusion.refs_0_.where_ref, bf16[256,128]{1,0:T(8,128)(2,1)} %refs_1_.1, f32[3,256]{1,0:T(4,128)} %refs_2_.1, f32[3,256]{1,0:T(4,128)} %refs_3_.1, ...), custom_call_target="tpu_custom_call" | custom-call | flops 12000000000 | bytes 9344512 | tf_op jit(solution)/shard_map/edges/pallas_call | solution.py:406
  22.8 3.8 %collective-permute-start.2 = (bf16[1,80,256]{2,1,0:T(8,128)(2,1)}, bf16[1,80,256]{2,1,0:T(8,128)(2,1)S(1)}, u32[]{:S(2)}, u32[]{:S(2)}) collective-permute-start(bf16[1,80,256]{2,1,0:T(8,128)(2,1)} %get-tuple-element.29), channel_id=1, source_target_pairs={{0,8},{2,10},{4,12},{6,14},{8,0},{10,2},{12,4},{14,6},{16,24},{18,... | collective-permute-start | bytes 122888 | tf_op jit(solution)/shard_map/ppermute | solution.py:422
  27.4 1.4 %collective-permute-done.2 = bf16[1,80,256]{2,1,0:T(8,128)(2,1)S(1)} collective-permute-done((bf16[1,80,256]{2,1,0:T(8,128)(2,1)}, bf16[1,80,256]{2,1,0:T(8,128)(2,1)S(1)}, u32[]{:S(2)}, u32[]{:S(2)}) %collective-permute-start.2) | collective-permute-done | bytes 40992 | tf_op jit(solution)/shard_map/ppermute | solution.py:422
  28.9 2.7 %collective-permute-start.7 = (bf16[4,80,256]{2,1,0:T(8,128)(2,1)S(1)}, bf16[4,80,256]{2,1,0:T(8,128)(2,1)S(1)}, u32[]{:S(2)}, u32[]{:S(2)}) collective-permute-start(bf16[4,80,256]{2,1,0:T(8,128)(2,1)S(1)} %constant_dynamic-update-slice_fusion.refs_1_), channel_id=1, source_target_pairs={{0,6},{2,4},{4,2},{6,0},{8,14},{10,12},{12,10},{14,8},{16,22},{18,... | collective-permute-start | bytes 491528 | tf_op jit(solution)/shard_map/ppermute | solution.py:422
  32.4 4.0 %collective-permute-done.7.refs_4_ = bf16[4,80,256]{2,1,0:T(8,128)(2,1)S(1)} collective-permute-done((bf16[4,80,256]{2,1,0:T(8,128)(2,1)S(1)}, bf16[4,80,256]{2,1,0:T(8,128)(2,1)S(1)}, u32[]{:S(2)}, u32[]{:S(2)}) %collective-permute-start.7) | collective-permute-done | bytes 163872 | tf_op jit(solution)/shard_map/ppermute | solution.py:422
  36.4 1.3 %collective-permute-done.6.refs_3_ = bf16[4,80,256]{2,1,0:T(8,128)(2,1)S(1)} collective-permute-done((bf16[4,80,256]{2,1,0:T(8,128)(2,1)S(1)}, bf16[4,80,256]{2,1,0:T(8,128)(2,1)S(1)}, u32[]{:S(2)}, u32[]{:S(2)}) %collective-permute-start.6) | collective-permute-done | bytes 163872 | tf_op jit(solution)/shard_map/ppermute | solution.py:422
  37.8 5.8 %structure.1 = (bf16[16,512,256]{2,1,0:T(8,128)(2,1)S(1)}, f32[192,512]{1,0:T(8,128)S(1)}, f32[3,16,256]{2,1,0:T(8,128)S(1)}, f32[3,16,256]{2,1,0:T(8,128)S(1)},...) custom-call(s32[3]{0:T(128)S(1)} %copy-done.4, bf16[4,80,256]{2,1,0:T(8,128)(2,1)S(1)} %constant_dynamic-update-slice_fusion.refs_1_, ...), custom_call_target="tpu_custom_call" | custom-call | flops 10000000000 | bytes 5451776 | tf_op jit(solution)/shard_map/structure/pallas_call | solution.py:406
  43.6 1.4 %collective-permute-start.8 = (f32[3,16,256]{2,1,0:T(8,128)S(1)}, f32[3,16,256]{2,1,0:T(8,128)S(1)}, u32[]{:S(2)}, u32[]{:S(2)}) collective-permute-start(f32[3,16,256]{2,1,0:T(8,128)S(1)} %get-tuple-element.31), channel_id=1, source_target_pairs={{0,2},{2,0},{4,6},{6,4},{8,10},{10,8},{12,14},{14,12},{16,18},{18,... | collective-permute-start | bytes 147464 | tf_op jit(solution)/shard_map/ppermute | solution.py:422
  45.5 1.6 %collective-permute-start.10 = (f32[3,16,256]{2,1,0:T(8,128)S(1)}, f32[3,16,256]{2,1,0:T(8,128)S(1)}, u32[]{:S(2)}, u32[]{:S(2)}) collective-permute-start(f32[3,16,256]{2,1,0:T(8,128)S(1)} %get-tuple-element.33), channel_id=1, source_target_pairs={{0,6},{2,4},{4,2},{6,0},{8,14},{10,12},{12,10},{14,8},{16,22},{18,... | collective-permute-start | bytes 147464 | tf_op jit(solution)/shard_map/ppermute | solution.py:422
  47.7 1.3 %collective-permute-done.9.refs_7_ = f32[3,16,256]{2,1,0:T(8,128)S(1)} collective-permute-done((f32[3,16,256]{2,1,0:T(8,128)S(1)}, f32[3,16,256]{2,1,0:T(8,128)S(1)}, u32[]{:S(2)}, u32[]{:S(2)}) %collective-permute-start.9) | collective-permute-done | bytes 49184 | tf_op jit(solution)/shard_map/ppermute | solution.py:422
  49.1 1.5 %collective-permute-done.10.refs_8_ = f32[3,16,256]{2,1,0:T(8,128)S(1)} collective-permute-done((f32[3,16,256]{2,1,0:T(8,128)S(1)}, f32[3,16,256]{2,1,0:T(8,128)S(1)}, u32[]{:S(2)}, u32[]{:S(2)}) %collective-permute-start.10) | collective-permute-done | bytes 49184 | tf_op jit(solution)/shard_map/ppermute | solution.py:422
  50.6 3.5 %gradient.1 = (f32[3,256]{1,0:T(4,128)}, bf16[64,256]{1,0:T(8,128)(2,1)S(1)}, bf16[64,256]{1,0:T(8,128)(2,1)S(1)}, bf16[64,256]{1,0:T(8,128)(2,1)S(1)}, bf16[64,256]{1,0:T(8,128)(2,1)S(1)}) custom-call(s32[3]{0:T(128)S(1)} %copy-done.4, bf16[4,80,256]{2,1,0:T(8,128)(2,1)S(1)} %constant_dynamic-update-slice_fusion.refs_1_, ...), custom_call_target="tpu_custom_call" | custom-call | flops 5000000000 | bytes 5635072 | tf_op jit(solution)/shard_map/gradient/pallas_call | solution.py:406
  54.0 1.3 %collective-permute-start.11 = (bf16[64,256]{1,0:T(8,128)(2,1)S(1)}, bf16[64,256]{1,0:T(8,128)(2,1)S(1)}, u32[]{:S(2)}, u32[]{:S(2)}) collective-permute-start(bf16[64,256]{1,0:T(8,128)(2,1)S(1)} %get-tuple-element.38), channel_id=1, source_target_pairs={{0,2},{2,0},{4,6},{6,4},{8,10},{10,8},{12,14},{14,12},{16,18},{18,... | collective-permute-start | bytes 98312 | tf_op jit(solution)/shard_map/ppermute | solution.py:422
  56.2 1.3 %collective-permute-start.13 = (bf16[64,256]{1,0:T(8,128)(2,1)S(1)}, bf16[64,256]{1,0:T(8,128)(2,1)S(1)}, u32[]{:S(2)}, u32[]{:S(2)}) collective-permute-start(bf16[64,256]{1,0:T(8,128)(2,1)S(1)} %get-tuple-element.40), channel_id=1, source_target_pairs={{0,6},{2,4},{4,2},{6,0},{8,14},{10,12},{12,10},{14,8},{16,22},{18,... | collective-permute-start | bytes 98312 | tf_op jit(solution)/shard_map/ppermute | solution.py:422
  58.0 1.3 %collective-permute-done.12.refs_3_ = bf16[64,256]{1,0:T(8,128)(2,1)S(1)} collective-permute-done((bf16[64,256]{1,0:T(8,128)(2,1)S(1)}, bf16[64,256]{1,0:T(8,128)(2,1)S(1)}, u32[]{:S(2)}, u32[]{:S(2)}) %collective-permute-start.12) | collective-permute-done | bytes 32800 | tf_op jit(solution)/shard_map/ppermute | solution.py:422
  59.3 1.8 %collective-permute-done.13.refs_4_ = bf16[64,256]{1,0:T(8,128)(2,1)S(1)} collective-permute-done((bf16[64,256]{1,0:T(8,128)(2,1)S(1)}, bf16[64,256]{1,0:T(8,128)(2,1)S(1)}, u32[]{:S(2)}, u32[]{:S(2)}) %collective-permute-start.13) | collective-permute-done | bytes 32800 | tf_op jit(solution)/shard_map/ppermute | solution.py:422
  61.1 1.7 %weights.1 = (f32[56,128]{1,0:T(8,128)S(1)}, f32[56,128]{1,0:T(8,128)S(1)}, f32[56,128]{1,0:T(8,128)S(1)}, f32[56,128]{1,0:T(8,128)S(1)}) custom-call(s32[3]{0:T(128)S(1)} %copy-done.4, bf16[64,256]{1,0:T(8,128)(2,1)S(1)} %get-tuple-element.37.refs_1_, bf16[64,256]{1,0:T(8,128)(2,1)S(1)} %collective-permute-done.11.refs_2_, ...), custom_call_target="tpu_custom_call" | custom-call | flops 3000000000 | bytes 2835456 | tf_op jit(solution)/shard_map/weights/pallas_call | solution.py:406
  62.8 1.4 %collective-permute-start.14 = (f32[56,128]{1,0:T(8,128)S(1)}, f32[56,128]{1,0:T(8,128)S(1)}, u32[]{:S(2)}, u32[]{:S(2)}) collective-permute-start(f32[56,128]{1,0:T(8,128)S(1)} %get-tuple-element.46), channel_id=1, source_target_pairs={{0,2},{2,0},{4,6},{6,4},{8,10},{10,8},{12,14},{14,12},{16,18},{18,... | collective-permute-start | bytes 86024 | tf_op jit(solution)/shard_map/ppermute | solution.py:422
  64.8 1.6 %collective-permute-start.16 = (f32[56,128]{1,0:T(8,128)S(1)}, f32[56,128]{1,0:T(8,128)S(1)}, u32[]{:S(2)}, u32[]{:S(2)}) collective-permute-start(f32[56,128]{1,0:T(8,128)S(1)} %get-tuple-element.48), channel_id=1, source_target_pairs={{0,6},{2,4},{4,2},{6,0},{8,14},{10,12},{12,10},{14,8},{16,22},{18,... | collective-permute-start | bytes 86024 | tf_op jit(solution)/shard_map/ppermute | solution.py:422
  66.7 1.4 %collective-permute-done.15 = f32[56,128]{1,0:T(8,128)S(1)} collective-permute-done((f32[56,128]{1,0:T(8,128)S(1)}, f32[56,128]{1,0:T(8,128)S(1)}, u32[]{:S(2)}, u32[]{:S(2)}) %collective-permute-start.15) | collective-permute-done | bytes 28704 | tf_op jit(solution)/shard_map/ppermute | solution.py:422
  68.1 1.5 %collective-permute-done.16 = f32[56,128]{1,0:T(8,128)S(1)} collective-permute-done((f32[56,128]{1,0:T(8,128)S(1)}, f32[56,128]{1,0:T(8,128)S(1)}, u32[]{:S(2)}, u32[]{:S(2)}) %collective-permute-start.16) | collective-permute-done | bytes 28704 | tf_op jit(solution)/shard_map/ppermute | solution.py:422
  69.6 2.1 %collective-permute-start.19 = (f32[56,128]{1,0:T(8,128)S(1)}, f32[56,128]{1,0:T(8,128)S(1)}, u32[]{:S(2)}, u32[]{:S(2)}) collective-permute-start(f32[56,128]{1,0:T(8,128)S(1)} %add_add_fusion.1), channel_id=1, source_target_pairs={{0,24},{2,26},{4,28},{6,30},{8,16},{10,18},{12,20},{14,22},{16,8},... | collective-permute-start | bytes 86024 | tf_op jit(solution)/shard_map/ppermute | solution.py:422
  72.1 1.9 %collective-permute-start.17 = (f32[56,128]{1,0:T(8,128)S(1)}, f32[56,128]{1,0:T(8,128)S(1)}, u32[]{:S(2)}, u32[]{:S(2)}) collective-permute-start(f32[56,128]{1,0:T(8,128)S(1)} %add_add_fusion.1), channel_id=1, source_target_pairs={{0,8},{2,10},{4,12},{6,14},{8,0},{10,2},{12,4},{14,6},{16,24},{18,... | collective-permute-start | bytes 86024 | tf_op jit(solution)/shard_map/ppermute | solution.py:422
  74.0 1.3 %collective-permute-done.19 = f32[56,128]{1,0:T(8,128)S(1)} collective-permute-done((f32[56,128]{1,0:T(8,128)S(1)}, f32[56,128]{1,0:T(8,128)S(1)}, u32[]{:S(2)}, u32[]{:S(2)}) %collective-permute-start.19) | collective-permute-done | bytes 28704 | tf_op jit(solution)/shard_map/ppermute | solution.py:422
  75.3 1.3 %collective-permute-done.18 = f32[56,128]{1,0:T(8,128)S(1)} collective-permute-done((f32[56,128]{1,0:T(8,128)S(1)}, f32[56,128]{1,0:T(8,128)S(1)}, u32[]{:S(2)}, u32[]{:S(2)}) %collective-permute-start.18) | collective-permute-done | bytes 28704 | tf_op jit(solution)/shard_map/ppermute | solution.py:422
  76.6 1.4 %collective-permute-start.22 = (f32[56,128]{1,0:T(8,128)S(1)}, f32[56,128]{1,0:T(8,128)S(1)}, u32[]{:S(2)}, u32[]{:S(2)}) collective-permute-start(f32[56,128]{1,0:T(8,128)S(1)} %add_add_fusion.refs_0_), channel_id=1, source_target_pairs={{0,6},{2,4},{4,2},{6,0},{8,14},{10,12},{12,10},{14,8},{16,22},{18,... | collective-permute-start | bytes 86024 | tf_op jit(solution)/shard_map/ppermute | solution.py:422
  80.2 1.3 %collective-permute-done.22.refs_3_ = f32[56,128]{1,0:T(8,128)S(1)} collective-permute-done((f32[56,128]{1,0:T(8,128)S(1)}, f32[56,128]{1,0:T(8,128)S(1)}, u32[]{:S(2)}, u32[]{:S(2)}) %collective-permute-start.22) | collective-permute-done | bytes 28704 | tf_op jit(solution)/shard_map/ppermute | solution.py:422
  82.9 1.3 %steps.1 = (f32[16,128]{1,0:T(8,128)}, f32[128,128]{1,0:T(8,128)}, f32[64,128]{1,0:T(8,128)}, f32[6,64]{1,0:T(8,128)}) custom-call(s32[3]{0:T(128)S(1)} %copy-done.4, f32[56,128]{1,0:T(8,128)S(1)} %add_add_fusion.refs_0_, f32[56,128]{1,0:T(8,128)S(1)} %collective-permute-done.20.refs_1_, f32[56,128]{1,0:T(8,128)S(1)} %collective-permute-done.21.refs_2_, ...), custom_call_target="tpu_custom_call" | custom-call | flops 2000000000 | bytes 337408 | tf_op jit(solution)/shard_map/steps/pallas_call | solution.py:406
  (49 shorter events, 11.0 us)
Async XLA Ops:
  2.1 9.5 %collective-permute-start.1 = (bf16[288,128]{1,0:T(8,128)(2,1)}, bf16[288,128]{1,0:T(8,128)(2,1)S(1)}, u32[]{:S(2)}, u32[]{:S(2)}) collective-permute-start(bf16[288,128]{1,0:T(8,128)(2,1)} %pack.1), channel_id=1, source_target_pairs={{0,30},{2,4},{4,2},{6,8},{8,6},{10,12},{12,10},{14,16},{16,14},{18... | collective-permute-start | bytes 221192 | tf_op jit(solution)/shard_map/ppermute | solution.py:478
  9.1 4.6 %collective-permute-start = (bf16[288,128]{1,0:T(8,128)(2,1)}, bf16[288,128]{1,0:T(8,128)(2,1)S(1)}, u32[]{:S(2)}, u32[]{:S(2)}) collective-permute-start(bf16[288,128]{1,0:T(8,128)(2,1)} %pack.1), channel_id=1, source_target_pairs={{0,2},{2,0},{4,6},{6,4},{8,10},{10,8},{12,14},{14,12},{16,18},{18,... | collective-permute-start | bytes 221192 | tf_op jit(solution)/shard_map/ppermute | solution.py:422
  14.3 23.5 %copy-start.1 = (s32[3,1024]{1,0:T(4,128)S(1)}, s32[3,1024]{1,0:T(4,128)}, u32[]{:S(2)}) copy-start(s32[3,1024]{1,0:T(4,128)} %refs_9_.3) | copy-start | bytes 36868
  14.3 23.5 %copy-start.4 = (s32[3]{0:T(128)S(1)}, s32[3]{0:T(128)}, u32[]{:S(2)}) copy-start(s32[3]{0:T(128)} %pad_add_fusion.refs_0_.where_ref) | copy-start | bytes 40
  22.2 6.7 %collective-permute-start.4 = (bf16[1,80,256]{2,1,0:T(8,128)(2,1)}, bf16[1,80,256]{2,1,0:T(8,128)(2,1)S(1)}, u32[]{:S(2)}, u32[]{:S(2)}) collective-permute-start(bf16[1,80,256]{2,1,0:T(8,128)(2,1)} %get-tuple-element.29), channel_id=1, source_target_pairs={{0,24},{2,26},{4,28},{6,30},{8,16},{10,18},{12,20},{14,22},{16,8},... | collective-permute-start | bytes 122888 | tf_op jit(solution)/shard_map/ppermute | solution.py:422
  22.8 6.1 %collective-permute-start.3 = (bf16[1,80,256]{2,1,0:T(8,128)(2,1)}, bf16[1,80,256]{2,1,0:T(8,128)(2,1)S(1)}, u32[]{:S(2)}, u32[]{:S(2)}) collective-permute-start(bf16[1,80,256]{2,1,0:T(8,128)(2,1)} %get-tuple-element.29), channel_id=1, source_target_pairs={{0,16},{2,18},{4,20},{6,22},{8,24},{10,26},{12,28},{14,30},{16,0},... | collective-permute-start | bytes 122888 | tf_op jit(solution)/shard_map/ppermute | solution.py:422
  22.8 6.0 %collective-permute-start.2 = (bf16[1,80,256]{2,1,0:T(8,128)(2,1)}, bf16[1,80,256]{2,1,0:T(8,128)(2,1)S(1)}, u32[]{:S(2)}, u32[]{:S(2)}) collective-permute-start(bf16[1,80,256]{2,1,0:T(8,128)(2,1)} %get-tuple-element.29), channel_id=1, source_target_pairs={{0,8},{2,10},{4,12},{6,14},{8,0},{10,2},{12,4},{14,6},{16,24},{18,... | collective-permute-start | bytes 122888 | tf_op jit(solution)/shard_map/ppermute | solution.py:422
  28.9 7.6 %collective-permute-start.7 = (bf16[4,80,256]{2,1,0:T(8,128)(2,1)S(1)}, bf16[4,80,256]{2,1,0:T(8,128)(2,1)S(1)}, u32[]{:S(2)}, u32[]{:S(2)}) collective-permute-start(bf16[4,80,256]{2,1,0:T(8,128)(2,1)S(1)} %constant_dynamic-update-slice_fusion.refs_1_), channel_id=1, source_target_pairs={{0,6},{2,4},{4,2},{6,0},{8,14},{10,12},{12,10},{14,8},{16,22},{18,... | collective-permute-start | bytes 491528 | tf_op jit(solution)/shard_map/ppermute | solution.py:422
  31.6 6.2 %collective-permute-start.6 = (bf16[4,80,256]{2,1,0:T(8,128)(2,1)S(1)}, bf16[4,80,256]{2,1,0:T(8,128)(2,1)S(1)}, u32[]{:S(2)}, u32[]{:S(2)}) collective-permute-start(bf16[4,80,256]{2,1,0:T(8,128)(2,1)S(1)} %constant_dynamic-update-slice_fusion.refs_1_), channel_id=1, source_target_pairs={{0,4},{2,6},{4,0},{6,2},{8,12},{10,14},{12,8},{14,10},{16,20},{18,... | collective-permute-start | bytes 491528 | tf_op jit(solution)/shard_map/ppermute | solution.py:422
  31.6 6.2 %collective-permute-start.5 = (bf16[4,80,256]{2,1,0:T(8,128)(2,1)S(1)}, bf16[4,80,256]{2,1,0:T(8,128)(2,1)S(1)}, u32[]{:S(2)}, u32[]{:S(2)}) collective-permute-start(bf16[4,80,256]{2,1,0:T(8,128)(2,1)S(1)} %constant_dynamic-update-slice_fusion.refs_1_), channel_id=1, source_target_pairs={{0,2},{2,0},{4,6},{6,4},{8,10},{10,8},{12,14},{14,12},{16,18},{18,... | collective-permute-start | bytes 491528 | tf_op jit(solution)/shard_map/ppermute | solution.py:422
  43.6 4.2 %collective-permute-start.8 = (f32[3,16,256]{2,1,0:T(8,128)S(1)}, f32[3,16,256]{2,1,0:T(8,128)S(1)}, u32[]{:S(2)}, u32[]{:S(2)}) collective-permute-start(f32[3,16,256]{2,1,0:T(8,128)S(1)} %get-tuple-element.31), channel_id=1, source_target_pairs={{0,2},{2,0},{4,6},{6,4},{8,10},{10,8},{12,14},{14,12},{16,18},{18,... | collective-permute-start | bytes 147464 | tf_op jit(solution)/shard_map/ppermute | solution.py:422
  45.0 4.1 %collective-permute-start.9 = (f32[3,16,256]{2,1,0:T(8,128)S(1)}, f32[3,16,256]{2,1,0:T(8,128)S(1)}, u32[]{:S(2)}, u32[]{:S(2)}) collective-permute-start(f32[3,16,256]{2,1,0:T(8,128)S(1)} %get-tuple-element.32), channel_id=1, source_target_pairs={{0,4},{2,6},{4,0},{6,2},{8,12},{10,14},{12,8},{14,10},{16,20},{18,... | collective-permute-start | bytes 147464 | tf_op jit(solution)/shard_map/ppermute | solution.py:422
  45.5 5.0 %collective-permute-start.10 = (f32[3,16,256]{2,1,0:T(8,128)S(1)}, f32[3,16,256]{2,1,0:T(8,128)S(1)}, u32[]{:S(2)}, u32[]{:S(2)}) collective-permute-start(f32[3,16,256]{2,1,0:T(8,128)S(1)} %get-tuple-element.33), channel_id=1, source_target_pairs={{0,6},{2,4},{4,2},{6,0},{8,14},{10,12},{12,10},{14,8},{16,22},{18,... | collective-permute-start | bytes 147464 | tf_op jit(solution)/shard_map/ppermute | solution.py:422
  50.5 10.5 %copy-start = (bf16[128,128]{1,0:T(8,128)(2,1)S(1)}, bf16[128,128]{1,0:T(8,128)(2,1)}, u32[]{:S(2)}) copy-start(bf16[128,128]{1,0:T(8,128)(2,1)} %refs_10_.3) | copy-start | bytes 98308
  50.5 10.5 %copy-start.2 = (bf16[128,64]{0,1:T(8,128)(2,1)S(1)}, bf16[128,64]{0,1:T(8,128)(2,1)}, u32[]{:S(2)}) copy-start(bf16[128,64]{0,1:T(8,128)(2,1)} %param.22) | copy-start | bytes 49156
  50.5 10.5 %copy-start.3 = (s32[256]{0:T(256)S(1)}, s32[256]{0:T(256)}, u32[]{:S(2)}) copy-start(s32[256]{0:T(256)} %param.17) | copy-start | bytes 3076
  50.5 10.5 %copy-start.5 = (f32[16,128,256]{2,1,0:T(8,128)S(1)}, f32[16,128,256]{2,1,0:T(8,128)}, u32[]{:S(2)}) copy-start(f32[16,128,256]{2,1,0:T(8,128)} %get-tuple-element.41.refs_5_) | copy-start | bytes 6291460
  50.5 10.5 %copy-start.6 = (f32[128,256]{1,0:T(8,128)S(1)}, f32[128,256]{1,0:T(8,128)}, u32[]{:S(2)}) copy-start(f32[128,256]{1,0:T(8,128)} %get-tuple-element.42.refs_6_) | copy-start | bytes 393220
  50.5 10.5 %copy-start.7 = (f32[128,256]{1,0:T(8,128)S(1)}, f32[128,256]{1,0:T(8,128)}, u32[]{:S(2)}) copy-start(f32[128,256]{1,0:T(8,128)} %get-tuple-element.43.refs_7_) | copy-start | bytes 393220
  50.6 10.5 %copy-start.8 = (bf16[128,256]{1,0:T(8,128)(2,1)S(1)}, bf16[128,256]{1,0:T(8,128)(2,1)}, u32[]{:S(2)}) copy-start(bf16[128,256]{1,0:T(8,128)(2,1)} %get-tuple-element.44.refs_8_) | copy-start | bytes 196612
  54.0 3.9 %collective-permute-start.11 = (bf16[64,256]{1,0:T(8,128)(2,1)S(1)}, bf16[64,256]{1,0:T(8,128)(2,1)S(1)}, u32[]{:S(2)}, u32[]{:S(2)}) collective-permute-start(bf16[64,256]{1,0:T(8,128)(2,1)S(1)} %get-tuple-element.38), channel_id=1, source_target_pairs={{0,2},{2,0},{4,6},{6,4},{8,10},{10,8},{12,14},{14,12},{16,18},{18,... | collective-permute-start | bytes 98312 | tf_op jit(solution)/shard_map/ppermute | solution.py:422
  55.4 3.9 %collective-permute-start.12 = (bf16[64,256]{1,0:T(8,128)(2,1)S(1)}, bf16[64,256]{1,0:T(8,128)(2,1)S(1)}, u32[]{:S(2)}, u32[]{:S(2)}) collective-permute-start(bf16[64,256]{1,0:T(8,128)(2,1)S(1)} %get-tuple-element.39), channel_id=1, source_target_pairs={{0,4},{2,6},{4,0},{6,2},{8,12},{10,14},{12,8},{14,10},{16,20},{18,... | collective-permute-start | bytes 98312 | tf_op jit(solution)/shard_map/ppermute | solution.py:422
  56.2 4.8 %collective-permute-start.13 = (bf16[64,256]{1,0:T(8,128)(2,1)S(1)}, bf16[64,256]{1,0:T(8,128)(2,1)S(1)}, u32[]{:S(2)}, u32[]{:S(2)}) collective-permute-start(bf16[64,256]{1,0:T(8,128)(2,1)S(1)} %get-tuple-element.40), channel_id=1, source_target_pairs={{0,6},{2,4},{4,2},{6,0},{8,14},{10,12},{12,10},{14,8},{16,22},{18,... | collective-permute-start | bytes 98312 | tf_op jit(solution)/shard_map/ppermute | solution.py:422
  62.8 3.9 %collective-permute-start.14 = (f32[56,128]{1,0:T(8,128)S(1)}, f32[56,128]{1,0:T(8,128)S(1)}, u32[]{:S(2)}, u32[]{:S(2)}) collective-permute-start(f32[56,128]{1,0:T(8,128)S(1)} %get-tuple-element.46), channel_id=1, source_target_pairs={{0,2},{2,0},{4,6},{6,4},{8,10},{10,8},{12,14},{14,12},{16,18},{18,... | collective-permute-start | bytes 86024 | tf_op jit(solution)/shard_map/ppermute | solution.py:422
  64.2 3.9 %collective-permute-start.15 = (f32[56,128]{1,0:T(8,128)S(1)}, f32[56,128]{1,0:T(8,128)S(1)}, u32[]{:S(2)}, u32[]{:S(2)}) collective-permute-start(f32[56,128]{1,0:T(8,128)S(1)} %get-tuple-element.47), channel_id=1, source_target_pairs={{0,4},{2,6},{4,0},{6,2},{8,12},{10,14},{12,8},{14,10},{16,20},{18,... | collective-permute-start | bytes 86024 | tf_op jit(solution)/shard_map/ppermute | solution.py:422
  64.8 4.8 %collective-permute-start.16 = (f32[56,128]{1,0:T(8,128)S(1)}, f32[56,128]{1,0:T(8,128)S(1)}, u32[]{:S(2)}, u32[]{:S(2)}) collective-permute-start(f32[56,128]{1,0:T(8,128)S(1)} %get-tuple-element.48), channel_id=1, source_target_pairs={{0,6},{2,4},{4,2},{6,0},{8,14},{10,12},{12,10},{14,8},{16,22},{18,... | collective-permute-start | bytes 86024 | tf_op jit(solution)/shard_map/ppermute | solution.py:422
  69.6 5.7 %collective-permute-start.19 = (f32[56,128]{1,0:T(8,128)S(1)}, f32[56,128]{1,0:T(8,128)S(1)}, u32[]{:S(2)}, u32[]{:S(2)}) collective-permute-start(f32[56,128]{1,0:T(8,128)S(1)} %add_add_fusion.1), channel_id=1, source_target_pairs={{0,24},{2,26},{4,28},{6,30},{8,16},{10,18},{12,20},{14,22},{16,8},... | collective-permute-start | bytes 86024 | tf_op jit(solution)/shard_map/ppermute | solution.py:422
  71.7 4.9 %collective-permute-start.18 = (f32[56,128]{1,0:T(8,128)S(1)}, f32[56,128]{1,0:T(8,128)S(1)}, u32[]{:S(2)}, u32[]{:S(2)}) collective-permute-start(f32[56,128]{1,0:T(8,128)S(1)} %add_add_fusion.1), channel_id=1, source_target_pairs={{0,16},{2,18},{4,20},{6,22},{8,24},{10,26},{12,28},{14,30},{16,0},... | collective-permute-start | bytes 86024 | tf_op jit(solution)/shard_map/ppermute | solution.py:422
  72.1 4.5 %collective-permute-start.17 = (f32[56,128]{1,0:T(8,128)S(1)}, f32[56,128]{1,0:T(8,128)S(1)}, u32[]{:S(2)}, u32[]{:S(2)}) collective-permute-start(f32[56,128]{1,0:T(8,128)S(1)} %add_add_fusion.1), channel_id=1, source_target_pairs={{0,8},{2,10},{4,12},{6,14},{8,0},{10,2},{12,4},{14,6},{16,24},{18,... | collective-permute-start | bytes 86024 | tf_op jit(solution)/shard_map/ppermute | solution.py:422
  76.6 4.8 %collective-permute-start.22 = (f32[56,128]{1,0:T(8,128)S(1)}, f32[56,128]{1,0:T(8,128)S(1)}, u32[]{:S(2)}, u32[]{:S(2)}) collective-permute-start(f32[56,128]{1,0:T(8,128)S(1)} %add_add_fusion.refs_0_), channel_id=1, source_target_pairs={{0,6},{2,4},{4,2},{6,0},{8,14},{10,12},{12,10},{14,8},{16,22},{18,... | collective-permute-start | bytes 86024 | tf_op jit(solution)/shard_map/ppermute | solution.py:422
  78.0 3.9 %collective-permute-start.21 = (f32[56,128]{1,0:T(8,128)S(1)}, f32[56,128]{1,0:T(8,128)S(1)}, u32[]{:S(2)}, u32[]{:S(2)}) collective-permute-start(f32[56,128]{1,0:T(8,128)S(1)} %add_add_fusion.refs_0_), channel_id=1, source_target_pairs={{0,4},{2,6},{4,0},{6,2},{8,12},{10,14},{12,8},{14,10},{16,20},{18,... | collective-permute-start | bytes 86024 | tf_op jit(solution)/shard_map/ppermute | solution.py:422
  79.0 3.9 %collective-permute-start.20 = (f32[56,128]{1,0:T(8,128)S(1)}, f32[56,128]{1,0:T(8,128)S(1)}, u32[]{:S(2)}, u32[]{:S(2)}) collective-permute-start(f32[56,128]{1,0:T(8,128)S(1)} %add_add_fusion.refs_0_), channel_id=1, source_target_pairs={{0,2},{2,0},{4,6},{6,4},{8,10},{10,8},{12,14},{14,12},{16,18},{18,... | collective-permute-start | bytes 86024 | tf_op jit(solution)/shard_map/ppermute | solution.py:422
  (2 other events, 2.6 us)

commit v5 on v4

--- a/solution.py
+++ b/solution.py
@@ -17,7 +17,8 @@
 f32 = jnp.float32
 bf16 = jnp.bfloat16
 spare_vmem = 4 * 1024 * 1024
-waves_bytes = 4 * 1024 * 1024
+waves_bytes = 8 * 1024 * 1024
+own_vmem = 50 * 1024 * 1024
 
 
 def fitted(function, degrees, reach):
@@ -78,71 +79,8 @@
         packed_ref[first : first + 16, :] = extra[:, part * width : (part + 1) * width]
 
 
-def edge_kernel(
-    where_ref,
-    feat_ref,
-    positions_ref,
-    force_ref,
-    near_ref,
-    far_ref,
-    slots_ref,
-    count_ref,
-    species_ref,
-    radial_ref,
-    mix_ref,
-    charge_ref,
-    offset_ref,
-    filtered_ref,
-    messages_ref,
-    before_ref,
-    hidden_ref,
-    shared_ref,
-    words_ref,
-    coords_ref,
-    table_ref,
-    pair_ref,
-    *,
-    box_x,
-):
-    atoms, width = feat_ref.shape
-    slots = slots_ref.shape[0]
-    basis_count = radial_ref.shape[0]
-    ghosts = atoms
-    entries = atoms + 2 * ghosts
-    own_rows = positions_ref[...]
-    site = lax.broadcasted_iota(jnp.int32, (atoms, ghosts), 0).astype(f32)
-
-    own_feat = turned(feat_ref[...])
-    table_ref[:, 0:atoms] = own_feat
-    padding = jnp.zeros((5, atoms), f32)
-    coords_ref[0:atoms, :] = jnp.transpose(jnp.concatenate([own_rows, padding], axis=0))
-    for ref, is_low in ((near_ref, where_ref[0] == 1), (far_ref, where_ref[0] == 0)):
-        extra = jnp.concatenate(
-            [ref[atoms + part * 16 : atoms + part * 16 + 16, :] for part in range(atoms // width)],
-            axis=1,
-        )
-        sends = extra[8:16, :].astype(f32)
-        sends = jnp.where(is_low, sends[2:3, :], sends[1:2, :])
-        chosen = (site == sends).astype(bf16)
-        first = pl.multiple_of(jnp.where(is_low, atoms, atoms + ghosts), ghosts)
-        places = pl.ds(first, ghosts)
-        table_ref[:, places] = matmul(turned(ref[0:atoms, :]), chosen).astype(bf16)
-        moved = matmul(extra, chosen)
-        moved = moved[0:3, :] + (moved[3:6, :] + moved[6:9, :])
-        coords_ref[places, :] = jnp.transpose(jnp.concatenate([moved, padding], axis=0))
-
-    listed = slots_ref[...]
-    live = lax.broadcasted_iota(jnp.int32, (slots, atoms), 0) < count_ref[...]
-    word_of = jnp.where(live, listed >> 5, -1)
-    bit = jnp.left_shift(jnp.ones_like(listed), listed & 31)
-    for word in range(entries // 32):
-        value = jnp.where(word_of == word, bit, 0)
-        rows = slots
-        while rows > 1:
-            rows //= 2
-            value = value[:rows] | value[rows:]
-        words_ref[word : word + 1, :] = value
-
+def pair_blocks(count, coords_ref, own_rows, words_ref, pair_ref, box_x):
+    basis_count, _, atoms = pair_ref.shape
     centers = [
         0.5 + (cutoff_radius - 0.5) * float(b) / (basis_count - 1) for b in range(basis_count)
     ]
@@ -153,8 +91,8 @@
     step = 32
 
     def block(index, carry):
-        first = pl.multiple_of(index * step, step)
-        coords = coords_ref[pl.ds(first, step), :]
+        places = pl.ds(pl.multiple_of(index * step, step), step)
+        coords = coords_ref[places, :]
         total = jnp.zeros((step, atoms), f32)
         for axis, (mine, length) in enumerate(
             ((own_x, box_x), (own_y, box_side), (own_z, box_side))
@@ -179,37 +117,174 @@
                     running = running * ratio
                 basis = running * math.exp(-(((b - middle) * gap / basis_width) ** 2))
                 basis = basis.astype(bf16).astype(f32)
-                pair_ref[b, pl.ds(first, step), :] = (weight * basis).astype(bf16)
+                pair_ref[b, places, :] = (weight * basis).astype(bf16)
         return carry
 
-    lax.fori_loop(0, entries // step, block, 0, unroll=8)
-
-    radial = jnp.transpose(radial_ref[...].astype(f32))
-    messages = jnp.zeros((width, atoms), f32)
+    lax.fori_loop(0, count // step, block, 0, unroll=8)
+
+
+def own_kernel(
+    feat_ref,
+    positions_ref,
+    force_ref,
+    slots_ref,
+    count_ref,
+    species_ref,
+    radial_ref,
+    mix_ref,
+    charge_ref,
+    offset_ref,
+    filtered_ref,
+    words_ref,
+    own_ref,
+    shift_ref,
+    weights_ref,
+    extra_ref,
+    coords_ref,
+    pair_ref,
+    *,
+    box_x,
+):
+    atoms, width = feat_ref.shape
+    slots = slots_ref.shape[0]
+    basis_count = radial_ref.shape[0]
+    own_rows = positions_ref[...]
+    own_feat = turned(feat_ref[...])
+    own_ref[...] = own_feat
+    coords_ref[...] = jnp.transpose(
+        jnp.concatenate([own_rows, jnp.zeros((5, atoms), f32)], axis=0)
+    )
+
+    listed = slots_ref[...]
+    live = lax.broadcasted_iota(jnp.int32, (slots, atoms), 0) < count_ref[...]
+    word_of = jnp.where(live, listed >> 5, -1)
+    bit = jnp.left_shift(jnp.ones_like(listed), listed & 31)
+    for word in range(words_ref.shape[0]):
+        value = jnp.where(word_of == word, bit, 0)
+        rows = slots
+        while rows > 1:
+            rows //= 2
+            value = value[:rows] | value[rows:]
+        words_ref[word : word + 1, :] = value
+
+    pair_blocks(atoms, coords_ref, own_rows, words_ref, pair_ref, box_x)
     for b in range(basis_count):
-        filtered = matmul(table_ref[...], pair_ref[b])
-        filtered_ref[b] = filtered
-        messages = messages + radial[:, b : b + 1] * filtered
-    messages_ref[...] = messages
-    before = matmul(jnp.transpose(mix_ref[...].astype(f32)), messages, highest)
-    before_ref[...] = before
-    hidden = (own_feat.astype(f32) + before * sigmoid(before)).astype(bf16)
-    hidden_ref[...] = hidden
+        filtered_ref[b] = matmul(own_feat, pair_ref[b])
+
     kinds = offset_ref.shape[0]
     one_hot = (
         lax.broadcasted_iota(jnp.int32, (kinds, atoms), 0) == species_ref[...]
     ).astype(f32)
-    charges = matmul(charge_ref[...], hidden) + matmul(
-        jnp.transpose(offset_ref[...]), one_hot, highest
+    shift_ref[...] = matmul(jnp.transpose(offset_ref[...]), one_hot, highest)
+    charge_count = charge_ref.shape[0]
+    weights_ref[0:width, :] = jnp.transpose(mix_ref[...].astype(f32))
+    weights_ref[width : width + charge_count, :] = charge_ref[...].astype(f32)
+    weights_ref[width + charge_count :, 0:basis_count] = jnp.transpose(
+        radial_ref[...].astype(f32)
     )
     lengths = (box_x, box_side, box_side)
     turns = jnp.concatenate([own_rows[a : a + 1, :] * (1.0 / lengths[a]) for a in range(3)], axis=0)
     target = force_ref[...]
     high = target.astype(bf16).astype(f32)
-    rows = jnp.concatenate(
-        (charges,) + pieces_of(turns) + (high, target - high, jnp.zeros((1, atoms), f32)), axis=0
-    ).astype(bf16)
-    shared_ref[0] = rows
+    extra_ref[0:16, :] = jnp.concatenate(
+        pieces_of(turns) + (high, target - high, jnp.zeros((1, atoms), f32)), axis=0
+    )
+    extra_ref[16:24, :] = jnp.concatenate([own_rows, jnp.zeros((5, atoms), f32)], axis=0)
+
+
+def ghost_pairs(ref, is_low, words_ref, extra_ref, ghost_words_ref, coords_ref, pair_ref, box_x):
+    _, ghosts, atoms = pair_ref.shape
+    width = ref.shape[1]
+    extra = jnp.concatenate(
+        [ref[atoms + part * 16 : atoms + part * 16 + 16, :] for part in range(atoms // width)],
+        axis=1,
+    )
+    sends = extra[8:16, :].astype(f32)
+    sends = jnp.where(is_low, sends[2:3, :], sends[1:2, :])
+    site = lax.broadcasted_iota(jnp.int32, (atoms, ghosts), 0).astype(f32)
+    chosen = (site == sends).astype(bf16)
+    moved = matmul(extra, chosen)
+    moved = moved[0:3, :] + (moved[3:6, :] + moved[6:9, :])
+    coords_ref[...] = jnp.transpose(jnp.concatenate([moved, jnp.zeros((5, ghosts), f32)], axis=0))
+    count = ghosts // 32
+    first = jnp.where(is_low, atoms // 32, atoms // 32 + count)
+    ghost_words_ref[...] = words_ref[pl.ds(pl.multiple_of(first, 8), count), :]
+    pair_blocks(ghosts, coords_ref, extra_ref[16:24, :], ghost_words_ref, pair_ref, box_x)
+    return matmul(turned(ref[0:atoms, :]), chosen).astype(bf16)
+
+
+def near_kernel(
+    where_ref,
+    near_ref,
+    sofar_ref,
+    words_ref,
+    extra_ref,
+    filtered_ref,
+    ghost_words_ref,
+    coords_ref,
+    pair_ref,
+    *,
+    box_x,
+):
+    feat = ghost_pairs(
+        near_ref,
+        where_ref[0] == 1,
+        words_ref,
+        extra_ref,
+        ghost_words_ref,
+        coords_ref,
+        pair_ref,
+        box_x,
+    )
+    for b in range(filtered_ref.shape[0]):
+        filtered_ref[b] = sofar_ref[b] + matmul(feat, pair_ref[b])
+
+
+def edge_kernel(
+    where_ref,
+    far_ref,
+    sofar_ref,
+    words_ref,
+    own_ref,
+    shift_ref,
+    weights_ref,
+    extra_ref,
+    filtered_ref,
+    messages_ref,
+    before_ref,
+    hidden_ref,
+    shared_ref,
+    ghost_words_ref,
+    coords_ref,
+    pair_ref,
+    *,
+    box_x,
+):
+    width, atoms = own_ref.shape
+    charge_count = shift_ref.shape[0]
+    feat = ghost_pairs(
+        far_ref,
+        where_ref[0] == 0,
+        words_ref,
+        extra_ref,
+        ghost_words_ref,
+        coords_ref,
+        pair_ref,
+        box_x,
+    )
+    messages = jnp.zeros((width, atoms), f32)
+    for b in range(filtered_ref.shape[0]):
+        filtered = sofar_ref[b] + matmul(feat, pair_ref[b])
+        filtered_ref[b] = filtered
+        messages = messages + weights_ref[width + charge_count :, b : b + 1] * filtered
+    messages_ref[...] = messages
+    before = matmul(weights_ref[0:width, :], messages, highest)
+    before_ref[...] = before
+    hidden = (own_ref[...].astype(f32) + before * sigmoid(before)).astype(bf16)
+    hidden_ref[...] = hidden
+    charges = matmul(weights_ref[width : width + charge_count, :].astype(bf16), hidden)
+    shared_ref[0, 0:charge_count, :] = (charges + shift_ref[...]).astype(bf16)
+    shared_ref[0, charge_count : charge_count + 16, :] = extra_ref[0:16, :].astype(bf16)
 
 
 def wave_rows(wave_ref, first, count, box_x, total_atoms):
@@ -221,38 +296,70 @@
     return index, waves, damping
 
 
-def structure_kernel(
-    where_ref, *refs, group, blocks, charge_count, box_x
-):
-    shared_refs, (wave_ref, waves_ref, weights_ref, *force_refs) = refs[:blocks], refs[blocks:]
-    columns_count, _, atoms = shared_refs[0].shape
+def wave_columns(wave_ref, first, share):
+    index = wave_ref[:, pl.ds(first, share)].astype(f32)
+    return jnp.transpose(
+        jnp.concatenate([index] * 3 + [jnp.zeros((7, share), f32)], axis=0)
+    ).astype(bf16)
+
+
+def fill_waves(columns, shared_ref, j, charge_count, waves_ref, place):
+    share = columns.shape[0]
+    shift = 12582912.0
+    turns = matmul(columns, shared_ref[j, charge_count : charge_count + 16, :])
+    turns = turns - ((turns + shift) - shift)
+    square = turns * turns
+    half_sine = turns * horner(short_sine, square)
+    half_cosine = horner(short_cosine, square)
+    waves_ref[place, 0:share, :] = (2.0 * half_sine * half_cosine).astype(bf16)
+    waves_ref[place, share : 2 * share, :] = (1.0 - 2.0 * half_sine * half_sine).astype(bf16)
+
+
+def phase_kernel(where_ref, shared_ref, wave_ref, waves_ref, part_ref, *, charge_count):
+    count = shared_ref.shape[0]
+    share = waves_ref.shape[1] // 2
+    columns = wave_columns(wave_ref, pl.multiple_of(where_ref[1] * share, share), share)
+
+    def block(j, carry):
+        fill_waves(columns, shared_ref, j, charge_count, waves_ref, j)
+        return carry
+
+    lax.fori_loop(0, count, block, 0, unroll=4)
+    part = jnp.zeros(part_ref.shape, f32)
+    for j in range(count):
+        part = part + matmul_nt(shared_ref[j, 0:charge_count, :], waves_ref[j])
+    part_ref[...] = part
+
+
+def structure_kernel(where_ref, *refs, group, blocks, charge_count, box_x):
+    shared_refs = refs[:blocks]
+    early_ref, part_ref, wave_ref, waves_ref, weights_ref, *force_refs = refs[blocks:]
+    count, _, atoms = shared_refs[0].shape
     share = waves_ref.shape[1] // 2
     first = pl.multiple_of(where_ref[1] * share, share)
-    index, waves, damping = wave_rows(
-        wave_ref, first, share, box_x, blocks * columns_count * atoms
-    )
-    columns = jnp.transpose(
-        jnp.concatenate([index] * 3 + [jnp.zeros((7, share), f32)], axis=0)
-    ).astype(bf16)
-    shift = 12582912.0
+    _, waves, damping = wave_rows(wave_ref, first, share, box_x, blocks * count * atoms)
+    columns = wave_columns(wave_ref, first, share)
 
     def block(j, carry):
-        for r in range(blocks):
-            turns = matmul(columns, shared_refs[r][j, charge_count : charge_count + 16, :])
-            turns = turns - ((turns + shift) - shift)
-            square = turns * turns
-            half_sine = turns * horner(short_sine, square)
-            half_cosine = horner(short_cosine, square)
-            d = j * blocks + r
-            waves_ref[d, 0:share, :] = (2.0 * half_sine * half_cosine).astype(bf16)
-            waves_ref[d, share : 2 * share, :] = (1.0 - 2.0 * half_sine * half_sine).astype(bf16)
+        for r in range(1, blocks):
+            fill_waves(
+                columns, shared_refs[r], j, charge_count, waves_ref, j * (blocks - 1) + r - 1
+            )
         return carry
 
-    lax.fori_loop(0, columns_count, block, 0, unroll=4)
-    structure = jnp.zeros((charge_count, 2 * share), f32)
-    for d in range(blocks * columns_count):
+    lax.fori_loop(0, count, block, 0, unroll=4)
+    waves_of = [
+        waves_ref.at[j * (blocks - 1) + r - 1] if r else early_ref.at[j]
+        for j in range(count)
+        for r in range(blocks)
+    ]
+    structure = part_ref[...]
+    for d in range(blocks * count):
         j, r = divmod(d, blocks)
-        structure = structure + matmul_nt(shared_refs[r][j, 0:charge_count, :], waves_ref[d])
+        if r:
+            structure = structure + matmul_nt(
+                shared_refs[r][j, 0:charge_count, :], waves_of[d][...]
+            )
     along_sin = structure[:, :share] * damping
     along_cos = structure[:, share:] * damping
     to_sine = jnp.concatenate([along_cos * waves[a] for a in range(3)], axis=0)
@@ -260,9 +367,9 @@
     weights = jnp.concatenate([to_sine, to_cosine], axis=1)
     weights_ref[...] = weights
     weights = weights.astype(bf16)
-    for d in range(blocks * columns_count):
+    for d in range(blocks * count):
         j, r = divmod(d, blocks)
-        field = matmul(weights, waves_ref[d])
+        field = matmul(weights, waves_of[d][...])
         charges = shared_refs[r][j, 0:charge_count, :].astype(f32)
         for a in range(3):
             row = jnp.sum(
@@ -276,11 +383,18 @@
 
 def gradient_kernel(where_ref, *refs, group, blocks, charge_count, box_x):
     shared_refs, part_refs = refs[:blocks], refs[blocks : blocks + group]
-    wave_ref, waves_ref, weights_ref, forces_ref, *grad_refs, total_ref = refs[blocks + group :]
-    columns_count, _, atoms = shared_refs[0].shape
+    wave_ref, early_ref, waves_ref, weights_ref, forces_ref, *grad_refs, total_ref = refs[
+        blocks + group :
+    ]
+    count, _, atoms = shared_refs[0].shape
     share = waves_ref.shape[1] // 2
     first = pl.multiple_of(where_ref[1] * share, share)
-    _, waves, damping = wave_rows(wave_ref, first, share, box_x, blocks * columns_count * atoms)
+    _, waves, damping = wave_rows(wave_ref, first, share, box_x, blocks * count * atoms)
+    waves_of = [
+        waves_ref.at[j * (blocks - 1) + r - 1] if r else early_ref.at[j]
+        for j in range(count)
+        for r in range(blocks)
+    ]
     total = part_refs[0][...]
     for m in range(1, group):
         total = total + part_refs[m][...]
@@ -295,12 +409,12 @@
         return [2.0 * (total_ref[a, d : d + 1, :] - target[a : a + 1, :]) for a in range(3)]
 
     summed = jnp.zeros((3 * charge_count, 2 * share), f32)
-    for d in range(blocks * columns_count):
+    for d in range(blocks * count):
         j, r = divmod(d, blocks)
         charges = shared_refs[r][j, 0:charge_count, :].astype(f32)
         errors = errors_of(d)
         scaled = jnp.concatenate([errors[a] * charges for a in range(3)], axis=0).astype(bf16)
-        summed = summed + matmul_nt(scaled, waves_ref[d])
+        summed = summed + matmul_nt(scaled, waves_of[d][...])
 
     def along(value):
         return sum(
@@ -317,8 +431,9 @@
     weights_low = (weights - weights_high.astype(f32)).astype(bf16)
     for m in range(group):
         errors = errors_of(m)
-        grad = matmul(back_high, waves_ref[m]) + matmul(back_low, waves_ref[m])
-        field = matmul(weights_high, waves_ref[m]) + matmul(weights_low, waves_ref[m])
+        block = waves_of[m][...]
+        grad = matmul(back_high, block) + matmul(back_low, block)
+        field = matmul(weights_high, block) + matmul(weights_low, block)
         for a in range(3):
             grad = grad + errors[a] * field[a * charge_count : (a + 1) * charge_count, :]
         grad_refs[m][...] = grad.astype(grad_refs[m].dtype)
@@ -480,6 +595,52 @@
     slots = neighbours.T
     charge_rows = charge_weight.T
 
+    sofar, words, *local, extra = kernel(
+        lambda *refs: own_kernel(*refs, box_x=box_x),
+        "own",
+        (
+            shaped(basis_count, width, atoms),
+            shaped(entries // 32, atoms, kind=jnp.int32),
+            shaped(width, atoms, kind=bf16),
+            shaped(charge_count, atoms),
+            shaped(2 * width + charge_count, width),
+            shaped(24, atoms),
+        ),
+        (
+            shaped(atoms, 8),
+            shaped(basis_count, atoms, atoms, kind=bf16),
+        ),
+        4_000,
+        features,
+        positions,
+        force_ref,
+        slots,
+        neighbour_count[None, :],
+        species_row,
+        radial_weight,
+        mix_weight,
+        charge_rows,
+        species_charge,
+        wanted=own_vmem,
+    )
+    ghosts = ghost_sends.shape[1]
+    scratch = (
+        shaped(ghosts // 32, atoms, kind=jnp.int32),
+        shaped(ghosts, 8),
+        shaped(basis_count, ghosts, atoms, kind=bf16),
+    )
+    sofar = kernel(
+        lambda *refs: near_kernel(*refs, box_x=box_x),
+        "near",
+        shaped(basis_count, width, atoms),
+        scratch,
+        3_000,
+        near,
+        sofar,
+        words,
+        extra,
+        scalars=(where,),
+    )
     filtered, messages, before, hidden, shared = kernel(
         lambda *refs: edge_kernel(*refs, box_x=box_x),
         "edges",
@@ -490,45 +651,47 @@
             shaped(width, atoms, kind=bf16),
             shaped(1, charge_count + 16, atoms, kind=bf16),
         ),
-        (
-            shaped(entries // 32, atoms, kind=jnp.int32),
-            shaped(entries, 8),
-            shaped(width, entries, kind=bf16),
-            shaped(basis_count, entries, atoms, kind=bf16),
-        ),
-        12_000,
-        features,
-        positions,
-        force_ref,
-        near,
+        scratch,
+        4_000,
         far,
-        slots,
-        neighbour_count[None, :],
-        species_row,
-        radial_weight,
-        mix_weight,
-        charge_rows,
-        species_charge,
+        sofar,
+        words,
+        *local,
+        extra,
         scalars=(where,),
-        wanted=60 * 1024 * 1024,
     )
     column = jnp.concatenate(
         [shared] + [across(shared, bits) for bits in range(blocks, domains, blocks)], axis=0
     )
     columns = [column] + [across(column, bits) for bits in range(1, blocks)]
+    early, part = kernel(
+        lambda *refs: phase_kernel(*refs, charge_count=charge_count),
+        "phases",
+        (
+            shaped(domains // blocks, 2 * share, atoms, kind=bf16),
+            shaped(charge_count, 2 * share),
+        ),
+        (),
+        3_000,
+        column,
+        wave_index,
+        scalars=(where,),
+    )
     waves, weights, *force_parts = kernel(
         lambda *refs: structure_kernel(
             *refs, group=group, blocks=blocks, charge_count=charge_count, box_x=box_x
         ),
         "structure",
         (
-            shaped(domains, 2 * share, atoms, kind=bf16),
+            shaped(domains - domains // blocks, 2 * share, atoms, kind=bf16),
             shaped(3 * charge_count, 2 * share),
         )
         + (shaped(3, domains, atoms),) * group,
         (),
-        10_000,
+        8_000,
         *columns,
+        early,
+        part,
         wave_index,
         scalars=(where,),
     )
@@ -544,6 +707,7 @@
         *columns,
         *force_parts,
         wave_index,
+        early,
         waves,
         weights,
         scalars=(where,),

time: 84.5 us -> 78.5 us (0.929)
  Pallas kernels: 21.8 us -> 28.6 us
  waiting for transfers between devices: 26.1 us -> 19.3 us
  starting transfers between devices: 33.5 us -> 29.4 us
  local copies, waits for them, and re-layouts: 1.5 us -> 0.06 us
    pallas_call x6 -> x9, Pallas kernels: 21.8 us -> 28.6 us  [kernel(): pl.pallas_call(body, out_shape=out_shape, in_specs=[in_smem] * len(scalar...]
    ppermute x22 -> x18, waiting for transfers between devices: 24.1 us -> 19.3 us  [across(): return lax.ppermute(value, 'dom', [(i, i ^ bits) for i in range(domains)])]
    ppermute x1, starting transfers between devices: 6.93 us -> 4.53 us  [on_device(): far = lax.ppermute(packed, 'dom', beyond)]
    ppermute x1, waiting for transfers between devices: 2.01 us -> 0.01 us  [on_device(): far = lax.ppermute(packed, 'dom', beyond)]
    ppermute x22 -> x18, starting transfers between devices: 26.5 us -> 24.9 us  [across(): return lax.ppermute(value, 'dom', [(i, i ^ bits) for i in range(domains)])]
    unnamed x25, local copies, waits for them, and re-layouts: 1.49 us -> 0.06 us
  transfers between devices with their start and end apart: 23 -> 19, of which waited for: 19 -> 14; matrix products, arithmetic and copies ran while one was open for 2% -> 0% of each run, Pallas kernels for 0% -> 9%
where the time goes in v5:
time: 78.5 us; the launch traced here: 78.4 us
  starting transfers between devices  29.4 us (37%)
  Pallas kernels  28.6 us (36%)
  waiting for transfers between devices  19.3 us (25%)
  between operations  0.85 us (1%)
    pallas_call x9, Pallas kernels, kernel(): pl.pallas_call(body, out_shape=out_shape, in_specs=[in_smem] * len(scalar...  28.6 us
    ppermute x18, starting transfers between devices, across(): return lax.ppermute(value, 'dom', [(i, i ^ bits) for i in range(domains)])  24.9 us
    ppermute x18, waiting for transfers between devices, across(): return lax.ppermute(value, 'dom', [(i, i ^ bits) for i in range(domains)])  19.3 us
    ppermute x1, starting transfers between devices, on_device(): far = lax.ppermute(packed, 'dom', beyond)  4.53 us
  transfers between devices with their start and end apart: 19, of which 14 were waited for; matrix products, arithmetic and copies ran while one was open for 0% of the time, Pallas kernels for 9%

profile of v5, /device:TPU:0, one launch (start us, length us, event | category | flops | bytes accessed | tf_op | source)
XLA Modules:
  0.0 78.4 jit_solution(1107668138566117241)
XLA Ops:
  0.7 1.6 %pack.1 = bf16[288,128]{1,0:T(8,128)(2,1)} custom-call(bf16[256,128]{1,0:T(8,128)(2,1)} %refs_0_.1, f32[3,256]{1,0:T(4,128)} %refs_1_.1, s32[2,256]{1,0:T(2,128)} %ghost_ref.1), custom_call_target="tpu_custom_call" | custom-call | flops 1000000000 | bytes 144384 | tf_op jit(solution)/shard_map/pack/pallas_call | solution.py:521
  2.3 2.9 %collective-permute-start.1 = (bf16[288,128]{1,0:T(8,128)(2,1)}, bf16[288,128]{1,0:T(8,128)(2,1)S(1)}, u32[]{:S(2)}, u32[]{:S(2)}) collective-permute-start(bf16[288,128]{1,0:T(8,128)(2,1)} %pack.1), channel_id=1, source_target_pairs={{0,2},{2,0},{4,6},{6,4},{8,10},{10,8},{12,14},{14,12},{16,18},{18,... | collective-permute-start | bytes 221192 | tf_op jit(solution)/shard_map/ppermute | solution.py:537
  5.3 4.5 %collective-permute-start = (bf16[288,128]{1,0:T(8,128)(2,1)}, bf16[288,128]{1,0:T(8,128)(2,1)S(1)}, u32[]{:S(2)}, u32[]{:S(2)}) collective-permute-start(bf16[288,128]{1,0:T(8,128)(2,1)} %pack.1), channel_id=1, source_target_pairs={{0,30},{2,4},{4,2},{6,8},{8,6},{10,12},{12,10},{14,16},{16,14},{18... | collective-permute-start | bytes 221192 | tf_op jit(solution)/shard_map/ppermute | solution.py:593
  9.9 1.9 %own.1 = (f32[16,128,256]{2,1,0:T(8,128)S(1)}, s32[24,256]{1,0:T(8,128)S(1)}, bf16[128,256]{1,0:T(8,128)(2,1)S(1)}, f32[64,256]{1,0:T(8,128)S(1)}, f32[320,128]{1,0:T(8,128)S(1)}, /*index=5*/f32[24,256]{1,0:T(8,128)S(1)}) custom-call(bf16[256,128]{1,0:T(8,128)(2,1)S(1)} %copy-done, f32[3,256]{1,0:T(4,128)S(1)} %copy-done.5, f32[3,256]{1,0:T(4,128)S(1)} %copy-done.6, ...), custom_call_target="tpu_custom_call" | custom-call | flops 4000000000 | bytes 4740608 | tf_op jit(solution)/shard_map/own/pallas_call | solution.py:521
  11.9 2.5 %near.1.refs_2_ = f32[16,128,256]{2,1,0:T(8,128)S(1)} custom-call(s32[3]{0:T(128)S(1)} %pad_add_fusion.refs_0_.where_ref, bf16[288,128]{1,0:T(8,128)(2,1)S(1)} %collective-permute-done.1.refs_1_, f32[16,128,256]{2,1,0:T(8,128)S(1)} %get-tuple-element.33.refs_2_, s32[24,256]{1,0:T(8,128)S(1)} %get-tuple-element.34.refs_3_, ...), custom_call_target="tpu_custom_call" | custom-call | flops 3000000000 | bytes 6430720 | tf_op jit(solution)/shard_map/near/pallas_call | solution.py:521
  14.4 3.1 %edges.1 = (f32[16,128,256]{2,1,0:T(8,128)S(1)}, f32[128,256]{1,0:T(8,128)S(1)}, f32[128,256]{1,0:T(8,128)S(1)}, bf16[128,256]{1,0:T(8,128)(2,1)S(1)}, bf16[1,80,256]{2,1,0:T(8,128)(2,1)S(1)}) custom-call(s32[3]{0:T(128)S(1)} %pad_add_fusion.refs_0_.where_ref, bf16[288,128]{1,0:T(8,128)(2,1)S(1)} %collective-permute-done.refs_1_, ...), custom_call_target="tpu_custom_call" | custom-call | flops 4000000000 | bytes 7094272 | tf_op jit(solution)/shard_map/edges/pallas_call | solution.py:521
  18.4 3.6 %collective-permute-start.2 = (bf16[1,80,256]{2,1,0:T(8,128)(2,1)S(1)}, bf16[1,80,256]{2,1,0:T(8,128)(2,1)S(1)}, u32[]{:S(2)}, u32[]{:S(2)}) collective-permute-start(bf16[1,80,256]{2,1,0:T(8,128)(2,1)S(1)} %get-tuple-element.39), channel_id=1, source_target_pairs={{0,8},{2,10},{4,12},{6,14},{8,0},{10,2},{12,4},{14,6},{16,24},{18,... | collective-permute-start | bytes 122888 | tf_op jit(solution)/shard_map/ppermute | solution.py:537
  22.0 2.0 %collective-permute-done.2 = bf16[1,80,256]{2,1,0:T(8,128)(2,1)S(1)} collective-permute-done((bf16[1,80,256]{2,1,0:T(8,128)(2,1)S(1)}, bf16[1,80,256]{2,1,0:T(8,128)(2,1)S(1)}, u32[]{:S(2)}, u32[]{:S(2)}) %collective-permute-start.2) | collective-permute-done | bytes 40992 | tf_op jit(solution)/shard_map/ppermute | solution.py:537
  24.3 2.4 %collective-permute-start.7 = (bf16[4,80,256]{2,1,0:T(8,128)(2,1)S(1)}, bf16[4,80,256]{2,1,0:T(8,128)(2,1)S(1)}, u32[]{:S(2)}, u32[]{:S(2)}) collective-permute-start(bf16[4,80,256]{2,1,0:T(8,128)(2,1)S(1)} %constant_dynamic-update-slice_fusion.refs_1_), channel_id=1, source_target_pairs={{0,6},{2,4},{4,2},{6,0},{8,14},{10,12},{12,10},{14,8},{16,22},{18,... | collective-permute-start | bytes 491528 | tf_op jit(solution)/shard_map/ppermute | solution.py:537
  26.7 1.1 %collective-permute-start.5 = (bf16[4,80,256]{2,1,0:T(8,128)(2,1)S(1)}, bf16[4,80,256]{2,1,0:T(8,128)(2,1)S(1)}, u32[]{:S(2)}, u32[]{:S(2)}) collective-permute-start(bf16[4,80,256]{2,1,0:T(8,128)(2,1)S(1)} %constant_dynamic-update-slice_fusion.refs_1_), channel_id=1, source_target_pairs={{0,2},{2,0},{4,6},{6,4},{8,10},{10,8},{12,14},{14,12},{16,18},{18,... | collective-permute-start | bytes 491528 | tf_op jit(solution)/shard_map/ppermute | solution.py:537
  27.8 2.8 %phases.1 = (bf16[4,1024,256]{2,1,0:T(8,128)(2,1)S(1)}, f32[64,1024]{1,0:T(8,128)S(1)}) custom-call(s32[3]{0:T(128)S(1)} %pad_add_fusion.refs_0_.where_ref, bf16[4,80,256]{2,1,0:T(8,128)(2,1)S(1)} %constant_dynamic-update-slice_fusion.refs_1_, s32[3,1024]{1,0:T(4,128)S(1)} %copy-done.3), custom_call_target="tpu_custom_call" | custom-call | flops 3000000000 | bytes 2535424 | tf_op jit(solution)/shard_map/phases/pallas_call | solution.py:521
  31.6 1.5 %collective-permute-done.6.refs_3_ = bf16[4,80,256]{2,1,0:T(8,128)(2,1)S(1)} collective-permute-done((bf16[4,80,256]{2,1,0:T(8,128)(2,1)S(1)}, bf16[4,80,256]{2,1,0:T(8,128)(2,1)S(1)}, u32[]{:S(2)}, u32[]{:S(2)}) %collective-permute-start.6) | collective-permute-done | bytes 163872 | tf_op jit(solution)/shard_map/ppermute | solution.py:537
  33.0 8.9 %structure.1 = (bf16[12,1024,256]{2,1,0:T(8,128)(2,1)S(1)}, f32[192,1024]{1,0:T(8,128)S(1)}, f32[3,16,256]{2,1,0:T(8,128)S(1)}, f32[3,16,256]{2,1,0:T(8,128)S(1)}) custom-call(s32[3]{0:T(128)S(1)} %pad_add_fusion.refs_0_.where_ref, bf16[4,80,256]{2,1,0:T(8,128)(2,1)S(1)} %constant_dynamic-update-slice_fusion.refs_1_, ...), custom_call_target="tpu_custom_call" | custom-call | flops 8000000000 | bytes 10203136 | tf_op jit(solution)/shard_map/structure/pallas_call | solution.py:521
  41.9 1.2 %collective-permute-start.8 = (f32[3,16,256]{2,1,0:T(8,128)S(1)}, f32[3,16,256]{2,1,0:T(8,128)S(1)}, u32[]{:S(2)}, u32[]{:S(2)}) collective-permute-start(f32[3,16,256]{2,1,0:T(8,128)S(1)} %get-tuple-element.43), channel_id=1, source_target_pairs={{0,2},{2,0},{4,6},{6,4},{8,10},{10,8},{12,14},{14,12},{16,18},{18,... | collective-permute-start | bytes 147464 | tf_op jit(solution)/shard_map/ppermute | solution.py:537
  43.1 2.9 %collective-permute-done.8.refs_6_ = f32[3,16,256]{2,1,0:T(8,128)S(1)} collective-permute-done((f32[3,16,256]{2,1,0:T(8,128)S(1)}, f32[3,16,256]{2,1,0:T(8,128)S(1)}, u32[]{:S(2)}, u32[]{:S(2)}) %collective-permute-start.8) | collective-permute-done | bytes 49184 | tf_op jit(solution)/shard_map/ppermute | solution.py:537
  46.1 4.8 %gradient.1 = (f32[3,256]{1,0:T(4,128)}, bf16[64,256]{1,0:T(8,128)(2,1)S(1)}, bf16[64,256]{1,0:T(8,128)(2,1)S(1)}) custom-call(s32[3]{0:T(128)S(1)} %pad_add_fusion.refs_0_.where_ref, bf16[4,80,256]{2,1,0:T(8,128)(2,1)S(1)} %constant_dynamic-update-slice_fusion.refs_1_, bf16[4,80,256]{2,1,0:T(8,128)(2,1)S(1)} %collective-permute-done.5.refs_2_, ...), custom_call_target="tpu_custom_call" | custom-call | flops 5000000000 | bytes 10058752 | tf_op jit(solution)/shard_map/gradient/pallas_call | solution.py:521
  50.9 1.2 %collective-permute-start.9 = (bf16[64,256]{1,0:T(8,128)(2,1)S(1)}, bf16[64,256]{1,0:T(8,128)(2,1)S(1)}, u32[]{:S(2)}, u32[]{:S(2)}) collective-permute-start(bf16[64,256]{1,0:T(8,128)(2,1)S(1)} %get-tuple-element.48), channel_id=1, source_target_pairs={{0,2},{2,0},{4,6},{6,4},{8,10},{10,8},{12,14},{14,12},{16,18},{18,... | collective-permute-start | bytes 98312 | tf_op jit(solution)/shard_map/ppermute | solution.py:537
  52.0 2.8 %collective-permute-done.9.refs_2_ = bf16[64,256]{1,0:T(8,128)(2,1)S(1)} collective-permute-done((bf16[64,256]{1,0:T(8,128)(2,1)S(1)}, bf16[64,256]{1,0:T(8,128)(2,1)S(1)}, u32[]{:S(2)}, u32[]{:S(2)}) %collective-permute-start.9) | collective-permute-done | bytes 32800 | tf_op jit(solution)/shard_map/ppermute | solution.py:537
  54.8 1.7 %weights.1 = (f32[56,128]{1,0:T(8,128)S(1)}, f32[56,128]{1,0:T(8,128)S(1)}, f32[56,128]{1,0:T(8,128)S(1)}, f32[56,128]{1,0:T(8,128)S(1)}) custom-call(s32[3]{0:T(128)S(1)} %pad_add_fusion.refs_0_.where_ref, bf16[64,256]{1,0:T(8,128)(2,1)S(1)} %get-tuple-element.47.refs_1_, bf16[64,256]{1,0:T(8,128)(2,1)S(1)} %collective-permute-done.9.refs_2_, ...), custom_call_target="tpu_custom_call" | custom-call | flops 3000000000 | bytes 2769920 | tf_op jit(solution)/shard_map/weights/pallas_call | solution.py:521
  56.5 1.2 %collective-permute-start.10 = (f32[56,128]{1,0:T(8,128)S(1)}, f32[56,128]{1,0:T(8,128)S(1)}, u32[]{:S(2)}, u32[]{:S(2)}) collective-permute-start(f32[56,128]{1,0:T(8,128)S(1)} %get-tuple-element.54), channel_id=1, source_target_pairs={{0,2},{2,0},{4,6},{6,4},{8,10},{10,8},{12,14},{14,12},{16,18},{18,... | collective-permute-start | bytes 86024 | tf_op jit(solution)/shard_map/ppermute | solution.py:537
  58.4 1.6 %collective-permute-start.12 = (f32[56,128]{1,0:T(8,128)S(1)}, f32[56,128]{1,0:T(8,128)S(1)}, u32[]{:S(2)}, u32[]{:S(2)}) collective-permute-start(f32[56,128]{1,0:T(8,128)S(1)} %get-tuple-element.56), channel_id=1, source_target_pairs={{0,6},{2,4},{4,2},{6,0},{8,14},{10,12},{12,10},{14,8},{16,22},{18,... | collective-permute-start | bytes 86024 | tf_op jit(solution)/shard_map/ppermute | solution.py:537
  60.4 1.2 %collective-permute-done.11 = f32[56,128]{1,0:T(8,128)S(1)} collective-permute-done((f32[56,128]{1,0:T(8,128)S(1)}, f32[56,128]{1,0:T(8,128)S(1)}, u32[]{:S(2)}, u32[]{:S(2)}) %collective-permute-start.11) | collective-permute-done | bytes 28704 | tf_op jit(solution)/shard_map/ppermute | solution.py:537
  61.6 1.6 %collective-permute-done.12 = f32[56,128]{1,0:T(8,128)S(1)} collective-permute-done((f32[56,128]{1,0:T(8,128)S(1)}, f32[56,128]{1,0:T(8,128)S(1)}, u32[]{:S(2)}, u32[]{:S(2)}) %collective-permute-start.12) | collective-permute-done | bytes 28704 | tf_op jit(solution)/shard_map/ppermute | solution.py:537
  63.2 2.1 %collective-permute-start.15 = (f32[56,128]{1,0:T(8,128)S(1)}, f32[56,128]{1,0:T(8,128)S(1)}, u32[]{:S(2)}, u32[]{:S(2)}) collective-permute-start(f32[56,128]{1,0:T(8,128)S(1)} %add_add_fusion.1), channel_id=1, source_target_pairs={{0,24},{2,26},{4,28},{6,30},{8,16},{10,18},{12,20},{14,22},{16,8},... | collective-permute-start | bytes 86024 | tf_op jit(solution)/shard_map/ppermute | solution.py:537
  65.7 1.9 %collective-permute-start.13 = (f32[56,128]{1,0:T(8,128)S(1)}, f32[56,128]{1,0:T(8,128)S(1)}, u32[]{:S(2)}, u32[]{:S(2)}) collective-permute-start(f32[56,128]{1,0:T(8,128)S(1)} %add_add_fusion.1), channel_id=1, source_target_pairs={{0,8},{2,10},{4,12},{6,14},{8,0},{10,2},{12,4},{14,6},{16,24},{18,... | collective-permute-start | bytes 86024 | tf_op jit(solution)/shard_map/ppermute | solution.py:537
  67.6 1.3 %collective-permute-done.15 = f32[56,128]{1,0:T(8,128)S(1)} collective-permute-done((f32[56,128]{1,0:T(8,128)S(1)}, f32[56,128]{1,0:T(8,128)S(1)}, u32[]{:S(2)}, u32[]{:S(2)}) %collective-permute-start.15) | collective-permute-done | bytes 28704 | tf_op jit(solution)/shard_map/ppermute | solution.py:537
  68.9 1.1 %collective-permute-done.14 = f32[56,128]{1,0:T(8,128)S(1)} collective-permute-done((f32[56,128]{1,0:T(8,128)S(1)}, f32[56,128]{1,0:T(8,128)S(1)}, u32[]{:S(2)}, u32[]{:S(2)}) %collective-permute-start.14) | collective-permute-done | bytes 28704 | tf_op jit(solution)/shard_map/ppermute | solution.py:537
  70.0 1.8 %collective-permute-start.18 = (f32[56,128]{1,0:T(8,128)S(1)}, f32[56,128]{1,0:T(8,128)S(1)}, u32[]{:S(2)}, u32[]{:S(2)}) collective-permute-start(f32[56,128]{1,0:T(8,128)S(1)} %add_add_fusion.refs_0_), channel_id=1, source_target_pairs={{0,6},{2,4},{4,2},{6,0},{8,14},{10,12},{12,10},{14,8},{16,22},{18,... | collective-permute-start | bytes 86024 | tf_op jit(solution)/shard_map/ppermute | solution.py:537
  71.8 1.3 %collective-permute-start.17 = (f32[56,128]{1,0:T(8,128)S(1)}, f32[56,128]{1,0:T(8,128)S(1)}, u32[]{:S(2)}, u32[]{:S(2)}) collective-permute-start(f32[56,128]{1,0:T(8,128)S(1)} %add_add_fusion.refs_0_), channel_id=1, source_target_pairs={{0,4},{2,6},{4,0},{6,2},{8,12},{10,14},{12,8},{14,10},{16,20},{18,... | collective-permute-start | bytes 86024 | tf_op jit(solution)/shard_map/ppermute | solution.py:537
  73.6 1.3 %collective-permute-done.18.refs_3_ = f32[56,128]{1,0:T(8,128)S(1)} collective-permute-done((f32[56,128]{1,0:T(8,128)S(1)}, f32[56,128]{1,0:T(8,128)S(1)}, u32[]{:S(2)}, u32[]{:S(2)}) %collective-permute-start.18) | collective-permute-done | bytes 28704 | tf_op jit(solution)/shard_map/ppermute | solution.py:537
  75.7 1.3 %collective-permute-done.16.refs_1_ = f32[56,128]{1,0:T(8,128)S(1)} collective-permute-done((f32[56,128]{1,0:T(8,128)S(1)}, f32[56,128]{1,0:T(8,128)S(1)}, u32[]{:S(2)}, u32[]{:S(2)}) %collective-permute-start.16) | collective-permute-done | bytes 28704 | tf_op jit(solution)/shard_map/ppermute | solution.py:537
  77.0 1.3 %steps.1 = (f32[16,128]{1,0:T(8,128)}, f32[128,128]{1,0:T(8,128)}, f32[64,128]{1,0:T(8,128)}, f32[6,64]{1,0:T(8,128)}) custom-call(s32[3]{0:T(128)S(1)} %pad_add_fusion.refs_0_.where_ref, f32[56,128]{1,0:T(8,128)S(1)} %add_add_fusion.refs_0_, f32[56,128]{1,0:T(8,128)S(1)} %collective-permute-done.16.refs_1_, f32[56,128]{1,0:T(8,128)S(1)} %collective-permute-done.17.refs_2_, ...), custom_call_target="tpu_custom_call" | custom-call | flops 2000000000 | bytes 337408 | tf_op jit(solution)/shard_map/steps/pallas_call | solution.py:521
  (44 shorter events, 5.1 us)
Async XLA Ops:
  0.6 9.2 %copy-start.5 = (f32[3,256]{1,0:T(4,128)S(1)}, f32[3,256]{1,0:T(4,128)}, u32[]{:S(2)}) copy-start(f32[3,256]{1,0:T(4,128)} %refs_1_.1) | copy-start | bytes 9220
  0.6 9.2 %copy-start = (bf16[256,128]{1,0:T(8,128)(2,1)S(1)}, bf16[256,128]{1,0:T(8,128)(2,1)}, u32[]{:S(2)}) copy-start(bf16[256,128]{1,0:T(8,128)(2,1)} %refs_0_.1) | copy-start | bytes 196612
  0.7 9.2 %copy-start.2 = (bf16[128,128]{1,0:T(8,128)(2,1)S(1)}, bf16[128,128]{1,0:T(8,128)(2,1)}, u32[]{:S(2)}) copy-start(bf16[128,128]{1,0:T(8,128)(2,1)} %refs_8_.1) | copy-start | bytes 98308
  0.7 9.1 %copy-start.8 = (f32[6,64]{1,0:T(8,128)S(1)}, f32[6,64]{1,0:T(8,128)}, u32[]{:S(2)}) copy-start(f32[6,64]{1,0:T(8,128)} %refs_9_.1) | copy-start | bytes 4612
  0.7 9.1 %copy-start.4 = (bf16[128,64]{0,1:T(8,128)(2,1)S(1)}, bf16[128,64]{0,1:T(8,128)(2,1)}, u32[]{:S(2)}) copy-start(bf16[128,64]{0,1:T(8,128)(2,1)} %param.22) | copy-start | bytes 49156
  0.7 9.1 %copy-start.7 = (bf16[16,128]{1,0:T(8,128)(2,1)S(1)}, bf16[16,128]{1,0:T(8,128)(2,1)}, u32[]{:S(2)}) copy-start(bf16[16,128]{1,0:T(8,128)(2,1)} %refs_6_.1) | copy-start | bytes 12292
  0.7 9.1 %copy-start.6 = (f32[3,256]{1,0:T(4,128)S(1)}, f32[3,256]{1,0:T(4,128)}, u32[]{:S(2)}) copy-start(f32[3,256]{1,0:T(4,128)} %refs_2_.2) | copy-start | bytes 9220
  0.7 9.1 %copy-start.10 = (s32[256]{0:T(256)S(1)}, s32[256]{0:T(256)}, u32[]{:S(2)}) copy-start(s32[256]{0:T(256)} %param.17) | copy-start | bytes 3076
  0.7 9.1 %copy-start.9 = (s32[256]{0:T(256)S(1)}, s32[256]{0:T(256)}, u32[]{:S(2)}) copy-start(s32[256]{0:T(256)} %param.15) | copy-start | bytes 3076
  0.7 9.1 %copy-start.1 = (s32[256,64]{0,1:T(8,128)S(1)}, s32[256,64]{0,1:T(8,128)}, u32[]{:S(2)}) copy-start(s32[256,64]{0,1:T(8,128)} %param.14) | copy-start | bytes 196612
  2.3 9.5 %collective-permute-start.1 = (bf16[288,128]{1,0:T(8,128)(2,1)}, bf16[288,128]{1,0:T(8,128)(2,1)S(1)}, u32[]{:S(2)}, u32[]{:S(2)}) collective-permute-start(bf16[288,128]{1,0:T(8,128)(2,1)} %pack.1), channel_id=1, source_target_pairs={{0,2},{2,0},{4,6},{6,4},{8,10},{10,8},{12,14},{14,12},{16,18},{18,... | collective-permute-start | bytes 221192 | tf_op jit(solution)/shard_map/ppermute | solution.py:537
  5.3 9.1 %collective-permute-start = (bf16[288,128]{1,0:T(8,128)(2,1)}, bf16[288,128]{1,0:T(8,128)(2,1)S(1)}, u32[]{:S(2)}, u32[]{:S(2)}) collective-permute-start(bf16[288,128]{1,0:T(8,128)(2,1)} %pack.1), channel_id=1, source_target_pairs={{0,30},{2,4},{4,2},{6,8},{8,6},{10,12},{12,10},{14,16},{16,14},{18... | collective-permute-start | bytes 221192 | tf_op jit(solution)/shard_map/ppermute | solution.py:593
  14.4 13.4 %copy-start.3 = (s32[3,1024]{1,0:T(4,128)S(1)}, s32[3,1024]{1,0:T(4,128)}, u32[]{:S(2)}) copy-start(s32[3,1024]{1,0:T(4,128)} %refs_7_.5) | copy-start | bytes 36868
  17.5 6.7 %collective-permute-start.4 = (bf16[1,80,256]{2,1,0:T(8,128)(2,1)S(1)}, bf16[1,80,256]{2,1,0:T(8,128)(2,1)S(1)}, u32[]{:S(2)}, u32[]{:S(2)}) collective-permute-start(bf16[1,80,256]{2,1,0:T(8,128)(2,1)S(1)} %get-tuple-element.39), channel_id=1, source_target_pairs={{0,24},{2,26},{4,28},{6,30},{8,16},{10,18},{12,20},{14,22},{16,8},... | collective-permute-start | bytes 122888 | tf_op jit(solution)/shard_map/ppermute | solution.py:537
  18.4 5.8 %collective-permute-start.3 = (bf16[1,80,256]{2,1,0:T(8,128)(2,1)S(1)}, bf16[1,80,256]{2,1,0:T(8,128)(2,1)S(1)}, u32[]{:S(2)}, u32[]{:S(2)}) collective-permute-start(bf16[1,80,256]{2,1,0:T(8,128)(2,1)S(1)} %get-tuple-element.39), channel_id=1, source_target_pairs={{0,16},{2,18},{4,20},{6,22},{8,24},{10,26},{12,28},{14,30},{16,0},... | collective-permute-start | bytes 122888 | tf_op jit(solution)/shard_map/ppermute | solution.py:537
  18.4 5.5 %collective-permute-start.2 = (bf16[1,80,256]{2,1,0:T(8,128)(2,1)S(1)}, bf16[1,80,256]{2,1,0:T(8,128)(2,1)S(1)}, u32[]{:S(2)}, u32[]{:S(2)}) collective-permute-start(bf16[1,80,256]{2,1,0:T(8,128)(2,1)S(1)} %get-tuple-element.39), channel_id=1, source_target_pairs={{0,8},{2,10},{4,12},{6,14},{8,0},{10,2},{12,4},{14,6},{16,24},{18,... | collective-permute-start | bytes 122888 | tf_op jit(solution)/shard_map/ppermute | solution.py:537
  24.3 7.3 %collective-permute-start.7 = (bf16[4,80,256]{2,1,0:T(8,128)(2,1)S(1)}, bf16[4,80,256]{2,1,0:T(8,128)(2,1)S(1)}, u32[]{:S(2)}, u32[]{:S(2)}) collective-permute-start(bf16[4,80,256]{2,1,0:T(8,128)(2,1)S(1)} %constant_dynamic-update-slice_fusion.refs_1_), channel_id=1, source_target_pairs={{0,6},{2,4},{4,2},{6,0},{8,14},{10,12},{12,10},{14,8},{16,22},{18,... | collective-permute-start | bytes 491528 | tf_op jit(solution)/shard_map/ppermute | solution.py:537
  26.7 6.3 %collective-permute-start.6 = (bf16[4,80,256]{2,1,0:T(8,128)(2,1)S(1)}, bf16[4,80,256]{2,1,0:T(8,128)(2,1)S(1)}, u32[]{:S(2)}, u32[]{:S(2)}) collective-permute-start(bf16[4,80,256]{2,1,0:T(8,128)(2,1)S(1)} %constant_dynamic-update-slice_fusion.refs_1_), channel_id=1, source_target_pairs={{0,4},{2,6},{4,0},{6,2},{8,12},{10,14},{12,8},{14,10},{16,20},{18,... | collective-permute-start | bytes 491528 | tf_op jit(solution)/shard_map/ppermute | solution.py:537
  26.7 6.3 %collective-permute-start.5 = (bf16[4,80,256]{2,1,0:T(8,128)(2,1)S(1)}, bf16[4,80,256]{2,1,0:T(8,128)(2,1)S(1)}, u32[]{:S(2)}, u32[]{:S(2)}) collective-permute-start(bf16[4,80,256]{2,1,0:T(8,128)(2,1)S(1)} %constant_dynamic-update-slice_fusion.refs_1_), channel_id=1, source_target_pairs={{0,2},{2,0},{4,6},{6,4},{8,10},{10,8},{12,14},{14,12},{16,18},{18,... | collective-permute-start | bytes 491528 | tf_op jit(solution)/shard_map/ppermute | solution.py:537
  41.9 4.2 %collective-permute-start.8 = (f32[3,16,256]{2,1,0:T(8,128)S(1)}, f32[3,16,256]{2,1,0:T(8,128)S(1)}, u32[]{:S(2)}, u32[]{:S(2)}) collective-permute-start(f32[3,16,256]{2,1,0:T(8,128)S(1)} %get-tuple-element.43), channel_id=1, source_target_pairs={{0,2},{2,0},{4,6},{6,4},{8,10},{10,8},{12,14},{14,12},{16,18},{18,... | collective-permute-start | bytes 147464 | tf_op jit(solution)/shard_map/ppermute | solution.py:537
  50.9 3.9 %collective-permute-start.9 = (bf16[64,256]{1,0:T(8,128)(2,1)S(1)}, bf16[64,256]{1,0:T(8,128)(2,1)S(1)}, u32[]{:S(2)}, u32[]{:S(2)}) collective-permute-start(bf16[64,256]{1,0:T(8,128)(2,1)S(1)} %get-tuple-element.48), channel_id=1, source_target_pairs={{0,2},{2,0},{4,6},{6,4},{8,10},{10,8},{12,14},{14,12},{16,18},{18,... | collective-permute-start | bytes 98312 | tf_op jit(solution)/shard_map/ppermute | solution.py:537
  56.5 3.9 %collective-permute-start.10 = (f32[56,128]{1,0:T(8,128)S(1)}, f32[56,128]{1,0:T(8,128)S(1)}, u32[]{:S(2)}, u32[]{:S(2)}) collective-permute-start(f32[56,128]{1,0:T(8,128)S(1)} %get-tuple-element.54), channel_id=1, source_target_pairs={{0,2},{2,0},{4,6},{6,4},{8,10},{10,8},{12,14},{14,12},{16,18},{18,... | collective-permute-start | bytes 86024 | tf_op jit(solution)/shard_map/ppermute | solution.py:537
  57.7 3.9 %collective-permute-start.11 = (f32[56,128]{1,0:T(8,128)S(1)}, f32[56,128]{1,0:T(8,128)S(1)}, u32[]{:S(2)}, u32[]{:S(2)}) collective-permute-start(f32[56,128]{1,0:T(8,128)S(1)} %get-tuple-element.55), channel_id=1, source_target_pairs={{0,4},{2,6},{4,0},{6,2},{8,12},{10,14},{12,8},{14,10},{16,20},{18,... | collective-permute-start | bytes 86024 | tf_op jit(solution)/shard_map/ppermute | solution.py:537
  58.4 4.8 %collective-permute-start.12 = (f32[56,128]{1,0:T(8,128)S(1)}, f32[56,128]{1,0:T(8,128)S(1)}, u32[]{:S(2)}, u32[]{:S(2)}) collective-permute-start(f32[56,128]{1,0:T(8,128)S(1)} %get-tuple-element.56), channel_id=1, source_target_pairs={{0,6},{2,4},{4,2},{6,0},{8,14},{10,12},{12,10},{14,8},{16,22},{18,... | collective-permute-start | bytes 86024 | tf_op jit(solution)/shard_map/ppermute | solution.py:537
  63.2 5.7 %collective-permute-start.15 = (f32[56,128]{1,0:T(8,128)S(1)}, f32[56,128]{1,0:T(8,128)S(1)}, u32[]{:S(2)}, u32[]{:S(2)}) collective-permute-start(f32[56,128]{1,0:T(8,128)S(1)} %add_add_fusion.1), channel_id=1, source_target_pairs={{0,24},{2,26},{4,28},{6,30},{8,16},{10,18},{12,20},{14,22},{16,8},... | collective-permute-start | bytes 86024 | tf_op jit(solution)/shard_map/ppermute | solution.py:537
  65.2 4.8 %collective-permute-start.14 = (f32[56,128]{1,0:T(8,128)S(1)}, f32[56,128]{1,0:T(8,128)S(1)}, u32[]{:S(2)}, u32[]{:S(2)}) collective-permute-start(f32[56,128]{1,0:T(8,128)S(1)} %add_add_fusion.1), channel_id=1, source_target_pairs={{0,16},{2,18},{4,20},{6,22},{8,24},{10,26},{12,28},{14,30},{16,0},... | collective-permute-start | bytes 86024 | tf_op jit(solution)/shard_map/ppermute | solution.py:537
  65.7 4.3 %collective-permute-start.13 = (f32[56,128]{1,0:T(8,128)S(1)}, f32[56,128]{1,0:T(8,128)S(1)}, u32[]{:S(2)}, u32[]{:S(2)}) collective-permute-start(f32[56,128]{1,0:T(8,128)S(1)} %add_add_fusion.1), channel_id=1, source_target_pairs={{0,8},{2,10},{4,12},{6,14},{8,0},{10,2},{12,4},{14,6},{16,24},{18,... | collective-permute-start | bytes 86024 | tf_op jit(solution)/shard_map/ppermute | solution.py:537
  70.0 4.8 %collective-permute-start.18 = (f32[56,128]{1,0:T(8,128)S(1)}, f32[56,128]{1,0:T(8,128)S(1)}, u32[]{:S(2)}, u32[]{:S(2)}) collective-permute-start(f32[56,128]{1,0:T(8,128)S(1)} %add_add_fusion.refs_0_), channel_id=1, source_target_pairs={{0,6},{2,4},{4,2},{6,0},{8,14},{10,12},{12,10},{14,8},{16,22},{18,... | collective-permute-start | bytes 86024 | tf_op jit(solution)/shard_map/ppermute | solution.py:537
  71.8 3.9 %collective-permute-start.17 = (f32[56,128]{1,0:T(8,128)S(1)}, f32[56,128]{1,0:T(8,128)S(1)}, u32[]{:S(2)}, u32[]{:S(2)}) collective-permute-start(f32[56,128]{1,0:T(8,128)S(1)} %add_add_fusion.refs_0_), channel_id=1, source_target_pairs={{0,4},{2,6},{4,0},{6,2},{8,12},{10,14},{12,8},{14,10},{16,20},{18,... | collective-permute-start | bytes 86024 | tf_op jit(solution)/shard_map/ppermute | solution.py:537
  73.1 3.9 %collective-permute-start.16 = (f32[56,128]{1,0:T(8,128)S(1)}, f32[56,128]{1,0:T(8,128)S(1)}, u32[]{:S(2)}, u32[]{:S(2)}) collective-permute-start(f32[56,128]{1,0:T(8,128)S(1)} %add_add_fusion.refs_0_), channel_id=1, source_target_pairs={{0,2},{2,0},{4,6},{6,4},{8,10},{10,8},{12,14},{14,12},{16,18},{18,... | collective-permute-start | bytes 86024 | tf_op jit(solution)/shard_map/ppermute | solution.py:537

commit v6 on v5

--- a/solution.py
+++ b/solution.py
@@ -331,9 +331,21 @@
     part_ref[...] = part
 
 
-def structure_kernel(where_ref, *refs, group, blocks, charge_count, box_x):
-    shared_refs = refs[:blocks]
-    early_ref, part_ref, wave_ref, waves_ref, weights_ref, *force_refs = refs[blocks:]
+def placed_waves(early, early_refs, late, waves_ref, count):
+    return [
+        early_refs[early.index(r)].at[j]
+        if r in early
+        else waves_ref.at[j * len(late) + late.index(r)]
+        for j in range(count)
+        for r in range(len(early) + len(late))
+    ]
+
+
+def structure_kernel(where_ref, *refs, group, blocks, early, charge_count, box_x):
+    shared_refs, early_refs = refs[:blocks], refs[blocks : blocks + len(early)]
+    part_refs, refs = refs[blocks + len(early) : blocks + 2 * len(early)], refs[blocks + 2 * len(early) :]
+    wave_ref, waves_ref, weights_ref, *force_refs = refs
+    late = [r for r in range(blocks) if r not in early]
     count, _, atoms = shared_refs[0].shape
     share = waves_ref.shape[1] // 2
     first = pl.multiple_of(where_ref[1] * share, share)
@@ -341,22 +353,16 @@
     columns = wave_columns(wave_ref, first, share)
 
     def block(j, carry):
-        for r in range(1, blocks):
-            fill_waves(
-                columns, shared_refs[r], j, charge_count, waves_ref, j * (blocks - 1) + r - 1
-            )
+        for i, r in enumerate(late):
+            fill_waves(columns, shared_refs[r], j, charge_count, waves_ref, j * len(late) + i)
         return carry
 
     lax.fori_loop(0, count, block, 0, unroll=4)
-    waves_of = [
-        waves_ref.at[j * (blocks - 1) + r - 1] if r else early_ref.at[j]
-        for j in range(count)
-        for r in range(blocks)
-    ]
-    structure = part_ref[...]
+    waves_of = placed_waves(early, early_refs, late, waves_ref, count)
+    structure = sum(ref[...] for ref in part_refs)
     for d in range(blocks * count):
         j, r = divmod(d, blocks)
-        if r:
+        if r in late:
             structure = structure + matmul_nt(
                 shared_refs[r][j, 0:charge_count, :], waves_of[d][...]
             )
@@ -381,20 +387,17 @@
                 force_refs[m][a, d ^ m : (d ^ m) + 1, :] = row
 
 
-def gradient_kernel(where_ref, *refs, group, blocks, charge_count, box_x):
+def gradient_kernel(where_ref, *refs, group, blocks, early, charge_count, box_x):
     shared_refs, part_refs = refs[:blocks], refs[blocks : blocks + group]
-    wave_ref, early_ref, waves_ref, weights_ref, forces_ref, *grad_refs, total_ref = refs[
-        blocks + group :
-    ]
+    refs = refs[blocks + group :]
+    early_refs, refs = refs[: len(early)], refs[len(early) :]
+    wave_ref, waves_ref, weights_ref, forces_ref, *grad_refs, total_ref = refs
+    late = [r for r in range(blocks) if r not in early]
     count, _, atoms = shared_refs[0].shape
     share = waves_ref.shape[1] // 2
     first = pl.multiple_of(where_ref[1] * share, share)
     _, waves, damping = wave_rows(wave_ref, first, share, box_x, blocks * count * atoms)
-    waves_of = [
-        waves_ref.at[j * (blocks - 1) + r - 1] if r else early_ref.at[j]
-        for j in range(count)
-        for r in range(blocks)
-    ]
+    waves_of = placed_waves(early, early_refs, late, waves_ref, count)
     total = part_refs[0][...]
     for m in range(1, group):
         total = total + part_refs[m][...]
@@ -439,7 +442,7 @@
         grad_refs[m][...] = grad.astype(grad_refs[m].dtype)
 
 
-def weights_kernel(where_ref, *refs, group, kinds):
+def weights_kernel(*refs, group, kinds):
     part_refs = refs[:group]
     (
         filtered_ref,
@@ -449,7 +452,6 @@
         species_ref,
         mix_ref,
         charge_ref,
-        *piece_refs,
         packed_ref,
     ) = refs[group:]
     charge_count, atoms = part_refs[0].shape
@@ -480,20 +482,20 @@
         lax.broadcasted_iota(jnp.int32, (kinds, atoms), 0) == species_ref[...]
     ).astype(f32)
     packed_ref[row : row + kinds, 0:charge_count] = matmul_nt(one_hot, grad, highest)
-    count = piece_refs[0].shape[0]
-    for r, ref in enumerate(piece_refs):
-        ref[...] = packed_ref[pl.ds(pl.multiple_of((where_ref[2] ^ r) * count, 8), count), :]
-
-
-def step_kernel(where_ref, *refs):
-    *piece_refs, radial_ref, mix_ref, charge_ref, species_ref, total_ref = refs
+
+
+def summed(values):
+    while len(values) > 1:
+        values = [values[i] + values[i + 1] for i in range(0, len(values), 2)]
+    return values[0]
+
+
+def step_kernel(*refs):
+    *total_refs, radial_ref, mix_ref, charge_ref, species_ref, total_ref = refs
     basis_count, width = radial_ref.shape
     charge_count = charge_ref.shape[0]
     kinds = species_ref.shape[0]
-
-    count = piece_refs[0].shape[0]
-    for r, ref in enumerate(piece_refs):
-        total_ref[pl.ds(pl.multiple_of((where_ref[2] ^ r) * count, 8), count), :] = ref[...]
+    total_ref[...] = summed([ref[...] for ref in total_refs])
 
     def normalized(gradient):
         mean = jnp.sum(gradient * gradient, keepdims=True) * (1.0 / gradient.size)
@@ -535,12 +537,6 @@
 def across(value, bits):
     domains = lax.axis_size("dom")
     return lax.ppermute(value, "dom", [(i, i ^ bits) for i in range(domains)])
-
-
-def summed(values):
-    while len(values) > 1:
-        values = [values[i] + values[i + 1] for i in range(0, len(values), 2)]
-    return values[0]
 
 
 def on_device(
@@ -664,41 +660,47 @@
         [shared] + [across(shared, bits) for bits in range(blocks, domains, blocks)], axis=0
     )
     columns = [column] + [across(column, bits) for bits in range(1, blocks)]
-    early, part = kernel(
-        lambda *refs: phase_kernel(*refs, charge_count=charge_count),
-        "phases",
-        (
-            shaped(domains // blocks, 2 * share, atoms, kind=bf16),
-            shaped(charge_count, 2 * share),
-        ),
-        (),
-        3_000,
-        column,
-        wave_index,
-        scalars=(where,),
+    early = (0, blocks - 1) if blocks > 2 else (0,)
+    waves_early, parts = zip(
+        *[
+            kernel(
+                lambda *refs: phase_kernel(*refs, charge_count=charge_count),
+                "phases",
+                (
+                    shaped(domains // blocks, 2 * share, atoms, kind=bf16),
+                    shaped(charge_count, 2 * share),
+                ),
+                (),
+                3_000,
+                columns[r],
+                wave_index,
+                scalars=(where,),
+            )
+            for r in early
+        ]
     )
     waves, weights, *force_parts = kernel(
         lambda *refs: structure_kernel(
-            *refs, group=group, blocks=blocks, charge_count=charge_count, box_x=box_x
+            *refs, group=group, blocks=blocks, early=early, charge_count=charge_count, box_x=box_x
         ),
         "structure",
         (
-            shaped(domains - domains // blocks, 2 * share, atoms, kind=bf16),
+            shaped(domains - len(early) * (domains // blocks), 2 * share, atoms, kind=bf16),
             shaped(3 * charge_count, 2 * share),
         )
         + (shaped(3, domains, atoms),) * group,
         (),
         8_000,
         *columns,
-        early,
-        part,
+        *waves_early,
+        *parts,
         wave_index,
         scalars=(where,),
     )
     force_parts = force_parts[:1] + [across(force_parts[m], m) for m in range(1, group)]
     forces, *grad_parts = kernel(
         lambda *refs: gradient_kernel(
-            *refs, group=group, blocks=blocks, charge_count=charge_count, box_x=box_x
+            *refs, group=group, blocks=blocks, early=early, charge_count=charge_count, box_x=box_x
         ),
         "gradient",
         (shaped(3, atoms),) + (shaped(charge_count, atoms, kind=bf16),) * group,
@@ -706,8 +708,8 @@
         5_000,
         *columns,
         *force_parts,
+        *waves_early,
         wave_index,
-        early,
         waves,
         weights,
         scalars=(where,),
@@ -715,12 +717,12 @@
     grad_parts = grad_parts[:1] + [across(grad_parts[m], m) for m in range(1, group)]
 
     rows = basis_count + width + charge_count + kinds
-    rows = -(-rows // (8 * blocks)) * 8
-    pieces = kernel(
+    rows = -(-rows // 8) * 8
+    packed = kernel(
         lambda *refs: weights_kernel(*refs, group=group, kinds=kinds),
         "weights",
-        (shaped(rows, width),) * blocks,
-        (shaped(blocks * rows, width),),
+        shaped(rows, width),
+        (),
         3_000,
         *grad_parts,
         filtered,
@@ -730,11 +732,9 @@
         species_row,
         mix_weight,
         charge_rows,
-        scalars=(where,),
-    )
-    piece = summed([pieces[0]] + [across(pieces[r], r) for r in range(1, blocks)])
-    piece = summed([piece] + [across(piece, bits) for bits in range(blocks, domains, blocks)])
-    pieces = [piece] + [across(piece, r) for r in range(1, blocks)]
+    )
+    packed = summed([packed] + [across(packed, r) for r in range(1, blocks)])
+    totals = [packed] + [across(packed, bits) for bits in range(blocks, domains, blocks)]
     radial_step, mix_step, charge_step, species_step = kernel(
         step_kernel,
         "steps",
@@ -744,10 +744,9 @@
             shaped(charge_count, width),
             shaped(kinds, charge_count),
         ),
-        (shaped(blocks * rows, width),),
+        (shaped(rows, width),),
         2_000,
-        *pieces,
-        scalars=(where,),
+        *totals,
     )
     return forces, radial_step, mix_step, charge_step.T, species_step
 

time: 78.5 us -> 72.5 us (0.924)
  starting transfers between devices: 29.4 us -> 24.1 us
    ppermute x18 -> x15, starting transfers between devices: 24.9 us -> 19.6 us  [across(): return lax.ppermute(value, 'dom', [(i, i ^ bits) for i in range(domains)])]
    ppermute x18 -> x15, waiting for transfers between devices: 19.3 us -> 18.9 us  [across(): return lax.ppermute(value, 'dom', [(i, i ^ bits) for i in range(domains)])]
    pallas_call x9 -> x10, Pallas kernels: 28.6 us -> 28.3 us  [kernel(): pl.pallas_call(body, out_shape=out_shape, in_specs=[in_smem] * len(scalar...]
  transfers between devices with their start and end apart: 19 -> 16, of which waited for: 14 -> 9; matrix products, arithmetic and copies ran while one was open for 0% -> 0% of each run, Pallas kernels for 9% -> 14%
where the time goes in v6:
time: 72.5 us; the launch traced here: 72.3 us
  Pallas kernels  28.3 us (39%)
  starting transfers between devices  24.1 us (33%)
  waiting for transfers between devices  18.9 us (26%)
  between operations  0.85 us (1%)
    pallas_call x10, Pallas kernels, kernel(): pl.pallas_call(body, out_shape=out_shape, in_specs=[in_smem] * len(scalar...  28.3 us
    ppermute x15, starting transfers between devices, across(): return lax.ppermute(value, 'dom', [(i, i ^ bits) for i in range(domains)])  19.6 us
    ppermute x15, waiting for transfers between devices, across(): return lax.ppermute(value, 'dom', [(i, i ^ bits) for i in range(domains)])  18.9 us
    ppermute x1, starting transfers between devices, on_device(): far = lax.ppermute(packed, 'dom', beyond)  4.53 us
  transfers between devices with their start and end apart: 16, of which 9 were waited for; matrix products, arithmetic and copies ran while one was open for 0% of the time, Pallas kernels for 14%

profile of v6, /device:TPU:0, one launch (start us, length us, event | category | flops | bytes accessed | tf_op | source)
XLA Modules:
  0.0 72.3 jit_solution(15096470179168754101)
XLA Ops:
  0.7 1.6 %pack.1 = bf16[288,128]{1,0:T(8,128)(2,1)} custom-call(bf16[256,128]{1,0:T(8,128)(2,1)} %refs_0_.1, f32[3,256]{1,0:T(4,128)} %refs_1_.1, s32[2,256]{1,0:T(2,128)} %ghost_ref.1), custom_call_target="tpu_custom_call" | custom-call | flops 1000000000 | bytes 144384 | tf_op jit(solution)/shard_map/pack/pallas_call | solution.py:523
  2.3 2.9 %collective-permute-start.1 = (bf16[288,128]{1,0:T(8,128)(2,1)}, bf16[288,128]{1,0:T(8,128)(2,1)S(1)}, u32[]{:S(2)}, u32[]{:S(2)}) collective-permute-start(bf16[288,128]{1,0:T(8,128)(2,1)} %pack.1), channel_id=1, source_target_pairs={{0,2},{2,0},{4,6},{6,4},{8,10},{10,8},{12,14},{14,12},{16,18},{18,... | collective-permute-start | bytes 221192 | tf_op jit(solution)/shard_map/ppermute | solution.py:539
  5.3 4.5 %collective-permute-start = (bf16[288,128]{1,0:T(8,128)(2,1)}, bf16[288,128]{1,0:T(8,128)(2,1)S(1)}, u32[]{:S(2)}, u32[]{:S(2)}) collective-permute-start(bf16[288,128]{1,0:T(8,128)(2,1)} %pack.1), channel_id=1, source_target_pairs={{0,30},{2,4},{4,2},{6,8},{8,6},{10,12},{12,10},{14,16},{16,14},{18... | collective-permute-start | bytes 221192 | tf_op jit(solution)/shard_map/ppermute | solution.py:589
  9.9 1.9 %own.1 = (f32[16,128,256]{2,1,0:T(8,128)S(1)}, s32[24,256]{1,0:T(8,128)S(1)}, bf16[128,256]{1,0:T(8,128)(2,1)S(1)}, f32[64,256]{1,0:T(8,128)S(1)}, f32[320,128]{1,0:T(8,128)S(1)}, /*index=5*/f32[24,256]{1,0:T(8,128)S(1)}) custom-call(bf16[256,128]{1,0:T(8,128)(2,1)S(1)} %copy-done, f32[3,256]{1,0:T(4,128)S(1)} %copy-done.5, f32[3,256]{1,0:T(4,128)S(1)} %copy-done.6, ...), custom_call_target="tpu_custom_call" | custom-call | flops 4000000000 | bytes 4740608 | tf_op jit(solution)/shard_map/own/pallas_call | solution.py:523
  11.8 0.1 pad_add_fusion.refs_0_
  11.8 2.5 %near.1.refs_2_ = f32[16,128,256]{2,1,0:T(8,128)S(1)} custom-call(s32[3]{0:T(128)S(1)} %pad_add_fusion.refs_0_, bf16[288,128]{1,0:T(8,128)(2,1)S(1)} %collective-permute-done.1.refs_1_, f32[16,128,256]{2,1,0:T(8,128)S(1)} %get-tuple-element.31.refs_2_, s32[24,256]{1,0:T(8,128)S(1)} %get-tuple-element.32.refs_3_, f32[24,256]{1,0:T(8,128)S(1)} %get-tuple-element.33.refs_4_.refs_7_), custom_call_target="tpu_custom_call" | custom-call | flops 3000000000 | bytes 6430720 | tf_op jit(solution)/shard_map/near/pallas_call | solution.py:523
  14.4 3.2 %edges.1 = (f32[16,128,256]{2,1,0:T(8,128)S(1)}, f32[128,256]{1,0:T(8,128)S(1)}, f32[128,256]{1,0:T(8,128)S(1)}, bf16[128,256]{1,0:T(8,128)(2,1)S(1)}, bf16[1,80,256]{2,1,0:T(8,128)(2,1)S(1)}) custom-call(s32[3]{0:T(128)S(1)} %pad_add_fusion.refs_0_, bf16[288,128]{1,0:T(8,128)(2,1)S(1)} %collective-permute-done.refs_1_, f32[16,128,256]{2,1,0:T(8,128)S(1)} %near.1.refs_2_, ...), custom_call_target="tpu_custom_call" | custom-call | flops 4000000000 | bytes 7094272 | tf_op jit(solution)/shard_map/edges/pallas_call | solution.py:523
  17.6 0.9 %collective-permute-start.4 = (bf16[1,80,256]{2,1,0:T(8,128)(2,1)S(1)}, bf16[1,80,256]{2,1,0:T(8,128)(2,1)S(1)}, u32[]{:S(2)}, u32[]{:S(2)}) collective-permute-start(bf16[1,80,256]{2,1,0:T(8,128)(2,1)S(1)} %get-tuple-element.37), channel_id=1, source_target_pairs={{0,24},{2,26},{4,28},{6,30},{8,16},{10,18},{12,20},{14,22},{16,8},... | collective-permute-start | bytes 122888 | tf_op jit(solution)/shard_map/ppermute | solution.py:539
  18.5 3.6 %collective-permute-start.2 = (bf16[1,80,256]{2,1,0:T(8,128)(2,1)S(1)}, bf16[1,80,256]{2,1,0:T(8,128)(2,1)S(1)}, u32[]{:S(2)}, u32[]{:S(2)}) collective-permute-start(bf16[1,80,256]{2,1,0:T(8,128)(2,1)S(1)} %get-tuple-element.37), channel_id=1, source_target_pairs={{0,8},{2,10},{4,12},{6,14},{8,0},{10,2},{12,4},{14,6},{16,24},{18,... | collective-permute-start | bytes 122888 | tf_op jit(solution)/shard_map/ppermute | solution.py:539
  22.1 2.0 %collective-permute-done.2 = bf16[1,80,256]{2,1,0:T(8,128)(2,1)S(1)} collective-permute-done((bf16[1,80,256]{2,1,0:T(8,128)(2,1)S(1)}, bf16[1,80,256]{2,1,0:T(8,128)(2,1)S(1)}, u32[]{:S(2)}, u32[]{:S(2)}) %collective-permute-start.2) | collective-permute-done | bytes 40992 | tf_op jit(solution)/shard_map/ppermute | solution.py:539
  24.1 0.2 collective-permute-done.3
  24.3 2.4 %collective-permute-start.7 = (bf16[4,80,256]{2,1,0:T(8,128)(2,1)S(1)}, bf16[4,80,256]{2,1,0:T(8,128)(2,1)S(1)}, u32[]{:S(2)}, u32[]{:S(2)}) collective-permute-start(bf16[4,80,256]{2,1,0:T(8,128)(2,1)S(1)} %constant_dynamic-update-slice_fusion.refs_1_), channel_id=1, source_target_pairs={{0,6},{2,4},{4,2},{6,0},{8,14},{10,12},{12,10},{14,8},{16,22},{18,... | collective-permute-start | bytes 491528 | tf_op jit(solution)/shard_map/ppermute | solution.py:539
  26.8 1.1 %collective-permute-start.5 = (bf16[4,80,256]{2,1,0:T(8,128)(2,1)S(1)}, bf16[4,80,256]{2,1,0:T(8,128)(2,1)S(1)}, u32[]{:S(2)}, u32[]{:S(2)}) collective-permute-start(bf16[4,80,256]{2,1,0:T(8,128)(2,1)S(1)} %constant_dynamic-update-slice_fusion.refs_1_), channel_id=1, source_target_pairs={{0,2},{2,0},{4,6},{6,4},{8,10},{10,8},{12,14},{14,12},{16,18},{18,... | collective-permute-start | bytes 491528 | tf_op jit(solution)/shard_map/ppermute | solution.py:539
  27.9 2.8 %phases.2 = (bf16[4,1024,256]{2,1,0:T(8,128)(2,1)S(1)}, f32[64,1024]{1,0:T(8,128)S(1)}) custom-call(s32[3]{0:T(128)S(1)} %pad_add_fusion.refs_0_, bf16[4,80,256]{2,1,0:T(8,128)(2,1)S(1)} %constant_dynamic-update-slice_fusion.refs_1_, s32[3,1024]{1,0:T(4,128)S(1)} %copy-done.3), custom_call_target="tpu_custom_call" | custom-call | flops 3000000000 | bytes 2535424 | tf_op jit(solution)/shard_map/phases/pallas_call | solution.py:523
  30.6 1.0 %collective-permute-done.7.refs_1_.refs_4_ = bf16[4,80,256]{2,1,0:T(8,128)(2,1)S(1)} collective-permute-done((bf16[4,80,256]{2,1,0:T(8,128)(2,1)S(1)}, bf16[4,80,256]{2,1,0:T(8,128)(2,1)S(1)}, u32[]{:S(2)}, u32[]{:S(2)}) %collective-permute-start.7) | collective-permute-done | bytes 163872 | tf_op jit(solution)/shard_map/ppermute | solution.py:539
  31.6 2.8 %phases.3 = (bf16[4,1024,256]{2,1,0:T(8,128)(2,1)S(1)}, f32[64,1024]{1,0:T(8,128)S(1)}) custom-call(s32[3]{0:T(128)S(1)} %pad_add_fusion.refs_0_, bf16[4,80,256]{2,1,0:T(8,128)(2,1)S(1)} %collective-permute-done.7.refs_1_.refs_4_, s32[3,1024]{1,0:T(4,128)S(1)} %copy-done.3), custom_call_target="tpu_custom_call" | custom-call | flops 3000000000 | bytes 2535424 | tf_op jit(solution)/shard_map/phases/pallas_call | solution.py:523
  34.4 6.9 %structure.1 = (bf16[8,1024,256]{2,1,0:T(8,128)(2,1)S(1)}, f32[192,1024]{1,0:T(8,128)S(1)}, f32[3,16,256]{2,1,0:T(8,128)S(1)}, f32[3,16,256]{2,1,0:T(8,128)S(1)}) custom-call(s32[3]{0:T(128)S(1)} %pad_add_fusion.refs_0_, bf16[4,80,256]{2,1,0:T(8,128)(2,1)S(1)} %constant_dynamic-update-slice_fusion.refs_1_, ...), custom_call_target="tpu_custom_call" | custom-call | flops 8000000000 | bytes 10465280 | tf_op jit(solution)/shard_map/structure/pallas_call | solution.py:523
  41.3 0.3 collective-permute-start.8
  41.6 3.8 %collective-permute-done.8.refs_6_ = f32[3,16,256]{2,1,0:T(8,128)S(1)} collective-permute-done((f32[3,16,256]{2,1,0:T(8,128)S(1)}, f32[3,16,256]{2,1,0:T(8,128)S(1)}, u32[]{:S(2)}, u32[]{:S(2)}) %collective-permute-start.8) | collective-permute-done | bytes 49184 | tf_op jit(solution)/shard_map/ppermute | solution.py:539
  45.4 4.8 %gradient.1 = (f32[3,256]{1,0:T(4,128)}, bf16[64,256]{1,0:T(8,128)(2,1)S(1)}, bf16[64,256]{1,0:T(8,128)(2,1)S(1)}) custom-call(s32[3]{0:T(128)S(1)} %pad_add_fusion.refs_0_, bf16[4,80,256]{2,1,0:T(8,128)(2,1)S(1)} %constant_dynamic-update-slice_fusion.refs_1_, bf16[4,80,256]{2,1,0:T(8,128)(2,1)S(1)} %collective-permute-done.5.refs_2_, ...), custom_call_target="tpu_custom_call" | custom-call | flops 5000000000 | bytes 10058752 | tf_op jit(solution)/shard_map/gradient/pallas_call | solution.py:523
  50.2 0.3 collective-permute-start.9
  50.5 4.0 %collective-permute-done.9.refs_1_ = bf16[64,256]{1,0:T(8,128)(2,1)S(1)} collective-permute-done((bf16[64,256]{1,0:T(8,128)(2,1)S(1)}, bf16[64,256]{1,0:T(8,128)(2,1)S(1)}, u32[]{:S(2)}, u32[]{:S(2)}) %collective-permute-start.9) | collective-permute-done | bytes 32800 | tf_op jit(solution)/shard_map/ppermute | solution.py:539
  54.5 1.1 %weights.1 = f32[216,128]{1,0:T(8,128)S(1)} custom-call(bf16[64,256]{1,0:T(8,128)(2,1)S(1)} %get-tuple-element.47.refs_0_, bf16[64,256]{1,0:T(8,128)(2,1)S(1)} %collective-permute-done.9.refs_1_, f32[16,128,256]{2,1,0:T(8,128)S(1)} %get-tuple-element.49.refs_2_, f32[128,256]{1,0:T(8,128)S(1)} %get-tuple-element.50.refs_3_, ...), custom_call_target="tpu_custom_call" | custom-call | flops 3000000000 | bytes 2651136 | tf_op jit(solution)/shard_map/weights/pallas_call | solution.py:523
  55.6 1.8 %collective-permute-start.12 = (f32[216,128]{1,0:T(8,128)S(1)}, f32[216,128]{1,0:T(8,128)S(1)}, u32[]{:S(2)}, u32[]{:S(2)}) collective-permute-start(f32[216,128]{1,0:T(8,128)S(1)} %weights.1), channel_id=1, source_target_pairs={{0,6},{2,4},{4,2},{6,0},{8,14},{10,12},{12,10},{14,8},{16,22},{18,... | collective-permute-start | bytes 331784 | tf_op jit(solution)/shard_map/ppermute | solution.py:539
  57.4 1.7 %collective-permute-start.10 = (f32[216,128]{1,0:T(8,128)S(1)}, f32[216,128]{1,0:T(8,128)S(1)}, u32[]{:S(2)}, u32[]{:S(2)}) collective-permute-start(f32[216,128]{1,0:T(8,128)S(1)} %weights.1), channel_id=1, source_target_pairs={{0,2},{2,0},{4,6},{6,4},{8,10},{10,8},{12,14},{14,12},{16,18},{18,... | collective-permute-start | bytes 331784 | tf_op jit(solution)/shard_map/ppermute | solution.py:539
  59.1 2.2 %collective-permute-done.12 = f32[216,128]{1,0:T(8,128)S(1)} collective-permute-done((f32[216,128]{1,0:T(8,128)S(1)}, f32[216,128]{1,0:T(8,128)S(1)}, u32[]{:S(2)}, u32[]{:S(2)}) %collective-permute-start.12) | collective-permute-done | bytes 110624 | tf_op jit(solution)/shard_map/ppermute | solution.py:539
  61.3 1.2 %collective-permute-done.11 = f32[216,128]{1,0:T(8,128)S(1)} collective-permute-done((f32[216,128]{1,0:T(8,128)S(1)}, f32[216,128]{1,0:T(8,128)S(1)}, u32[]{:S(2)}, u32[]{:S(2)}) %collective-permute-start.11) | collective-permute-done | bytes 110624 | tf_op jit(solution)/shard_map/ppermute | solution.py:539
  62.5 2.5 %collective-permute-start.15 = (f32[216,128]{1,0:T(8,128)S(1)}, f32[216,128]{1,0:T(8,128)S(1)}, u32[]{:S(2)}, u32[]{:S(2)}) collective-permute-start(f32[216,128]{1,0:T(8,128)S(1)} %add_add_fusion.refs_0_), channel_id=1, source_target_pairs={{0,24},{2,26},{4,28},{6,30},{8,16},{10,18},{12,20},{14,22},{16,8},... | collective-permute-start | bytes 331784 | tf_op jit(solution)/shard_map/ppermute | solution.py:539
  65.0 2.0 %collective-permute-start.13 = (f32[216,128]{1,0:T(8,128)S(1)}, f32[216,128]{1,0:T(8,128)S(1)}, u32[]{:S(2)}, u32[]{:S(2)}) collective-permute-start(f32[216,128]{1,0:T(8,128)S(1)} %add_add_fusion.refs_0_), channel_id=1, source_target_pairs={{0,8},{2,10},{4,12},{6,14},{8,0},{10,2},{12,4},{14,6},{16,24},{18,... | collective-permute-start | bytes 331784 | tf_op jit(solution)/shard_map/ppermute | solution.py:539
  67.0 2.2 %collective-permute-done.15.refs_3_ = f32[216,128]{1,0:T(8,128)S(1)} collective-permute-done((f32[216,128]{1,0:T(8,128)S(1)}, f32[216,128]{1,0:T(8,128)S(1)}, u32[]{:S(2)}, u32[]{:S(2)}) %collective-permute-start.15) | collective-permute-done | bytes 110624 | tf_op jit(solution)/shard_map/ppermute | solution.py:539
  69.2 2.3 %collective-permute-done.14.refs_2_ = f32[216,128]{1,0:T(8,128)S(1)} collective-permute-done((f32[216,128]{1,0:T(8,128)S(1)}, f32[216,128]{1,0:T(8,128)S(1)}, u32[]{:S(2)}, u32[]{:S(2)}) %collective-permute-start.14) | collective-permute-done | bytes 110624 | tf_op jit(solution)/shard_map/ppermute | solution.py:539
  71.5 0.8 %steps.1 = (f32[16,128]{1,0:T(8,128)}, f32[128,128]{1,0:T(8,128)}, f32[64,128]{1,0:T(8,128)}, f32[6,64]{1,0:T(8,128)}) custom-call(f32[216,128]{1,0:T(8,128)S(1)} %add_add_fusion.refs_0_, f32[216,128]{1,0:T(8,128)S(1)} %collective-permute-done.13.refs_1_, f32[216,128]{1,0:T(8,128)S(1)} %collective-permute-done.14.refs_2_, ...), custom_call_target="tpu_custom_call" | custom-call | flops 2000000000 | bytes 660992 | tf_op jit(solution)/shard_map/steps/pallas_call | solution.py:523
  (38 shorter events, 0.1 us)
Async XLA Ops:
  0.6 9.2 %copy-start.5 = (f32[3,256]{1,0:T(4,128)S(1)}, f32[3,256]{1,0:T(4,128)}, u32[]{:S(2)}) copy-start(f32[3,256]{1,0:T(4,128)} %refs_1_.1) | copy-start | bytes 9220
  0.6 9.1 %copy-start = (bf16[256,128]{1,0:T(8,128)(2,1)S(1)}, bf16[256,128]{1,0:T(8,128)(2,1)}, u32[]{:S(2)}) copy-start(bf16[256,128]{1,0:T(8,128)(2,1)} %refs_0_.1) | copy-start | bytes 196612
  0.7 9.1 %copy-start.2 = (bf16[128,128]{1,0:T(8,128)(2,1)S(1)}, bf16[128,128]{1,0:T(8,128)(2,1)}, u32[]{:S(2)}) copy-start(bf16[128,128]{1,0:T(8,128)(2,1)} %refs_7_.3) | copy-start | bytes 98308
  0.7 9.1 %copy-start.8 = (f32[6,64]{1,0:T(8,128)S(1)}, f32[6,64]{1,0:T(8,128)}, u32[]{:S(2)}) copy-start(f32[6,64]{1,0:T(8,128)} %refs_9_.3) | copy-start | bytes 4612
  0.7 9.1 %copy-start.4 = (bf16[128,64]{0,1:T(8,128)(2,1)S(1)}, bf16[128,64]{0,1:T(8,128)(2,1)}, u32[]{:S(2)}) copy-start(bf16[128,64]{0,1:T(8,128)(2,1)} %param.22) | copy-start | bytes 49156
  0.7 9.1 %copy-start.7 = (bf16[16,128]{1,0:T(8,128)(2,1)S(1)}, bf16[16,128]{1,0:T(8,128)(2,1)}, u32[]{:S(2)}) copy-start(bf16[16,128]{1,0:T(8,128)(2,1)} %refs_6_.1) | copy-start | bytes 12292
  0.7 9.1 %copy-start.6 = (f32[3,256]{1,0:T(4,128)S(1)}, f32[3,256]{1,0:T(4,128)}, u32[]{:S(2)}) copy-start(f32[3,256]{1,0:T(4,128)} %refs_2_.3) | copy-start | bytes 9220
  0.7 9.1 %copy-start.10 = (s32[256]{0:T(256)S(1)}, s32[256]{0:T(256)}, u32[]{:S(2)}) copy-start(s32[256]{0:T(256)} %param.17) | copy-start | bytes 3076
  0.7 9.1 %copy-start.9 = (s32[256]{0:T(256)S(1)}, s32[256]{0:T(256)}, u32[]{:S(2)}) copy-start(s32[256]{0:T(256)} %param.15) | copy-start | bytes 3076
  0.7 9.1 %copy-start.1 = (s32[256,64]{0,1:T(8,128)S(1)}, s32[256,64]{0,1:T(8,128)}, u32[]{:S(2)}) copy-start(s32[256,64]{0,1:T(8,128)} %param.14) | copy-start | bytes 196612
  2.3 9.5 %collective-permute-start.1 = (bf16[288,128]{1,0:T(8,128)(2,1)}, bf16[288,128]{1,0:T(8,128)(2,1)S(1)}, u32[]{:S(2)}, u32[]{:S(2)}) collective-permute-start(bf16[288,128]{1,0:T(8,128)(2,1)} %pack.1), channel_id=1, source_target_pairs={{0,2},{2,0},{4,6},{6,4},{8,10},{10,8},{12,14},{14,12},{16,18},{18,... | collective-permute-start | bytes 221192 | tf_op jit(solution)/shard_map/ppermute | solution.py:539
  5.3 9.1 %collective-permute-start = (bf16[288,128]{1,0:T(8,128)(2,1)}, bf16[288,128]{1,0:T(8,128)(2,1)S(1)}, u32[]{:S(2)}, u32[]{:S(2)}) collective-permute-start(bf16[288,128]{1,0:T(8,128)(2,1)} %pack.1), channel_id=1, source_target_pairs={{0,30},{2,4},{4,2},{6,8},{8,6},{10,12},{12,10},{14,16},{16,14},{18... | collective-permute-start | bytes 221192 | tf_op jit(solution)/shard_map/ppermute | solution.py:589
  14.4 13.5 %copy-start.3 = (s32[3,1024]{1,0:T(4,128)S(1)}, s32[3,1024]{1,0:T(4,128)}, u32[]{:S(2)}) copy-start(s32[3,1024]{1,0:T(4,128)} %refs_9_.5) | copy-start | bytes 36868
  17.6 6.7 %collective-permute-start.4 = (bf16[1,80,256]{2,1,0:T(8,128)(2,1)S(1)}, bf16[1,80,256]{2,1,0:T(8,128)(2,1)S(1)}, u32[]{:S(2)}, u32[]{:S(2)}) collective-permute-start(bf16[1,80,256]{2,1,0:T(8,128)(2,1)S(1)} %get-tuple-element.37), channel_id=1, source_target_pairs={{0,24},{2,26},{4,28},{6,30},{8,16},{10,18},{12,20},{14,22},{16,8},... | collective-permute-start | bytes 122888 | tf_op jit(solution)/shard_map/ppermute | solution.py:539
  18.5 5.8 %collective-permute-start.3 = (bf16[1,80,256]{2,1,0:T(8,128)(2,1)S(1)}, bf16[1,80,256]{2,1,0:T(8,128)(2,1)S(1)}, u32[]{:S(2)}, u32[]{:S(2)}) collective-permute-start(bf16[1,80,256]{2,1,0:T(8,128)(2,1)S(1)} %get-tuple-element.37), channel_id=1, source_target_pairs={{0,16},{2,18},{4,20},{6,22},{8,24},{10,26},{12,28},{14,30},{16,0},... | collective-permute-start | bytes 122888 | tf_op jit(solution)/shard_map/ppermute | solution.py:539
  18.5 5.5 %collective-permute-start.2 = (bf16[1,80,256]{2,1,0:T(8,128)(2,1)S(1)}, bf16[1,80,256]{2,1,0:T(8,128)(2,1)S(1)}, u32[]{:S(2)}, u32[]{:S(2)}) collective-permute-start(bf16[1,80,256]{2,1,0:T(8,128)(2,1)S(1)} %get-tuple-element.37), channel_id=1, source_target_pairs={{0,8},{2,10},{4,12},{6,14},{8,0},{10,2},{12,4},{14,6},{16,24},{18,... | collective-permute-start | bytes 122888 | tf_op jit(solution)/shard_map/ppermute | solution.py:539
  24.3 7.3 %collective-permute-start.7 = (bf16[4,80,256]{2,1,0:T(8,128)(2,1)S(1)}, bf16[4,80,256]{2,1,0:T(8,128)(2,1)S(1)}, u32[]{:S(2)}, u32[]{:S(2)}) collective-permute-start(bf16[4,80,256]{2,1,0:T(8,128)(2,1)S(1)} %constant_dynamic-update-slice_fusion.refs_1_), channel_id=1, source_target_pairs={{0,6},{2,4},{4,2},{6,0},{8,14},{10,12},{12,10},{14,8},{16,22},{18,... | collective-permute-start | bytes 491528 | tf_op jit(solution)/shard_map/ppermute | solution.py:539
  26.8 7.6 %collective-permute-start.6 = (bf16[4,80,256]{2,1,0:T(8,128)(2,1)S(1)}, bf16[4,80,256]{2,1,0:T(8,128)(2,1)S(1)}, u32[]{:S(2)}, u32[]{:S(2)}) collective-permute-start(bf16[4,80,256]{2,1,0:T(8,128)(2,1)S(1)} %constant_dynamic-update-slice_fusion.refs_1_), channel_id=1, source_target_pairs={{0,4},{2,6},{4,0},{6,2},{8,12},{10,14},{12,8},{14,10},{16,20},{18,... | collective-permute-start | bytes 491528 | tf_op jit(solution)/shard_map/ppermute | solution.py:539
  26.8 7.6 %collective-permute-start.5 = (bf16[4,80,256]{2,1,0:T(8,128)(2,1)S(1)}, bf16[4,80,256]{2,1,0:T(8,128)(2,1)S(1)}, u32[]{:S(2)}, u32[]{:S(2)}) collective-permute-start(bf16[4,80,256]{2,1,0:T(8,128)(2,1)S(1)} %constant_dynamic-update-slice_fusion.refs_1_), channel_id=1, source_target_pairs={{0,2},{2,0},{4,6},{6,4},{8,10},{10,8},{12,14},{14,12},{16,18},{18,... | collective-permute-start | bytes 491528 | tf_op jit(solution)/shard_map/ppermute | solution.py:539
  41.3 4.2 %collective-permute-start.8 = (f32[3,16,256]{2,1,0:T(8,128)S(1)}, f32[3,16,256]{2,1,0:T(8,128)S(1)}, u32[]{:S(2)}, u32[]{:S(2)}) collective-permute-start(f32[3,16,256]{2,1,0:T(8,128)S(1)} %get-tuple-element.43), channel_id=1, source_target_pairs={{0,2},{2,0},{4,6},{6,4},{8,10},{10,8},{12,14},{14,12},{16,18},{18,... | collective-permute-start | bytes 147464 | tf_op jit(solution)/shard_map/ppermute | solution.py:539
  50.2 4.3 %collective-permute-start.9 = (bf16[64,256]{1,0:T(8,128)(2,1)S(1)}, bf16[64,256]{1,0:T(8,128)(2,1)S(1)}, u32[]{:S(2)}, u32[]{:S(2)}) collective-permute-start(bf16[64,256]{1,0:T(8,128)(2,1)S(1)} %get-tuple-element.48), channel_id=1, source_target_pairs={{0,2},{2,0},{4,6},{6,4},{8,10},{10,8},{12,14},{14,12},{16,18},{18,... | collective-permute-start | bytes 98312 | tf_op jit(solution)/shard_map/ppermute | solution.py:539
  55.6 5.7 %collective-permute-start.12 = (f32[216,128]{1,0:T(8,128)S(1)}, f32[216,128]{1,0:T(8,128)S(1)}, u32[]{:S(2)}, u32[]{:S(2)}) collective-permute-start(f32[216,128]{1,0:T(8,128)S(1)} %weights.1), channel_id=1, source_target_pairs={{0,6},{2,4},{4,2},{6,0},{8,14},{10,12},{12,10},{14,8},{16,22},{18,... | collective-permute-start | bytes 331784 | tf_op jit(solution)/shard_map/ppermute | solution.py:539
  57.4 5.1 %collective-permute-start.11 = (f32[216,128]{1,0:T(8,128)S(1)}, f32[216,128]{1,0:T(8,128)S(1)}, u32[]{:S(2)}, u32[]{:S(2)}) collective-permute-start(f32[216,128]{1,0:T(8,128)S(1)} %weights.1), channel_id=1, source_target_pairs={{0,4},{2,6},{4,0},{6,2},{8,12},{10,14},{12,8},{14,10},{16,20},{18,... | collective-permute-start | bytes 331784 | tf_op jit(solution)/shard_map/ppermute | solution.py:539
  57.4 5.1 %collective-permute-start.10 = (f32[216,128]{1,0:T(8,128)S(1)}, f32[216,128]{1,0:T(8,128)S(1)}, u32[]{:S(2)}, u32[]{:S(2)}) collective-permute-start(f32[216,128]{1,0:T(8,128)S(1)} %weights.1), channel_id=1, source_target_pairs={{0,2},{2,0},{4,6},{6,4},{8,10},{10,8},{12,14},{14,12},{16,18},{18,... | collective-permute-start | bytes 331784 | tf_op jit(solution)/shard_map/ppermute | solution.py:539
  62.5 6.7 %collective-permute-start.15 = (f32[216,128]{1,0:T(8,128)S(1)}, f32[216,128]{1,0:T(8,128)S(1)}, u32[]{:S(2)}, u32[]{:S(2)}) collective-permute-start(f32[216,128]{1,0:T(8,128)S(1)} %add_add_fusion.refs_0_), channel_id=1, source_target_pairs={{0,24},{2,26},{4,28},{6,30},{8,16},{10,18},{12,20},{14,22},{16,8},... | collective-permute-start | bytes 331784 | tf_op jit(solution)/shard_map/ppermute | solution.py:539
  65.0 6.5 %collective-permute-start.14 = (f32[216,128]{1,0:T(8,128)S(1)}, f32[216,128]{1,0:T(8,128)S(1)}, u32[]{:S(2)}, u32[]{:S(2)}) collective-permute-start(f32[216,128]{1,0:T(8,128)S(1)} %add_add_fusion.refs_0_), channel_id=1, source_target_pairs={{0,16},{2,18},{4,20},{6,22},{8,24},{10,26},{12,28},{14,30},{16,0},... | collective-permute-start | bytes 331784 | tf_op jit(solution)/shard_map/ppermute | solution.py:539
  65.0 6.5 %collective-permute-start.13 = (f32[216,128]{1,0:T(8,128)S(1)}, f32[216,128]{1,0:T(8,128)S(1)}, u32[]{:S(2)}, u32[]{:S(2)}) collective-permute-start(f32[216,128]{1,0:T(8,128)S(1)} %add_add_fusion.refs_0_), channel_id=1, source_target_pairs={{0,8},{2,10},{4,12},{6,14},{8,0},{10,2},{12,4},{14,6},{16,24},{18,... | collective-permute-start | bytes 331784 | tf_op jit(solution)/shard_map/ppermute | solution.py:539

commit v7 on v6

--- a/solution.py
+++ b/solution.py
@@ -387,11 +387,35 @@
                 force_refs[m][a, d ^ m : (d ^ m) + 1, :] = row
 
 
+def field_kernel(*refs, group, blocks, early, count):
+    weights_ref, refs = refs[0], refs[1:]
+    early_refs, waves_ref, field_refs = refs[: len(early)], refs[len(early)], refs[len(early) + 1 :]
+    late = [r for r in range(blocks) if r not in early]
+    waves_of = placed_waves(early, early_refs, late, waves_ref, count)
+    weights = weights_ref[...]
+    weights_high = weights.astype(bf16)
+    weights_low = (weights - weights_high.astype(f32)).astype(bf16)
+    for m in range(group):
+        block = waves_of[m][...]
+        field_refs[m][...] = matmul(weights_high, block) + matmul(weights_low, block)
+
+
+def charge_gradient(errors, field, back, block):
+    charge_count = back.shape[0]
+    high = back.astype(bf16)
+    low = (back - high.astype(f32)).astype(bf16)
+    grad = matmul(high, block) + matmul(low, block)
+    for a in range(3):
+        grad = grad + errors[a] * field[a * charge_count : (a + 1) * charge_count, :]
+    return grad
+
+
 def gradient_kernel(where_ref, *refs, group, blocks, early, charge_count, box_x):
     shared_refs, part_refs = refs[:blocks], refs[blocks : blocks + group]
     refs = refs[blocks + group :]
     early_refs, refs = refs[: len(early)], refs[len(early) :]
-    wave_ref, waves_ref, weights_ref, forces_ref, *grad_refs, total_ref = refs
+    field_refs, refs = refs[: group - 1], refs[group - 1 :]
+    wave_ref, waves_ref, forces_ref, errors_ref, back_ref, *grad_refs, total_ref = refs
     late = [r for r in range(blocks) if r not in early]
     count, _, atoms = shared_refs[0].shape
     share = waves_ref.shape[1] // 2
@@ -411,35 +435,36 @@
         target = target[9:12, :] + target[12:15, :]
         return [2.0 * (total_ref[a, d : d + 1, :] - target[a : a + 1, :]) for a in range(3)]
 
-    summed = jnp.zeros((3 * charge_count, 2 * share), f32)
+    by_wave = jnp.zeros((3 * charge_count, 2 * share), f32)
     for d in range(blocks * count):
         j, r = divmod(d, blocks)
         charges = shared_refs[r][j, 0:charge_count, :].astype(f32)
         errors = errors_of(d)
         scaled = jnp.concatenate([errors[a] * charges for a in range(3)], axis=0).astype(bf16)
-        summed = summed + matmul_nt(scaled, waves_of[d][...])
+        by_wave = by_wave + matmul_nt(scaled, waves_of[d][...])
+        if d == 0:
+            errors_ref[...] = jnp.concatenate(errors + [jnp.zeros((5, atoms), f32)], axis=0)
 
     def along(value):
         return sum(
             waves[a] * value[a * charge_count : (a + 1) * charge_count, :] for a in range(3)
         )
 
-    back_cos = damping * along(summed[:, :share])
-    back_sin = -damping * along(summed[:, share:])
+    back_cos = damping * along(by_wave[:, :share])
+    back_sin = -damping * along(by_wave[:, share:])
     back = jnp.concatenate([back_sin, back_cos], axis=1)
-    back_high = back.astype(bf16)
-    back_low = (back - back_high.astype(f32)).astype(bf16)
-    weights = weights_ref[...]
-    weights_high = weights.astype(bf16)
-    weights_low = (weights - weights_high.astype(f32)).astype(bf16)
-    for m in range(group):
-        errors = errors_of(m)
-        block = waves_of[m][...]
-        grad = matmul(back_high, block) + matmul(back_low, block)
-        field = matmul(weights_high, block) + matmul(weights_low, block)
-        for a in range(3):
-            grad = grad + errors[a] * field[a * charge_count : (a + 1) * charge_count, :]
-        grad_refs[m][...] = grad.astype(grad_refs[m].dtype)
+    back_ref[...] = back
+    for m in range(1, group):
+        grad_refs[m - 1][...] = charge_gradient(
+            errors_of(m), field_refs[m - 1][...], back, waves_of[m][...]
+        ).astype(bf16)
+
+
+def own_gradient_kernel(errors_ref, field_ref, back_ref, waves_ref, grad_ref):
+    errors = errors_ref[...]
+    grad_ref[...] = charge_gradient(
+        [errors[a : a + 1, :] for a in range(3)], field_ref[...], back_ref[...], waves_ref[0]
+    )
 
 
 def weights_kernel(*refs, group, kinds):
@@ -495,7 +520,7 @@
     basis_count, width = radial_ref.shape
     charge_count = charge_ref.shape[0]
     kinds = species_ref.shape[0]
-    total_ref[...] = summed([ref[...] for ref in total_refs])
+    total_ref[...] = summed([ref[...].astype(f32) for ref in total_refs])
 
     def normalized(gradient):
         mean = jnp.sum(gradient * gradient, keepdims=True) * (1.0 / gradient.size)
@@ -698,26 +723,54 @@
         scalars=(where,),
     )
     force_parts = force_parts[:1] + [across(force_parts[m], m) for m in range(1, group)]
-    forces, *grad_parts = kernel(
+    fields = kernel(
+        lambda *refs: field_kernel(
+            *refs, group=group, blocks=blocks, early=early, count=domains // blocks
+        ),
+        "fields",
+        (shaped(3 * charge_count, atoms),) * group,
+        (),
+        2_000,
+        weights,
+        *waves_early,
+        waves,
+    )
+    forces, errors, back, *grad_parts = kernel(
         lambda *refs: gradient_kernel(
             *refs, group=group, blocks=blocks, early=early, charge_count=charge_count, box_x=box_x
         ),
         "gradient",
-        (shaped(3, atoms),) + (shaped(charge_count, atoms, kind=bf16),) * group,
+        (
+            shaped(3, atoms),
+            shaped(8, atoms),
+            shaped(charge_count, 2 * share),
+        )
+        + (shaped(charge_count, atoms, kind=bf16),) * (group - 1),
         (shaped(3, domains, atoms),),
         5_000,
         *columns,
         *force_parts,
         *waves_early,
+        *fields[1:],
         wave_index,
         waves,
-        weights,
         scalars=(where,),
     )
-    grad_parts = grad_parts[:1] + [across(grad_parts[m], m) for m in range(1, group)]
+    own_part = kernel(
+        own_gradient_kernel,
+        "own_gradient",
+        shaped(charge_count, atoms),
+        (),
+        1_500,
+        errors,
+        fields[0],
+        back,
+        waves_early[0],
+    )
+    grad_parts = [own_part] + [across(grad_parts[m - 1], m) for m in range(1, group)]
 
     rows = basis_count + width + charge_count + kinds
-    rows = -(-rows // 8) * 8
+    rows = -(-rows // 16) * 16
     packed = kernel(
         lambda *refs: weights_kernel(*refs, group=group, kinds=kinds),
         "weights",
@@ -733,7 +786,7 @@
         mix_weight,
         charge_rows,
     )
-    packed = summed([packed] + [across(packed, r) for r in range(1, blocks)])
+    packed = summed([packed] + [across(packed, r) for r in range(1, blocks)]).astype(bf16)
     totals = [packed] + [across(packed, bits) for bits in range(blocks, domains, blocks)]
     radial_step, mix_step, charge_step, species_step = kernel(
         step_kernel,

time: 72.5 us -> 70.8 us (0.977)
  waiting for transfers between devices: 18.9 us -> 16.7 us
    ppermute x15, waiting for transfers between devices: 18.9 us -> 16.7 us  [across(): return lax.ppermute(value, 'dom', [(i, i ^ bits) for i in range(domains)])]
    pallas_call x10 -> x12, Pallas kernels: 28.3 us -> 28.8 us  [kernel(): pl.pallas_call(body, out_shape=out_shape, in_specs=[in_smem] * len(scalar...]
  transfers between devices with their start and end apart: 16 -> 16, of which waited for: 9 -> 9; matrix products, arithmetic and copies ran while one was open for 0% -> 0% of each run, Pallas kernels for 14% -> 15%
where the time goes in v7:
time: 70.8 us; the launch traced here: 70.6 us
  Pallas kernels  28.8 us (41%)
  starting transfers between devices  24.1 us (34%)
  waiting for transfers between devices  16.7 us (24%)
  between operations  0.87 us (1%)
    pallas_call x12, Pallas kernels, kernel(): pl.pallas_call(body, out_shape=out_shape, in_specs=[in_smem] * len(scalar...  28.8 us
    ppermute x15, starting transfers between devices, across(): return lax.ppermute(value, 'dom', [(i, i ^ bits) for i in range(domains)])  19.5 us
    ppermute x15, waiting for transfers between devices, across(): return lax.ppermute(value, 'dom', [(i, i ^ bits) for i in range(domains)])  16.7 us
    ppermute x1, starting transfers between devices, on_device(): far = lax.ppermute(packed, 'dom', beyond)  4.53 us
  transfers between devices with their start and end apart: 16, of which 9 were waited for; matrix products, arithmetic and copies ran while one was open for 0% of the time, Pallas kernels for 15%

profile of v7, /device:TPU:0, one launch (start us, length us, event | category | flops | bytes accessed | tf_op | source)
XLA Modules:
  0.0 70.6 jit_solution(16533684425236811441)
XLA Ops:
  0.7 1.6 %pack.1 = bf16[288,128]{1,0:T(8,128)(2,1)} custom-call(bf16[256,128]{1,0:T(8,128)(2,1)} %refs_0_.1, f32[3,256]{1,0:T(4,128)} %refs_1_.1, s32[2,256]{1,0:T(2,128)} %ghost_ref.1), custom_call_target="tpu_custom_call" | custom-call | flops 1000000000 | bytes 144384 | tf_op jit(solution)/shard_map/pack/pallas_call | solution.py:548
  2.3 2.9 %collective-permute-start.1 = (bf16[288,128]{1,0:T(8,128)(2,1)}, bf16[288,128]{1,0:T(8,128)(2,1)S(1)}, u32[]{:S(2)}, u32[]{:S(2)}) collective-permute-start(bf16[288,128]{1,0:T(8,128)(2,1)} %pack.1), channel_id=1, source_target_pairs={{0,2},{2,0},{4,6},{6,4},{8,10},{10,8},{12,14},{14,12},{16,18},{18,... | collective-permute-start | bytes 221192 | tf_op jit(solution)/shard_map/ppermute | solution.py:564
  5.3 4.5 %collective-permute-start = (bf16[288,128]{1,0:T(8,128)(2,1)}, bf16[288,128]{1,0:T(8,128)(2,1)S(1)}, u32[]{:S(2)}, u32[]{:S(2)}) collective-permute-start(bf16[288,128]{1,0:T(8,128)(2,1)} %pack.1), channel_id=1, source_target_pairs={{0,30},{2,4},{4,2},{6,8},{8,6},{10,12},{12,10},{14,16},{16,14},{18... | collective-permute-start | bytes 221192 | tf_op jit(solution)/shard_map/ppermute | solution.py:614
  9.9 1.9 %own.1 = (f32[16,128,256]{2,1,0:T(8,128)S(1)}, s32[24,256]{1,0:T(8,128)S(1)}, bf16[128,256]{1,0:T(8,128)(2,1)S(1)}, f32[64,256]{1,0:T(8,128)S(1)}, f32[320,128]{1,0:T(8,128)S(1)}, /*index=5*/f32[24,256]{1,0:T(8,128)S(1)}) custom-call(bf16[256,128]{1,0:T(8,128)(2,1)S(1)} %copy-done, f32[3,256]{1,0:T(4,128)S(1)} %copy-done.5, f32[3,256]{1,0:T(4,128)S(1)} %copy-done.6, ...), custom_call_target="tpu_custom_call" | custom-call | flops 4000000000 | bytes 4740608 | tf_op jit(solution)/shard_map/own/pallas_call | solution.py:548
  11.9 2.5 %near.1.refs_2_ = f32[16,128,256]{2,1,0:T(8,128)S(1)} custom-call(s32[3]{0:T(128)S(1)} %pad_add_fusion.refs_0_, bf16[288,128]{1,0:T(8,128)(2,1)S(1)} %collective-permute-done.1.refs_1_, f32[16,128,256]{2,1,0:T(8,128)S(1)} %get-tuple-element.34.refs_2_, s32[24,256]{1,0:T(8,128)S(1)} %get-tuple-element.35.refs_3_, f32[24,256]{1,0:T(8,128)S(1)} %get-tuple-element.36.refs_4_.refs_7_), custom_call_target="tpu_custom_call" | custom-call | flops 3000000000 | bytes 6430720 | tf_op jit(solution)/shard_map/near/pallas_call | solution.py:548
  14.4 3.2 %edges.1 = (f32[16,128,256]{2,1,0:T(8,128)S(1)}, f32[128,256]{1,0:T(8,128)S(1)}, f32[128,256]{1,0:T(8,128)S(1)}, bf16[128,256]{1,0:T(8,128)(2,1)S(1)}, bf16[1,80,256]{2,1,0:T(8,128)(2,1)S(1)}) custom-call(s32[3]{0:T(128)S(1)} %pad_add_fusion.refs_0_, bf16[288,128]{1,0:T(8,128)(2,1)S(1)} %collective-permute-done.refs_1_, f32[16,128,256]{2,1,0:T(8,128)S(1)} %near.1.refs_2_, ...), custom_call_target="tpu_custom_call" | custom-call | flops 4000000000 | bytes 7094272 | tf_op jit(solution)/shard_map/edges/pallas_call | solution.py:548
  17.6 0.9 %collective-permute-start.4 = (bf16[1,80,256]{2,1,0:T(8,128)(2,1)S(1)}, bf16[1,80,256]{2,1,0:T(8,128)(2,1)S(1)}, u32[]{:S(2)}, u32[]{:S(2)}) collective-permute-start(bf16[1,80,256]{2,1,0:T(8,128)(2,1)S(1)} %get-tuple-element.40), channel_id=1, source_target_pairs={{0,24},{2,26},{4,28},{6,30},{8,16},{10,18},{12,20},{14,22},{16,8},... | collective-permute-start | bytes 122888 | tf_op jit(solution)/shard_map/ppermute | solution.py:564
  18.5 3.6 %collective-permute-start.2 = (bf16[1,80,256]{2,1,0:T(8,128)(2,1)S(1)}, bf16[1,80,256]{2,1,0:T(8,128)(2,1)S(1)}, u32[]{:S(2)}, u32[]{:S(2)}) collective-permute-start(bf16[1,80,256]{2,1,0:T(8,128)(2,1)S(1)} %get-tuple-element.40), channel_id=1, source_target_pairs={{0,8},{2,10},{4,12},{6,14},{8,0},{10,2},{12,4},{14,6},{16,24},{18,... | collective-permute-start | bytes 122888 | tf_op jit(solution)/shard_map/ppermute | solution.py:564
  22.1 2.0 %collective-permute-done.2 = bf16[1,80,256]{2,1,0:T(8,128)(2,1)S(1)} collective-permute-done((bf16[1,80,256]{2,1,0:T(8,128)(2,1)S(1)}, bf16[1,80,256]{2,1,0:T(8,128)(2,1)S(1)}, u32[]{:S(2)}, u32[]{:S(2)}) %collective-permute-start.2) | collective-permute-done | bytes 40992 | tf_op jit(solution)/shard_map/ppermute | solution.py:564
  24.3 2.4 %collective-permute-start.7 = (bf16[4,80,256]{2,1,0:T(8,128)(2,1)S(1)}, bf16[4,80,256]{2,1,0:T(8,128)(2,1)S(1)}, u32[]{:S(2)}, u32[]{:S(2)}) collective-permute-start(bf16[4,80,256]{2,1,0:T(8,128)(2,1)S(1)} %constant_dynamic-update-slice_fusion.refs_1_), channel_id=1, source_target_pairs={{0,6},{2,4},{4,2},{6,0},{8,14},{10,12},{12,10},{14,8},{16,22},{18,... | collective-permute-start | bytes 491528 | tf_op jit(solution)/shard_map/ppermute | solution.py:564
  26.8 1.1 %collective-permute-start.5 = (bf16[4,80,256]{2,1,0:T(8,128)(2,1)S(1)}, bf16[4,80,256]{2,1,0:T(8,128)(2,1)S(1)}, u32[]{:S(2)}, u32[]{:S(2)}) collective-permute-start(bf16[4,80,256]{2,1,0:T(8,128)(2,1)S(1)} %constant_dynamic-update-slice_fusion.refs_1_), channel_id=1, source_target_pairs={{0,2},{2,0},{4,6},{6,4},{8,10},{10,8},{12,14},{14,12},{16,18},{18,... | collective-permute-start | bytes 491528 | tf_op jit(solution)/shard_map/ppermute | solution.py:564
  27.9 2.8 %phases.2 = (bf16[4,1024,256]{2,1,0:T(8,128)(2,1)S(1)}, f32[64,1024]{1,0:T(8,128)S(1)}) custom-call(s32[3]{0:T(128)S(1)} %pad_add_fusion.refs_0_, bf16[4,80,256]{2,1,0:T(8,128)(2,1)S(1)} %constant_dynamic-update-slice_fusion.refs_1_, s32[3,1024]{1,0:T(4,128)S(1)} %copy-done.3), custom_call_target="tpu_custom_call" | custom-call | flops 3000000000 | bytes 2535424 | tf_op jit(solution)/shard_map/phases/pallas_call | solution.py:548
  30.7 1.0 %collective-permute-done.7.refs_1_.refs_4_ = bf16[4,80,256]{2,1,0:T(8,128)(2,1)S(1)} collective-permute-done((bf16[4,80,256]{2,1,0:T(8,128)(2,1)S(1)}, bf16[4,80,256]{2,1,0:T(8,128)(2,1)S(1)}, u32[]{:S(2)}, u32[]{:S(2)}) %collective-permute-start.7) | collective-permute-done | bytes 163872 | tf_op jit(solution)/shard_map/ppermute | solution.py:564
  31.6 2.8 %phases.3 = (bf16[4,1024,256]{2,1,0:T(8,128)(2,1)S(1)}, f32[64,1024]{1,0:T(8,128)S(1)}) custom-call(s32[3]{0:T(128)S(1)} %pad_add_fusion.refs_0_, bf16[4,80,256]{2,1,0:T(8,128)(2,1)S(1)} %collective-permute-done.7.refs_1_.refs_4_, s32[3,1024]{1,0:T(4,128)S(1)} %copy-done.3), custom_call_target="tpu_custom_call" | custom-call | flops 3000000000 | bytes 2535424 | tf_op jit(solution)/shard_map/phases/pallas_call | solution.py:548
  34.4 6.9 %structure.1 = (bf16[8,1024,256]{2,1,0:T(8,128)(2,1)S(1)}, f32[192,1024]{1,0:T(8,128)S(1)}, f32[3,16,256]{2,1,0:T(8,128)S(1)}, f32[3,16,256]{2,1,0:T(8,128)S(1)}) custom-call(s32[3]{0:T(128)S(1)} %pad_add_fusion.refs_0_, bf16[4,80,256]{2,1,0:T(8,128)(2,1)S(1)} %constant_dynamic-update-slice_fusion.refs_1_, ...), custom_call_target="tpu_custom_call" | custom-call | flops 8000000000 | bytes 10465280 | tf_op jit(solution)/shard_map/structure/pallas_call | solution.py:548
  41.3 0.3 collective-permute-start.8
  41.6 0.6 fields.1
  42.2 3.2 %collective-permute-done.8.refs_6_ = f32[3,16,256]{2,1,0:T(8,128)S(1)} collective-permute-done((f32[3,16,256]{2,1,0:T(8,128)S(1)}, f32[3,16,256]{2,1,0:T(8,128)S(1)}, u32[]{:S(2)}, u32[]{:S(2)}) %collective-permute-start.8) | collective-permute-done | bytes 49184 | tf_op jit(solution)/shard_map/ppermute | solution.py:564
  45.4 4.4 %gradient.1 = (f32[3,256]{1,0:T(4,128)}, f32[8,256]{1,0:T(8,128)S(1)}, f32[64,1024]{1,0:T(8,128)S(1)}, bf16[64,256]{1,0:T(8,128)(2,1)S(1)}) custom-call(s32[3]{0:T(128)S(1)} %pad_add_fusion.refs_0_, bf16[4,80,256]{2,1,0:T(8,128)(2,1)S(1)} %constant_dynamic-update-slice_fusion.refs_1_, bf16[4,80,256]{2,1,0:T(8,128)(2,1)S(1)} %collective-permute-done.5.refs_2_, ...), custom_call_target="tpu_custom_call" | custom-call | flops 5000000000 | bytes 9706496 | tf_op jit(solution)/shard_map/gradient/pallas_call | solution.py:548
  49.8 0.3 collective-permute-start.9
  50.1 0.3 own_gradient.1.refs_0_
  50.4 3.7 %collective-permute-done.9.refs_1_ = bf16[64,256]{1,0:T(8,128)(2,1)S(1)} collective-permute-done((bf16[64,256]{1,0:T(8,128)(2,1)S(1)}, bf16[64,256]{1,0:T(8,128)(2,1)S(1)}, u32[]{:S(2)}, u32[]{:S(2)}) %collective-permute-start.9) | collective-permute-done | bytes 32800 | tf_op jit(solution)/shard_map/ppermute | solution.py:564
  54.1 1.1 %weights.1 = f32[224,128]{1,0:T(8,128)S(1)} custom-call(f32[64,256]{1,0:T(8,128)S(1)} %own_gradient.1.refs_0_, bf16[64,256]{1,0:T(8,128)(2,1)S(1)} %collective-permute-done.9.refs_1_, f32[16,128,256]{2,1,0:T(8,128)S(1)} %get-tuple-element.55.refs_2_, f32[128,256]{1,0:T(8,128)S(1)} %get-tuple-element.56.refs_3_, f32[128,256]{1,0:T(8,128)S(1)} %get-tuple-element.57.refs_4_, ...), custom_call_target="tpu_custom_call" | custom-call | flops 3000000000 | bytes 2688000 | tf_op jit(solution)/shard_map/weights/pallas_call | solution.py:548
  55.2 1.8 %collective-permute-start.12 = (f32[224,128]{1,0:T(8,128)S(1)}, f32[224,128]{1,0:T(8,128)S(1)}, u32[]{:S(2)}, u32[]{:S(2)}) collective-permute-start(f32[224,128]{1,0:T(8,128)S(1)} %weights.1), channel_id=1, source_target_pairs={{0,6},{2,4},{4,2},{6,0},{8,14},{10,12},{12,10},{14,8},{16,22},{18,... | collective-permute-start | bytes 344072 | tf_op jit(solution)/shard_map/ppermute | solution.py:564
  57.0 1.7 %collective-permute-start.10 = (f32[224,128]{1,0:T(8,128)S(1)}, f32[224,128]{1,0:T(8,128)S(1)}, u32[]{:S(2)}, u32[]{:S(2)}) collective-permute-start(f32[224,128]{1,0:T(8,128)S(1)} %weights.1), channel_id=1, source_target_pairs={{0,2},{2,0},{4,6},{6,4},{8,10},{10,8},{12,14},{14,12},{16,18},{18,... | collective-permute-start | bytes 344072 | tf_op jit(solution)/shard_map/ppermute | solution.py:564
  58.7 2.2 %collective-permute-done.12 = f32[224,128]{1,0:T(8,128)S(1)} collective-permute-done((f32[224,128]{1,0:T(8,128)S(1)}, f32[224,128]{1,0:T(8,128)S(1)}, u32[]{:S(2)}, u32[]{:S(2)}) %collective-permute-start.12) | collective-permute-done | bytes 114720 | tf_op jit(solution)/shard_map/ppermute | solution.py:564
  60.9 1.2 %collective-permute-done.11 = f32[224,128]{1,0:T(8,128)S(1)} collective-permute-done((f32[224,128]{1,0:T(8,128)S(1)}, f32[224,128]{1,0:T(8,128)S(1)}, u32[]{:S(2)}, u32[]{:S(2)}) %collective-permute-start.11) | collective-permute-done | bytes 114720 | tf_op jit(solution)/shard_map/ppermute | solution.py:564
  62.2 2.5 %collective-permute-start.15 = (bf16[224,128]{1,0:T(8,128)(2,1)S(1)}, bf16[224,128]{1,0:T(8,128)(2,1)S(1)}, u32[]{:S(2)}, u32[]{:S(2)}) collective-permute-start(bf16[224,128]{1,0:T(8,128)(2,1)S(1)} %add_convert_fusion.refs_0_), channel_id=1, source_target_pairs={{0,24},{2,26},{4,28},{6,30},{8,16},{10,18},{12,20},{14,22},{16,8},... | collective-permute-start | bytes 172040 | tf_op jit(solution)/shard_map/ppermute | solution.py:564
  64.7 2.0 %collective-permute-start.13 = (bf16[224,128]{1,0:T(8,128)(2,1)S(1)}, bf16[224,128]{1,0:T(8,128)(2,1)S(1)}, u32[]{:S(2)}, u32[]{:S(2)}) collective-permute-start(bf16[224,128]{1,0:T(8,128)(2,1)S(1)} %add_convert_fusion.refs_0_), channel_id=1, source_target_pairs={{0,8},{2,10},{4,12},{6,14},{8,0},{10,2},{12,4},{14,6},{16,24},{18,... | collective-permute-start | bytes 172040 | tf_op jit(solution)/shard_map/ppermute | solution.py:564
  66.6 1.6 %collective-permute-done.15.refs_3_ = bf16[224,128]{1,0:T(8,128)(2,1)S(1)} collective-permute-done((bf16[224,128]{1,0:T(8,128)(2,1)S(1)}, bf16[224,128]{1,0:T(8,128)(2,1)S(1)}, u32[]{:S(2)}, u32[]{:S(2)}) %collective-permute-start.15) | collective-permute-done | bytes 57376 | tf_op jit(solution)/shard_map/ppermute | solution.py:564
  68.2 1.5 %collective-permute-done.14.refs_2_ = bf16[224,128]{1,0:T(8,128)(2,1)S(1)} collective-permute-done((bf16[224,128]{1,0:T(8,128)(2,1)S(1)}, bf16[224,128]{1,0:T(8,128)(2,1)S(1)}, u32[]{:S(2)}, u32[]{:S(2)}) %collective-permute-start.14) | collective-permute-done | bytes 57376 | tf_op jit(solution)/shard_map/ppermute | solution.py:564
  69.8 0.8 %steps.1 = (f32[16,128]{1,0:T(8,128)}, f32[128,128]{1,0:T(8,128)}, f32[64,128]{1,0:T(8,128)}, f32[6,64]{1,0:T(8,128)}) custom-call(bf16[224,128]{1,0:T(8,128)(2,1)S(1)} %add_convert_fusion.refs_0_, bf16[224,128]{1,0:T(8,128)(2,1)S(1)} %collective-permute-done.13.refs_1_, bf16[224,128]{1,0:T(8,128)(2,1)S(1)} %collective-permute-done.14.refs_2_, ...), custom_call_target="tpu_custom_call" | custom-call | flops 2000000000 | bytes 452096 | tf_op jit(solution)/shard_map/steps/pallas_call | solution.py:548
  (40 shorter events, 0.5 us)
Async XLA Ops:
  0.6 9.2 %copy-start.5 = (f32[3,256]{1,0:T(4,128)S(1)}, f32[3,256]{1,0:T(4,128)}, u32[]{:S(2)}) copy-start(f32[3,256]{1,0:T(4,128)} %refs_1_.1) | copy-start | bytes 9220
  0.6 9.1 %copy-start = (bf16[256,128]{1,0:T(8,128)(2,1)S(1)}, bf16[256,128]{1,0:T(8,128)(2,1)}, u32[]{:S(2)}) copy-start(bf16[256,128]{1,0:T(8,128)(2,1)} %refs_0_.1) | copy-start | bytes 196612
  0.7 9.1 %copy-start.2 = (bf16[128,128]{1,0:T(8,128)(2,1)S(1)}, bf16[128,128]{1,0:T(8,128)(2,1)}, u32[]{:S(2)}) copy-start(bf16[128,128]{1,0:T(8,128)(2,1)} %refs_7_.3) | copy-start | bytes 98308
  0.7 9.1 %copy-start.8 = (f32[6,64]{1,0:T(8,128)S(1)}, f32[6,64]{1,0:T(8,128)}, u32[]{:S(2)}) copy-start(f32[6,64]{1,0:T(8,128)} %refs_9_.2) | copy-start | bytes 4612
  0.7 9.1 %copy-start.4 = (bf16[128,64]{0,1:T(8,128)(2,1)S(1)}, bf16[128,64]{0,1:T(8,128)(2,1)}, u32[]{:S(2)}) copy-start(bf16[128,64]{0,1:T(8,128)(2,1)} %param.22) | copy-start | bytes 49156
  0.7 9.1 %copy-start.7 = (bf16[16,128]{1,0:T(8,128)(2,1)S(1)}, bf16[16,128]{1,0:T(8,128)(2,1)}, u32[]{:S(2)}) copy-start(bf16[16,128]{1,0:T(8,128)(2,1)} %refs_6_.1) | copy-start | bytes 12292
  0.7 9.1 %copy-start.6 = (f32[3,256]{1,0:T(4,128)S(1)}, f32[3,256]{1,0:T(4,128)}, u32[]{:S(2)}) copy-start(f32[3,256]{1,0:T(4,128)} %refs_2_.3) | copy-start | bytes 9220
  0.7 9.1 %copy-start.10 = (s32[256]{0:T(256)S(1)}, s32[256]{0:T(256)}, u32[]{:S(2)}) copy-start(s32[256]{0:T(256)} %param.17) | copy-start | bytes 3076
  0.7 9.1 %copy-start.9 = (s32[256]{0:T(256)S(1)}, s32[256]{0:T(256)}, u32[]{:S(2)}) copy-start(s32[256]{0:T(256)} %param.15) | copy-start | bytes 3076
  0.7 9.1 %copy-start.1 = (s32[256,64]{0,1:T(8,128)S(1)}, s32[256,64]{0,1:T(8,128)}, u32[]{:S(2)}) copy-start(s32[256,64]{0,1:T(8,128)} %param.14) | copy-start | bytes 196612
  2.3 9.5 %collective-permute-start.1 = (bf16[288,128]{1,0:T(8,128)(2,1)}, bf16[288,128]{1,0:T(8,128)(2,1)S(1)}, u32[]{:S(2)}, u32[]{:S(2)}) collective-permute-start(bf16[288,128]{1,0:T(8,128)(2,1)} %pack.1), channel_id=1, source_target_pairs={{0,2},{2,0},{4,6},{6,4},{8,10},{10,8},{12,14},{14,12},{16,18},{18,... | collective-permute-start | bytes 221192 | tf_op jit(solution)/shard_map/ppermute | solution.py:564
  5.3 9.1 %collective-permute-start = (bf16[288,128]{1,0:T(8,128)(2,1)}, bf16[288,128]{1,0:T(8,128)(2,1)S(1)}, u32[]{:S(2)}, u32[]{:S(2)}) collective-permute-start(bf16[288,128]{1,0:T(8,128)(2,1)} %pack.1), channel_id=1, source_target_pairs={{0,30},{2,4},{4,2},{6,8},{8,6},{10,12},{12,10},{14,16},{16,14},{18... | collective-permute-start | bytes 221192 | tf_op jit(solution)/shard_map/ppermute | solution.py:614
  14.4 13.5 %copy-start.3 = (s32[3,1024]{1,0:T(4,128)S(1)}, s32[3,1024]{1,0:T(4,128)}, u32[]{:S(2)}) copy-start(s32[3,1024]{1,0:T(4,128)} %refs_10_.1) | copy-start | bytes 36868
  17.6 6.7 %collective-permute-start.4 = (bf16[1,80,256]{2,1,0:T(8,128)(2,1)S(1)}, bf16[1,80,256]{2,1,0:T(8,128)(2,1)S(1)}, u32[]{:S(2)}, u32[]{:S(2)}) collective-permute-start(bf16[1,80,256]{2,1,0:T(8,128)(2,1)S(1)} %get-tuple-element.40), channel_id=1, source_target_pairs={{0,24},{2,26},{4,28},{6,30},{8,16},{10,18},{12,20},{14,22},{16,8},... | collective-permute-start | bytes 122888 | tf_op jit(solution)/shard_map/ppermute | solution.py:564
  18.5 5.8 %collective-permute-start.3 = (bf16[1,80,256]{2,1,0:T(8,128)(2,1)S(1)}, bf16[1,80,256]{2,1,0:T(8,128)(2,1)S(1)}, u32[]{:S(2)}, u32[]{:S(2)}) collective-permute-start(bf16[1,80,256]{2,1,0:T(8,128)(2,1)S(1)} %get-tuple-element.40), channel_id=1, source_target_pairs={{0,16},{2,18},{4,20},{6,22},{8,24},{10,26},{12,28},{14,30},{16,0},... | collective-permute-start | bytes 122888 | tf_op jit(solution)/shard_map/ppermute | solution.py:564
  18.5 5.6 %collective-permute-start.2 = (bf16[1,80,256]{2,1,0:T(8,128)(2,1)S(1)}, bf16[1,80,256]{2,1,0:T(8,128)(2,1)S(1)}, u32[]{:S(2)}, u32[]{:S(2)}) collective-permute-start(bf16[1,80,256]{2,1,0:T(8,128)(2,1)S(1)} %get-tuple-element.40), channel_id=1, source_target_pairs={{0,8},{2,10},{4,12},{6,14},{8,0},{10,2},{12,4},{14,6},{16,24},{18,... | collective-permute-start | bytes 122888 | tf_op jit(solution)/shard_map/ppermute | solution.py:564
  24.3 7.3 %collective-permute-start.7 = (bf16[4,80,256]{2,1,0:T(8,128)(2,1)S(1)}, bf16[4,80,256]{2,1,0:T(8,128)(2,1)S(1)}, u32[]{:S(2)}, u32[]{:S(2)}) collective-permute-start(bf16[4,80,256]{2,1,0:T(8,128)(2,1)S(1)} %constant_dynamic-update-slice_fusion.refs_1_), channel_id=1, source_target_pairs={{0,6},{2,4},{4,2},{6,0},{8,14},{10,12},{12,10},{14,8},{16,22},{18,... | collective-permute-start | bytes 491528 | tf_op jit(solution)/shard_map/ppermute | solution.py:564
  26.8 7.6 %collective-permute-start.6 = (bf16[4,80,256]{2,1,0:T(8,128)(2,1)S(1)}, bf16[4,80,256]{2,1,0:T(8,128)(2,1)S(1)}, u32[]{:S(2)}, u32[]{:S(2)}) collective-permute-start(bf16[4,80,256]{2,1,0:T(8,128)(2,1)S(1)} %constant_dynamic-update-slice_fusion.refs_1_), channel_id=1, source_target_pairs={{0,4},{2,6},{4,0},{6,2},{8,12},{10,14},{12,8},{14,10},{16,20},{18,... | collective-permute-start | bytes 491528 | tf_op jit(solution)/shard_map/ppermute | solution.py:564
  26.8 7.6 %collective-permute-start.5 = (bf16[4,80,256]{2,1,0:T(8,128)(2,1)S(1)}, bf16[4,80,256]{2,1,0:T(8,128)(2,1)S(1)}, u32[]{:S(2)}, u32[]{:S(2)}) collective-permute-start(bf16[4,80,256]{2,1,0:T(8,128)(2,1)S(1)} %constant_dynamic-update-slice_fusion.refs_1_), channel_id=1, source_target_pairs={{0,2},{2,0},{4,6},{6,4},{8,10},{10,8},{12,14},{14,12},{16,18},{18,... | collective-permute-start | bytes 491528 | tf_op jit(solution)/shard_map/ppermute | solution.py:564
  41.3 4.2 %collective-permute-start.8 = (f32[3,16,256]{2,1,0:T(8,128)S(1)}, f32[3,16,256]{2,1,0:T(8,128)S(1)}, u32[]{:S(2)}, u32[]{:S(2)}) collective-permute-start(f32[3,16,256]{2,1,0:T(8,128)S(1)} %get-tuple-element.46), channel_id=1, source_target_pairs={{0,2},{2,0},{4,6},{6,4},{8,10},{10,8},{12,14},{14,12},{16,18},{18,... | collective-permute-start | bytes 147464 | tf_op jit(solution)/shard_map/ppermute | solution.py:564
  49.8 4.3 %collective-permute-start.9 = (bf16[64,256]{1,0:T(8,128)(2,1)S(1)}, bf16[64,256]{1,0:T(8,128)(2,1)S(1)}, u32[]{:S(2)}, u32[]{:S(2)}) collective-permute-start(bf16[64,256]{1,0:T(8,128)(2,1)S(1)} %get-tuple-element.54), channel_id=1, source_target_pairs={{0,2},{2,0},{4,6},{6,4},{8,10},{10,8},{12,14},{14,12},{16,18},{18,... | collective-permute-start | bytes 98312 | tf_op jit(solution)/shard_map/ppermute | solution.py:564
  55.2 5.8 %collective-permute-start.12 = (f32[224,128]{1,0:T(8,128)S(1)}, f32[224,128]{1,0:T(8,128)S(1)}, u32[]{:S(2)}, u32[]{:S(2)}) collective-permute-start(f32[224,128]{1,0:T(8,128)S(1)} %weights.1), channel_id=1, source_target_pairs={{0,6},{2,4},{4,2},{6,0},{8,14},{10,12},{12,10},{14,8},{16,22},{18,... | collective-permute-start | bytes 344072 | tf_op jit(solution)/shard_map/ppermute | solution.py:564
  57.0 5.1 %collective-permute-start.11 = (f32[224,128]{1,0:T(8,128)S(1)}, f32[224,128]{1,0:T(8,128)S(1)}, u32[]{:S(2)}, u32[]{:S(2)}) collective-permute-start(f32[224,128]{1,0:T(8,128)S(1)} %weights.1), channel_id=1, source_target_pairs={{0,4},{2,6},{4,0},{6,2},{8,12},{10,14},{12,8},{14,10},{16,20},{18,... | collective-permute-start | bytes 344072 | tf_op jit(solution)/shard_map/ppermute | solution.py:564
  57.0 5.1 %collective-permute-start.10 = (f32[224,128]{1,0:T(8,128)S(1)}, f32[224,128]{1,0:T(8,128)S(1)}, u32[]{:S(2)}, u32[]{:S(2)}) collective-permute-start(f32[224,128]{1,0:T(8,128)S(1)} %weights.1), channel_id=1, source_target_pairs={{0,2},{2,0},{4,6},{6,4},{8,10},{10,8},{12,14},{14,12},{16,18},{18,... | collective-permute-start | bytes 344072 | tf_op jit(solution)/shard_map/ppermute | solution.py:564
  62.2 6.0 %collective-permute-start.15 = (bf16[224,128]{1,0:T(8,128)(2,1)S(1)}, bf16[224,128]{1,0:T(8,128)(2,1)S(1)}, u32[]{:S(2)}, u32[]{:S(2)}) collective-permute-start(bf16[224,128]{1,0:T(8,128)(2,1)S(1)} %add_convert_fusion.refs_0_), channel_id=1, source_target_pairs={{0,24},{2,26},{4,28},{6,30},{8,16},{10,18},{12,20},{14,22},{16,8},... | collective-permute-start | bytes 172040 | tf_op jit(solution)/shard_map/ppermute | solution.py:564
  64.7 5.1 %collective-permute-start.14 = (bf16[224,128]{1,0:T(8,128)(2,1)S(1)}, bf16[224,128]{1,0:T(8,128)(2,1)S(1)}, u32[]{:S(2)}, u32[]{:S(2)}) collective-permute-start(bf16[224,128]{1,0:T(8,128)(2,1)S(1)} %add_convert_fusion.refs_0_), channel_id=1, source_target_pairs={{0,16},{2,18},{4,20},{6,22},{8,24},{10,26},{12,28},{14,30},{16,0},... | collective-permute-start | bytes 172040 | tf_op jit(solution)/shard_map/ppermute | solution.py:564
  64.7 5.1 %collective-permute-start.13 = (bf16[224,128]{1,0:T(8,128)(2,1)S(1)}, bf16[224,128]{1,0:T(8,128)(2,1)S(1)}, u32[]{:S(2)}, u32[]{:S(2)}) collective-permute-start(bf16[224,128]{1,0:T(8,128)(2,1)S(1)} %add_convert_fusion.refs_0_), channel_id=1, source_target_pairs={{0,8},{2,10},{4,12},{6,14},{8,0},{10,2},{12,4},{14,6},{16,24},{18,... | collective-permute-start | bytes 172040 | tf_op jit(solution)/shard_map/ppermute | solution.py:564

commit v8 on v7

--- a/solution.py
+++ b/solution.py
@@ -515,12 +515,24 @@
     return values[0]
 
 
+def halves_kernel(*refs, first, count):
+    *value_refs, sum_ref = refs
+    value = summed([ref[...] for ref in value_refs])
+    high = value.astype(bf16)
+    sum_ref[0 : value.shape[0], :] = high
+    rest = value[first : first + count, :] - high[first : first + count, :].astype(f32)
+    sum_ref[value.shape[0] :, :] = rest.astype(bf16)
+
+
 def step_kernel(*refs):
     *total_refs, radial_ref, mix_ref, charge_ref, species_ref, total_ref = refs
     basis_count, width = radial_ref.shape
     charge_count = charge_ref.shape[0]
     kinds = species_ref.shape[0]
-    total_ref[...] = summed([ref[...].astype(f32) for ref in total_refs])
+    total = summed([ref[...].astype(f32) for ref in total_refs])
+    rows = total_ref.shape[0]
+    total_ref[...] = total[0:rows, :]
+    total_ref[basis_count : basis_count + width, :] += total[rows:, :]
 
     def normalized(gradient):
         mean = jnp.sum(gradient * gradient, keepdims=True) * (1.0 / gradient.size)
@@ -786,7 +798,15 @@
         mix_weight,
         charge_rows,
     )
-    packed = summed([packed] + [across(packed, r) for r in range(1, blocks)]).astype(bf16)
+    packed = kernel(
+        lambda *refs: halves_kernel(*refs, first=basis_count, count=width),
+        "halves",
+        shaped(rows + width, width, kind=bf16),
+        (),
+        1_000,
+        packed,
+        *[across(packed, r) for r in range(1, blocks)],
+    )
     totals = [packed] + [across(packed, bits) for bits in range(blocks, domains, blocks)]
     radial_step, mix_step, charge_step, species_step = kernel(
         step_kernel,

time: 70.8 us -> 71.5 us (level)
    ppermute x15, waiting for transfers between devices: 16.7 us -> 17.4 us  [across(): return lax.ppermute(value, 'dom', [(i, i ^ bits) for i in range(domains)])]
    pallas_call x12 -> x13, Pallas kernels: 28.8 us -> 28.9 us  [kernel(): pl.pallas_call(body, out_shape=out_shape, in_specs=[in_smem] * len(scalar...]
where the time goes in v8:
time: 71.5 us; the launch traced here: 71.3 us
  Pallas kernels  28.9 us (40%)
  starting transfers between devices  24.1 us (34%)
  waiting for transfers between devices  17.4 us (24%)
  between operations  0.87 us (1%)
    pallas_call x13, Pallas kernels, kernel(): pl.pallas_call(body, out_shape=out_shape, in_specs=[in_smem] * len(scalar...  28.9 us
    ppermute x15, starting transfers between devices, across(): return lax.ppermute(value, 'dom', [(i, i ^ bits) for i in range(domains)])  19.5 us
    ppermute x15, waiting for transfers between devices, across(): return lax.ppermute(value, 'dom', [(i, i ^ bits) for i in range(domains)])  17.4 us
    ppermute x1, starting transfers between devices, on_device(): far = lax.ppermute(packed, 'dom', beyond)  4.53 us
  transfers between devices with their start and end apart: 16, of which 9 were waited for; matrix products, arithmetic and copies ran while one was open for 0% of the time, Pallas kernels for 15%

profile of v8, /device:TPU:0, one launch (start us, length us, event | category | flops | bytes accessed | tf_op | source)
XLA Modules:
  0.0 71.3 jit_solution(16722571326104828247)
XLA Ops:
  0.7 1.6 %pack.1 = bf16[288,128]{1,0:T(8,128)(2,1)} custom-call(bf16[256,128]{1,0:T(8,128)(2,1)} %refs_0_.1, f32[3,256]{1,0:T(4,128)} %refs_1_.1, s32[2,256]{1,0:T(2,128)} %ghost_ref.1), custom_call_target="tpu_custom_call" | custom-call | flops 1000000000 | bytes 144384 | tf_op jit(solution)/shard_map/pack/pallas_call | solution.py:560
  2.3 2.9 %collective-permute-start.1 = (bf16[288,128]{1,0:T(8,128)(2,1)}, bf16[288,128]{1,0:T(8,128)(2,1)S(1)}, u32[]{:S(2)}, u32[]{:S(2)}) collective-permute-start(bf16[288,128]{1,0:T(8,128)(2,1)} %pack.1), channel_id=1, source_target_pairs={{0,2},{2,0},{4,6},{6,4},{8,10},{10,8},{12,14},{14,12},{16,18},{18,... | collective-permute-start | bytes 221192 | tf_op jit(solution)/shard_map/ppermute | solution.py:576
  5.3 4.5 %collective-permute-start = (bf16[288,128]{1,0:T(8,128)(2,1)}, bf16[288,128]{1,0:T(8,128)(2,1)S(1)}, u32[]{:S(2)}, u32[]{:S(2)}) collective-permute-start(bf16[288,128]{1,0:T(8,128)(2,1)} %pack.1), channel_id=1, source_target_pairs={{0,30},{2,4},{4,2},{6,8},{8,6},{10,12},{12,10},{14,16},{16,14},{18... | collective-permute-start | bytes 221192 | tf_op jit(solution)/shard_map/ppermute | solution.py:626
  9.9 1.9 %own.1 = (f32[16,128,256]{2,1,0:T(8,128)S(1)}, s32[24,256]{1,0:T(8,128)S(1)}, bf16[128,256]{1,0:T(8,128)(2,1)S(1)}, f32[64,256]{1,0:T(8,128)S(1)}, f32[320,128]{1,0:T(8,128)S(1)}, /*index=5*/f32[24,256]{1,0:T(8,128)S(1)}) custom-call(bf16[256,128]{1,0:T(8,128)(2,1)S(1)} %copy-done, f32[3,256]{1,0:T(4,128)S(1)} %copy-done.5, f32[3,256]{1,0:T(4,128)S(1)} %copy-done.6, ...), custom_call_target="tpu_custom_call" | custom-call | flops 4000000000 | bytes 4740608 | tf_op jit(solution)/shard_map/own/pallas_call | solution.py:560
  11.9 2.5 %near.1.refs_2_ = f32[16,128,256]{2,1,0:T(8,128)S(1)} custom-call(s32[3]{0:T(128)S(1)} %pad_add_fusion.refs_0_, bf16[288,128]{1,0:T(8,128)(2,1)S(1)} %collective-permute-done.1.refs_1_, f32[16,128,256]{2,1,0:T(8,128)S(1)} %get-tuple-element.34.refs_2_, s32[24,256]{1,0:T(8,128)S(1)} %get-tuple-element.35.refs_3_, f32[24,256]{1,0:T(8,128)S(1)} %get-tuple-element.36.refs_4_.refs_7_), custom_call_target="tpu_custom_call" | custom-call | flops 3000000000 | bytes 6430720 | tf_op jit(solution)/shard_map/near/pallas_call | solution.py:560
  14.4 3.2 %edges.1 = (f32[16,128,256]{2,1,0:T(8,128)S(1)}, f32[128,256]{1,0:T(8,128)S(1)}, f32[128,256]{1,0:T(8,128)S(1)}, bf16[128,256]{1,0:T(8,128)(2,1)S(1)}, bf16[1,80,256]{2,1,0:T(8,128)(2,1)S(1)}) custom-call(s32[3]{0:T(128)S(1)} %pad_add_fusion.refs_0_, bf16[288,128]{1,0:T(8,128)(2,1)S(1)} %collective-permute-done.refs_1_, f32[16,128,256]{2,1,0:T(8,128)S(1)} %near.1.refs_2_, ...), custom_call_target="tpu_custom_call" | custom-call | flops 4000000000 | bytes 7094272 | tf_op jit(solution)/shard_map/edges/pallas_call | solution.py:560
  17.6 0.9 %collective-permute-start.4 = (bf16[1,80,256]{2,1,0:T(8,128)(2,1)S(1)}, bf16[1,80,256]{2,1,0:T(8,128)(2,1)S(1)}, u32[]{:S(2)}, u32[]{:S(2)}) collective-permute-start(bf16[1,80,256]{2,1,0:T(8,128)(2,1)S(1)} %get-tuple-element.40), channel_id=1, source_target_pairs={{0,24},{2,26},{4,28},{6,30},{8,16},{10,18},{12,20},{14,22},{16,8},... | collective-permute-start | bytes 122888 | tf_op jit(solution)/shard_map/ppermute | solution.py:576
  18.5 3.6 %collective-permute-start.2 = (bf16[1,80,256]{2,1,0:T(8,128)(2,1)S(1)}, bf16[1,80,256]{2,1,0:T(8,128)(2,1)S(1)}, u32[]{:S(2)}, u32[]{:S(2)}) collective-permute-start(bf16[1,80,256]{2,1,0:T(8,128)(2,1)S(1)} %get-tuple-element.40), channel_id=1, source_target_pairs={{0,8},{2,10},{4,12},{6,14},{8,0},{10,2},{12,4},{14,6},{16,24},{18,... | collective-permute-start | bytes 122888 | tf_op jit(solution)/shard_map/ppermute | solution.py:576
  22.1 2.0 %collective-permute-done.2 = bf16[1,80,256]{2,1,0:T(8,128)(2,1)S(1)} collective-permute-done((bf16[1,80,256]{2,1,0:T(8,128)(2,1)S(1)}, bf16[1,80,256]{2,1,0:T(8,128)(2,1)S(1)}, u32[]{:S(2)}, u32[]{:S(2)}) %collective-permute-start.2) | collective-permute-done | bytes 40992 | tf_op jit(solution)/shard_map/ppermute | solution.py:576
  24.3 2.4 %collective-permute-start.7 = (bf16[4,80,256]{2,1,0:T(8,128)(2,1)S(1)}, bf16[4,80,256]{2,1,0:T(8,128)(2,1)S(1)}, u32[]{:S(2)}, u32[]{:S(2)}) collective-permute-start(bf16[4,80,256]{2,1,0:T(8,128)(2,1)S(1)} %constant_dynamic-update-slice_fusion.refs_1_), channel_id=1, source_target_pairs={{0,6},{2,4},{4,2},{6,0},{8,14},{10,12},{12,10},{14,8},{16,22},{18,... | collective-permute-start | bytes 491528 | tf_op jit(solution)/shard_map/ppermute | solution.py:576
  26.8 1.1 %collective-permute-start.5 = (bf16[4,80,256]{2,1,0:T(8,128)(2,1)S(1)}, bf16[4,80,256]{2,1,0:T(8,128)(2,1)S(1)}, u32[]{:S(2)}, u32[]{:S(2)}) collective-permute-start(bf16[4,80,256]{2,1,0:T(8,128)(2,1)S(1)} %constant_dynamic-update-slice_fusion.refs_1_), channel_id=1, source_target_pairs={{0,2},{2,0},{4,6},{6,4},{8,10},{10,8},{12,14},{14,12},{16,18},{18,... | collective-permute-start | bytes 491528 | tf_op jit(solution)/shard_map/ppermute | solution.py:576
  27.9 2.8 %phases.2 = (bf16[4,1024,256]{2,1,0:T(8,128)(2,1)S(1)}, f32[64,1024]{1,0:T(8,128)S(1)}) custom-call(s32[3]{0:T(128)S(1)} %pad_add_fusion.refs_0_, bf16[4,80,256]{2,1,0:T(8,128)(2,1)S(1)} %constant_dynamic-update-slice_fusion.refs_1_, s32[3,1024]{1,0:T(4,128)S(1)} %copy-done.3), custom_call_target="tpu_custom_call" | custom-call | flops 3000000000 | bytes 2535424 | tf_op jit(solution)/shard_map/phases/pallas_call | solution.py:560
  30.7 1.0 %collective-permute-done.7.refs_1_.refs_4_ = bf16[4,80,256]{2,1,0:T(8,128)(2,1)S(1)} collective-permute-done((bf16[4,80,256]{2,1,0:T(8,128)(2,1)S(1)}, bf16[4,80,256]{2,1,0:T(8,128)(2,1)S(1)}, u32[]{:S(2)}, u32[]{:S(2)}) %collective-permute-start.7) | collective-permute-done | bytes 163872 | tf_op jit(solution)/shard_map/ppermute | solution.py:576
  31.6 2.8 %phases.3 = (bf16[4,1024,256]{2,1,0:T(8,128)(2,1)S(1)}, f32[64,1024]{1,0:T(8,128)S(1)}) custom-call(s32[3]{0:T(128)S(1)} %pad_add_fusion.refs_0_, bf16[4,80,256]{2,1,0:T(8,128)(2,1)S(1)} %collective-permute-done.7.refs_1_.refs_4_, s32[3,1024]{1,0:T(4,128)S(1)} %copy-done.3), custom_call_target="tpu_custom_call" | custom-call | flops 3000000000 | bytes 2535424 | tf_op jit(solution)/shard_map/phases/pallas_call | solution.py:560
  34.4 6.9 %structure.1 = (bf16[8,1024,256]{2,1,0:T(8,128)(2,1)S(1)}, f32[192,1024]{1,0:T(8,128)S(1)}, f32[3,16,256]{2,1,0:T(8,128)S(1)}, f32[3,16,256]{2,1,0:T(8,128)S(1)}) custom-call(s32[3]{0:T(128)S(1)} %pad_add_fusion.refs_0_, bf16[4,80,256]{2,1,0:T(8,128)(2,1)S(1)} %constant_dynamic-update-slice_fusion.refs_1_, ...), custom_call_target="tpu_custom_call" | custom-call | flops 8000000000 | bytes 10465280 | tf_op jit(solution)/shard_map/structure/pallas_call | solution.py:560
  41.3 0.3 collective-permute-start.8
  41.6 0.6 fields.1
  42.2 3.2 %collective-permute-done.8.refs_6_ = f32[3,16,256]{2,1,0:T(8,128)S(1)} collective-permute-done((f32[3,16,256]{2,1,0:T(8,128)S(1)}, f32[3,16,256]{2,1,0:T(8,128)S(1)}, u32[]{:S(2)}, u32[]{:S(2)}) %collective-permute-start.8) | collective-permute-done | bytes 49184 | tf_op jit(solution)/shard_map/ppermute | solution.py:576
  45.4 4.4 %gradient.1 = (f32[3,256]{1,0:T(4,128)}, f32[8,256]{1,0:T(8,128)S(1)}, f32[64,1024]{1,0:T(8,128)S(1)}, bf16[64,256]{1,0:T(8,128)(2,1)S(1)}) custom-call(s32[3]{0:T(128)S(1)} %pad_add_fusion.refs_0_, bf16[4,80,256]{2,1,0:T(8,128)(2,1)S(1)} %constant_dynamic-update-slice_fusion.refs_1_, bf16[4,80,256]{2,1,0:T(8,128)(2,1)S(1)} %collective-permute-done.5.refs_2_, ...), custom_call_target="tpu_custom_call" | custom-call | flops 5000000000 | bytes 9706496 | tf_op jit(solution)/shard_map/gradient/pallas_call | solution.py:560
  49.8 0.3 collective-permute-start.9
  50.1 0.3 own_gradient.1.refs_0_
  50.4 3.7 %collective-permute-done.9.refs_1_ = bf16[64,256]{1,0:T(8,128)(2,1)S(1)} collective-permute-done((bf16[64,256]{1,0:T(8,128)(2,1)S(1)}, bf16[64,256]{1,0:T(8,128)(2,1)S(1)}, u32[]{:S(2)}, u32[]{:S(2)}) %collective-permute-start.9) | collective-permute-done | bytes 32800 | tf_op jit(solution)/shard_map/ppermute | solution.py:576
  54.1 1.1 %weights.1.refs_0_ = f32[224,128]{1,0:T(8,128)S(1)} custom-call(f32[64,256]{1,0:T(8,128)S(1)} %own_gradient.1.refs_0_, bf16[64,256]{1,0:T(8,128)(2,1)S(1)} %collective-permute-done.9.refs_1_, f32[16,128,256]{2,1,0:T(8,128)S(1)} %get-tuple-element.55.refs_2_, f32[128,256]{1,0:T(8,128)S(1)} %get-tuple-element.56.refs_3_, ...), custom_call_target="tpu_custom_call" | custom-call | flops 3000000000 | bytes 2688000 | tf_op jit(solution)/shard_map/weights/pallas_call | solution.py:560
  55.2 1.8 %collective-permute-start.12 = (f32[224,128]{1,0:T(8,128)S(1)}, f32[224,128]{1,0:T(8,128)S(1)}, u32[]{:S(2)}, u32[]{:S(2)}) collective-permute-start(f32[224,128]{1,0:T(8,128)S(1)} %weights.1.refs_0_), channel_id=1, source_target_pairs={{0,6},{2,4},{4,2},{6,0},{8,14},{10,12},{12,10},{14,8},{16,22},{18,... | collective-permute-start | bytes 344072 | tf_op jit(solution)/shard_map/ppermute | solution.py:576
  57.0 1.7 %collective-permute-start.10 = (f32[224,128]{1,0:T(8,128)S(1)}, f32[224,128]{1,0:T(8,128)S(1)}, u32[]{:S(2)}, u32[]{:S(2)}) collective-permute-start(f32[224,128]{1,0:T(8,128)S(1)} %weights.1.refs_0_), channel_id=1, source_target_pairs={{0,2},{2,0},{4,6},{6,4},{8,10},{10,8},{12,14},{14,12},{16,18},{18,... | collective-permute-start | bytes 344072 | tf_op jit(solution)/shard_map/ppermute | solution.py:576
  58.7 2.2 %collective-permute-done.12.refs_3_ = f32[224,128]{1,0:T(8,128)S(1)} collective-permute-done((f32[224,128]{1,0:T(8,128)S(1)}, f32[224,128]{1,0:T(8,128)S(1)}, u32[]{:S(2)}, u32[]{:S(2)}) %collective-permute-start.12) | collective-permute-done | bytes 114720 | tf_op jit(solution)/shard_map/ppermute | solution.py:576
  60.9 1.2 %collective-permute-done.11.refs_2_ = f32[224,128]{1,0:T(8,128)S(1)} collective-permute-done((f32[224,128]{1,0:T(8,128)S(1)}, f32[224,128]{1,0:T(8,128)S(1)}, u32[]{:S(2)}, u32[]{:S(2)}) %collective-permute-start.11) | collective-permute-done | bytes 114720 | tf_op jit(solution)/shard_map/ppermute | solution.py:576
  62.2 2.5 %collective-permute-start.15 = (bf16[352,128]{1,0:T(8,128)(2,1)S(1)}, bf16[352,128]{1,0:T(8,128)(2,1)S(1)}, u32[]{:S(2)}, u32[]{:S(2)}) collective-permute-start(bf16[352,128]{1,0:T(8,128)(2,1)S(1)} %halves.1.refs_0_), channel_id=1, source_target_pairs={{0,24},{2,26},{4,28},{6,30},{8,16},{10,18},{12,20},{14,22},{16,8},... | collective-permute-start | bytes 270344 | tf_op jit(solution)/shard_map/ppermute | solution.py:576
  64.7 2.0 %collective-permute-start.13 = (bf16[352,128]{1,0:T(8,128)(2,1)S(1)}, bf16[352,128]{1,0:T(8,128)(2,1)S(1)}, u32[]{:S(2)}, u32[]{:S(2)}) collective-permute-start(bf16[352,128]{1,0:T(8,128)(2,1)S(1)} %halves.1.refs_0_), channel_id=1, source_target_pairs={{0,8},{2,10},{4,12},{6,14},{8,0},{10,2},{12,4},{14,6},{16,24},{18,... | collective-permute-start | bytes 270344 | tf_op jit(solution)/shard_map/ppermute | solution.py:576
  66.6 2.0 %collective-permute-done.15.refs_3_ = bf16[352,128]{1,0:T(8,128)(2,1)S(1)} collective-permute-done((bf16[352,128]{1,0:T(8,128)(2,1)S(1)}, bf16[352,128]{1,0:T(8,128)(2,1)S(1)}, u32[]{:S(2)}, u32[]{:S(2)}) %collective-permute-start.15) | collective-permute-done | bytes 90144 | tf_op jit(solution)/shard_map/ppermute | solution.py:576
  68.6 1.9 %collective-permute-done.14.refs_2_ = bf16[352,128]{1,0:T(8,128)(2,1)S(1)} collective-permute-done((bf16[352,128]{1,0:T(8,128)(2,1)S(1)}, bf16[352,128]{1,0:T(8,128)(2,1)S(1)}, u32[]{:S(2)}, u32[]{:S(2)}) %collective-permute-start.14) | collective-permute-done | bytes 90144 | tf_op jit(solution)/shard_map/ppermute | solution.py:576
  70.5 0.8 %steps.1 = (f32[16,128]{1,0:T(8,128)}, f32[128,128]{1,0:T(8,128)}, f32[64,128]{1,0:T(8,128)}, f32[6,64]{1,0:T(8,128)}) custom-call(bf16[352,128]{1,0:T(8,128)(2,1)S(1)} %halves.1.refs_0_, bf16[352,128]{1,0:T(8,128)(2,1)S(1)} %collective-permute-done.13.refs_1_, bf16[352,128]{1,0:T(8,128)(2,1)S(1)} %collective-permute-done.14.refs_2_, ...), custom_call_target="tpu_custom_call" | custom-call | flops 2000000000 | bytes 583168 | tf_op jit(solution)/shard_map/steps/pallas_call | solution.py:560
  (40 shorter events, 0.4 us)
Async XLA Ops:
  0.6 9.2 %copy-start.5 = (f32[3,256]{1,0:T(4,128)S(1)}, f32[3,256]{1,0:T(4,128)}, u32[]{:S(2)}) copy-start(f32[3,256]{1,0:T(4,128)} %refs_1_.1) | copy-start | bytes 9220
  0.6 9.1 %copy-start = (bf16[256,128]{1,0:T(8,128)(2,1)S(1)}, bf16[256,128]{1,0:T(8,128)(2,1)}, u32[]{:S(2)}) copy-start(bf16[256,128]{1,0:T(8,128)(2,1)} %refs_0_.1) | copy-start | bytes 196612
  0.7 9.1 %copy-start.2 = (bf16[128,128]{1,0:T(8,128)(2,1)S(1)}, bf16[128,128]{1,0:T(8,128)(2,1)}, u32[]{:S(2)}) copy-start(bf16[128,128]{1,0:T(8,128)(2,1)} %refs_7_.3) | copy-start | bytes 98308
  0.7 9.1 %copy-start.8 = (f32[6,64]{1,0:T(8,128)S(1)}, f32[6,64]{1,0:T(8,128)}, u32[]{:S(2)}) copy-start(f32[6,64]{1,0:T(8,128)} %refs_9_.2) | copy-start | bytes 4612
  0.7 9.1 %copy-start.4 = (bf16[128,64]{0,1:T(8,128)(2,1)S(1)}, bf16[128,64]{0,1:T(8,128)(2,1)}, u32[]{:S(2)}) copy-start(bf16[128,64]{0,1:T(8,128)(2,1)} %param.22) | copy-start | bytes 49156
  0.7 9.1 %copy-start.7 = (bf16[16,128]{1,0:T(8,128)(2,1)S(1)}, bf16[16,128]{1,0:T(8,128)(2,1)}, u32[]{:S(2)}) copy-start(bf16[16,128]{1,0:T(8,128)(2,1)} %refs_6_.1) | copy-start | bytes 12292
  0.7 9.1 %copy-start.6 = (f32[3,256]{1,0:T(4,128)S(1)}, f32[3,256]{1,0:T(4,128)}, u32[]{:S(2)}) copy-start(f32[3,256]{1,0:T(4,128)} %refs_2_.3) | copy-start | bytes 9220
  0.7 9.1 %copy-start.10 = (s32[256]{0:T(256)S(1)}, s32[256]{0:T(256)}, u32[]{:S(2)}) copy-start(s32[256]{0:T(256)} %param.17) | copy-start | bytes 3076
  0.7 9.1 %copy-start.9 = (s32[256]{0:T(256)S(1)}, s32[256]{0:T(256)}, u32[]{:S(2)}) copy-start(s32[256]{0:T(256)} %param.15) | copy-start | bytes 3076
  0.7 9.1 %copy-start.1 = (s32[256,64]{0,1:T(8,128)S(1)}, s32[256,64]{0,1:T(8,128)}, u32[]{:S(2)}) copy-start(s32[256,64]{0,1:T(8,128)} %param.14) | copy-start | bytes 196612
  2.3 9.5 %collective-permute-start.1 = (bf16[288,128]{1,0:T(8,128)(2,1)}, bf16[288,128]{1,0:T(8,128)(2,1)S(1)}, u32[]{:S(2)}, u32[]{:S(2)}) collective-permute-start(bf16[288,128]{1,0:T(8,128)(2,1)} %pack.1), channel_id=1, source_target_pairs={{0,2},{2,0},{4,6},{6,4},{8,10},{10,8},{12,14},{14,12},{16,18},{18,... | collective-permute-start | bytes 221192 | tf_op jit(solution)/shard_map/ppermute | solution.py:576
  5.3 9.1 %collective-permute-start = (bf16[288,128]{1,0:T(8,128)(2,1)}, bf16[288,128]{1,0:T(8,128)(2,1)S(1)}, u32[]{:S(2)}, u32[]{:S(2)}) collective-permute-start(bf16[288,128]{1,0:T(8,128)(2,1)} %pack.1), channel_id=1, source_target_pairs={{0,30},{2,4},{4,2},{6,8},{8,6},{10,12},{12,10},{14,16},{16,14},{18... | collective-permute-start | bytes 221192 | tf_op jit(solution)/shard_map/ppermute | solution.py:626
  14.4 13.5 %copy-start.3 = (s32[3,1024]{1,0:T(4,128)S(1)}, s32[3,1024]{1,0:T(4,128)}, u32[]{:S(2)}) copy-start(s32[3,1024]{1,0:T(4,128)} %refs_10_.1) | copy-start | bytes 36868
  17.6 6.7 %collective-permute-start.4 = (bf16[1,80,256]{2,1,0:T(8,128)(2,1)S(1)}, bf16[1,80,256]{2,1,0:T(8,128)(2,1)S(1)}, u32[]{:S(2)}, u32[]{:S(2)}) collective-permute-start(bf16[1,80,256]{2,1,0:T(8,128)(2,1)S(1)} %get-tuple-element.40), channel_id=1, source_target_pairs={{0,24},{2,26},{4,28},{6,30},{8,16},{10,18},{12,20},{14,22},{16,8},... | collective-permute-start | bytes 122888 | tf_op jit(solution)/shard_map/ppermute | solution.py:576
  18.5 5.8 %collective-permute-start.3 = (bf16[1,80,256]{2,1,0:T(8,128)(2,1)S(1)}, bf16[1,80,256]{2,1,0:T(8,128)(2,1)S(1)}, u32[]{:S(2)}, u32[]{:S(2)}) collective-permute-start(bf16[1,80,256]{2,1,0:T(8,128)(2,1)S(1)} %get-tuple-element.40), channel_id=1, source_target_pairs={{0,16},{2,18},{4,20},{6,22},{8,24},{10,26},{12,28},{14,30},{16,0},... | collective-permute-start | bytes 122888 | tf_op jit(solution)/shard_map/ppermute | solution.py:576
  18.5 5.6 %collective-permute-start.2 = (bf16[1,80,256]{2,1,0:T(8,128)(2,1)S(1)}, bf16[1,80,256]{2,1,0:T(8,128)(2,1)S(1)}, u32[]{:S(2)}, u32[]{:S(2)}) collective-permute-start(bf16[1,80,256]{2,1,0:T(8,128)(2,1)S(1)} %get-tuple-element.40), channel_id=1, source_target_pairs={{0,8},{2,10},{4,12},{6,14},{8,0},{10,2},{12,4},{14,6},{16,24},{18,... | collective-permute-start | bytes 122888 | tf_op jit(solution)/shard_map/ppermute | solution.py:576
  24.3 7.3 %collective-permute-start.7 = (bf16[4,80,256]{2,1,0:T(8,128)(2,1)S(1)}, bf16[4,80,256]{2,1,0:T(8,128)(2,1)S(1)}, u32[]{:S(2)}, u32[]{:S(2)}) collective-permute-start(bf16[4,80,256]{2,1,0:T(8,128)(2,1)S(1)} %constant_dynamic-update-slice_fusion.refs_1_), channel_id=1, source_target_pairs={{0,6},{2,4},{4,2},{6,0},{8,14},{10,12},{12,10},{14,8},{16,22},{18,... | collective-permute-start | bytes 491528 | tf_op jit(solution)/shard_map/ppermute | solution.py:576
  26.8 7.6 %collective-permute-start.6 = (bf16[4,80,256]{2,1,0:T(8,128)(2,1)S(1)}, bf16[4,80,256]{2,1,0:T(8,128)(2,1)S(1)}, u32[]{:S(2)}, u32[]{:S(2)}) collective-permute-start(bf16[4,80,256]{2,1,0:T(8,128)(2,1)S(1)} %constant_dynamic-update-slice_fusion.refs_1_), channel_id=1, source_target_pairs={{0,4},{2,6},{4,0},{6,2},{8,12},{10,14},{12,8},{14,10},{16,20},{18,... | collective-permute-start | bytes 491528 | tf_op jit(solution)/shard_map/ppermute | solution.py:576
  26.8 7.6 %collective-permute-start.5 = (bf16[4,80,256]{2,1,0:T(8,128)(2,1)S(1)}, bf16[4,80,256]{2,1,0:T(8,128)(2,1)S(1)}, u32[]{:S(2)}, u32[]{:S(2)}) collective-permute-start(bf16[4,80,256]{2,1,0:T(8,128)(2,1)S(1)} %constant_dynamic-update-slice_fusion.refs_1_), channel_id=1, source_target_pairs={{0,2},{2,0},{4,6},{6,4},{8,10},{10,8},{12,14},{14,12},{16,18},{18,... | collective-permute-start | bytes 491528 | tf_op jit(solution)/shard_map/ppermute | solution.py:576
  41.3 4.2 %collective-permute-start.8 = (f32[3,16,256]{2,1,0:T(8,128)S(1)}, f32[3,16,256]{2,1,0:T(8,128)S(1)}, u32[]{:S(2)}, u32[]{:S(2)}) collective-permute-start(f32[3,16,256]{2,1,0:T(8,128)S(1)} %get-tuple-element.46), channel_id=1, source_target_pairs={{0,2},{2,0},{4,6},{6,4},{8,10},{10,8},{12,14},{14,12},{16,18},{18,... | collective-permute-start | bytes 147464 | tf_op jit(solution)/shard_map/ppermute | solution.py:576
  49.8 4.3 %collective-permute-start.9 = (bf16[64,256]{1,0:T(8,128)(2,1)S(1)}, bf16[64,256]{1,0:T(8,128)(2,1)S(1)}, u32[]{:S(2)}, u32[]{:S(2)}) collective-permute-start(bf16[64,256]{1,0:T(8,128)(2,1)S(1)} %get-tuple-element.54), channel_id=1, source_target_pairs={{0,2},{2,0},{4,6},{6,4},{8,10},{10,8},{12,14},{14,12},{16,18},{18,... | collective-permute-start | bytes 98312 | tf_op jit(solution)/shard_map/ppermute | solution.py:576
  55.2 5.8 %collective-permute-start.12 = (f32[224,128]{1,0:T(8,128)S(1)}, f32[224,128]{1,0:T(8,128)S(1)}, u32[]{:S(2)}, u32[]{:S(2)}) collective-permute-start(f32[224,128]{1,0:T(8,128)S(1)} %weights.1.refs_0_), channel_id=1, source_target_pairs={{0,6},{2,4},{4,2},{6,0},{8,14},{10,12},{12,10},{14,8},{16,22},{18,... | collective-permute-start | bytes 344072 | tf_op jit(solution)/shard_map/ppermute | solution.py:576
  57.0 5.1 %collective-permute-start.11 = (f32[224,128]{1,0:T(8,128)S(1)}, f32[224,128]{1,0:T(8,128)S(1)}, u32[]{:S(2)}, u32[]{:S(2)}) collective-permute-start(f32[224,128]{1,0:T(8,128)S(1)} %weights.1.refs_0_), channel_id=1, source_target_pairs={{0,4},{2,6},{4,0},{6,2},{8,12},{10,14},{12,8},{14,10},{16,20},{18,... | collective-permute-start | bytes 344072 | tf_op jit(solution)/shard_map/ppermute | solution.py:576
  57.0 5.1 %collective-permute-start.10 = (f32[224,128]{1,0:T(8,128)S(1)}, f32[224,128]{1,0:T(8,128)S(1)}, u32[]{:S(2)}, u32[]{:S(2)}) collective-permute-start(f32[224,128]{1,0:T(8,128)S(1)} %weights.1.refs_0_), channel_id=1, source_target_pairs={{0,2},{2,0},{4,6},{6,4},{8,10},{10,8},{12,14},{14,12},{16,18},{18,... | collective-permute-start | bytes 344072 | tf_op jit(solution)/shard_map/ppermute | solution.py:576
  62.2 6.4 %collective-permute-start.15 = (bf16[352,128]{1,0:T(8,128)(2,1)S(1)}, bf16[352,128]{1,0:T(8,128)(2,1)S(1)}, u32[]{:S(2)}, u32[]{:S(2)}) collective-permute-start(bf16[352,128]{1,0:T(8,128)(2,1)S(1)} %halves.1.refs_0_), channel_id=1, source_target_pairs={{0,24},{2,26},{4,28},{6,30},{8,16},{10,18},{12,20},{14,22},{16,8},... | collective-permute-start | bytes 270344 | tf_op jit(solution)/shard_map/ppermute | solution.py:576
  64.7 5.8 %collective-permute-start.14 = (bf16[352,128]{1,0:T(8,128)(2,1)S(1)}, bf16[352,128]{1,0:T(8,128)(2,1)S(1)}, u32[]{:S(2)}, u32[]{:S(2)}) collective-permute-start(bf16[352,128]{1,0:T(8,128)(2,1)S(1)} %halves.1.refs_0_), channel_id=1, source_target_pairs={{0,16},{2,18},{4,20},{6,22},{8,24},{10,26},{12,28},{14,30},{16,0},... | collective-permute-start | bytes 270344 | tf_op jit(solution)/shard_map/ppermute | solution.py:576
  64.7 5.8 %collective-permute-start.13 = (bf16[352,128]{1,0:T(8,128)(2,1)S(1)}, bf16[352,128]{1,0:T(8,128)(2,1)S(1)}, u32[]{:S(2)}, u32[]{:S(2)}) collective-permute-start(bf16[352,128]{1,0:T(8,128)(2,1)S(1)} %halves.1.refs_0_), channel_id=1, source_target_pairs={{0,8},{2,10},{4,12},{6,14},{8,0},{10,2},{12,4},{14,6},{16,24},{18,... | collective-permute-start | bytes 270344 | tf_op jit(solution)/shard_map/ppermute | solution.py:576

commit v9 on v7

--- a/solution.py
+++ b/solution.py
@@ -28,8 +28,8 @@
 
 
 sine_terms = fitted(lambda x: np.sin(np.pi * x), (1, 3, 5, 7, 9), 0.5)
-short_sine = fitted(lambda x: np.sin(np.pi * x), (1, 3, 5, 7), 0.5)
-short_cosine = fitted(lambda x: np.cos(np.pi * x), (0, 2, 4, 6), 0.5)
+short_sine = fitted(lambda x: math.sqrt(2) * np.sin(np.pi * x), (1, 3, 5, 7), 0.5)
+short_cosine = fitted(lambda x: math.sqrt(2) * np.cos(np.pi * x), (0, 2, 4, 6), 0.5)
 
 
 def horner(terms, square):
@@ -311,8 +311,8 @@
     square = turns * turns
     half_sine = turns * horner(short_sine, square)
     half_cosine = horner(short_cosine, square)
-    waves_ref[place, 0:share, :] = (2.0 * half_sine * half_cosine).astype(bf16)
-    waves_ref[place, share : 2 * share, :] = (1.0 - 2.0 * half_sine * half_sine).astype(bf16)
+    waves_ref[place, 0:share, :] = (half_sine * half_cosine).astype(bf16)
+    waves_ref[place, share : 2 * share, :] = (1.0 - half_sine * half_sine).astype(bf16)
 
 
 def phase_kernel(where_ref, shared_ref, wave_ref, waves_ref, part_ref, *, charge_count):
@@ -467,6 +467,33 @@
     )
 
 
+def summed(values):
+    while len(values) > 1:
+        values = [values[i] + values[i + 1] for i in range(0, len(values), 2)]
+    return values[0]
+
+
+def split_rows(value, first, count, sums_ref):
+    rows = value.shape[0]
+    high = value.astype(bf16)
+    sums_ref[0:rows, :] = high
+    rest = value[first : first + count, :] - high[first : first + count, :].astype(f32)
+    sums_ref[rows:, :] = rest.astype(bf16)
+
+
+def joined_rows(refs, first, count, value_ref):
+    total = summed([ref[...].astype(f32) for ref in refs])
+    rows = value_ref.shape[0]
+    value_ref[...] = total[0:rows, :]
+    value_ref[first : first + count, :] += total[rows:, :]
+
+
+def halves_kernel(*refs, first, count):
+    *part_refs, sums_ref, value_ref = refs
+    joined_rows(part_refs, first, count, value_ref)
+    split_rows(value_ref[...], first, count, sums_ref)
+
+
 def weights_kernel(*refs, group, kinds):
     part_refs = refs[:group]
     (
@@ -477,6 +504,7 @@
         species_ref,
         mix_ref,
         charge_ref,
+        sums_ref,
         packed_ref,
     ) = refs[group:]
     charge_count, atoms = part_refs[0].shape
@@ -507,12 +535,7 @@
         lax.broadcasted_iota(jnp.int32, (kinds, atoms), 0) == species_ref[...]
     ).astype(f32)
     packed_ref[row : row + kinds, 0:charge_count] = matmul_nt(one_hot, grad, highest)
-
-
-def summed(values):
-    while len(values) > 1:
-        values = [values[i] + values[i + 1] for i in range(0, len(values), 2)]
-    return values[0]
+    split_rows(packed_ref[...], basis_count, width, sums_ref)
 
 
 def step_kernel(*refs):
@@ -520,7 +543,7 @@
     basis_count, width = radial_ref.shape
     charge_count = charge_ref.shape[0]
     kinds = species_ref.shape[0]
-    total_ref[...] = summed([ref[...].astype(f32) for ref in total_refs])
+    joined_rows(total_refs, basis_count, width, total_ref)
 
     def normalized(gradient):
         mean = jnp.sum(gradient * gradient, keepdims=True) * (1.0 / gradient.size)
@@ -774,8 +797,8 @@
     packed = kernel(
         lambda *refs: weights_kernel(*refs, group=group, kinds=kinds),
         "weights",
-        shaped(rows, width),
-        (),
+        shaped(rows + width, width, kind=bf16),
+        (shaped(rows, width),),
         3_000,
         *grad_parts,
         filtered,
@@ -786,7 +809,15 @@
         mix_weight,
         charge_rows,
     )
-    packed = summed([packed] + [across(packed, r) for r in range(1, blocks)]).astype(bf16)
+    packed = kernel(
+        lambda *refs: halves_kernel(*refs, first=basis_count, count=width),
+        "halves",
+        shaped(rows + width, width, kind=bf16),
+        (shaped(rows, width),),
+        1_000,
+        packed,
+        *[across(packed, r) for r in range(1, blocks)],
+    )
     totals = [packed] + [across(packed, bits) for bits in range(blocks, domains, blocks)]
     radial_step, mix_step, charge_step, species_step = kernel(
         step_kernel,

time: 70.8 us -> 70.8 us (level)
    pallas_call x12 -> x13, Pallas kernels: 28.8 us -> 28.6 us  [kernel(): pl.pallas_call(body, out_shape=out_shape, in_specs=[in_smem] * len(scalar...]
where the time goes in v9:
time: 70.8 us; the launch traced here: 70.6 us
  Pallas kernels  28.6 us (40%)
  starting transfers between devices  24.1 us (34%)
  waiting for transfers between devices  16.9 us (24%)
  between operations  0.88 us (1%)
    pallas_call x13, Pallas kernels, kernel(): pl.pallas_call(body, out_shape=out_shape, in_specs=[in_smem] * len(scalar...  28.6 us
    ppermute x15, starting transfers between devices, across(): return lax.ppermute(value, 'dom', [(i, i ^ bits) for i in range(domains)])  19.6 us
    ppermute x15, waiting for transfers between devices, across(): return lax.ppermute(value, 'dom', [(i, i ^ bits) for i in range(domains)])  16.9 us
    ppermute x1, starting transfers between devices, on_device(): far = lax.ppermute(packed, 'dom', beyond)  4.53 us
  transfers between devices with their start and end apart: 16, of which 9 were waited for; matrix products, arithmetic and copies ran while one was open for 0% of the time, Pallas kernels for 15%

profile of v9, /device:TPU:0, one launch (start us, length us, event | category | flops | bytes accessed | tf_op | source)
XLA Modules:
  0.0 70.6 jit_solution(11813355870969436511)
XLA Ops:
  0.7 1.6 %pack.1 = bf16[288,128]{1,0:T(8,128)(2,1)} custom-call(bf16[256,128]{1,0:T(8,128)(2,1)} %refs_0_.1, f32[3,256]{1,0:T(4,128)} %refs_1_.1, s32[2,256]{1,0:T(2,128)} %ghost_ref.1), custom_call_target="tpu_custom_call" | custom-call | flops 1000000000 | bytes 144384 | tf_op jit(solution)/shard_map/pack/pallas_call | solution.py:571
  2.3 2.9 %collective-permute-start.1 = (bf16[288,128]{1,0:T(8,128)(2,1)}, bf16[288,128]{1,0:T(8,128)(2,1)S(1)}, u32[]{:S(2)}, u32[]{:S(2)}) collective-permute-start(bf16[288,128]{1,0:T(8,128)(2,1)} %pack.1), channel_id=1, source_target_pairs={{0,2},{2,0},{4,6},{6,4},{8,10},{10,8},{12,14},{14,12},{16,18},{18,... | collective-permute-start | bytes 221192 | tf_op jit(solution)/shard_map/ppermute | solution.py:587
  5.3 4.5 %collective-permute-start = (bf16[288,128]{1,0:T(8,128)(2,1)}, bf16[288,128]{1,0:T(8,128)(2,1)S(1)}, u32[]{:S(2)}, u32[]{:S(2)}) collective-permute-start(bf16[288,128]{1,0:T(8,128)(2,1)} %pack.1), channel_id=1, source_target_pairs={{0,30},{2,4},{4,2},{6,8},{8,6},{10,12},{12,10},{14,16},{16,14},{18... | collective-permute-start | bytes 221192 | tf_op jit(solution)/shard_map/ppermute | solution.py:637
  9.9 1.9 %own.1 = (f32[16,128,256]{2,1,0:T(8,128)S(1)}, s32[24,256]{1,0:T(8,128)S(1)}, bf16[128,256]{1,0:T(8,128)(2,1)S(1)}, f32[64,256]{1,0:T(8,128)S(1)}, f32[320,128]{1,0:T(8,128)S(1)}, /*index=5*/f32[24,256]{1,0:T(8,128)S(1)}) custom-call(bf16[256,128]{1,0:T(8,128)(2,1)S(1)} %copy-done, f32[3,256]{1,0:T(4,128)S(1)} %copy-done.5, f32[3,256]{1,0:T(4,128)S(1)} %copy-done.6, ...), custom_call_target="tpu_custom_call" | custom-call | flops 4000000000 | bytes 4740608 | tf_op jit(solution)/shard_map/own/pallas_call | solution.py:571
  11.9 2.5 %near.1.refs_2_ = f32[16,128,256]{2,1,0:T(8,128)S(1)} custom-call(s32[3]{0:T(128)S(1)} %pad_add_fusion.refs_0_, bf16[288,128]{1,0:T(8,128)(2,1)S(1)} %collective-permute-done.1.refs_1_, f32[16,128,256]{2,1,0:T(8,128)S(1)} %get-tuple-element.34.refs_2_, s32[24,256]{1,0:T(8,128)S(1)} %get-tuple-element.35.refs_3_, f32[24,256]{1,0:T(8,128)S(1)} %get-tuple-element.36.refs_4_.refs_7_), custom_call_target="tpu_custom_call" | custom-call | flops 3000000000 | bytes 6430720 | tf_op jit(solution)/shard_map/near/pallas_call | solution.py:571
  14.4 3.2 %edges.1 = (f32[16,128,256]{2,1,0:T(8,128)S(1)}, f32[128,256]{1,0:T(8,128)S(1)}, f32[128,256]{1,0:T(8,128)S(1)}, bf16[128,256]{1,0:T(8,128)(2,1)S(1)}, bf16[1,80,256]{2,1,0:T(8,128)(2,1)S(1)}) custom-call(s32[3]{0:T(128)S(1)} %pad_add_fusion.refs_0_, bf16[288,128]{1,0:T(8,128)(2,1)S(1)} %collective-permute-done.refs_1_, f32[16,128,256]{2,1,0:T(8,128)S(1)} %near.1.refs_2_, ...), custom_call_target="tpu_custom_call" | custom-call | flops 4000000000 | bytes 7094272 | tf_op jit(solution)/shard_map/edges/pallas_call | solution.py:571
  17.6 0.9 %collective-permute-start.4 = (bf16[1,80,256]{2,1,0:T(8,128)(2,1)S(1)}, bf16[1,80,256]{2,1,0:T(8,128)(2,1)S(1)}, u32[]{:S(2)}, u32[]{:S(2)}) collective-permute-start(bf16[1,80,256]{2,1,0:T(8,128)(2,1)S(1)} %get-tuple-element.40), channel_id=1, source_target_pairs={{0,24},{2,26},{4,28},{6,30},{8,16},{10,18},{12,20},{14,22},{16,8},... | collective-permute-start | bytes 122888 | tf_op jit(solution)/shard_map/ppermute | solution.py:587
  18.5 3.6 %collective-permute-start.2 = (bf16[1,80,256]{2,1,0:T(8,128)(2,1)S(1)}, bf16[1,80,256]{2,1,0:T(8,128)(2,1)S(1)}, u32[]{:S(2)}, u32[]{:S(2)}) collective-permute-start(bf16[1,80,256]{2,1,0:T(8,128)(2,1)S(1)} %get-tuple-element.40), channel_id=1, source_target_pairs={{0,8},{2,10},{4,12},{6,14},{8,0},{10,2},{12,4},{14,6},{16,24},{18,... | collective-permute-start | bytes 122888 | tf_op jit(solution)/shard_map/ppermute | solution.py:587
  22.1 2.0 %collective-permute-done.2 = bf16[1,80,256]{2,1,0:T(8,128)(2,1)S(1)} collective-permute-done((bf16[1,80,256]{2,1,0:T(8,128)(2,1)S(1)}, bf16[1,80,256]{2,1,0:T(8,128)(2,1)S(1)}, u32[]{:S(2)}, u32[]{:S(2)}) %collective-permute-start.2) | collective-permute-done | bytes 40992 | tf_op jit(solution)/shard_map/ppermute | solution.py:587
  24.3 2.4 %collective-permute-start.7 = (bf16[4,80,256]{2,1,0:T(8,128)(2,1)S(1)}, bf16[4,80,256]{2,1,0:T(8,128)(2,1)S(1)}, u32[]{:S(2)}, u32[]{:S(2)}) collective-permute-start(bf16[4,80,256]{2,1,0:T(8,128)(2,1)S(1)} %constant_dynamic-update-slice_fusion.refs_1_), channel_id=1, source_target_pairs={{0,6},{2,4},{4,2},{6,0},{8,14},{10,12},{12,10},{14,8},{16,22},{18,... | collective-permute-start | bytes 491528 | tf_op jit(solution)/shard_map/ppermute | solution.py:587
  26.8 1.1 %collective-permute-start.5 = (bf16[4,80,256]{2,1,0:T(8,128)(2,1)S(1)}, bf16[4,80,256]{2,1,0:T(8,128)(2,1)S(1)}, u32[]{:S(2)}, u32[]{:S(2)}) collective-permute-start(bf16[4,80,256]{2,1,0:T(8,128)(2,1)S(1)} %constant_dynamic-update-slice_fusion.refs_1_), channel_id=1, source_target_pairs={{0,2},{2,0},{4,6},{6,4},{8,10},{10,8},{12,14},{14,12},{16,18},{18,... | collective-permute-start | bytes 491528 | tf_op jit(solution)/shard_map/ppermute | solution.py:587
  27.9 2.7 %phases.2 = (bf16[4,1024,256]{2,1,0:T(8,128)(2,1)S(1)}, f32[64,1024]{1,0:T(8,128)S(1)}) custom-call(s32[3]{0:T(128)S(1)} %pad_add_fusion.refs_0_, bf16[4,80,256]{2,1,0:T(8,128)(2,1)S(1)} %constant_dynamic-update-slice_fusion.refs_1_, s32[3,1024]{1,0:T(4,128)S(1)} %copy-done.3), custom_call_target="tpu_custom_call" | custom-call | flops 3000000000 | bytes 2535424 | tf_op jit(solution)/shard_map/phases/pallas_call | solution.py:571
  30.6 1.0 %collective-permute-done.7.refs_1_.refs_4_ = bf16[4,80,256]{2,1,0:T(8,128)(2,1)S(1)} collective-permute-done((bf16[4,80,256]{2,1,0:T(8,128)(2,1)S(1)}, bf16[4,80,256]{2,1,0:T(8,128)(2,1)S(1)}, u32[]{:S(2)}, u32[]{:S(2)}) %collective-permute-start.7) | collective-permute-done | bytes 163872 | tf_op jit(solution)/shard_map/ppermute | solution.py:587
  31.6 2.7 %phases.3 = (bf16[4,1024,256]{2,1,0:T(8,128)(2,1)S(1)}, f32[64,1024]{1,0:T(8,128)S(1)}) custom-call(s32[3]{0:T(128)S(1)} %pad_add_fusion.refs_0_, bf16[4,80,256]{2,1,0:T(8,128)(2,1)S(1)} %collective-permute-done.7.refs_1_.refs_4_, s32[3,1024]{1,0:T(4,128)S(1)} %copy-done.3), custom_call_target="tpu_custom_call" | custom-call | flops 3000000000 | bytes 2535424 | tf_op jit(solution)/shard_map/phases/pallas_call | solution.py:571
  34.3 6.7 %structure.1 = (bf16[8,1024,256]{2,1,0:T(8,128)(2,1)S(1)}, f32[192,1024]{1,0:T(8,128)S(1)}, f32[3,16,256]{2,1,0:T(8,128)S(1)}, f32[3,16,256]{2,1,0:T(8,128)S(1)}) custom-call(s32[3]{0:T(128)S(1)} %pad_add_fusion.refs_0_, bf16[4,80,256]{2,1,0:T(8,128)(2,1)S(1)} %constant_dynamic-update-slice_fusion.refs_1_, ...), custom_call_target="tpu_custom_call" | custom-call | flops 8000000000 | bytes 10465280 | tf_op jit(solution)/shard_map/structure/pallas_call | solution.py:571
  41.1 0.3 collective-permute-start.8
  41.4 0.6 fields.1
  42.0 3.2 %collective-permute-done.8.refs_6_ = f32[3,16,256]{2,1,0:T(8,128)S(1)} collective-permute-done((f32[3,16,256]{2,1,0:T(8,128)S(1)}, f32[3,16,256]{2,1,0:T(8,128)S(1)}, u32[]{:S(2)}, u32[]{:S(2)}) %collective-permute-start.8) | collective-permute-done | bytes 49184 | tf_op jit(solution)/shard_map/ppermute | solution.py:587
  45.2 4.4 %gradient.1 = (f32[3,256]{1,0:T(4,128)}, f32[8,256]{1,0:T(8,128)S(1)}, f32[64,1024]{1,0:T(8,128)S(1)}, bf16[64,256]{1,0:T(8,128)(2,1)S(1)}) custom-call(s32[3]{0:T(128)S(1)} %pad_add_fusion.refs_0_, bf16[4,80,256]{2,1,0:T(8,128)(2,1)S(1)} %constant_dynamic-update-slice_fusion.refs_1_, bf16[4,80,256]{2,1,0:T(8,128)(2,1)S(1)} %collective-permute-done.5.refs_2_, ...), custom_call_target="tpu_custom_call" | custom-call | flops 5000000000 | bytes 9706496 | tf_op jit(solution)/shard_map/gradient/pallas_call | solution.py:571
  49.6 0.3 collective-permute-start.9
  49.9 0.3 own_gradient.1.refs_0_
  50.2 3.7 %collective-permute-done.9.refs_1_ = bf16[64,256]{1,0:T(8,128)(2,1)S(1)} collective-permute-done((bf16[64,256]{1,0:T(8,128)(2,1)S(1)}, bf16[64,256]{1,0:T(8,128)(2,1)S(1)}, u32[]{:S(2)}, u32[]{:S(2)}) %collective-permute-start.9) | collective-permute-done | bytes 32800 | tf_op jit(solution)/shard_map/ppermute | solution.py:587
  53.9 1.1 %weights.1.refs_0_ = bf16[352,128]{1,0:T(8,128)(2,1)S(1)} custom-call(f32[64,256]{1,0:T(8,128)S(1)} %own_gradient.1.refs_0_, bf16[64,256]{1,0:T(8,128)(2,1)S(1)} %collective-permute-done.9.refs_1_, f32[16,128,256]{2,1,0:T(8,128)S(1)} %get-tuple-element.55.refs_2_, f32[128,256]{1,0:T(8,128)S(1)} %get-tuple-element.56.refs_3_, ...), custom_call_target="tpu_custom_call" | custom-call | flops 3000000000 | bytes 2778112 | tf_op jit(solution)/shard_map/weights/pallas_call | solution.py:571
  55.0 1.8 %collective-permute-start.12 = (bf16[352,128]{1,0:T(8,128)(2,1)S(1)}, bf16[352,128]{1,0:T(8,128)(2,1)S(1)}, u32[]{:S(2)}, u32[]{:S(2)}) collective-permute-start(bf16[352,128]{1,0:T(8,128)(2,1)S(1)} %weights.1.refs_0_), channel_id=1, source_target_pairs={{0,6},{2,4},{4,2},{6,0},{8,14},{10,12},{12,10},{14,8},{16,22},{18,... | collective-permute-start | bytes 270344 | tf_op jit(solution)/shard_map/ppermute | solution.py:587
  56.8 1.7 %collective-permute-start.10 = (bf16[352,128]{1,0:T(8,128)(2,1)S(1)}, bf16[352,128]{1,0:T(8,128)(2,1)S(1)}, u32[]{:S(2)}, u32[]{:S(2)}) collective-permute-start(bf16[352,128]{1,0:T(8,128)(2,1)S(1)} %weights.1.refs_0_), channel_id=1, source_target_pairs={{0,2},{2,0},{4,6},{6,4},{8,10},{10,8},{12,14},{14,12},{16,18},{18,... | collective-permute-start | bytes 270344 | tf_op jit(solution)/shard_map/ppermute | solution.py:587
  58.5 1.9 %collective-permute-done.12.refs_3_ = bf16[352,128]{1,0:T(8,128)(2,1)S(1)} collective-permute-done((bf16[352,128]{1,0:T(8,128)(2,1)S(1)}, bf16[352,128]{1,0:T(8,128)(2,1)S(1)}, u32[]{:S(2)}, u32[]{:S(2)}) %collective-permute-start.12) | collective-permute-done | bytes 90144 | tf_op jit(solution)/shard_map/ppermute | solution.py:587
  60.4 1.0 %collective-permute-done.11.refs_2_ = bf16[352,128]{1,0:T(8,128)(2,1)S(1)} collective-permute-done((bf16[352,128]{1,0:T(8,128)(2,1)S(1)}, bf16[352,128]{1,0:T(8,128)(2,1)S(1)}, u32[]{:S(2)}, u32[]{:S(2)}) %collective-permute-start.11) | collective-permute-done | bytes 90144 | tf_op jit(solution)/shard_map/ppermute | solution.py:587
  61.5 2.4 %collective-permute-start.15 = (bf16[352,128]{1,0:T(8,128)(2,1)S(1)}, bf16[352,128]{1,0:T(8,128)(2,1)S(1)}, u32[]{:S(2)}, u32[]{:S(2)}) collective-permute-start(bf16[352,128]{1,0:T(8,128)(2,1)S(1)} %halves.1.refs_0_), channel_id=1, source_target_pairs={{0,24},{2,26},{4,28},{6,30},{8,16},{10,18},{12,20},{14,22},{16,8},... | collective-permute-start | bytes 270344 | tf_op jit(solution)/shard_map/ppermute | solution.py:587
  64.0 2.0 %collective-permute-start.13 = (bf16[352,128]{1,0:T(8,128)(2,1)S(1)}, bf16[352,128]{1,0:T(8,128)(2,1)S(1)}, u32[]{:S(2)}, u32[]{:S(2)}) collective-permute-start(bf16[352,128]{1,0:T(8,128)(2,1)S(1)} %halves.1.refs_0_), channel_id=1, source_target_pairs={{0,8},{2,10},{4,12},{6,14},{8,0},{10,2},{12,4},{14,6},{16,24},{18,... | collective-permute-start | bytes 270344 | tf_op jit(solution)/shard_map/ppermute | solution.py:587
  65.9 2.0 %collective-permute-done.15.refs_3_ = bf16[352,128]{1,0:T(8,128)(2,1)S(1)} collective-permute-done((bf16[352,128]{1,0:T(8,128)(2,1)S(1)}, bf16[352,128]{1,0:T(8,128)(2,1)S(1)}, u32[]{:S(2)}, u32[]{:S(2)}) %collective-permute-start.15) | collective-permute-done | bytes 90144 | tf_op jit(solution)/shard_map/ppermute | solution.py:587
  67.9 1.9 %collective-permute-done.14.refs_2_ = bf16[352,128]{1,0:T(8,128)(2,1)S(1)} collective-permute-done((bf16[352,128]{1,0:T(8,128)(2,1)S(1)}, bf16[352,128]{1,0:T(8,128)(2,1)S(1)}, u32[]{:S(2)}, u32[]{:S(2)}) %collective-permute-start.14) | collective-permute-done | bytes 90144 | tf_op jit(solution)/shard_map/ppermute | solution.py:587
  69.8 0.8 %steps.1 = (f32[16,128]{1,0:T(8,128)}, f32[128,128]{1,0:T(8,128)}, f32[64,128]{1,0:T(8,128)}, f32[6,64]{1,0:T(8,128)}) custom-call(bf16[352,128]{1,0:T(8,128)(2,1)S(1)} %halves.1.refs_0_, bf16[352,128]{1,0:T(8,128)(2,1)S(1)} %collective-permute-done.13.refs_1_, bf16[352,128]{1,0:T(8,128)(2,1)S(1)} %collective-permute-done.14.refs_2_, ...), custom_call_target="tpu_custom_call" | custom-call | flops 2000000000 | bytes 583168 | tf_op jit(solution)/shard_map/steps/pallas_call | solution.py:571
  (40 shorter events, 0.6 us)
Async XLA Ops:
  0.6 9.2 %copy-start.5 = (f32[3,256]{1,0:T(4,128)S(1)}, f32[3,256]{1,0:T(4,128)}, u32[]{:S(2)}) copy-start(f32[3,256]{1,0:T(4,128)} %refs_1_.1) | copy-start | bytes 9220
  0.6 9.1 %copy-start = (bf16[256,128]{1,0:T(8,128)(2,1)S(1)}, bf16[256,128]{1,0:T(8,128)(2,1)}, u32[]{:S(2)}) copy-start(bf16[256,128]{1,0:T(8,128)(2,1)} %refs_0_.1) | copy-start | bytes 196612
  0.7 9.1 %copy-start.2 = (bf16[128,128]{1,0:T(8,128)(2,1)S(1)}, bf16[128,128]{1,0:T(8,128)(2,1)}, u32[]{:S(2)}) copy-start(bf16[128,128]{1,0:T(8,128)(2,1)} %refs_7_.3) | copy-start | bytes 98308
  0.7 9.1 %copy-start.8 = (f32[6,64]{1,0:T(8,128)S(1)}, f32[6,64]{1,0:T(8,128)}, u32[]{:S(2)}) copy-start(f32[6,64]{1,0:T(8,128)} %refs_9_.2) | copy-start | bytes 4612
  0.7 9.1 %copy-start.4 = (bf16[128,64]{0,1:T(8,128)(2,1)S(1)}, bf16[128,64]{0,1:T(8,128)(2,1)}, u32[]{:S(2)}) copy-start(bf16[128,64]{0,1:T(8,128)(2,1)} %param.22) | copy-start | bytes 49156
  0.7 9.1 %copy-start.7 = (bf16[16,128]{1,0:T(8,128)(2,1)S(1)}, bf16[16,128]{1,0:T(8,128)(2,1)}, u32[]{:S(2)}) copy-start(bf16[16,128]{1,0:T(8,128)(2,1)} %refs_6_.1) | copy-start | bytes 12292
  0.7 9.1 %copy-start.6 = (f32[3,256]{1,0:T(4,128)S(1)}, f32[3,256]{1,0:T(4,128)}, u32[]{:S(2)}) copy-start(f32[3,256]{1,0:T(4,128)} %refs_2_.3) | copy-start | bytes 9220
  0.7 9.1 %copy-start.10 = (s32[256]{0:T(256)S(1)}, s32[256]{0:T(256)}, u32[]{:S(2)}) copy-start(s32[256]{0:T(256)} %param.17) | copy-start | bytes 3076
  0.7 9.1 %copy-start.9 = (s32[256]{0:T(256)S(1)}, s32[256]{0:T(256)}, u32[]{:S(2)}) copy-start(s32[256]{0:T(256)} %param.15) | copy-start | bytes 3076
  0.7 9.1 %copy-start.1 = (s32[256,64]{0,1:T(8,128)S(1)}, s32[256,64]{0,1:T(8,128)}, u32[]{:S(2)}) copy-start(s32[256,64]{0,1:T(8,128)} %param.14) | copy-start | bytes 196612
  2.3 9.5 %collective-permute-start.1 = (bf16[288,128]{1,0:T(8,128)(2,1)}, bf16[288,128]{1,0:T(8,128)(2,1)S(1)}, u32[]{:S(2)}, u32[]{:S(2)}) collective-permute-start(bf16[288,128]{1,0:T(8,128)(2,1)} %pack.1), channel_id=1, source_target_pairs={{0,2},{2,0},{4,6},{6,4},{8,10},{10,8},{12,14},{14,12},{16,18},{18,... | collective-permute-start | bytes 221192 | tf_op jit(solution)/shard_map/ppermute | solution.py:587
  5.3 9.1 %collective-permute-start = (bf16[288,128]{1,0:T(8,128)(2,1)}, bf16[288,128]{1,0:T(8,128)(2,1)S(1)}, u32[]{:S(2)}, u32[]{:S(2)}) collective-permute-start(bf16[288,128]{1,0:T(8,128)(2,1)} %pack.1), channel_id=1, source_target_pairs={{0,30},{2,4},{4,2},{6,8},{8,6},{10,12},{12,10},{14,16},{16,14},{18... | collective-permute-start | bytes 221192 | tf_op jit(solution)/shard_map/ppermute | solution.py:637
  14.4 13.5 %copy-start.3 = (s32[3,1024]{1,0:T(4,128)S(1)}, s32[3,1024]{1,0:T(4,128)}, u32[]{:S(2)}) copy-start(s32[3,1024]{1,0:T(4,128)} %refs_10_.1) | copy-start | bytes 36868
  17.6 6.7 %collective-permute-start.4 = (bf16[1,80,256]{2,1,0:T(8,128)(2,1)S(1)}, bf16[1,80,256]{2,1,0:T(8,128)(2,1)S(1)}, u32[]{:S(2)}, u32[]{:S(2)}) collective-permute-start(bf16[1,80,256]{2,1,0:T(8,128)(2,1)S(1)} %get-tuple-element.40), channel_id=1, source_target_pairs={{0,24},{2,26},{4,28},{6,30},{8,16},{10,18},{12,20},{14,22},{16,8},... | collective-permute-start | bytes 122888 | tf_op jit(solution)/shard_map/ppermute | solution.py:587
  18.5 5.8 %collective-permute-start.3 = (bf16[1,80,256]{2,1,0:T(8,128)(2,1)S(1)}, bf16[1,80,256]{2,1,0:T(8,128)(2,1)S(1)}, u32[]{:S(2)}, u32[]{:S(2)}) collective-permute-start(bf16[1,80,256]{2,1,0:T(8,128)(2,1)S(1)} %get-tuple-element.40), channel_id=1, source_target_pairs={{0,16},{2,18},{4,20},{6,22},{8,24},{10,26},{12,28},{14,30},{16,0},... | collective-permute-start | bytes 122888 | tf_op jit(solution)/shard_map/ppermute | solution.py:587
  18.5 5.6 %collective-permute-start.2 = (bf16[1,80,256]{2,1,0:T(8,128)(2,1)S(1)}, bf16[1,80,256]{2,1,0:T(8,128)(2,1)S(1)}, u32[]{:S(2)}, u32[]{:S(2)}) collective-permute-start(bf16[1,80,256]{2,1,0:T(8,128)(2,1)S(1)} %get-tuple-element.40), channel_id=1, source_target_pairs={{0,8},{2,10},{4,12},{6,14},{8,0},{10,2},{12,4},{14,6},{16,24},{18,... | collective-permute-start | bytes 122888 | tf_op jit(solution)/shard_map/ppermute | solution.py:587
  24.3 7.3 %collective-permute-start.7 = (bf16[4,80,256]{2,1,0:T(8,128)(2,1)S(1)}, bf16[4,80,256]{2,1,0:T(8,128)(2,1)S(1)}, u32[]{:S(2)}, u32[]{:S(2)}) collective-permute-start(bf16[4,80,256]{2,1,0:T(8,128)(2,1)S(1)} %constant_dynamic-update-slice_fusion.refs_1_), channel_id=1, source_target_pairs={{0,6},{2,4},{4,2},{6,0},{8,14},{10,12},{12,10},{14,8},{16,22},{18,... | collective-permute-start | bytes 491528 | tf_op jit(solution)/shard_map/ppermute | solution.py:587
  26.8 7.6 %collective-permute-start.6 = (bf16[4,80,256]{2,1,0:T(8,128)(2,1)S(1)}, bf16[4,80,256]{2,1,0:T(8,128)(2,1)S(1)}, u32[]{:S(2)}, u32[]{:S(2)}) collective-permute-start(bf16[4,80,256]{2,1,0:T(8,128)(2,1)S(1)} %constant_dynamic-update-slice_fusion.refs_1_), channel_id=1, source_target_pairs={{0,4},{2,6},{4,0},{6,2},{8,12},{10,14},{12,8},{14,10},{16,20},{18,... | collective-permute-start | bytes 491528 | tf_op jit(solution)/shard_map/ppermute | solution.py:587
  26.8 7.6 %collective-permute-start.5 = (bf16[4,80,256]{2,1,0:T(8,128)(2,1)S(1)}, bf16[4,80,256]{2,1,0:T(8,128)(2,1)S(1)}, u32[]{:S(2)}, u32[]{:S(2)}) collective-permute-start(bf16[4,80,256]{2,1,0:T(8,128)(2,1)S(1)} %constant_dynamic-update-slice_fusion.refs_1_), channel_id=1, source_target_pairs={{0,2},{2,0},{4,6},{6,4},{8,10},{10,8},{12,14},{14,12},{16,18},{18,... | collective-permute-start | bytes 491528 | tf_op jit(solution)/shard_map/ppermute | solution.py:587
  41.1 4.2 %collective-permute-start.8 = (f32[3,16,256]{2,1,0:T(8,128)S(1)}, f32[3,16,256]{2,1,0:T(8,128)S(1)}, u32[]{:S(2)}, u32[]{:S(2)}) collective-permute-start(f32[3,16,256]{2,1,0:T(8,128)S(1)} %get-tuple-element.46), channel_id=1, source_target_pairs={{0,2},{2,0},{4,6},{6,4},{8,10},{10,8},{12,14},{14,12},{16,18},{18,... | collective-permute-start | bytes 147464 | tf_op jit(solution)/shard_map/ppermute | solution.py:587
  49.6 4.3 %collective-permute-start.9 = (bf16[64,256]{1,0:T(8,128)(2,1)S(1)}, bf16[64,256]{1,0:T(8,128)(2,1)S(1)}, u32[]{:S(2)}, u32[]{:S(2)}) collective-permute-start(bf16[64,256]{1,0:T(8,128)(2,1)S(1)} %get-tuple-element.54), channel_id=1, source_target_pairs={{0,2},{2,0},{4,6},{6,4},{8,10},{10,8},{12,14},{14,12},{16,18},{18,... | collective-permute-start | bytes 98312 | tf_op jit(solution)/shard_map/ppermute | solution.py:587
  55.0 5.5 %collective-permute-start.12 = (bf16[352,128]{1,0:T(8,128)(2,1)S(1)}, bf16[352,128]{1,0:T(8,128)(2,1)S(1)}, u32[]{:S(2)}, u32[]{:S(2)}) collective-permute-start(bf16[352,128]{1,0:T(8,128)(2,1)S(1)} %weights.1.refs_0_), channel_id=1, source_target_pairs={{0,6},{2,4},{4,2},{6,0},{8,14},{10,12},{12,10},{14,8},{16,22},{18,... | collective-permute-start | bytes 270344 | tf_op jit(solution)/shard_map/ppermute | solution.py:587
  56.8 4.6 %collective-permute-start.11 = (bf16[352,128]{1,0:T(8,128)(2,1)S(1)}, bf16[352,128]{1,0:T(8,128)(2,1)S(1)}, u32[]{:S(2)}, u32[]{:S(2)}) collective-permute-start(bf16[352,128]{1,0:T(8,128)(2,1)S(1)} %weights.1.refs_0_), channel_id=1, source_target_pairs={{0,4},{2,6},{4,0},{6,2},{8,12},{10,14},{12,8},{14,10},{16,20},{18,... | collective-permute-start | bytes 270344 | tf_op jit(solution)/shard_map/ppermute | solution.py:587
  56.8 4.6 %collective-permute-start.10 = (bf16[352,128]{1,0:T(8,128)(2,1)S(1)}, bf16[352,128]{1,0:T(8,128)(2,1)S(1)}, u32[]{:S(2)}, u32[]{:S(2)}) collective-permute-start(bf16[352,128]{1,0:T(8,128)(2,1)S(1)} %weights.1.refs_0_), channel_id=1, source_target_pairs={{0,2},{2,0},{4,6},{6,4},{8,10},{10,8},{12,14},{14,12},{16,18},{18,... | collective-permute-start | bytes 270344 | tf_op jit(solution)/shard_map/ppermute | solution.py:587
  61.5 6.4 %collective-permute-start.15 = (bf16[352,128]{1,0:T(8,128)(2,1)S(1)}, bf16[352,128]{1,0:T(8,128)(2,1)S(1)}, u32[]{:S(2)}, u32[]{:S(2)}) collective-permute-start(bf16[352,128]{1,0:T(8,128)(2,1)S(1)} %halves.1.refs_0_), channel_id=1, source_target_pairs={{0,24},{2,26},{4,28},{6,30},{8,16},{10,18},{12,20},{14,22},{16,8},... | collective-permute-start | bytes 270344 | tf_op jit(solution)/shard_map/ppermute | solution.py:587
  63.8 6.0 %collective-permute-start.14 = (bf16[352,128]{1,0:T(8,128)(2,1)S(1)}, bf16[352,128]{1,0:T(8,128)(2,1)S(1)}, u32[]{:S(2)}, u32[]{:S(2)}) collective-permute-start(bf16[352,128]{1,0:T(8,128)(2,1)S(1)} %halves.1.refs_0_), channel_id=1, source_target_pairs={{0,16},{2,18},{4,20},{6,22},{8,24},{10,26},{12,28},{14,30},{16,0},... | collective-permute-start | bytes 270344 | tf_op jit(solution)/shard_map/ppermute | solution.py:587
  64.0 5.8 %collective-permute-start.13 = (bf16[352,128]{1,0:T(8,128)(2,1)S(1)}, bf16[352,128]{1,0:T(8,128)(2,1)S(1)}, u32[]{:S(2)}, u32[]{:S(2)}) collective-permute-start(bf16[352,128]{1,0:T(8,128)(2,1)S(1)} %halves.1.refs_0_), channel_id=1, source_target_pairs={{0,8},{2,10},{4,12},{6,14},{8,0},{10,2},{12,4},{14,6},{16,24},{18,... | collective-permute-start | bytes 270344 | tf_op jit(solution)/shard_map/ppermute | solution.py:587

commit v10 on v9

--- a/solution.py
+++ b/solution.py
@@ -51,6 +51,16 @@
     )
 
 
+def terms_of(value):
+    high = value.astype(bf16)
+    return high, (value - high.astype(f32)).astype(bf16)
+
+
+def exact_matmul(left, value, product=matmul):
+    high, low = terms_of(value)
+    return product(left, high) + product(left, low)
+
+
 def turned(value):
     return jnp.transpose(value.astype(f32)).astype(value.dtype)
 
@@ -100,7 +110,8 @@
             away = coords[:, axis : axis + 1] - mine
             away = away - length * jnp.floor(away * (1.0 / length) + 0.5)
             total = total + away * away
-        distance = jnp.sqrt(total)
+        total = jnp.maximum(total, 1e-20)
+        distance = total * lax.rsqrt(total)
         word = words_ref[pl.ds(index, 1), :]
         sublane = lax.broadcasted_iota(jnp.int32, (step, atoms), 0)
         is_live = (jnp.right_shift(jnp.broadcast_to(word, (step, atoms)), sublane) & 1) != 0
@@ -278,7 +289,7 @@
         filtered_ref[b] = filtered
         messages = messages + weights_ref[width + charge_count :, b : b + 1] * filtered
     messages_ref[...] = messages
-    before = matmul(weights_ref[0:width, :], messages, highest)
+    before = exact_matmul(weights_ref[0:width, :].astype(bf16), messages)
     before_ref[...] = before
     hidden = (own_ref[...].astype(f32) + before * sigmoid(before)).astype(bf16)
     hidden_ref[...] = hidden
@@ -514,9 +525,9 @@
         grad = grad + part_refs[m][...].astype(f32)
     before = before_ref[...]
     gate = sigmoid(before)
-    upstream = matmul(jnp.transpose(charge_ref[...].astype(f32)), grad, highest)
+    upstream = exact_matmul(turned(charge_ref[...]), grad)
     before_grad = upstream * (gate * (1.0 + before * (1.0 - gate)))
-    message_grad = matmul(mix_ref[...].astype(f32), before_grad, highest)
+    message_grad = exact_matmul(mix_ref[...], before_grad)
     columns = [
         jnp.sum(message_grad * filtered_ref[b], axis=1, keepdims=True) for b in range(basis_count)
     ]
@@ -524,10 +535,14 @@
     row = 0
     packed_ref[row : row + basis_count, :] = jnp.transpose(radial)
     row += basis_count
-    packed_ref[row : row + width, :] = matmul_nt(messages_ref[...], before_grad, highest)
+    high, low = terms_of(messages_ref[...])
+    packed_ref[row : row + width, :] = exact_matmul(high, before_grad, matmul_nt) + matmul_nt(
+        low, before_grad.astype(bf16)
+    )
     row += width
-    packed_ref[row : row + charge_count, :] = matmul_nt(
-        grad, hidden_ref[...].astype(f32), highest
+    high, low = terms_of(grad)
+    packed_ref[row : row + charge_count, :] = matmul_nt(high, hidden_ref[...]) + matmul_nt(
+        low, hidden_ref[...]
     )
     row += charge_count
     packed_ref[row:, :] = jnp.zeros((packed_ref.shape[0] - row, width), f32)

time: 70.8 us -> 70.2 us (level)
  no operation moved by 1% of the time
where the time goes in v10:
time: 70.2 us; the launch traced here: 70.1 us
  Pallas kernels  28 us (40%)
  starting transfers between devices  24.1 us (34%)
  waiting for transfers between devices  16.9 us (24%)
  between operations  0.89 us (1%)
    pallas_call x13, Pallas kernels, kernel(): pl.pallas_call(body, out_shape=out_shape, in_specs=[in_smem] * len(scalar...  28 us
    ppermute x15, starting transfers between devices, across(): return lax.ppermute(value, 'dom', [(i, i ^ bits) for i in range(domains)])  19.6 us
    ppermute x15, waiting for transfers between devices, across(): return lax.ppermute(value, 'dom', [(i, i ^ bits) for i in range(domains)])  16.9 us
    ppermute x1, starting transfers between devices, on_device(): far = lax.ppermute(packed, 'dom', beyond)  4.53 us
  transfers between devices with their start and end apart: 16, of which 9 were waited for; matrix products, arithmetic and copies ran while one was open for 0% of the time, Pallas kernels for 15%

profile of v10, /device:TPU:0, one launch (start us, length us, event | category | flops | bytes accessed | tf_op | source)
XLA Modules:
  0.0 70.1 jit_solution(3664272127238523547)
XLA Ops:
  0.7 1.6 %pack.1 = bf16[288,128]{1,0:T(8,128)(2,1)} custom-call(bf16[256,128]{1,0:T(8,128)(2,1)} %refs_0_.1, f32[3,256]{1,0:T(4,128)} %refs_1_.1, s32[2,256]{1,0:T(2,128)} %ghost_ref.1), custom_call_target="tpu_custom_call" | custom-call | flops 1000000000 | bytes 144384 | tf_op jit(solution)/shard_map/pack/pallas_call | solution.py:586
  2.3 2.9 %collective-permute-start.1 = (bf16[288,128]{1,0:T(8,128)(2,1)}, bf16[288,128]{1,0:T(8,128)(2,1)S(1)}, u32[]{:S(2)}, u32[]{:S(2)}) collective-permute-start(bf16[288,128]{1,0:T(8,128)(2,1)} %pack.1), channel_id=1, source_target_pairs={{0,2},{2,0},{4,6},{6,4},{8,10},{10,8},{12,14},{14,12},{16,18},{18,... | collective-permute-start | bytes 221192 | tf_op jit(solution)/shard_map/ppermute | solution.py:602
  5.3 4.5 %collective-permute-start = (bf16[288,128]{1,0:T(8,128)(2,1)}, bf16[288,128]{1,0:T(8,128)(2,1)S(1)}, u32[]{:S(2)}, u32[]{:S(2)}) collective-permute-start(bf16[288,128]{1,0:T(8,128)(2,1)} %pack.1), channel_id=1, source_target_pairs={{0,30},{2,4},{4,2},{6,8},{8,6},{10,12},{12,10},{14,16},{16,14},{18... | collective-permute-start | bytes 221192 | tf_op jit(solution)/shard_map/ppermute | solution.py:652
  9.9 1.9 %own.1 = (f32[16,128,256]{2,1,0:T(8,128)S(1)}, s32[24,256]{1,0:T(8,128)S(1)}, bf16[128,256]{1,0:T(8,128)(2,1)S(1)}, f32[64,256]{1,0:T(8,128)S(1)}, f32[320,128]{1,0:T(8,128)S(1)}, /*index=5*/f32[24,256]{1,0:T(8,128)S(1)}) custom-call(bf16[256,128]{1,0:T(8,128)(2,1)S(1)} %copy-done, f32[3,256]{1,0:T(4,128)S(1)} %copy-done.5, f32[3,256]{1,0:T(4,128)S(1)} %copy-done.6, ...), custom_call_target="tpu_custom_call" | custom-call | flops 4000000000 | bytes 4740608 | tf_op jit(solution)/shard_map/own/pallas_call | solution.py:586
  11.8 2.5 %near.1.refs_2_ = f32[16,128,256]{2,1,0:T(8,128)S(1)} custom-call(s32[3]{0:T(128)S(1)} %pad_add_fusion.refs_0_, bf16[288,128]{1,0:T(8,128)(2,1)S(1)} %collective-permute-done.1.refs_1_, f32[16,128,256]{2,1,0:T(8,128)S(1)} %get-tuple-element.34.refs_2_, s32[24,256]{1,0:T(8,128)S(1)} %get-tuple-element.35.refs_3_, f32[24,256]{1,0:T(8,128)S(1)} %get-tuple-element.36.refs_4_.refs_7_), custom_call_target="tpu_custom_call" | custom-call | flops 3000000000 | bytes 6430720 | tf_op jit(solution)/shard_map/near/pallas_call | solution.py:586
  14.3 2.9 %edges.1 = (f32[16,128,256]{2,1,0:T(8,128)S(1)}, f32[128,256]{1,0:T(8,128)S(1)}, f32[128,256]{1,0:T(8,128)S(1)}, bf16[128,256]{1,0:T(8,128)(2,1)S(1)}, bf16[1,80,256]{2,1,0:T(8,128)(2,1)S(1)}) custom-call(s32[3]{0:T(128)S(1)} %pad_add_fusion.refs_0_, bf16[288,128]{1,0:T(8,128)(2,1)S(1)} %collective-permute-done.refs_1_, f32[16,128,256]{2,1,0:T(8,128)S(1)} %near.1.refs_2_, ...), custom_call_target="tpu_custom_call" | custom-call | flops 4000000000 | bytes 7094272 | tf_op jit(solution)/shard_map/edges/pallas_call | solution.py:586
  17.3 1.0 %collective-permute-start.4 = (bf16[1,80,256]{2,1,0:T(8,128)(2,1)S(1)}, bf16[1,80,256]{2,1,0:T(8,128)(2,1)S(1)}, u32[]{:S(2)}, u32[]{:S(2)}) collective-permute-start(bf16[1,80,256]{2,1,0:T(8,128)(2,1)S(1)} %get-tuple-element.40), channel_id=1, source_target_pairs={{0,24},{2,26},{4,28},{6,30},{8,16},{10,18},{12,20},{14,22},{16,8},... | collective-permute-start | bytes 122888 | tf_op jit(solution)/shard_map/ppermute | solution.py:602
  18.2 3.5 %collective-permute-start.2 = (bf16[1,80,256]{2,1,0:T(8,128)(2,1)S(1)}, bf16[1,80,256]{2,1,0:T(8,128)(2,1)S(1)}, u32[]{:S(2)}, u32[]{:S(2)}) collective-permute-start(bf16[1,80,256]{2,1,0:T(8,128)(2,1)S(1)} %get-tuple-element.40), channel_id=1, source_target_pairs={{0,8},{2,10},{4,12},{6,14},{8,0},{10,2},{12,4},{14,6},{16,24},{18,... | collective-permute-start | bytes 122888 | tf_op jit(solution)/shard_map/ppermute | solution.py:602
  21.7 2.0 %collective-permute-done.2 = bf16[1,80,256]{2,1,0:T(8,128)(2,1)S(1)} collective-permute-done((bf16[1,80,256]{2,1,0:T(8,128)(2,1)S(1)}, bf16[1,80,256]{2,1,0:T(8,128)(2,1)S(1)}, u32[]{:S(2)}, u32[]{:S(2)}) %collective-permute-start.2) | collective-permute-done | bytes 40992 | tf_op jit(solution)/shard_map/ppermute | solution.py:602
  23.7 0.3 collective-permute-done.3
  24.1 2.5 %collective-permute-start.7 = (bf16[4,80,256]{2,1,0:T(8,128)(2,1)S(1)}, bf16[4,80,256]{2,1,0:T(8,128)(2,1)S(1)}, u32[]{:S(2)}, u32[]{:S(2)}) collective-permute-start(bf16[4,80,256]{2,1,0:T(8,128)(2,1)S(1)} %constant_dynamic-update-slice_fusion.refs_1_), channel_id=1, source_target_pairs={{0,6},{2,4},{4,2},{6,0},{8,14},{10,12},{12,10},{14,8},{16,22},{18,... | collective-permute-start | bytes 491528 | tf_op jit(solution)/shard_map/ppermute | solution.py:602
  26.5 1.1 %collective-permute-start.5 = (bf16[4,80,256]{2,1,0:T(8,128)(2,1)S(1)}, bf16[4,80,256]{2,1,0:T(8,128)(2,1)S(1)}, u32[]{:S(2)}, u32[]{:S(2)}) collective-permute-start(bf16[4,80,256]{2,1,0:T(8,128)(2,1)S(1)} %constant_dynamic-update-slice_fusion.refs_1_), channel_id=1, source_target_pairs={{0,2},{2,0},{4,6},{6,4},{8,10},{10,8},{12,14},{14,12},{16,18},{18,... | collective-permute-start | bytes 491528 | tf_op jit(solution)/shard_map/ppermute | solution.py:602
  27.6 2.7 %phases.2 = (bf16[4,1024,256]{2,1,0:T(8,128)(2,1)S(1)}, f32[64,1024]{1,0:T(8,128)S(1)}) custom-call(s32[3]{0:T(128)S(1)} %pad_add_fusion.refs_0_, bf16[4,80,256]{2,1,0:T(8,128)(2,1)S(1)} %constant_dynamic-update-slice_fusion.refs_1_, s32[3,1024]{1,0:T(4,128)S(1)} %copy-done.3), custom_call_target="tpu_custom_call" | custom-call | flops 3000000000 | bytes 2535424 | tf_op jit(solution)/shard_map/phases/pallas_call | solution.py:586
  30.3 1.0 %collective-permute-done.7.refs_1_.refs_4_ = bf16[4,80,256]{2,1,0:T(8,128)(2,1)S(1)} collective-permute-done((bf16[4,80,256]{2,1,0:T(8,128)(2,1)S(1)}, bf16[4,80,256]{2,1,0:T(8,128)(2,1)S(1)}, u32[]{:S(2)}, u32[]{:S(2)}) %collective-permute-start.7) | collective-permute-done | bytes 163872 | tf_op jit(solution)/shard_map/ppermute | solution.py:602
  31.4 2.7 %phases.3 = (bf16[4,1024,256]{2,1,0:T(8,128)(2,1)S(1)}, f32[64,1024]{1,0:T(8,128)S(1)}) custom-call(s32[3]{0:T(128)S(1)} %pad_add_fusion.refs_0_, bf16[4,80,256]{2,1,0:T(8,128)(2,1)S(1)} %collective-permute-done.7.refs_1_.refs_4_, s32[3,1024]{1,0:T(4,128)S(1)} %copy-done.3), custom_call_target="tpu_custom_call" | custom-call | flops 3000000000 | bytes 2535424 | tf_op jit(solution)/shard_map/phases/pallas_call | solution.py:586
  34.1 6.7 %structure.1 = (bf16[8,1024,256]{2,1,0:T(8,128)(2,1)S(1)}, f32[192,1024]{1,0:T(8,128)S(1)}, f32[3,16,256]{2,1,0:T(8,128)S(1)}, f32[3,16,256]{2,1,0:T(8,128)S(1)}) custom-call(s32[3]{0:T(128)S(1)} %pad_add_fusion.refs_0_, bf16[4,80,256]{2,1,0:T(8,128)(2,1)S(1)} %constant_dynamic-update-slice_fusion.refs_1_, ...), custom_call_target="tpu_custom_call" | custom-call | flops 8000000000 | bytes 10465280 | tf_op jit(solution)/shard_map/structure/pallas_call | solution.py:586
  40.8 0.3 collective-permute-start.8
  41.2 0.6 fields.1
  41.8 3.2 %collective-permute-done.8.refs_6_ = f32[3,16,256]{2,1,0:T(8,128)S(1)} collective-permute-done((f32[3,16,256]{2,1,0:T(8,128)S(1)}, f32[3,16,256]{2,1,0:T(8,128)S(1)}, u32[]{:S(2)}, u32[]{:S(2)}) %collective-permute-start.8) | collective-permute-done | bytes 49184 | tf_op jit(solution)/shard_map/ppermute | solution.py:602
  45.0 4.4 %gradient.1 = (f32[3,256]{1,0:T(4,128)}, f32[8,256]{1,0:T(8,128)S(1)}, f32[64,1024]{1,0:T(8,128)S(1)}, bf16[64,256]{1,0:T(8,128)(2,1)S(1)}) custom-call(s32[3]{0:T(128)S(1)} %pad_add_fusion.refs_0_, bf16[4,80,256]{2,1,0:T(8,128)(2,1)S(1)} %constant_dynamic-update-slice_fusion.refs_1_, bf16[4,80,256]{2,1,0:T(8,128)(2,1)S(1)} %collective-permute-done.5.refs_2_, ...), custom_call_target="tpu_custom_call" | custom-call | flops 5000000000 | bytes 9706496 | tf_op jit(solution)/shard_map/gradient/pallas_call | solution.py:586
  49.6 0.3 own_gradient.1.refs_0_
  50.0 3.6 %collective-permute-done.9.refs_1_ = bf16[64,256]{1,0:T(8,128)(2,1)S(1)} collective-permute-done((bf16[64,256]{1,0:T(8,128)(2,1)S(1)}, bf16[64,256]{1,0:T(8,128)(2,1)S(1)}, u32[]{:S(2)}, u32[]{:S(2)}) %collective-permute-start.9) | collective-permute-done | bytes 32800 | tf_op jit(solution)/shard_map/ppermute | solution.py:602
  53.5 0.9 %weights.1.refs_0_ = bf16[352,128]{1,0:T(8,128)(2,1)S(1)} custom-call(f32[64,256]{1,0:T(8,128)S(1)} %own_gradient.1.refs_0_, bf16[64,256]{1,0:T(8,128)(2,1)S(1)} %collective-permute-done.9.refs_1_, f32[16,128,256]{2,1,0:T(8,128)S(1)} %get-tuple-element.55.refs_2_, f32[128,256]{1,0:T(8,128)S(1)} %get-tuple-element.56.refs_3_, ...), custom_call_target="tpu_custom_call" | custom-call | flops 3000000000 | bytes 2778112 | tf_op jit(solution)/shard_map/weights/pallas_call | solution.py:586
  54.4 1.8 %collective-permute-start.12 = (bf16[352,128]{1,0:T(8,128)(2,1)S(1)}, bf16[352,128]{1,0:T(8,128)(2,1)S(1)}, u32[]{:S(2)}, u32[]{:S(2)}) collective-permute-start(bf16[352,128]{1,0:T(8,128)(2,1)S(1)} %weights.1.refs_0_), channel_id=1, source_target_pairs={{0,6},{2,4},{4,2},{6,0},{8,14},{10,12},{12,10},{14,8},{16,22},{18,... | collective-permute-start | bytes 270344 | tf_op jit(solution)/shard_map/ppermute | solution.py:602
  56.2 1.7 %collective-permute-start.10 = (bf16[352,128]{1,0:T(8,128)(2,1)S(1)}, bf16[352,128]{1,0:T(8,128)(2,1)S(1)}, u32[]{:S(2)}, u32[]{:S(2)}) collective-permute-start(bf16[352,128]{1,0:T(8,128)(2,1)S(1)} %weights.1.refs_0_), channel_id=1, source_target_pairs={{0,2},{2,0},{4,6},{6,4},{8,10},{10,8},{12,14},{14,12},{16,18},{18,... | collective-permute-start | bytes 270344 | tf_op jit(solution)/shard_map/ppermute | solution.py:602
  57.9 1.9 %collective-permute-done.12.refs_3_ = bf16[352,128]{1,0:T(8,128)(2,1)S(1)} collective-permute-done((bf16[352,128]{1,0:T(8,128)(2,1)S(1)}, bf16[352,128]{1,0:T(8,128)(2,1)S(1)}, u32[]{:S(2)}, u32[]{:S(2)}) %collective-permute-start.12) | collective-permute-done | bytes 90144 | tf_op jit(solution)/shard_map/ppermute | solution.py:602
  59.9 1.0 %collective-permute-done.11.refs_2_ = bf16[352,128]{1,0:T(8,128)(2,1)S(1)} collective-permute-done((bf16[352,128]{1,0:T(8,128)(2,1)S(1)}, bf16[352,128]{1,0:T(8,128)(2,1)S(1)}, u32[]{:S(2)}, u32[]{:S(2)}) %collective-permute-start.11) | collective-permute-done | bytes 90144 | tf_op jit(solution)/shard_map/ppermute | solution.py:602
  60.9 2.4 %collective-permute-start.15 = (bf16[352,128]{1,0:T(8,128)(2,1)S(1)}, bf16[352,128]{1,0:T(8,128)(2,1)S(1)}, u32[]{:S(2)}, u32[]{:S(2)}) collective-permute-start(bf16[352,128]{1,0:T(8,128)(2,1)S(1)} %halves.1.refs_0_), channel_id=1, source_target_pairs={{0,24},{2,26},{4,28},{6,30},{8,16},{10,18},{12,20},{14,22},{16,8},... | collective-permute-start | bytes 270344 | tf_op jit(solution)/shard_map/ppermute | solution.py:602
  63.3 2.1 %collective-permute-start.13 = (bf16[352,128]{1,0:T(8,128)(2,1)S(1)}, bf16[352,128]{1,0:T(8,128)(2,1)S(1)}, u32[]{:S(2)}, u32[]{:S(2)}) collective-permute-start(bf16[352,128]{1,0:T(8,128)(2,1)S(1)} %halves.1.refs_0_), channel_id=1, source_target_pairs={{0,8},{2,10},{4,12},{6,14},{8,0},{10,2},{12,4},{14,6},{16,24},{18,... | collective-permute-start | bytes 270344 | tf_op jit(solution)/shard_map/ppermute | solution.py:602
  65.3 2.0 %collective-permute-done.15.refs_3_ = bf16[352,128]{1,0:T(8,128)(2,1)S(1)} collective-permute-done((bf16[352,128]{1,0:T(8,128)(2,1)S(1)}, bf16[352,128]{1,0:T(8,128)(2,1)S(1)}, u32[]{:S(2)}, u32[]{:S(2)}) %collective-permute-start.15) | collective-permute-done | bytes 90144 | tf_op jit(solution)/shard_map/ppermute | solution.py:602
  67.3 1.9 %collective-permute-done.14.refs_2_ = bf16[352,128]{1,0:T(8,128)(2,1)S(1)} collective-permute-done((bf16[352,128]{1,0:T(8,128)(2,1)S(1)}, bf16[352,128]{1,0:T(8,128)(2,1)S(1)}, u32[]{:S(2)}, u32[]{:S(2)}) %collective-permute-start.14) | collective-permute-done | bytes 90144 | tf_op jit(solution)/shard_map/ppermute | solution.py:602
  69.2 0.8 %steps.1 = (f32[16,128]{1,0:T(8,128)}, f32[128,128]{1,0:T(8,128)}, f32[64,128]{1,0:T(8,128)}, f32[6,64]{1,0:T(8,128)}) custom-call(bf16[352,128]{1,0:T(8,128)(2,1)S(1)} %halves.1.refs_0_, bf16[352,128]{1,0:T(8,128)(2,1)S(1)} %collective-permute-done.13.refs_1_, bf16[352,128]{1,0:T(8,128)(2,1)S(1)} %collective-permute-done.14.refs_2_, ...), custom_call_target="tpu_custom_call" | custom-call | flops 2000000000 | bytes 583168 | tf_op jit(solution)/shard_map/steps/pallas_call | solution.py:586
  (40 shorter events, 0.5 us)
Async XLA Ops:
  0.6 9.2 %copy-start.5 = (f32[3,256]{1,0:T(4,128)S(1)}, f32[3,256]{1,0:T(4,128)}, u32[]{:S(2)}) copy-start(f32[3,256]{1,0:T(4,128)} %refs_1_.1) | copy-start | bytes 9220
  0.6 9.1 %copy-start = (bf16[256,128]{1,0:T(8,128)(2,1)S(1)}, bf16[256,128]{1,0:T(8,128)(2,1)}, u32[]{:S(2)}) copy-start(bf16[256,128]{1,0:T(8,128)(2,1)} %refs_0_.1) | copy-start | bytes 196612
  0.7 9.1 %copy-start.2 = (bf16[128,128]{1,0:T(8,128)(2,1)S(1)}, bf16[128,128]{1,0:T(8,128)(2,1)}, u32[]{:S(2)}) copy-start(bf16[128,128]{1,0:T(8,128)(2,1)} %refs_7_.3) | copy-start | bytes 98308
  0.7 9.1 %copy-start.8 = (f32[6,64]{1,0:T(8,128)S(1)}, f32[6,64]{1,0:T(8,128)}, u32[]{:S(2)}) copy-start(f32[6,64]{1,0:T(8,128)} %refs_9_.2) | copy-start | bytes 4612
  0.7 9.1 %copy-start.4 = (bf16[128,64]{0,1:T(8,128)(2,1)S(1)}, bf16[128,64]{0,1:T(8,128)(2,1)}, u32[]{:S(2)}) copy-start(bf16[128,64]{0,1:T(8,128)(2,1)} %param.22) | copy-start | bytes 49156
  0.7 9.1 %copy-start.7 = (bf16[16,128]{1,0:T(8,128)(2,1)S(1)}, bf16[16,128]{1,0:T(8,128)(2,1)}, u32[]{:S(2)}) copy-start(bf16[16,128]{1,0:T(8,128)(2,1)} %refs_6_.1) | copy-start | bytes 12292
  0.7 9.1 %copy-start.6 = (f32[3,256]{1,0:T(4,128)S(1)}, f32[3,256]{1,0:T(4,128)}, u32[]{:S(2)}) copy-start(f32[3,256]{1,0:T(4,128)} %refs_2_.3) | copy-start | bytes 9220
  0.7 9.1 %copy-start.10 = (s32[256]{0:T(256)S(1)}, s32[256]{0:T(256)}, u32[]{:S(2)}) copy-start(s32[256]{0:T(256)} %param.17) | copy-start | bytes 3076
  0.7 9.1 %copy-start.9 = (s32[256]{0:T(256)S(1)}, s32[256]{0:T(256)}, u32[]{:S(2)}) copy-start(s32[256]{0:T(256)} %param.15) | copy-start | bytes 3076
  0.7 9.1 %copy-start.1 = (s32[256,64]{0,1:T(8,128)S(1)}, s32[256,64]{0,1:T(8,128)}, u32[]{:S(2)}) copy-start(s32[256,64]{0,1:T(8,128)} %param.14) | copy-start | bytes 196612
  2.3 9.5 %collective-permute-start.1 = (bf16[288,128]{1,0:T(8,128)(2,1)}, bf16[288,128]{1,0:T(8,128)(2,1)S(1)}, u32[]{:S(2)}, u32[]{:S(2)}) collective-permute-start(bf16[288,128]{1,0:T(8,128)(2,1)} %pack.1), channel_id=1, source_target_pairs={{0,2},{2,0},{4,6},{6,4},{8,10},{10,8},{12,14},{14,12},{16,18},{18,... | collective-permute-start | bytes 221192 | tf_op jit(solution)/shard_map/ppermute | solution.py:602
  5.3 9.1 %collective-permute-start = (bf16[288,128]{1,0:T(8,128)(2,1)}, bf16[288,128]{1,0:T(8,128)(2,1)S(1)}, u32[]{:S(2)}, u32[]{:S(2)}) collective-permute-start(bf16[288,128]{1,0:T(8,128)(2,1)} %pack.1), channel_id=1, source_target_pairs={{0,30},{2,4},{4,2},{6,8},{8,6},{10,12},{12,10},{14,16},{16,14},{18... | collective-permute-start | bytes 221192 | tf_op jit(solution)/shard_map/ppermute | solution.py:652
  14.3 13.3 %copy-start.3 = (s32[3,1024]{1,0:T(4,128)S(1)}, s32[3,1024]{1,0:T(4,128)}, u32[]{:S(2)}) copy-start(s32[3,1024]{1,0:T(4,128)} %refs_10_.1) | copy-start | bytes 36868
  17.3 6.8 %collective-permute-start.4 = (bf16[1,80,256]{2,1,0:T(8,128)(2,1)S(1)}, bf16[1,80,256]{2,1,0:T(8,128)(2,1)S(1)}, u32[]{:S(2)}, u32[]{:S(2)}) collective-permute-start(bf16[1,80,256]{2,1,0:T(8,128)(2,1)S(1)} %get-tuple-element.40), channel_id=1, source_target_pairs={{0,24},{2,26},{4,28},{6,30},{8,16},{10,18},{12,20},{14,22},{16,8},... | collective-permute-start | bytes 122888 | tf_op jit(solution)/shard_map/ppermute | solution.py:602
  18.2 5.8 %collective-permute-start.3 = (bf16[1,80,256]{2,1,0:T(8,128)(2,1)S(1)}, bf16[1,80,256]{2,1,0:T(8,128)(2,1)S(1)}, u32[]{:S(2)}, u32[]{:S(2)}) collective-permute-start(bf16[1,80,256]{2,1,0:T(8,128)(2,1)S(1)} %get-tuple-element.40), channel_id=1, source_target_pairs={{0,16},{2,18},{4,20},{6,22},{8,24},{10,26},{12,28},{14,30},{16,0},... | collective-permute-start | bytes 122888 | tf_op jit(solution)/shard_map/ppermute | solution.py:602
  18.2 5.5 %collective-permute-start.2 = (bf16[1,80,256]{2,1,0:T(8,128)(2,1)S(1)}, bf16[1,80,256]{2,1,0:T(8,128)(2,1)S(1)}, u32[]{:S(2)}, u32[]{:S(2)}) collective-permute-start(bf16[1,80,256]{2,1,0:T(8,128)(2,1)S(1)} %get-tuple-element.40), channel_id=1, source_target_pairs={{0,8},{2,10},{4,12},{6,14},{8,0},{10,2},{12,4},{14,6},{16,24},{18,... | collective-permute-start | bytes 122888 | tf_op jit(solution)/shard_map/ppermute | solution.py:602
  24.1 7.3 %collective-permute-start.7 = (bf16[4,80,256]{2,1,0:T(8,128)(2,1)S(1)}, bf16[4,80,256]{2,1,0:T(8,128)(2,1)S(1)}, u32[]{:S(2)}, u32[]{:S(2)}) collective-permute-start(bf16[4,80,256]{2,1,0:T(8,128)(2,1)S(1)} %constant_dynamic-update-slice_fusion.refs_1_), channel_id=1, source_target_pairs={{0,6},{2,4},{4,2},{6,0},{8,14},{10,12},{12,10},{14,8},{16,22},{18,... | collective-permute-start | bytes 491528 | tf_op jit(solution)/shard_map/ppermute | solution.py:602
  26.5 7.6 %collective-permute-start.6 = (bf16[4,80,256]{2,1,0:T(8,128)(2,1)S(1)}, bf16[4,80,256]{2,1,0:T(8,128)(2,1)S(1)}, u32[]{:S(2)}, u32[]{:S(2)}) collective-permute-start(bf16[4,80,256]{2,1,0:T(8,128)(2,1)S(1)} %constant_dynamic-update-slice_fusion.refs_1_), channel_id=1, source_target_pairs={{0,4},{2,6},{4,0},{6,2},{8,12},{10,14},{12,8},{14,10},{16,20},{18,... | collective-permute-start | bytes 491528 | tf_op jit(solution)/shard_map/ppermute | solution.py:602
  26.5 7.6 %collective-permute-start.5 = (bf16[4,80,256]{2,1,0:T(8,128)(2,1)S(1)}, bf16[4,80,256]{2,1,0:T(8,128)(2,1)S(1)}, u32[]{:S(2)}, u32[]{:S(2)}) collective-permute-start(bf16[4,80,256]{2,1,0:T(8,128)(2,1)S(1)} %constant_dynamic-update-slice_fusion.refs_1_), channel_id=1, source_target_pairs={{0,2},{2,0},{4,6},{6,4},{8,10},{10,8},{12,14},{14,12},{16,18},{18,... | collective-permute-start | bytes 491528 | tf_op jit(solution)/shard_map/ppermute | solution.py:602
  40.8 4.2 %collective-permute-start.8 = (f32[3,16,256]{2,1,0:T(8,128)S(1)}, f32[3,16,256]{2,1,0:T(8,128)S(1)}, u32[]{:S(2)}, u32[]{:S(2)}) collective-permute-start(f32[3,16,256]{2,1,0:T(8,128)S(1)} %get-tuple-element.46), channel_id=1, source_target_pairs={{0,2},{2,0},{4,6},{6,4},{8,10},{10,8},{12,14},{14,12},{16,18},{18,... | collective-permute-start | bytes 147464 | tf_op jit(solution)/shard_map/ppermute | solution.py:602
  49.4 4.2 %collective-permute-start.9 = (bf16[64,256]{1,0:T(8,128)(2,1)S(1)}, bf16[64,256]{1,0:T(8,128)(2,1)S(1)}, u32[]{:S(2)}, u32[]{:S(2)}) collective-permute-start(bf16[64,256]{1,0:T(8,128)(2,1)S(1)} %get-tuple-element.54), channel_id=1, source_target_pairs={{0,2},{2,0},{4,6},{6,4},{8,10},{10,8},{12,14},{14,12},{16,18},{18,... | collective-permute-start | bytes 98312 | tf_op jit(solution)/shard_map/ppermute | solution.py:602
  54.4 5.5 %collective-permute-start.12 = (bf16[352,128]{1,0:T(8,128)(2,1)S(1)}, bf16[352,128]{1,0:T(8,128)(2,1)S(1)}, u32[]{:S(2)}, u32[]{:S(2)}) collective-permute-start(bf16[352,128]{1,0:T(8,128)(2,1)S(1)} %weights.1.refs_0_), channel_id=1, source_target_pairs={{0,6},{2,4},{4,2},{6,0},{8,14},{10,12},{12,10},{14,8},{16,22},{18,... | collective-permute-start | bytes 270344 | tf_op jit(solution)/shard_map/ppermute | solution.py:602
  56.2 4.7 %collective-permute-start.11 = (bf16[352,128]{1,0:T(8,128)(2,1)S(1)}, bf16[352,128]{1,0:T(8,128)(2,1)S(1)}, u32[]{:S(2)}, u32[]{:S(2)}) collective-permute-start(bf16[352,128]{1,0:T(8,128)(2,1)S(1)} %weights.1.refs_0_), channel_id=1, source_target_pairs={{0,4},{2,6},{4,0},{6,2},{8,12},{10,14},{12,8},{14,10},{16,20},{18,... | collective-permute-start | bytes 270344 | tf_op jit(solution)/shard_map/ppermute | solution.py:602
  56.2 4.7 %collective-permute-start.10 = (bf16[352,128]{1,0:T(8,128)(2,1)S(1)}, bf16[352,128]{1,0:T(8,128)(2,1)S(1)}, u32[]{:S(2)}, u32[]{:S(2)}) collective-permute-start(bf16[352,128]{1,0:T(8,128)(2,1)S(1)} %weights.1.refs_0_), channel_id=1, source_target_pairs={{0,2},{2,0},{4,6},{6,4},{8,10},{10,8},{12,14},{14,12},{16,18},{18,... | collective-permute-start | bytes 270344 | tf_op jit(solution)/shard_map/ppermute | solution.py:602
  60.9 6.4 %collective-permute-start.15 = (bf16[352,128]{1,0:T(8,128)(2,1)S(1)}, bf16[352,128]{1,0:T(8,128)(2,1)S(1)}, u32[]{:S(2)}, u32[]{:S(2)}) collective-permute-start(bf16[352,128]{1,0:T(8,128)(2,1)S(1)} %halves.1.refs_0_), channel_id=1, source_target_pairs={{0,24},{2,26},{4,28},{6,30},{8,16},{10,18},{12,20},{14,22},{16,8},... | collective-permute-start | bytes 270344 | tf_op jit(solution)/shard_map/ppermute | solution.py:602
  63.3 5.9 %collective-permute-start.14 = (bf16[352,128]{1,0:T(8,128)(2,1)S(1)}, bf16[352,128]{1,0:T(8,128)(2,1)S(1)}, u32[]{:S(2)}, u32[]{:S(2)}) collective-permute-start(bf16[352,128]{1,0:T(8,128)(2,1)S(1)} %halves.1.refs_0_), channel_id=1, source_target_pairs={{0,16},{2,18},{4,20},{6,22},{8,24},{10,26},{12,28},{14,30},{16,0},... | collective-permute-start | bytes 270344 | tf_op jit(solution)/shard_map/ppermute | solution.py:602
  63.3 5.9 %collective-permute-start.13 = (bf16[352,128]{1,0:T(8,128)(2,1)S(1)}, bf16[352,128]{1,0:T(8,128)(2,1)S(1)}, u32[]{:S(2)}, u32[]{:S(2)}) collective-permute-start(bf16[352,128]{1,0:T(8,128)(2,1)S(1)} %halves.1.refs_0_), channel_id=1, source_target_pairs={{0,8},{2,10},{4,12},{6,14},{8,0},{10,2},{12,4},{14,6},{16,24},{18,... | collective-permute-start | bytes 270344 | tf_op jit(solution)/shard_map/ppermute | solution.py:602

commit v11 on v10

--- a/solution.py
+++ b/solution.py
@@ -89,7 +89,7 @@
         packed_ref[first : first + 16, :] = extra[:, part * width : (part + 1) * width]
 
 
-def pair_blocks(count, coords_ref, own_rows, words_ref, pair_ref, box_x):
+def pair_blocks(count, coords_ref, own_rows, words_ref, pair_ref, box_x, rest_ref=None):
     basis_count, _, atoms = pair_ref.shape
     centers = [
         0.5 + (cutoff_radius - 0.5) * float(b) / (basis_count - 1) for b in range(basis_count)
@@ -128,7 +128,11 @@
                     running = running * ratio
                 basis = running * math.exp(-(((b - middle) * gap / basis_width) ** 2))
                 basis = basis.astype(bf16).astype(f32)
-                pair_ref[b, places, :] = (weight * basis).astype(bf16)
+                pair = weight * basis
+                high = pair.astype(bf16)
+                pair_ref[b, places, :] = high
+                if rest_ref is not None:
+                    rest_ref[b, places, :] = (pair - high.astype(f32)).astype(bf16)
         return carry
 
     lax.fori_loop(0, count // step, block, 0, unroll=8)
@@ -153,6 +157,7 @@
     extra_ref,
     coords_ref,
     pair_ref,
+    rest_ref,
     *,
     box_x,
 ):
@@ -178,9 +183,9 @@
             value = value[:rows] | value[rows:]
         words_ref[word : word + 1, :] = value
 
-    pair_blocks(atoms, coords_ref, own_rows, words_ref, pair_ref, box_x)
+    pair_blocks(atoms, coords_ref, own_rows, words_ref, pair_ref, box_x, rest_ref)
     for b in range(basis_count):
-        filtered_ref[b] = matmul(own_feat, pair_ref[b])
+        filtered_ref[b] = matmul(own_feat, pair_ref[b]) + matmul(own_feat, rest_ref[b])
 
     kinds = offset_ref.shape[0]
     one_hot = (
@@ -499,10 +504,10 @@
     value_ref[first : first + count, :] += total[rows:, :]
 
 
-def halves_kernel(*refs, first, count):
+def rounded_kernel(*refs, first, count):
     *part_refs, sums_ref, value_ref = refs
     joined_rows(part_refs, first, count, value_ref)
-    split_rows(value_ref[...], first, count, sums_ref)
+    sums_ref[...] = value_ref[...].astype(bf16)
 
 
 def weights_kernel(*refs, group, kinds):
@@ -558,7 +563,7 @@
     basis_count, width = radial_ref.shape
     charge_count = charge_ref.shape[0]
     kinds = species_ref.shape[0]
-    joined_rows(total_refs, basis_count, width, total_ref)
+    total_ref[...] = summed([ref[...].astype(f32) for ref in total_refs])
 
     def normalized(gradient):
         mean = jnp.sum(gradient * gradient, keepdims=True) * (1.0 / gradient.size)
@@ -668,6 +673,7 @@
         (
             shaped(atoms, 8),
             shaped(basis_count, atoms, atoms, kind=bf16),
+            shaped(basis_count, atoms, atoms, kind=bf16),
         ),
         4_000,
         features,
@@ -825,9 +831,9 @@
         charge_rows,
     )
     packed = kernel(
-        lambda *refs: halves_kernel(*refs, first=basis_count, count=width),
-        "halves",
-        shaped(rows + width, width, kind=bf16),
+        lambda *refs: rounded_kernel(*refs, first=basis_count, count=width),
+        "rounded",
+        shaped(rows, width, kind=bf16),
         (shaped(rows, width),),
         1_000,
         packed,

time: 70.2 us -> 69.6 us (level)
  waiting for transfers between devices: 16.9 us -> 15.6 us
    ppermute x15, waiting for transfers between devices: 16.9 us -> 15.6 us  [across(): return lax.ppermute(value, 'dom', [(i, i ^ bits) for i in range(domains)])]
  transfers between devices with their start and end apart: 16 -> 16, of which waited for: 9 -> 8; matrix products, arithmetic and copies ran while one was open for 0% -> 0% of each run, Pallas kernels for 15% -> 16%
where the time goes in v11:
time: 69.6 us; the launch traced here: 69.4 us
  Pallas kernels  28.5 us (41%)
  starting transfers between devices  24.4 us (35%)
  waiting for transfers between devices  15.6 us (22%)
  between operations  0.89 us (1%)
    pallas_call x13, Pallas kernels, kernel(): pl.pallas_call(body, out_shape=out_shape, in_specs=[in_smem] * len(scalar...  28.5 us
    ppermute x15, starting transfers between devices, across(): return lax.ppermute(value, 'dom', [(i, i ^ bits) for i in range(domains)])  19.9 us
    ppermute x15, waiting for transfers between devices, across(): return lax.ppermute(value, 'dom', [(i, i ^ bits) for i in range(domains)])  15.6 us
    ppermute x1, starting transfers between devices, on_device(): far = lax.ppermute(packed, 'dom', beyond)  4.53 us
  transfers between devices with their start and end apart: 16, of which 8 were waited for; matrix products, arithmetic and copies ran while one was open for 0% of the time, Pallas kernels for 16%

profile of v11, /device:TPU:0, one launch (start us, length us, event | category | flops | bytes accessed | tf_op | source)
XLA Modules:
  0.0 69.4 jit_solution(3001659349885535025)
XLA Ops:
  0.7 1.6 %pack.1 = bf16[288,128]{1,0:T(8,128)(2,1)} custom-call(bf16[256,128]{1,0:T(8,128)(2,1)} %refs_0_.1, f32[3,256]{1,0:T(4,128)} %refs_1_.1, s32[2,256]{1,0:T(2,128)} %ghost_ref.1), custom_call_target="tpu_custom_call" | custom-call | flops 1000000000 | bytes 144384 | tf_op jit(solution)/shard_map/pack/pallas_call | solution.py:591
  2.3 2.9 %collective-permute-start.1 = (bf16[288,128]{1,0:T(8,128)(2,1)}, bf16[288,128]{1,0:T(8,128)(2,1)S(1)}, u32[]{:S(2)}, u32[]{:S(2)}) collective-permute-start(bf16[288,128]{1,0:T(8,128)(2,1)} %pack.1), channel_id=1, source_target_pairs={{0,2},{2,0},{4,6},{6,4},{8,10},{10,8},{12,14},{14,12},{16,18},{18,... | collective-permute-start | bytes 221192 | tf_op jit(solution)/shard_map/ppermute | solution.py:607
  5.3 4.5 %collective-permute-start = (bf16[288,128]{1,0:T(8,128)(2,1)}, bf16[288,128]{1,0:T(8,128)(2,1)S(1)}, u32[]{:S(2)}, u32[]{:S(2)}) collective-permute-start(bf16[288,128]{1,0:T(8,128)(2,1)} %pack.1), channel_id=1, source_target_pairs={{0,30},{2,4},{4,2},{6,8},{8,6},{10,12},{12,10},{14,16},{16,14},{18... | collective-permute-start | bytes 221192 | tf_op jit(solution)/shard_map/ppermute | solution.py:657
  9.9 2.3 %own.1 = (f32[16,128,256]{2,1,0:T(8,128)S(1)}, s32[24,256]{1,0:T(8,128)S(1)}, bf16[128,256]{1,0:T(8,128)(2,1)S(1)}, f32[64,256]{1,0:T(8,128)S(1)}, f32[320,128]{1,0:T(8,128)S(1)}, /*index=5*/f32[24,256]{1,0:T(8,128)S(1)}) custom-call(bf16[256,128]{1,0:T(8,128)(2,1)S(1)} %copy-done, f32[3,256]{1,0:T(4,128)S(1)} %copy-done.5, f32[3,256]{1,0:T(4,128)S(1)} %copy-done.6, ...), custom_call_target="tpu_custom_call" | custom-call | flops 4000000000 | bytes 6837760 | tf_op jit(solution)/shard_map/own/pallas_call | solution.py:591
  12.3 2.5 %near.1.refs_2_ = f32[16,128,256]{2,1,0:T(8,128)S(1)} custom-call(s32[3]{0:T(128)S(1)} %pad_add_fusion.refs_0_, bf16[288,128]{1,0:T(8,128)(2,1)S(1)} %collective-permute-done.1.refs_1_, f32[16,128,256]{2,1,0:T(8,128)S(1)} %get-tuple-element.34.refs_2_, s32[24,256]{1,0:T(8,128)S(1)} %get-tuple-element.35.refs_3_, f32[24,256]{1,0:T(8,128)S(1)} %get-tuple-element.36.refs_4_.refs_7_), custom_call_target="tpu_custom_call" | custom-call | flops 3000000000 | bytes 6430720 | tf_op jit(solution)/shard_map/near/pallas_call | solution.py:591
  14.8 2.9 %edges.1 = (f32[16,128,256]{2,1,0:T(8,128)S(1)}, f32[128,256]{1,0:T(8,128)S(1)}, f32[128,256]{1,0:T(8,128)S(1)}, bf16[128,256]{1,0:T(8,128)(2,1)S(1)}, bf16[1,80,256]{2,1,0:T(8,128)(2,1)S(1)}) custom-call(s32[3]{0:T(128)S(1)} %pad_add_fusion.refs_0_, bf16[288,128]{1,0:T(8,128)(2,1)S(1)} %collective-permute-done.refs_1_, f32[16,128,256]{2,1,0:T(8,128)S(1)} %near.1.refs_2_, ...), custom_call_target="tpu_custom_call" | custom-call | flops 4000000000 | bytes 7094272 | tf_op jit(solution)/shard_map/edges/pallas_call | solution.py:591
  17.7 0.5 collective-permute-start.4
  18.2 3.9 %collective-permute-start.2 = (bf16[1,80,256]{2,1,0:T(8,128)(2,1)S(1)}, bf16[1,80,256]{2,1,0:T(8,128)(2,1)S(1)}, u32[]{:S(2)}, u32[]{:S(2)}) collective-permute-start(bf16[1,80,256]{2,1,0:T(8,128)(2,1)S(1)} %get-tuple-element.40), channel_id=1, source_target_pairs={{0,8},{2,10},{4,12},{6,14},{8,0},{10,2},{12,4},{14,6},{16,24},{18,... | collective-permute-start | bytes 122888 | tf_op jit(solution)/shard_map/ppermute | solution.py:607
  22.2 2.0 %collective-permute-done.2 = bf16[1,80,256]{2,1,0:T(8,128)(2,1)S(1)} collective-permute-done((bf16[1,80,256]{2,1,0:T(8,128)(2,1)S(1)}, bf16[1,80,256]{2,1,0:T(8,128)(2,1)S(1)}, u32[]{:S(2)}, u32[]{:S(2)}) %collective-permute-start.2) | collective-permute-done | bytes 40992 | tf_op jit(solution)/shard_map/ppermute | solution.py:607
  24.2 2.3 %collective-permute-start.7 = (bf16[4,80,256]{2,1,0:T(8,128)(2,1)S(1)}, bf16[4,80,256]{2,1,0:T(8,128)(2,1)S(1)}, u32[]{:S(2)}, u32[]{:S(2)}) collective-permute-start(bf16[4,80,256]{2,1,0:T(8,128)(2,1)S(1)} %constant_dynamic-update-slice_fusion.refs_1_), channel_id=1, source_target_pairs={{0,6},{2,4},{4,2},{6,0},{8,14},{10,12},{12,10},{14,8},{16,22},{18,... | collective-permute-start | bytes 491528 | tf_op jit(solution)/shard_map/ppermute | solution.py:607
  26.5 1.2 %collective-permute-start.5 = (bf16[4,80,256]{2,1,0:T(8,128)(2,1)S(1)}, bf16[4,80,256]{2,1,0:T(8,128)(2,1)S(1)}, u32[]{:S(2)}, u32[]{:S(2)}) collective-permute-start(bf16[4,80,256]{2,1,0:T(8,128)(2,1)S(1)} %constant_dynamic-update-slice_fusion.refs_1_), channel_id=1, source_target_pairs={{0,2},{2,0},{4,6},{6,4},{8,10},{10,8},{12,14},{14,12},{16,18},{18,... | collective-permute-start | bytes 491528 | tf_op jit(solution)/shard_map/ppermute | solution.py:607
  27.8 2.7 %phases.2 = (bf16[4,1024,256]{2,1,0:T(8,128)(2,1)S(1)}, f32[64,1024]{1,0:T(8,128)S(1)}) custom-call(s32[3]{0:T(128)S(1)} %pad_add_fusion.refs_0_, bf16[4,80,256]{2,1,0:T(8,128)(2,1)S(1)} %constant_dynamic-update-slice_fusion.refs_1_, s32[3,1024]{1,0:T(4,128)S(1)} %copy-done.3), custom_call_target="tpu_custom_call" | custom-call | flops 3000000000 | bytes 2535424 | tf_op jit(solution)/shard_map/phases/pallas_call | solution.py:591
  30.5 0.6 collective-permute-done.7.refs_1_.refs_4_
  31.1 2.7 %phases.3 = (bf16[4,1024,256]{2,1,0:T(8,128)(2,1)S(1)}, f32[64,1024]{1,0:T(8,128)S(1)}) custom-call(s32[3]{0:T(128)S(1)} %pad_add_fusion.refs_0_, bf16[4,80,256]{2,1,0:T(8,128)(2,1)S(1)} %collective-permute-done.7.refs_1_.refs_4_, s32[3,1024]{1,0:T(4,128)S(1)} %copy-done.3), custom_call_target="tpu_custom_call" | custom-call | flops 3000000000 | bytes 2535424 | tf_op jit(solution)/shard_map/phases/pallas_call | solution.py:591
  33.9 6.7 %structure.1 = (bf16[8,1024,256]{2,1,0:T(8,128)(2,1)S(1)}, f32[192,1024]{1,0:T(8,128)S(1)}, f32[3,16,256]{2,1,0:T(8,128)S(1)}, f32[3,16,256]{2,1,0:T(8,128)S(1)}) custom-call(s32[3]{0:T(128)S(1)} %pad_add_fusion.refs_0_, bf16[4,80,256]{2,1,0:T(8,128)(2,1)S(1)} %constant_dynamic-update-slice_fusion.refs_1_, ...), custom_call_target="tpu_custom_call" | custom-call | flops 8000000000 | bytes 10465280 | tf_op jit(solution)/shard_map/structure/pallas_call | solution.py:591
  40.6 0.5 collective-permute-start.8
  41.1 0.6 fields.1
  41.7 3.1 %collective-permute-done.8.refs_6_ = f32[3,16,256]{2,1,0:T(8,128)S(1)} collective-permute-done((f32[3,16,256]{2,1,0:T(8,128)S(1)}, f32[3,16,256]{2,1,0:T(8,128)S(1)}, u32[]{:S(2)}, u32[]{:S(2)}) %collective-permute-start.8) | collective-permute-done | bytes 49184 | tf_op jit(solution)/shard_map/ppermute | solution.py:607
  44.7 4.4 %gradient.1 = (f32[3,256]{1,0:T(4,128)}, f32[8,256]{1,0:T(8,128)S(1)}, f32[64,1024]{1,0:T(8,128)S(1)}, bf16[64,256]{1,0:T(8,128)(2,1)S(1)}) custom-call(s32[3]{0:T(128)S(1)} %pad_add_fusion.refs_0_, bf16[4,80,256]{2,1,0:T(8,128)(2,1)S(1)} %constant_dynamic-update-slice_fusion.refs_1_, bf16[4,80,256]{2,1,0:T(8,128)(2,1)S(1)} %collective-permute-done.5.refs_2_, ...), custom_call_target="tpu_custom_call" | custom-call | flops 5000000000 | bytes 9706496 | tf_op jit(solution)/shard_map/gradient/pallas_call | solution.py:591
  49.1 0.4 collective-permute-start.9
  49.9 3.2 %collective-permute-done.9.refs_1_ = bf16[64,256]{1,0:T(8,128)(2,1)S(1)} collective-permute-done((bf16[64,256]{1,0:T(8,128)(2,1)S(1)}, bf16[64,256]{1,0:T(8,128)(2,1)S(1)}, u32[]{:S(2)}, u32[]{:S(2)}) %collective-permute-start.9) | collective-permute-done | bytes 32800 | tf_op jit(solution)/shard_map/ppermute | solution.py:607
  53.0 0.9 %weights.1.refs_0_ = bf16[352,128]{1,0:T(8,128)(2,1)S(1)} custom-call(f32[64,256]{1,0:T(8,128)S(1)} %own_gradient.1.refs_0_, bf16[64,256]{1,0:T(8,128)(2,1)S(1)} %collective-permute-done.9.refs_1_, f32[16,128,256]{2,1,0:T(8,128)S(1)} %get-tuple-element.55.refs_2_, f32[128,256]{1,0:T(8,128)S(1)} %get-tuple-element.56.refs_3_, ...), custom_call_target="tpu_custom_call" | custom-call | flops 3000000000 | bytes 2778112 | tf_op jit(solution)/shard_map/weights/pallas_call | solution.py:591
  53.9 2.1 %collective-permute-start.12 = (bf16[352,128]{1,0:T(8,128)(2,1)S(1)}, bf16[352,128]{1,0:T(8,128)(2,1)S(1)}, u32[]{:S(2)}, u32[]{:S(2)}) collective-permute-start(bf16[352,128]{1,0:T(8,128)(2,1)S(1)} %weights.1.refs_0_), channel_id=1, source_target_pairs={{0,6},{2,4},{4,2},{6,0},{8,14},{10,12},{12,10},{14,8},{16,22},{18,... | collective-permute-start | bytes 270344 | tf_op jit(solution)/shard_map/ppermute | solution.py:607
  56.0 1.4 %collective-permute-start.10 = (bf16[352,128]{1,0:T(8,128)(2,1)S(1)}, bf16[352,128]{1,0:T(8,128)(2,1)S(1)}, u32[]{:S(2)}, u32[]{:S(2)}) collective-permute-start(bf16[352,128]{1,0:T(8,128)(2,1)S(1)} %weights.1.refs_0_), channel_id=1, source_target_pairs={{0,2},{2,0},{4,6},{6,4},{8,10},{10,8},{12,14},{14,12},{16,18},{18,... | collective-permute-start | bytes 270344 | tf_op jit(solution)/shard_map/ppermute | solution.py:607
  57.4 1.9 %collective-permute-done.12.refs_3_ = bf16[352,128]{1,0:T(8,128)(2,1)S(1)} collective-permute-done((bf16[352,128]{1,0:T(8,128)(2,1)S(1)}, bf16[352,128]{1,0:T(8,128)(2,1)S(1)}, u32[]{:S(2)}, u32[]{:S(2)}) %collective-permute-start.12) | collective-permute-done | bytes 90144 | tf_op jit(solution)/shard_map/ppermute | solution.py:607
  59.4 1.2 %collective-permute-done.11.refs_2_ = bf16[352,128]{1,0:T(8,128)(2,1)S(1)} collective-permute-done((bf16[352,128]{1,0:T(8,128)(2,1)S(1)}, bf16[352,128]{1,0:T(8,128)(2,1)S(1)}, u32[]{:S(2)}, u32[]{:S(2)}) %collective-permute-start.11) | collective-permute-done | bytes 90144 | tf_op jit(solution)/shard_map/ppermute | solution.py:607
  60.6 2.6 %collective-permute-start.15 = (bf16[224,128]{1,0:T(8,128)(2,1)S(1)}, bf16[224,128]{1,0:T(8,128)(2,1)S(1)}, u32[]{:S(2)}, u32[]{:S(2)}) collective-permute-start(bf16[224,128]{1,0:T(8,128)(2,1)S(1)} %rounded.1.refs_0_), channel_id=1, source_target_pairs={{0,24},{2,26},{4,28},{6,30},{8,16},{10,18},{12,20},{14,22},{16,8},... | collective-permute-start | bytes 172040 | tf_op jit(solution)/shard_map/ppermute | solution.py:607
  63.2 0.6 collective-permute-start.14
  63.8 1.3 %collective-permute-start.13 = (bf16[224,128]{1,0:T(8,128)(2,1)S(1)}, bf16[224,128]{1,0:T(8,128)(2,1)S(1)}, u32[]{:S(2)}, u32[]{:S(2)}) collective-permute-start(bf16[224,128]{1,0:T(8,128)(2,1)S(1)} %rounded.1.refs_0_), channel_id=1, source_target_pairs={{0,8},{2,10},{4,12},{6,14},{8,0},{10,2},{12,4},{14,6},{16,24},{18,... | collective-permute-start | bytes 172040 | tf_op jit(solution)/shard_map/ppermute | solution.py:607
  65.1 1.6 %collective-permute-done.15.refs_3_ = bf16[224,128]{1,0:T(8,128)(2,1)S(1)} collective-permute-done((bf16[224,128]{1,0:T(8,128)(2,1)S(1)}, bf16[224,128]{1,0:T(8,128)(2,1)S(1)}, u32[]{:S(2)}, u32[]{:S(2)}) %collective-permute-start.15) | collective-permute-done | bytes 57376 | tf_op jit(solution)/shard_map/ppermute | solution.py:607
  66.7 1.9 %collective-permute-done.14.refs_2_ = bf16[224,128]{1,0:T(8,128)(2,1)S(1)} collective-permute-done((bf16[224,128]{1,0:T(8,128)(2,1)S(1)}, bf16[224,128]{1,0:T(8,128)(2,1)S(1)}, u32[]{:S(2)}, u32[]{:S(2)}) %collective-permute-start.14) | collective-permute-done | bytes 57376 | tf_op jit(solution)/shard_map/ppermute | solution.py:607
  68.6 0.8 %steps.1 = (f32[16,128]{1,0:T(8,128)}, f32[128,128]{1,0:T(8,128)}, f32[64,128]{1,0:T(8,128)}, f32[6,64]{1,0:T(8,128)}) custom-call(bf16[224,128]{1,0:T(8,128)(2,1)S(1)} %rounded.1.refs_0_, bf16[224,128]{1,0:T(8,128)(2,1)S(1)} %collective-permute-done.13.refs_1_, bf16[224,128]{1,0:T(8,128)(2,1)S(1)} %collective-permute-done.14.refs_2_, ...), custom_call_target="tpu_custom_call" | custom-call | flops 2000000000 | bytes 452096 | tf_op jit(solution)/shard_map/steps/pallas_call | solution.py:591
  (40 shorter events, 0.5 us)
Async XLA Ops:
  0.6 9.2 %copy-start.5 = (f32[3,256]{1,0:T(4,128)S(1)}, f32[3,256]{1,0:T(4,128)}, u32[]{:S(2)}) copy-start(f32[3,256]{1,0:T(4,128)} %refs_1_.1) | copy-start | bytes 9220
  0.6 9.1 %copy-start = (bf16[256,128]{1,0:T(8,128)(2,1)S(1)}, bf16[256,128]{1,0:T(8,128)(2,1)}, u32[]{:S(2)}) copy-start(bf16[256,128]{1,0:T(8,128)(2,1)} %refs_0_.1) | copy-start | bytes 196612
  0.7 9.1 %copy-start.2 = (bf16[128,128]{1,0:T(8,128)(2,1)S(1)}, bf16[128,128]{1,0:T(8,128)(2,1)}, u32[]{:S(2)}) copy-start(bf16[128,128]{1,0:T(8,128)(2,1)} %refs_7_.3) | copy-start | bytes 98308
  0.7 9.1 %copy-start.8 = (f32[6,64]{1,0:T(8,128)S(1)}, f32[6,64]{1,0:T(8,128)}, u32[]{:S(2)}) copy-start(f32[6,64]{1,0:T(8,128)} %refs_9_.2) | copy-start | bytes 4612
  0.7 9.1 %copy-start.4 = (bf16[128,64]{0,1:T(8,128)(2,1)S(1)}, bf16[128,64]{0,1:T(8,128)(2,1)}, u32[]{:S(2)}) copy-start(bf16[128,64]{0,1:T(8,128)(2,1)} %param.22) | copy-start | bytes 49156
  0.7 9.1 %copy-start.7 = (bf16[16,128]{1,0:T(8,128)(2,1)S(1)}, bf16[16,128]{1,0:T(8,128)(2,1)}, u32[]{:S(2)}) copy-start(bf16[16,128]{1,0:T(8,128)(2,1)} %refs_6_.1) | copy-start | bytes 12292
  0.7 9.1 %copy-start.6 = (f32[3,256]{1,0:T(4,128)S(1)}, f32[3,256]{1,0:T(4,128)}, u32[]{:S(2)}) copy-start(f32[3,256]{1,0:T(4,128)} %refs_2_.3) | copy-start | bytes 9220
  0.7 9.1 %copy-start.10 = (s32[256]{0:T(256)S(1)}, s32[256]{0:T(256)}, u32[]{:S(2)}) copy-start(s32[256]{0:T(256)} %param.17) | copy-start | bytes 3076
  0.7 9.1 %copy-start.9 = (s32[256]{0:T(256)S(1)}, s32[256]{0:T(256)}, u32[]{:S(2)}) copy-start(s32[256]{0:T(256)} %param.15) | copy-start | bytes 3076
  0.7 9.1 %copy-start.1 = (s32[256,64]{0,1:T(8,128)S(1)}, s32[256,64]{0,1:T(8,128)}, u32[]{:S(2)}) copy-start(s32[256,64]{0,1:T(8,128)} %param.14) | copy-start | bytes 196612
  2.3 9.9 %collective-permute-start.1 = (bf16[288,128]{1,0:T(8,128)(2,1)}, bf16[288,128]{1,0:T(8,128)(2,1)S(1)}, u32[]{:S(2)}, u32[]{:S(2)}) collective-permute-start(bf16[288,128]{1,0:T(8,128)(2,1)} %pack.1), channel_id=1, source_target_pairs={{0,2},{2,0},{4,6},{6,4},{8,10},{10,8},{12,14},{14,12},{16,18},{18,... | collective-permute-start | bytes 221192 | tf_op jit(solution)/shard_map/ppermute | solution.py:607
  5.3 9.5 %collective-permute-start = (bf16[288,128]{1,0:T(8,128)(2,1)}, bf16[288,128]{1,0:T(8,128)(2,1)S(1)}, u32[]{:S(2)}, u32[]{:S(2)}) collective-permute-start(bf16[288,128]{1,0:T(8,128)(2,1)} %pack.1), channel_id=1, source_target_pairs={{0,30},{2,4},{4,2},{6,8},{8,6},{10,12},{12,10},{14,16},{16,14},{18... | collective-permute-start | bytes 221192 | tf_op jit(solution)/shard_map/ppermute | solution.py:657
  14.8 13.0 %copy-start.3 = (s32[3,1024]{1,0:T(4,128)S(1)}, s32[3,1024]{1,0:T(4,128)}, u32[]{:S(2)}) copy-start(s32[3,1024]{1,0:T(4,128)} %refs_10_.1) | copy-start | bytes 36868
  17.7 6.5 %collective-permute-start.4 = (bf16[1,80,256]{2,1,0:T(8,128)(2,1)S(1)}, bf16[1,80,256]{2,1,0:T(8,128)(2,1)S(1)}, u32[]{:S(2)}, u32[]{:S(2)}) collective-permute-start(bf16[1,80,256]{2,1,0:T(8,128)(2,1)S(1)} %get-tuple-element.40), channel_id=1, source_target_pairs={{0,24},{2,26},{4,28},{6,30},{8,16},{10,18},{12,20},{14,22},{16,8},... | collective-permute-start | bytes 122888 | tf_op jit(solution)/shard_map/ppermute | solution.py:607
  18.2 5.9 %collective-permute-start.3 = (bf16[1,80,256]{2,1,0:T(8,128)(2,1)S(1)}, bf16[1,80,256]{2,1,0:T(8,128)(2,1)S(1)}, u32[]{:S(2)}, u32[]{:S(2)}) collective-permute-start(bf16[1,80,256]{2,1,0:T(8,128)(2,1)S(1)} %get-tuple-element.40), channel_id=1, source_target_pairs={{0,16},{2,18},{4,20},{6,22},{8,24},{10,26},{12,28},{14,30},{16,0},... | collective-permute-start | bytes 122888 | tf_op jit(solution)/shard_map/ppermute | solution.py:607
  18.2 5.9 %collective-permute-start.2 = (bf16[1,80,256]{2,1,0:T(8,128)(2,1)S(1)}, bf16[1,80,256]{2,1,0:T(8,128)(2,1)S(1)}, u32[]{:S(2)}, u32[]{:S(2)}) collective-permute-start(bf16[1,80,256]{2,1,0:T(8,128)(2,1)S(1)} %get-tuple-element.40), channel_id=1, source_target_pairs={{0,8},{2,10},{4,12},{6,14},{8,0},{10,2},{12,4},{14,6},{16,24},{18,... | collective-permute-start | bytes 122888 | tf_op jit(solution)/shard_map/ppermute | solution.py:607
  24.2 6.9 %collective-permute-start.7 = (bf16[4,80,256]{2,1,0:T(8,128)(2,1)S(1)}, bf16[4,80,256]{2,1,0:T(8,128)(2,1)S(1)}, u32[]{:S(2)}, u32[]{:S(2)}) collective-permute-start(bf16[4,80,256]{2,1,0:T(8,128)(2,1)S(1)} %constant_dynamic-update-slice_fusion.refs_1_), channel_id=1, source_target_pairs={{0,6},{2,4},{4,2},{6,0},{8,14},{10,12},{12,10},{14,8},{16,22},{18,... | collective-permute-start | bytes 491528 | tf_op jit(solution)/shard_map/ppermute | solution.py:607
  26.5 7.3 %collective-permute-start.6 = (bf16[4,80,256]{2,1,0:T(8,128)(2,1)S(1)}, bf16[4,80,256]{2,1,0:T(8,128)(2,1)S(1)}, u32[]{:S(2)}, u32[]{:S(2)}) collective-permute-start(bf16[4,80,256]{2,1,0:T(8,128)(2,1)S(1)} %constant_dynamic-update-slice_fusion.refs_1_), channel_id=1, source_target_pairs={{0,4},{2,6},{4,0},{6,2},{8,12},{10,14},{12,8},{14,10},{16,20},{18,... | collective-permute-start | bytes 491528 | tf_op jit(solution)/shard_map/ppermute | solution.py:607
  26.5 7.3 %collective-permute-start.5 = (bf16[4,80,256]{2,1,0:T(8,128)(2,1)S(1)}, bf16[4,80,256]{2,1,0:T(8,128)(2,1)S(1)}, u32[]{:S(2)}, u32[]{:S(2)}) collective-permute-start(bf16[4,80,256]{2,1,0:T(8,128)(2,1)S(1)} %constant_dynamic-update-slice_fusion.refs_1_), channel_id=1, source_target_pairs={{0,2},{2,0},{4,6},{6,4},{8,10},{10,8},{12,14},{14,12},{16,18},{18,... | collective-permute-start | bytes 491528 | tf_op jit(solution)/shard_map/ppermute | solution.py:607
  40.6 4.2 %collective-permute-start.8 = (f32[3,16,256]{2,1,0:T(8,128)S(1)}, f32[3,16,256]{2,1,0:T(8,128)S(1)}, u32[]{:S(2)}, u32[]{:S(2)}) collective-permute-start(f32[3,16,256]{2,1,0:T(8,128)S(1)} %get-tuple-element.46), channel_id=1, source_target_pairs={{0,2},{2,0},{4,6},{6,4},{8,10},{10,8},{12,14},{14,12},{16,18},{18,... | collective-permute-start | bytes 147464 | tf_op jit(solution)/shard_map/ppermute | solution.py:607
  49.1 3.9 %collective-permute-start.9 = (bf16[64,256]{1,0:T(8,128)(2,1)S(1)}, bf16[64,256]{1,0:T(8,128)(2,1)S(1)}, u32[]{:S(2)}, u32[]{:S(2)}) collective-permute-start(bf16[64,256]{1,0:T(8,128)(2,1)S(1)} %get-tuple-element.54), channel_id=1, source_target_pairs={{0,2},{2,0},{4,6},{6,4},{8,10},{10,8},{12,14},{14,12},{16,18},{18,... | collective-permute-start | bytes 98312 | tf_op jit(solution)/shard_map/ppermute | solution.py:607
  53.9 5.5 %collective-permute-start.12 = (bf16[352,128]{1,0:T(8,128)(2,1)S(1)}, bf16[352,128]{1,0:T(8,128)(2,1)S(1)}, u32[]{:S(2)}, u32[]{:S(2)}) collective-permute-start(bf16[352,128]{1,0:T(8,128)(2,1)S(1)} %weights.1.refs_0_), channel_id=1, source_target_pairs={{0,6},{2,4},{4,2},{6,0},{8,14},{10,12},{12,10},{14,8},{16,22},{18,... | collective-permute-start | bytes 270344 | tf_op jit(solution)/shard_map/ppermute | solution.py:607
  56.0 4.5 %collective-permute-start.11 = (bf16[352,128]{1,0:T(8,128)(2,1)S(1)}, bf16[352,128]{1,0:T(8,128)(2,1)S(1)}, u32[]{:S(2)}, u32[]{:S(2)}) collective-permute-start(bf16[352,128]{1,0:T(8,128)(2,1)S(1)} %weights.1.refs_0_), channel_id=1, source_target_pairs={{0,4},{2,6},{4,0},{6,2},{8,12},{10,14},{12,8},{14,10},{16,20},{18,... | collective-permute-start | bytes 270344 | tf_op jit(solution)/shard_map/ppermute | solution.py:607
  56.0 4.5 %collective-permute-start.10 = (bf16[352,128]{1,0:T(8,128)(2,1)S(1)}, bf16[352,128]{1,0:T(8,128)(2,1)S(1)}, u32[]{:S(2)}, u32[]{:S(2)}) collective-permute-start(bf16[352,128]{1,0:T(8,128)(2,1)S(1)} %weights.1.refs_0_), channel_id=1, source_target_pairs={{0,2},{2,0},{4,6},{6,4},{8,10},{10,8},{12,14},{14,12},{16,18},{18,... | collective-permute-start | bytes 270344 | tf_op jit(solution)/shard_map/ppermute | solution.py:607
  60.6 6.0 %collective-permute-start.15 = (bf16[224,128]{1,0:T(8,128)(2,1)S(1)}, bf16[224,128]{1,0:T(8,128)(2,1)S(1)}, u32[]{:S(2)}, u32[]{:S(2)}) collective-permute-start(bf16[224,128]{1,0:T(8,128)(2,1)S(1)} %rounded.1.refs_0_), channel_id=1, source_target_pairs={{0,24},{2,26},{4,28},{6,30},{8,16},{10,18},{12,20},{14,22},{16,8},... | collective-permute-start | bytes 172040 | tf_op jit(solution)/shard_map/ppermute | solution.py:607
  63.2 5.4 %collective-permute-start.14 = (bf16[224,128]{1,0:T(8,128)(2,1)S(1)}, bf16[224,128]{1,0:T(8,128)(2,1)S(1)}, u32[]{:S(2)}, u32[]{:S(2)}) collective-permute-start(bf16[224,128]{1,0:T(8,128)(2,1)S(1)} %rounded.1.refs_0_), channel_id=1, source_target_pairs={{0,16},{2,18},{4,20},{6,22},{8,24},{10,26},{12,28},{14,30},{16,0},... | collective-permute-start | bytes 172040 | tf_op jit(solution)/shard_map/ppermute | solution.py:607
  63.8 4.8 %collective-permute-start.13 = (bf16[224,128]{1,0:T(8,128)(2,1)S(1)}, bf16[224,128]{1,0:T(8,128)(2,1)S(1)}, u32[]{:S(2)}, u32[]{:S(2)}) collective-permute-start(bf16[224,128]{1,0:T(8,128)(2,1)S(1)} %rounded.1.refs_0_), channel_id=1, source_target_pairs={{0,8},{2,10},{4,12},{6,14},{8,0},{10,2},{12,4},{14,6},{16,24},{18,... | collective-permute-start | bytes 172040 | tf_op jit(solution)/shard_map/ppermute | solution.py:607

commit v12 on v11

--- a/solution.py
+++ b/solution.py
@@ -504,10 +504,9 @@
     value_ref[first : first + count, :] += total[rows:, :]
 
 
-def rounded_kernel(*refs, first, count):
-    *part_refs, sums_ref, value_ref = refs
-    joined_rows(part_refs, first, count, value_ref)
-    sums_ref[...] = value_ref[...].astype(bf16)
+def column_kernel(*refs, first, count):
+    *part_refs, sums_ref = refs
+    split_rows(summed([ref[...].astype(f32) for ref in part_refs]), first, count, sums_ref)
 
 
 def weights_kernel(*refs, group, kinds):
@@ -555,7 +554,7 @@
         lax.broadcasted_iota(jnp.int32, (kinds, atoms), 0) == species_ref[...]
     ).astype(f32)
     packed_ref[row : row + kinds, 0:charge_count] = matmul_nt(one_hot, grad, highest)
-    split_rows(packed_ref[...], basis_count, width, sums_ref)
+    sums_ref[...] = packed_ref[...].astype(bf16)
 
 
 def step_kernel(*refs):
@@ -563,7 +562,7 @@
     basis_count, width = radial_ref.shape
     charge_count = charge_ref.shape[0]
     kinds = species_ref.shape[0]
-    total_ref[...] = summed([ref[...].astype(f32) for ref in total_refs])
+    joined_rows(total_refs, basis_count, width, total_ref)
 
     def normalized(gradient):
         mean = jnp.sum(gradient * gradient, keepdims=True) * (1.0 / gradient.size)
@@ -818,7 +817,7 @@
     packed = kernel(
         lambda *refs: weights_kernel(*refs, group=group, kinds=kinds),
         "weights",
-        shaped(rows + width, width, kind=bf16),
+        shaped(rows, width, kind=bf16),
         (shaped(rows, width),),
         3_000,
         *grad_parts,
@@ -831,15 +830,15 @@
         charge_rows,
     )
     packed = kernel(
-        lambda *refs: rounded_kernel(*refs, first=basis_count, count=width),
-        "rounded",
-        shaped(rows, width, kind=bf16),
-        (shaped(rows, width),),
+        lambda *refs: column_kernel(*refs, first=basis_count, count=width),
+        "column",
+        shaped(rows + width, width, kind=bf16),
+        (),
         1_000,
         packed,
-        *[across(packed, r) for r in range(1, blocks)],
-    )
-    totals = [packed] + [across(packed, bits) for bits in range(blocks, domains, blocks)]
+        *[across(packed, bits) for bits in range(blocks, domains, blocks)],
+    )
+    totals = [packed] + [across(packed, r) for r in range(1, blocks)]
     radial_step, mix_step, charge_step, species_step = kernel(
         step_kernel,
         "steps",

time: 69.6 us -> 69.3 us (level)
  transfers between devices with their start and end apart: 16 -> 16, of which waited for: 8 -> 9; matrix products, arithmetic and copies ran while one was open for 0% -> 0% of each run, Pallas kernels for 16% -> 16%
where the time goes in v12:
time: 69.3 us; the launch traced here: 69.2 us
  Pallas kernels  28.5 us (41%)
  starting transfers between devices  24.4 us (35%)
  waiting for transfers between devices  15.3 us (22%)
  between operations  0.89 us (1%)
    pallas_call x13, Pallas kernels, kernel(): pl.pallas_call(body, out_shape=out_shape, in_specs=[in_smem] * len(scalar...  28.5 us
    ppermute x15, starting transfers between devices, across(): return lax.ppermute(value, 'dom', [(i, i ^ bits) for i in range(domains)])  19.9 us
    ppermute x15, waiting for transfers between devices, across(): return lax.ppermute(value, 'dom', [(i, i ^ bits) for i in range(domains)])  15.3 us
    ppermute x1, starting transfers between devices, on_device(): far = lax.ppermute(packed, 'dom', beyond)  4.53 us
  transfers between devices with their start and end apart: 16, of which 9 were waited for; matrix products, arithmetic and copies ran while one was open for 0% of the time, Pallas kernels for 16%

profile of v12, /device:TPU:0, one launch (start us, length us, event | category | flops | bytes accessed | tf_op | source)
XLA Modules:
  0.0 69.2 jit_solution(13848975020862757743)
XLA Ops:
  0.7 1.6 %pack.1 = bf16[288,128]{1,0:T(8,128)(2,1)} custom-call(bf16[256,128]{1,0:T(8,128)(2,1)} %refs_0_.1, f32[3,256]{1,0:T(4,128)} %refs_1_.1, s32[2,256]{1,0:T(2,128)} %ghost_ref.1), custom_call_target="tpu_custom_call" | custom-call | flops 1000000000 | bytes 144384 | tf_op jit(solution)/shard_map/pack/pallas_call | solution.py:590
  2.3 2.9 %collective-permute-start.1 = (bf16[288,128]{1,0:T(8,128)(2,1)}, bf16[288,128]{1,0:T(8,128)(2,1)S(1)}, u32[]{:S(2)}, u32[]{:S(2)}) collective-permute-start(bf16[288,128]{1,0:T(8,128)(2,1)} %pack.1), channel_id=1, source_target_pairs={{0,2},{2,0},{4,6},{6,4},{8,10},{10,8},{12,14},{14,12},{16,18},{18,... | collective-permute-start | bytes 221192 | tf_op jit(solution)/shard_map/ppermute | solution.py:606
  5.3 4.5 %collective-permute-start = (bf16[288,128]{1,0:T(8,128)(2,1)}, bf16[288,128]{1,0:T(8,128)(2,1)S(1)}, u32[]{:S(2)}, u32[]{:S(2)}) collective-permute-start(bf16[288,128]{1,0:T(8,128)(2,1)} %pack.1), channel_id=1, source_target_pairs={{0,30},{2,4},{4,2},{6,8},{8,6},{10,12},{12,10},{14,16},{16,14},{18... | collective-permute-start | bytes 221192 | tf_op jit(solution)/shard_map/ppermute | solution.py:656
  9.9 2.3 %own.1 = (f32[16,128,256]{2,1,0:T(8,128)S(1)}, s32[24,256]{1,0:T(8,128)S(1)}, bf16[128,256]{1,0:T(8,128)(2,1)S(1)}, f32[64,256]{1,0:T(8,128)S(1)}, f32[320,128]{1,0:T(8,128)S(1)}, /*index=5*/f32[24,256]{1,0:T(8,128)S(1)}) custom-call(bf16[256,128]{1,0:T(8,128)(2,1)S(1)} %copy-done, f32[3,256]{1,0:T(4,128)S(1)} %copy-done.5, f32[3,256]{1,0:T(4,128)S(1)} %copy-done.6, ...), custom_call_target="tpu_custom_call" | custom-call | flops 4000000000 | bytes 6837760 | tf_op jit(solution)/shard_map/own/pallas_call | solution.py:590
  12.3 2.5 %near.1.refs_2_ = f32[16,128,256]{2,1,0:T(8,128)S(1)} custom-call(s32[3]{0:T(128)S(1)} %pad_add_fusion.refs_0_, bf16[288,128]{1,0:T(8,128)(2,1)S(1)} %collective-permute-done.1.refs_1_, f32[16,128,256]{2,1,0:T(8,128)S(1)} %get-tuple-element.34.refs_2_, s32[24,256]{1,0:T(8,128)S(1)} %get-tuple-element.35.refs_3_, f32[24,256]{1,0:T(8,128)S(1)} %get-tuple-element.36.refs_4_.refs_7_), custom_call_target="tpu_custom_call" | custom-call | flops 3000000000 | bytes 6430720 | tf_op jit(solution)/shard_map/near/pallas_call | solution.py:590
  14.8 2.9 %edges.1 = (f32[16,128,256]{2,1,0:T(8,128)S(1)}, f32[128,256]{1,0:T(8,128)S(1)}, f32[128,256]{1,0:T(8,128)S(1)}, bf16[128,256]{1,0:T(8,128)(2,1)S(1)}, bf16[1,80,256]{2,1,0:T(8,128)(2,1)S(1)}) custom-call(s32[3]{0:T(128)S(1)} %pad_add_fusion.refs_0_, bf16[288,128]{1,0:T(8,128)(2,1)S(1)} %collective-permute-done.refs_1_, f32[16,128,256]{2,1,0:T(8,128)S(1)} %near.1.refs_2_, ...), custom_call_target="tpu_custom_call" | custom-call | flops 4000000000 | bytes 7094272 | tf_op jit(solution)/shard_map/edges/pallas_call | solution.py:590
  17.7 0.5 collective-permute-start.4
  18.2 3.9 %collective-permute-start.2 = (bf16[1,80,256]{2,1,0:T(8,128)(2,1)S(1)}, bf16[1,80,256]{2,1,0:T(8,128)(2,1)S(1)}, u32[]{:S(2)}, u32[]{:S(2)}) collective-permute-start(bf16[1,80,256]{2,1,0:T(8,128)(2,1)S(1)} %get-tuple-element.40), channel_id=1, source_target_pairs={{0,8},{2,10},{4,12},{6,14},{8,0},{10,2},{12,4},{14,6},{16,24},{18,... | collective-permute-start | bytes 122888 | tf_op jit(solution)/shard_map/ppermute | solution.py:606
  22.2 2.0 %collective-permute-done.2 = bf16[1,80,256]{2,1,0:T(8,128)(2,1)S(1)} collective-permute-done((bf16[1,80,256]{2,1,0:T(8,128)(2,1)S(1)}, bf16[1,80,256]{2,1,0:T(8,128)(2,1)S(1)}, u32[]{:S(2)}, u32[]{:S(2)}) %collective-permute-start.2) | collective-permute-done | bytes 40992 | tf_op jit(solution)/shard_map/ppermute | solution.py:606
  24.2 2.3 %collective-permute-start.7 = (bf16[4,80,256]{2,1,0:T(8,128)(2,1)S(1)}, bf16[4,80,256]{2,1,0:T(8,128)(2,1)S(1)}, u32[]{:S(2)}, u32[]{:S(2)}) collective-permute-start(bf16[4,80,256]{2,1,0:T(8,128)(2,1)S(1)} %constant_dynamic-update-slice_fusion.refs_1_), channel_id=1, source_target_pairs={{0,6},{2,4},{4,2},{6,0},{8,14},{10,12},{12,10},{14,8},{16,22},{18,... | collective-permute-start | bytes 491528 | tf_op jit(solution)/shard_map/ppermute | solution.py:606
  26.5 1.2 %collective-permute-start.5 = (bf16[4,80,256]{2,1,0:T(8,128)(2,1)S(1)}, bf16[4,80,256]{2,1,0:T(8,128)(2,1)S(1)}, u32[]{:S(2)}, u32[]{:S(2)}) collective-permute-start(bf16[4,80,256]{2,1,0:T(8,128)(2,1)S(1)} %constant_dynamic-update-slice_fusion.refs_1_), channel_id=1, source_target_pairs={{0,2},{2,0},{4,6},{6,4},{8,10},{10,8},{12,14},{14,12},{16,18},{18,... | collective-permute-start | bytes 491528 | tf_op jit(solution)/shard_map/ppermute | solution.py:606
  27.8 2.7 %phases.2 = (bf16[4,1024,256]{2,1,0:T(8,128)(2,1)S(1)}, f32[64,1024]{1,0:T(8,128)S(1)}) custom-call(s32[3]{0:T(128)S(1)} %pad_add_fusion.refs_0_, bf16[4,80,256]{2,1,0:T(8,128)(2,1)S(1)} %constant_dynamic-update-slice_fusion.refs_1_, s32[3,1024]{1,0:T(4,128)S(1)} %copy-done.3), custom_call_target="tpu_custom_call" | custom-call | flops 3000000000 | bytes 2535424 | tf_op jit(solution)/shard_map/phases/pallas_call | solution.py:590
  30.5 0.6 collective-permute-done.7.refs_1_.refs_4_
  31.1 2.7 %phases.3 = (bf16[4,1024,256]{2,1,0:T(8,128)(2,1)S(1)}, f32[64,1024]{1,0:T(8,128)S(1)}) custom-call(s32[3]{0:T(128)S(1)} %pad_add_fusion.refs_0_, bf16[4,80,256]{2,1,0:T(8,128)(2,1)S(1)} %collective-permute-done.7.refs_1_.refs_4_, s32[3,1024]{1,0:T(4,128)S(1)} %copy-done.3), custom_call_target="tpu_custom_call" | custom-call | flops 3000000000 | bytes 2535424 | tf_op jit(solution)/shard_map/phases/pallas_call | solution.py:590
  33.9 6.7 %structure.1 = (bf16[8,1024,256]{2,1,0:T(8,128)(2,1)S(1)}, f32[192,1024]{1,0:T(8,128)S(1)}, f32[3,16,256]{2,1,0:T(8,128)S(1)}, f32[3,16,256]{2,1,0:T(8,128)S(1)}) custom-call(s32[3]{0:T(128)S(1)} %pad_add_fusion.refs_0_, bf16[4,80,256]{2,1,0:T(8,128)(2,1)S(1)} %constant_dynamic-update-slice_fusion.refs_1_, ...), custom_call_target="tpu_custom_call" | custom-call | flops 8000000000 | bytes 10465280 | tf_op jit(solution)/shard_map/structure/pallas_call | solution.py:590
  40.6 0.5 collective-permute-start.8
  41.1 0.6 fields.1
  41.7 3.1 %collective-permute-done.8.refs_6_ = f32[3,16,256]{2,1,0:T(8,128)S(1)} collective-permute-done((f32[3,16,256]{2,1,0:T(8,128)S(1)}, f32[3,16,256]{2,1,0:T(8,128)S(1)}, u32[]{:S(2)}, u32[]{:S(2)}) %collective-permute-start.8) | collective-permute-done | bytes 49184 | tf_op jit(solution)/shard_map/ppermute | solution.py:606
  44.7 4.4 %gradient.1 = (f32[3,256]{1,0:T(4,128)}, f32[8,256]{1,0:T(8,128)S(1)}, f32[64,1024]{1,0:T(8,128)S(1)}, bf16[64,256]{1,0:T(8,128)(2,1)S(1)}) custom-call(s32[3]{0:T(128)S(1)} %pad_add_fusion.refs_0_, bf16[4,80,256]{2,1,0:T(8,128)(2,1)S(1)} %constant_dynamic-update-slice_fusion.refs_1_, bf16[4,80,256]{2,1,0:T(8,128)(2,1)S(1)} %collective-permute-done.5.refs_2_, ...), custom_call_target="tpu_custom_call" | custom-call | flops 5000000000 | bytes 9706496 | tf_op jit(solution)/shard_map/gradient/pallas_call | solution.py:590
  49.1 0.4 collective-permute-start.9
  49.9 3.2 %collective-permute-done.9.refs_1_ = bf16[64,256]{1,0:T(8,128)(2,1)S(1)} collective-permute-done((bf16[64,256]{1,0:T(8,128)(2,1)S(1)}, bf16[64,256]{1,0:T(8,128)(2,1)S(1)}, u32[]{:S(2)}, u32[]{:S(2)}) %collective-permute-start.9) | collective-permute-done | bytes 32800 | tf_op jit(solution)/shard_map/ppermute | solution.py:606
  53.0 0.9 %weights.1.refs_0_ = bf16[224,128]{1,0:T(8,128)(2,1)S(1)} custom-call(f32[64,256]{1,0:T(8,128)S(1)} %own_gradient.1.refs_0_, bf16[64,256]{1,0:T(8,128)(2,1)S(1)} %collective-permute-done.9.refs_1_, f32[16,128,256]{2,1,0:T(8,128)S(1)} %get-tuple-element.55.refs_2_, f32[128,256]{1,0:T(8,128)S(1)} %get-tuple-element.56.refs_3_, ...), custom_call_target="tpu_custom_call" | custom-call | flops 3000000000 | bytes 2745344 | tf_op jit(solution)/shard_map/weights/pallas_call | solution.py:590
  53.9 2.7 %collective-permute-start.12 = (bf16[224,128]{1,0:T(8,128)(2,1)S(1)}, bf16[224,128]{1,0:T(8,128)(2,1)S(1)}, u32[]{:S(2)}, u32[]{:S(2)}) collective-permute-start(bf16[224,128]{1,0:T(8,128)(2,1)S(1)} %weights.1.refs_0_), channel_id=1, source_target_pairs={{0,24},{2,26},{4,28},{6,30},{8,16},{10,18},{12,20},{14,22},{16,8},... | collective-permute-start | bytes 172040 | tf_op jit(solution)/shard_map/ppermute | solution.py:606
  56.6 0.5 collective-permute-start.11
  57.0 1.3 %collective-permute-start.10 = (bf16[224,128]{1,0:T(8,128)(2,1)S(1)}, bf16[224,128]{1,0:T(8,128)(2,1)S(1)}, u32[]{:S(2)}, u32[]{:S(2)}) collective-permute-start(bf16[224,128]{1,0:T(8,128)(2,1)S(1)} %weights.1.refs_0_), channel_id=1, source_target_pairs={{0,8},{2,10},{4,12},{6,14},{8,0},{10,2},{12,4},{14,6},{16,24},{18,... | collective-permute-start | bytes 172040 | tf_op jit(solution)/shard_map/ppermute | solution.py:606
  58.3 1.6 %collective-permute-done.12.refs_3_ = bf16[224,128]{1,0:T(8,128)(2,1)S(1)} collective-permute-done((bf16[224,128]{1,0:T(8,128)(2,1)S(1)}, bf16[224,128]{1,0:T(8,128)(2,1)S(1)}, u32[]{:S(2)}, u32[]{:S(2)}) %collective-permute-start.12) | collective-permute-done | bytes 57376 | tf_op jit(solution)/shard_map/ppermute | solution.py:606
  59.9 1.8 %collective-permute-done.11.refs_2_ = bf16[224,128]{1,0:T(8,128)(2,1)S(1)} collective-permute-done((bf16[224,128]{1,0:T(8,128)(2,1)S(1)}, bf16[224,128]{1,0:T(8,128)(2,1)S(1)}, u32[]{:S(2)}, u32[]{:S(2)}) %collective-permute-start.11) | collective-permute-done | bytes 57376 | tf_op jit(solution)/shard_map/ppermute | solution.py:606
  61.9 1.6 %collective-permute-start.15 = (bf16[352,128]{1,0:T(8,128)(2,1)S(1)}, bf16[352,128]{1,0:T(8,128)(2,1)S(1)}, u32[]{:S(2)}, u32[]{:S(2)}) collective-permute-start(bf16[352,128]{1,0:T(8,128)(2,1)S(1)} %column.1.refs_0_), channel_id=1, source_target_pairs={{0,6},{2,4},{4,2},{6,0},{8,14},{10,12},{12,10},{14,8},{16,22},{18,... | collective-permute-start | bytes 270344 | tf_op jit(solution)/shard_map/ppermute | solution.py:606
  63.7 1.8 %collective-permute-start.13 = (bf16[352,128]{1,0:T(8,128)(2,1)S(1)}, bf16[352,128]{1,0:T(8,128)(2,1)S(1)}, u32[]{:S(2)}, u32[]{:S(2)}) collective-permute-start(bf16[352,128]{1,0:T(8,128)(2,1)S(1)} %column.1.refs_0_), channel_id=1, source_target_pairs={{0,2},{2,0},{4,6},{6,4},{8,10},{10,8},{12,14},{14,12},{16,18},{18,... | collective-permute-start | bytes 270344 | tf_op jit(solution)/shard_map/ppermute | solution.py:606
  65.4 2.0 %collective-permute-done.15.refs_3_ = bf16[352,128]{1,0:T(8,128)(2,1)S(1)} collective-permute-done((bf16[352,128]{1,0:T(8,128)(2,1)S(1)}, bf16[352,128]{1,0:T(8,128)(2,1)S(1)}, u32[]{:S(2)}, u32[]{:S(2)}) %collective-permute-start.15) | collective-permute-done | bytes 90144 | tf_op jit(solution)/shard_map/ppermute | solution.py:606
  67.4 0.9 %collective-permute-done.14.refs_2_ = bf16[352,128]{1,0:T(8,128)(2,1)S(1)} collective-permute-done((bf16[352,128]{1,0:T(8,128)(2,1)S(1)}, bf16[352,128]{1,0:T(8,128)(2,1)S(1)}, u32[]{:S(2)}, u32[]{:S(2)}) %collective-permute-start.14) | collective-permute-done | bytes 90144 | tf_op jit(solution)/shard_map/ppermute | solution.py:606
  68.3 0.8 %steps.1 = (f32[16,128]{1,0:T(8,128)}, f32[128,128]{1,0:T(8,128)}, f32[64,128]{1,0:T(8,128)}, f32[6,64]{1,0:T(8,128)}) custom-call(bf16[352,128]{1,0:T(8,128)(2,1)S(1)} %column.1.refs_0_, bf16[352,128]{1,0:T(8,128)(2,1)S(1)} %collective-permute-done.13.refs_1_, bf16[352,128]{1,0:T(8,128)(2,1)S(1)} %collective-permute-done.14.refs_2_, ...), custom_call_target="tpu_custom_call" | custom-call | flops 2000000000 | bytes 583168 | tf_op jit(solution)/shard_map/steps/pallas_call | solution.py:590
  (40 shorter events, 0.8 us)
Async XLA Ops:
  0.6 9.2 %copy-start.5 = (f32[3,256]{1,0:T(4,128)S(1)}, f32[3,256]{1,0:T(4,128)}, u32[]{:S(2)}) copy-start(f32[3,256]{1,0:T(4,128)} %refs_1_.1) | copy-start | bytes 9220
  0.6 9.1 %copy-start = (bf16[256,128]{1,0:T(8,128)(2,1)S(1)}, bf16[256,128]{1,0:T(8,128)(2,1)}, u32[]{:S(2)}) copy-start(bf16[256,128]{1,0:T(8,128)(2,1)} %refs_0_.1) | copy-start | bytes 196612
  0.7 9.1 %copy-start.2 = (bf16[128,128]{1,0:T(8,128)(2,1)S(1)}, bf16[128,128]{1,0:T(8,128)(2,1)}, u32[]{:S(2)}) copy-start(bf16[128,128]{1,0:T(8,128)(2,1)} %refs_7_.3) | copy-start | bytes 98308
  0.7 9.1 %copy-start.8 = (f32[6,64]{1,0:T(8,128)S(1)}, f32[6,64]{1,0:T(8,128)}, u32[]{:S(2)}) copy-start(f32[6,64]{1,0:T(8,128)} %refs_9_.2) | copy-start | bytes 4612
  0.7 9.1 %copy-start.4 = (bf16[128,64]{0,1:T(8,128)(2,1)S(1)}, bf16[128,64]{0,1:T(8,128)(2,1)}, u32[]{:S(2)}) copy-start(bf16[128,64]{0,1:T(8,128)(2,1)} %param.22) | copy-start | bytes 49156
  0.7 9.1 %copy-start.7 = (bf16[16,128]{1,0:T(8,128)(2,1)S(1)}, bf16[16,128]{1,0:T(8,128)(2,1)}, u32[]{:S(2)}) copy-start(bf16[16,128]{1,0:T(8,128)(2,1)} %refs_6_.1) | copy-start | bytes 12292
  0.7 9.1 %copy-start.6 = (f32[3,256]{1,0:T(4,128)S(1)}, f32[3,256]{1,0:T(4,128)}, u32[]{:S(2)}) copy-start(f32[3,256]{1,0:T(4,128)} %refs_2_.3) | copy-start | bytes 9220
  0.7 9.1 %copy-start.10 = (s32[256]{0:T(256)S(1)}, s32[256]{0:T(256)}, u32[]{:S(2)}) copy-start(s32[256]{0:T(256)} %param.17) | copy-start | bytes 3076
  0.7 9.1 %copy-start.9 = (s32[256]{0:T(256)S(1)}, s32[256]{0:T(256)}, u32[]{:S(2)}) copy-start(s32[256]{0:T(256)} %param.15) | copy-start | bytes 3076
  0.7 9.1 %copy-start.1 = (s32[256,64]{0,1:T(8,128)S(1)}, s32[256,64]{0,1:T(8,128)}, u32[]{:S(2)}) copy-start(s32[256,64]{0,1:T(8,128)} %param.14) | copy-start | bytes 196612
  2.3 9.9 %collective-permute-start.1 = (bf16[288,128]{1,0:T(8,128)(2,1)}, bf16[288,128]{1,0:T(8,128)(2,1)S(1)}, u32[]{:S(2)}, u32[]{:S(2)}) collective-permute-start(bf16[288,128]{1,0:T(8,128)(2,1)} %pack.1), channel_id=1, source_target_pairs={{0,2},{2,0},{4,6},{6,4},{8,10},{10,8},{12,14},{14,12},{16,18},{18,... | collective-permute-start | bytes 221192 | tf_op jit(solution)/shard_map/ppermute | solution.py:606
  5.3 9.5 %collective-permute-start = (bf16[288,128]{1,0:T(8,128)(2,1)}, bf16[288,128]{1,0:T(8,128)(2,1)S(1)}, u32[]{:S(2)}, u32[]{:S(2)}) collective-permute-start(bf16[288,128]{1,0:T(8,128)(2,1)} %pack.1), channel_id=1, source_target_pairs={{0,30},{2,4},{4,2},{6,8},{8,6},{10,12},{12,10},{14,16},{16,14},{18... | collective-permute-start | bytes 221192 | tf_op jit(solution)/shard_map/ppermute | solution.py:656
  14.8 13.0 %copy-start.3 = (s32[3,1024]{1,0:T(4,128)S(1)}, s32[3,1024]{1,0:T(4,128)}, u32[]{:S(2)}) copy-start(s32[3,1024]{1,0:T(4,128)} %refs_10_.1) | copy-start | bytes 36868
  17.7 6.5 %collective-permute-start.4 = (bf16[1,80,256]{2,1,0:T(8,128)(2,1)S(1)}, bf16[1,80,256]{2,1,0:T(8,128)(2,1)S(1)}, u32[]{:S(2)}, u32[]{:S(2)}) collective-permute-start(bf16[1,80,256]{2,1,0:T(8,128)(2,1)S(1)} %get-tuple-element.40), channel_id=1, source_target_pairs={{0,24},{2,26},{4,28},{6,30},{8,16},{10,18},{12,20},{14,22},{16,8},... | collective-permute-start | bytes 122888 | tf_op jit(solution)/shard_map/ppermute | solution.py:606
  18.2 5.9 %collective-permute-start.3 = (bf16[1,80,256]{2,1,0:T(8,128)(2,1)S(1)}, bf16[1,80,256]{2,1,0:T(8,128)(2,1)S(1)}, u32[]{:S(2)}, u32[]{:S(2)}) collective-permute-start(bf16[1,80,256]{2,1,0:T(8,128)(2,1)S(1)} %get-tuple-element.40), channel_id=1, source_target_pairs={{0,16},{2,18},{4,20},{6,22},{8,24},{10,26},{12,28},{14,30},{16,0},... | collective-permute-start | bytes 122888 | tf_op jit(solution)/shard_map/ppermute | solution.py:606
  18.2 5.9 %collective-permute-start.2 = (bf16[1,80,256]{2,1,0:T(8,128)(2,1)S(1)}, bf16[1,80,256]{2,1,0:T(8,128)(2,1)S(1)}, u32[]{:S(2)}, u32[]{:S(2)}) collective-permute-start(bf16[1,80,256]{2,1,0:T(8,128)(2,1)S(1)} %get-tuple-element.40), channel_id=1, source_target_pairs={{0,8},{2,10},{4,12},{6,14},{8,0},{10,2},{12,4},{14,6},{16,24},{18,... | collective-permute-start | bytes 122888 | tf_op jit(solution)/shard_map/ppermute | solution.py:606
  24.2 6.9 %collective-permute-start.7 = (bf16[4,80,256]{2,1,0:T(8,128)(2,1)S(1)}, bf16[4,80,256]{2,1,0:T(8,128)(2,1)S(1)}, u32[]{:S(2)}, u32[]{:S(2)}) collective-permute-start(bf16[4,80,256]{2,1,0:T(8,128)(2,1)S(1)} %constant_dynamic-update-slice_fusion.refs_1_), channel_id=1, source_target_pairs={{0,6},{2,4},{4,2},{6,0},{8,14},{10,12},{12,10},{14,8},{16,22},{18,... | collective-permute-start | bytes 491528 | tf_op jit(solution)/shard_map/ppermute | solution.py:606
  26.5 7.3 %collective-permute-start.6 = (bf16[4,80,256]{2,1,0:T(8,128)(2,1)S(1)}, bf16[4,80,256]{2,1,0:T(8,128)(2,1)S(1)}, u32[]{:S(2)}, u32[]{:S(2)}) collective-permute-start(bf16[4,80,256]{2,1,0:T(8,128)(2,1)S(1)} %constant_dynamic-update-slice_fusion.refs_1_), channel_id=1, source_target_pairs={{0,4},{2,6},{4,0},{6,2},{8,12},{10,14},{12,8},{14,10},{16,20},{18,... | collective-permute-start | bytes 491528 | tf_op jit(solution)/shard_map/ppermute | solution.py:606
  26.5 7.3 %collective-permute-start.5 = (bf16[4,80,256]{2,1,0:T(8,128)(2,1)S(1)}, bf16[4,80,256]{2,1,0:T(8,128)(2,1)S(1)}, u32[]{:S(2)}, u32[]{:S(2)}) collective-permute-start(bf16[4,80,256]{2,1,0:T(8,128)(2,1)S(1)} %constant_dynamic-update-slice_fusion.refs_1_), channel_id=1, source_target_pairs={{0,2},{2,0},{4,6},{6,4},{8,10},{10,8},{12,14},{14,12},{16,18},{18,... | collective-permute-start | bytes 491528 | tf_op jit(solution)/shard_map/ppermute | solution.py:606
  40.6 4.2 %collective-permute-start.8 = (f32[3,16,256]{2,1,0:T(8,128)S(1)}, f32[3,16,256]{2,1,0:T(8,128)S(1)}, u32[]{:S(2)}, u32[]{:S(2)}) collective-permute-start(f32[3,16,256]{2,1,0:T(8,128)S(1)} %get-tuple-element.46), channel_id=1, source_target_pairs={{0,2},{2,0},{4,6},{6,4},{8,10},{10,8},{12,14},{14,12},{16,18},{18,... | collective-permute-start | bytes 147464 | tf_op jit(solution)/shard_map/ppermute | solution.py:606
  49.1 3.9 %collective-permute-start.9 = (bf16[64,256]{1,0:T(8,128)(2,1)S(1)}, bf16[64,256]{1,0:T(8,128)(2,1)S(1)}, u32[]{:S(2)}, u32[]{:S(2)}) collective-permute-start(bf16[64,256]{1,0:T(8,128)(2,1)S(1)} %get-tuple-element.54), channel_id=1, source_target_pairs={{0,2},{2,0},{4,6},{6,4},{8,10},{10,8},{12,14},{14,12},{16,18},{18,... | collective-permute-start | bytes 98312 | tf_op jit(solution)/shard_map/ppermute | solution.py:606
  53.9 6.0 %collective-permute-start.12 = (bf16[224,128]{1,0:T(8,128)(2,1)S(1)}, bf16[224,128]{1,0:T(8,128)(2,1)S(1)}, u32[]{:S(2)}, u32[]{:S(2)}) collective-permute-start(bf16[224,128]{1,0:T(8,128)(2,1)S(1)} %weights.1.refs_0_), channel_id=1, source_target_pairs={{0,24},{2,26},{4,28},{6,30},{8,16},{10,18},{12,20},{14,22},{16,8},... | collective-permute-start | bytes 172040 | tf_op jit(solution)/shard_map/ppermute | solution.py:606
  56.6 5.2 %collective-permute-start.11 = (bf16[224,128]{1,0:T(8,128)(2,1)S(1)}, bf16[224,128]{1,0:T(8,128)(2,1)S(1)}, u32[]{:S(2)}, u32[]{:S(2)}) collective-permute-start(bf16[224,128]{1,0:T(8,128)(2,1)S(1)} %weights.1.refs_0_), channel_id=1, source_target_pairs={{0,16},{2,18},{4,20},{6,22},{8,24},{10,26},{12,28},{14,30},{16,0},... | collective-permute-start | bytes 172040 | tf_op jit(solution)/shard_map/ppermute | solution.py:606
  57.0 4.8 %collective-permute-start.10 = (bf16[224,128]{1,0:T(8,128)(2,1)S(1)}, bf16[224,128]{1,0:T(8,128)(2,1)S(1)}, u32[]{:S(2)}, u32[]{:S(2)}) collective-permute-start(bf16[224,128]{1,0:T(8,128)(2,1)S(1)} %weights.1.refs_0_), channel_id=1, source_target_pairs={{0,8},{2,10},{4,12},{6,14},{8,0},{10,2},{12,4},{14,6},{16,24},{18,... | collective-permute-start | bytes 172040 | tf_op jit(solution)/shard_map/ppermute | solution.py:606
  61.9 5.5 %collective-permute-start.15 = (bf16[352,128]{1,0:T(8,128)(2,1)S(1)}, bf16[352,128]{1,0:T(8,128)(2,1)S(1)}, u32[]{:S(2)}, u32[]{:S(2)}) collective-permute-start(bf16[352,128]{1,0:T(8,128)(2,1)S(1)} %column.1.refs_0_), channel_id=1, source_target_pairs={{0,6},{2,4},{4,2},{6,0},{8,14},{10,12},{12,10},{14,8},{16,22},{18,... | collective-permute-start | bytes 270344 | tf_op jit(solution)/shard_map/ppermute | solution.py:606
  63.5 4.8 %collective-permute-start.14 = (bf16[352,128]{1,0:T(8,128)(2,1)S(1)}, bf16[352,128]{1,0:T(8,128)(2,1)S(1)}, u32[]{:S(2)}, u32[]{:S(2)}) collective-permute-start(bf16[352,128]{1,0:T(8,128)(2,1)S(1)} %column.1.refs_0_), channel_id=1, source_target_pairs={{0,4},{2,6},{4,0},{6,2},{8,12},{10,14},{12,8},{14,10},{16,20},{18,... | collective-permute-start | bytes 270344 | tf_op jit(solution)/shard_map/ppermute | solution.py:606
  63.7 4.7 %collective-permute-start.13 = (bf16[352,128]{1,0:T(8,128)(2,1)S(1)}, bf16[352,128]{1,0:T(8,128)(2,1)S(1)}, u32[]{:S(2)}, u32[]{:S(2)}) collective-permute-start(bf16[352,128]{1,0:T(8,128)(2,1)S(1)} %column.1.refs_0_), channel_id=1, source_target_pairs={{0,2},{2,0},{4,6},{6,4},{8,10},{10,8},{12,14},{14,12},{16,18},{18,... | collective-permute-start | bytes 270344 | tf_op jit(solution)/shard_map/ppermute | solution.py:606

commit v13 on v12

--- a/solution.py
+++ b/solution.py
@@ -360,7 +360,9 @@
 def structure_kernel(where_ref, *refs, group, blocks, early, charge_count, box_x):
     shared_refs, early_refs = refs[:blocks], refs[blocks : blocks + len(early)]
     part_refs, refs = refs[blocks + len(early) : blocks + 2 * len(early)], refs[blocks + 2 * len(early) :]
-    wave_ref, waves_ref, weights_ref, *force_refs = refs
+    wave_ref, waves_ref, weights_ref, *refs = refs
+    force_refs, sent_refs = refs[:group], refs[group:]
+    rows_refs = [force_refs[0], *sent_refs]
     late = [r for r in range(blocks) if r not in early]
     count, _, atoms = shared_refs[0].shape
     share = waves_ref.shape[1] // 2
@@ -400,7 +402,9 @@
                 keepdims=True,
             )
             for m in range(group):
-                force_refs[m][a, d ^ m : (d ^ m) + 1, :] = row
+                rows_refs[m][a, d ^ m : (d ^ m) + 1, :] = row
+    for m in range(1, group):
+        force_refs[m][...] = rows_refs[m][...].astype(bf16)
 
 
 def field_kernel(*refs, group, blocks, early, count):
@@ -440,7 +444,7 @@
     waves_of = placed_waves(early, early_refs, late, waves_ref, count)
     total = part_refs[0][...]
     for m in range(1, group):
-        total = total + part_refs[m][...]
+        total = total + part_refs[m][...].astype(f32)
     total_ref[...] = total
     for a in range(3):
         forces_ref[a : a + 1, :] = total[a, 0:1, :]
@@ -756,8 +760,9 @@
             shaped(domains - len(early) * (domains // blocks), 2 * share, atoms, kind=bf16),
             shaped(3 * charge_count, 2 * share),
         )
-        + (shaped(3, domains, atoms),) * group,
-        (),
+        + (shaped(3, domains, atoms),)
+        + (shaped(3, domains, atoms, kind=bf16),) * (group - 1),
+        (shaped(3, domains, atoms),) * (group - 1),
         8_000,
         *columns,
         *waves_early,

time: 69.3 us -> 69.1 us (level)
  no operation moved by 1% of the time
where the time goes in v13:
time: 69.1 us; the launch traced here: 68.9 us
  Pallas kernels  28.5 us (41%)
  starting transfers between devices  24.4 us (35%)
  waiting for transfers between devices  15 us (22%)
  between operations  0.89 us (1%)
    pallas_call x13, Pallas kernels, kernel(): pl.pallas_call(body, out_shape=out_shape, in_specs=[in_smem] * len(scalar...  28.5 us
    ppermute x15, starting transfers between devices, across(): return lax.ppermute(value, 'dom', [(i, i ^ bits) for i in range(domains)])  19.9 us
    ppermute x15, waiting for transfers between devices, across(): return lax.ppermute(value, 'dom', [(i, i ^ bits) for i in range(domains)])  15 us
    ppermute x1, starting transfers between devices, on_device(): far = lax.ppermute(packed, 'dom', beyond)  4.53 us
  transfers between devices with their start and end apart: 16, of which 9 were waited for; matrix products, arithmetic and copies ran while one was open for 0% of the time, Pallas kernels for 16%

profile of v13, /device:TPU:0, one launch (start us, length us, event | category | flops | bytes accessed | tf_op | source)
XLA Modules:
  0.0 68.9 jit_solution(14626238271923483260)
XLA Ops:
  0.7 1.6 %pack.1 = bf16[288,128]{1,0:T(8,128)(2,1)} custom-call(bf16[256,128]{1,0:T(8,128)(2,1)} %refs_0_.1, f32[3,256]{1,0:T(4,128)} %refs_1_.1, s32[2,256]{1,0:T(2,128)} %ghost_ref.1), custom_call_target="tpu_custom_call" | custom-call | flops 1000000000 | bytes 144384 | tf_op jit(solution)/shard_map/pack/pallas_call | solution.py:594
  2.3 2.9 %collective-permute-start.1 = (bf16[288,128]{1,0:T(8,128)(2,1)}, bf16[288,128]{1,0:T(8,128)(2,1)S(1)}, u32[]{:S(2)}, u32[]{:S(2)}) collective-permute-start(bf16[288,128]{1,0:T(8,128)(2,1)} %pack.1), channel_id=1, source_target_pairs={{0,2},{2,0},{4,6},{6,4},{8,10},{10,8},{12,14},{14,12},{16,18},{18,... | collective-permute-start | bytes 221192 | tf_op jit(solution)/shard_map/ppermute | solution.py:610
  5.3 4.5 %collective-permute-start = (bf16[288,128]{1,0:T(8,128)(2,1)}, bf16[288,128]{1,0:T(8,128)(2,1)S(1)}, u32[]{:S(2)}, u32[]{:S(2)}) collective-permute-start(bf16[288,128]{1,0:T(8,128)(2,1)} %pack.1), channel_id=1, source_target_pairs={{0,30},{2,4},{4,2},{6,8},{8,6},{10,12},{12,10},{14,16},{16,14},{18... | collective-permute-start | bytes 221192 | tf_op jit(solution)/shard_map/ppermute | solution.py:660
  9.9 2.3 %own.1 = (f32[16,128,256]{2,1,0:T(8,128)S(1)}, s32[24,256]{1,0:T(8,128)S(1)}, bf16[128,256]{1,0:T(8,128)(2,1)S(1)}, f32[64,256]{1,0:T(8,128)S(1)}, f32[320,128]{1,0:T(8,128)S(1)}, /*index=5*/f32[24,256]{1,0:T(8,128)S(1)}) custom-call(bf16[256,128]{1,0:T(8,128)(2,1)S(1)} %copy-done, f32[3,256]{1,0:T(4,128)S(1)} %copy-done.5, f32[3,256]{1,0:T(4,128)S(1)} %copy-done.6, ...), custom_call_target="tpu_custom_call" | custom-call | flops 4000000000 | bytes 6837760 | tf_op jit(solution)/shard_map/own/pallas_call | solution.py:594
  12.3 2.5 %near.1.refs_2_ = f32[16,128,256]{2,1,0:T(8,128)S(1)} custom-call(s32[3]{0:T(128)S(1)} %pad_add_fusion.refs_0_, bf16[288,128]{1,0:T(8,128)(2,1)S(1)} %collective-permute-done.1.refs_1_, f32[16,128,256]{2,1,0:T(8,128)S(1)} %get-tuple-element.34.refs_2_, s32[24,256]{1,0:T(8,128)S(1)} %get-tuple-element.35.refs_3_, f32[24,256]{1,0:T(8,128)S(1)} %get-tuple-element.36.refs_4_.refs_7_), custom_call_target="tpu_custom_call" | custom-call | flops 3000000000 | bytes 6430720 | tf_op jit(solution)/shard_map/near/pallas_call | solution.py:594
  14.8 2.9 %edges.1 = (f32[16,128,256]{2,1,0:T(8,128)S(1)}, f32[128,256]{1,0:T(8,128)S(1)}, f32[128,256]{1,0:T(8,128)S(1)}, bf16[128,256]{1,0:T(8,128)(2,1)S(1)}, bf16[1,80,256]{2,1,0:T(8,128)(2,1)S(1)}) custom-call(s32[3]{0:T(128)S(1)} %pad_add_fusion.refs_0_, bf16[288,128]{1,0:T(8,128)(2,1)S(1)} %collective-permute-done.refs_1_, f32[16,128,256]{2,1,0:T(8,128)S(1)} %near.1.refs_2_, ...), custom_call_target="tpu_custom_call" | custom-call | flops 4000000000 | bytes 7094272 | tf_op jit(solution)/shard_map/edges/pallas_call | solution.py:594
  17.7 0.5 collective-permute-start.4
  18.2 3.9 %collective-permute-start.2 = (bf16[1,80,256]{2,1,0:T(8,128)(2,1)S(1)}, bf16[1,80,256]{2,1,0:T(8,128)(2,1)S(1)}, u32[]{:S(2)}, u32[]{:S(2)}) collective-permute-start(bf16[1,80,256]{2,1,0:T(8,128)(2,1)S(1)} %get-tuple-element.40), channel_id=1, source_target_pairs={{0,8},{2,10},{4,12},{6,14},{8,0},{10,2},{12,4},{14,6},{16,24},{18,... | collective-permute-start | bytes 122888 | tf_op jit(solution)/shard_map/ppermute | solution.py:610
  22.2 2.0 %collective-permute-done.2 = bf16[1,80,256]{2,1,0:T(8,128)(2,1)S(1)} collective-permute-done((bf16[1,80,256]{2,1,0:T(8,128)(2,1)S(1)}, bf16[1,80,256]{2,1,0:T(8,128)(2,1)S(1)}, u32[]{:S(2)}, u32[]{:S(2)}) %collective-permute-start.2) | collective-permute-done | bytes 40992 | tf_op jit(solution)/shard_map/ppermute | solution.py:610
  24.2 2.3 %collective-permute-start.7 = (bf16[4,80,256]{2,1,0:T(8,128)(2,1)S(1)}, bf16[4,80,256]{2,1,0:T(8,128)(2,1)S(1)}, u32[]{:S(2)}, u32[]{:S(2)}) collective-permute-start(bf16[4,80,256]{2,1,0:T(8,128)(2,1)S(1)} %constant_dynamic-update-slice_fusion.refs_1_), channel_id=1, source_target_pairs={{0,6},{2,4},{4,2},{6,0},{8,14},{10,12},{12,10},{14,8},{16,22},{18,... | collective-permute-start | bytes 491528 | tf_op jit(solution)/shard_map/ppermute | solution.py:610
  26.5 1.2 %collective-permute-start.5 = (bf16[4,80,256]{2,1,0:T(8,128)(2,1)S(1)}, bf16[4,80,256]{2,1,0:T(8,128)(2,1)S(1)}, u32[]{:S(2)}, u32[]{:S(2)}) collective-permute-start(bf16[4,80,256]{2,1,0:T(8,128)(2,1)S(1)} %constant_dynamic-update-slice_fusion.refs_1_), channel_id=1, source_target_pairs={{0,2},{2,0},{4,6},{6,4},{8,10},{10,8},{12,14},{14,12},{16,18},{18,... | collective-permute-start | bytes 491528 | tf_op jit(solution)/shard_map/ppermute | solution.py:610
  27.8 2.7 %phases.2 = (bf16[4,1024,256]{2,1,0:T(8,128)(2,1)S(1)}, f32[64,1024]{1,0:T(8,128)S(1)}) custom-call(s32[3]{0:T(128)S(1)} %pad_add_fusion.refs_0_, bf16[4,80,256]{2,1,0:T(8,128)(2,1)S(1)} %constant_dynamic-update-slice_fusion.refs_1_, s32[3,1024]{1,0:T(4,128)S(1)} %copy-done.3), custom_call_target="tpu_custom_call" | custom-call | flops 3000000000 | bytes 2535424 | tf_op jit(solution)/shard_map/phases/pallas_call | solution.py:594
  30.5 0.6 collective-permute-done.7.refs_1_.refs_4_
  31.1 2.7 %phases.3 = (bf16[4,1024,256]{2,1,0:T(8,128)(2,1)S(1)}, f32[64,1024]{1,0:T(8,128)S(1)}) custom-call(s32[3]{0:T(128)S(1)} %pad_add_fusion.refs_0_, bf16[4,80,256]{2,1,0:T(8,128)(2,1)S(1)} %collective-permute-done.7.refs_1_.refs_4_, s32[3,1024]{1,0:T(4,128)S(1)} %copy-done.3), custom_call_target="tpu_custom_call" | custom-call | flops 3000000000 | bytes 2535424 | tf_op jit(solution)/shard_map/phases/pallas_call | solution.py:594
  33.9 6.7 %structure.1 = (bf16[8,1024,256]{2,1,0:T(8,128)(2,1)S(1)}, f32[192,1024]{1,0:T(8,128)S(1)}, f32[3,16,256]{2,1,0:T(8,128)S(1)}, bf16[3,16,256]{2,1,0:T(8,128)(2,1)S(1)}) custom-call(s32[3]{0:T(128)S(1)} %pad_add_fusion.refs_0_, bf16[4,80,256]{2,1,0:T(8,128)(2,1)S(1)} %constant_dynamic-update-slice_fusion.refs_1_, ...), custom_call_target="tpu_custom_call" | custom-call | flops 8000000000 | bytes 10489856 | tf_op jit(solution)/shard_map/structure/pallas_call | solution.py:594
  40.6 0.5 collective-permute-start.8
  41.1 0.6 fields.1
  41.7 2.8 %collective-permute-done.8.refs_6_ = bf16[3,16,256]{2,1,0:T(8,128)(2,1)S(1)} collective-permute-done((bf16[3,16,256]{2,1,0:T(8,128)(2,1)S(1)}, bf16[3,16,256]{2,1,0:T(8,128)(2,1)S(1)}, u32[]{:S(2)}, u32[]{:S(2)}) %collective-permute-start.8) | collective-permute-done | bytes 24608 | tf_op jit(solution)/shard_map/ppermute | solution.py:610
  44.5 4.4 %gradient.1 = (f32[3,256]{1,0:T(4,128)}, f32[8,256]{1,0:T(8,128)S(1)}, f32[64,1024]{1,0:T(8,128)S(1)}, bf16[64,256]{1,0:T(8,128)(2,1)S(1)}) custom-call(s32[3]{0:T(128)S(1)} %pad_add_fusion.refs_0_, bf16[4,80,256]{2,1,0:T(8,128)(2,1)S(1)} %constant_dynamic-update-slice_fusion.refs_1_, bf16[4,80,256]{2,1,0:T(8,128)(2,1)S(1)} %collective-permute-done.5.refs_2_, ...), custom_call_target="tpu_custom_call" | custom-call | flops 5000000000 | bytes 9681920 | tf_op jit(solution)/shard_map/gradient/pallas_call | solution.py:594
  48.9 0.4 collective-permute-start.9
  49.6 3.2 %collective-permute-done.9.refs_1_ = bf16[64,256]{1,0:T(8,128)(2,1)S(1)} collective-permute-done((bf16[64,256]{1,0:T(8,128)(2,1)S(1)}, bf16[64,256]{1,0:T(8,128)(2,1)S(1)}, u32[]{:S(2)}, u32[]{:S(2)}) %collective-permute-start.9) | collective-permute-done | bytes 32800 | tf_op jit(solution)/shard_map/ppermute | solution.py:610
  52.8 0.9 %weights.1.refs_0_ = bf16[224,128]{1,0:T(8,128)(2,1)S(1)} custom-call(f32[64,256]{1,0:T(8,128)S(1)} %own_gradient.1.refs_0_, bf16[64,256]{1,0:T(8,128)(2,1)S(1)} %collective-permute-done.9.refs_1_, f32[16,128,256]{2,1,0:T(8,128)S(1)} %get-tuple-element.55.refs_2_, f32[128,256]{1,0:T(8,128)S(1)} %get-tuple-element.56.refs_3_, ...), custom_call_target="tpu_custom_call" | custom-call | flops 3000000000 | bytes 2745344 | tf_op jit(solution)/shard_map/weights/pallas_call | solution.py:594
  53.7 2.6 %collective-permute-start.12 = (bf16[224,128]{1,0:T(8,128)(2,1)S(1)}, bf16[224,128]{1,0:T(8,128)(2,1)S(1)}, u32[]{:S(2)}, u32[]{:S(2)}) collective-permute-start(bf16[224,128]{1,0:T(8,128)(2,1)S(1)} %weights.1.refs_0_), channel_id=1, source_target_pairs={{0,24},{2,26},{4,28},{6,30},{8,16},{10,18},{12,20},{14,22},{16,8},... | collective-permute-start | bytes 172040 | tf_op jit(solution)/shard_map/ppermute | solution.py:610
  56.3 0.5 collective-permute-start.11
  56.8 1.3 %collective-permute-start.10 = (bf16[224,128]{1,0:T(8,128)(2,1)S(1)}, bf16[224,128]{1,0:T(8,128)(2,1)S(1)}, u32[]{:S(2)}, u32[]{:S(2)}) collective-permute-start(bf16[224,128]{1,0:T(8,128)(2,1)S(1)} %weights.1.refs_0_), channel_id=1, source_target_pairs={{0,8},{2,10},{4,12},{6,14},{8,0},{10,2},{12,4},{14,6},{16,24},{18,... | collective-permute-start | bytes 172040 | tf_op jit(solution)/shard_map/ppermute | solution.py:610
  58.1 1.6 %collective-permute-done.12.refs_3_ = bf16[224,128]{1,0:T(8,128)(2,1)S(1)} collective-permute-done((bf16[224,128]{1,0:T(8,128)(2,1)S(1)}, bf16[224,128]{1,0:T(8,128)(2,1)S(1)}, u32[]{:S(2)}, u32[]{:S(2)}) %collective-permute-start.12) | collective-permute-done | bytes 57376 | tf_op jit(solution)/shard_map/ppermute | solution.py:610
  59.7 1.8 %collective-permute-done.11.refs_2_ = bf16[224,128]{1,0:T(8,128)(2,1)S(1)} collective-permute-done((bf16[224,128]{1,0:T(8,128)(2,1)S(1)}, bf16[224,128]{1,0:T(8,128)(2,1)S(1)}, u32[]{:S(2)}, u32[]{:S(2)}) %collective-permute-start.11) | collective-permute-done | bytes 57376 | tf_op jit(solution)/shard_map/ppermute | solution.py:610
  61.6 1.6 %collective-permute-start.15 = (bf16[352,128]{1,0:T(8,128)(2,1)S(1)}, bf16[352,128]{1,0:T(8,128)(2,1)S(1)}, u32[]{:S(2)}, u32[]{:S(2)}) collective-permute-start(bf16[352,128]{1,0:T(8,128)(2,1)S(1)} %column.1.refs_0_), channel_id=1, source_target_pairs={{0,6},{2,4},{4,2},{6,0},{8,14},{10,12},{12,10},{14,8},{16,22},{18,... | collective-permute-start | bytes 270344 | tf_op jit(solution)/shard_map/ppermute | solution.py:610
  63.4 1.8 %collective-permute-start.13 = (bf16[352,128]{1,0:T(8,128)(2,1)S(1)}, bf16[352,128]{1,0:T(8,128)(2,1)S(1)}, u32[]{:S(2)}, u32[]{:S(2)}) collective-permute-start(bf16[352,128]{1,0:T(8,128)(2,1)S(1)} %column.1.refs_0_), channel_id=1, source_target_pairs={{0,2},{2,0},{4,6},{6,4},{8,10},{10,8},{12,14},{14,12},{16,18},{18,... | collective-permute-start | bytes 270344 | tf_op jit(solution)/shard_map/ppermute | solution.py:610
  65.2 2.0 %collective-permute-done.15.refs_3_ = bf16[352,128]{1,0:T(8,128)(2,1)S(1)} collective-permute-done((bf16[352,128]{1,0:T(8,128)(2,1)S(1)}, bf16[352,128]{1,0:T(8,128)(2,1)S(1)}, u32[]{:S(2)}, u32[]{:S(2)}) %collective-permute-start.15) | collective-permute-done | bytes 90144 | tf_op jit(solution)/shard_map/ppermute | solution.py:610
  67.2 0.9 %collective-permute-done.14.refs_2_ = bf16[352,128]{1,0:T(8,128)(2,1)S(1)} collective-permute-done((bf16[352,128]{1,0:T(8,128)(2,1)S(1)}, bf16[352,128]{1,0:T(8,128)(2,1)S(1)}, u32[]{:S(2)}, u32[]{:S(2)}) %collective-permute-start.14) | collective-permute-done | bytes 90144 | tf_op jit(solution)/shard_map/ppermute | solution.py:610
  68.1 0.8 %steps.1 = (f32[16,128]{1,0:T(8,128)}, f32[128,128]{1,0:T(8,128)}, f32[64,128]{1,0:T(8,128)}, f32[6,64]{1,0:T(8,128)}) custom-call(bf16[352,128]{1,0:T(8,128)(2,1)S(1)} %column.1.refs_0_, bf16[352,128]{1,0:T(8,128)(2,1)S(1)} %collective-permute-done.13.refs_1_, bf16[352,128]{1,0:T(8,128)(2,1)S(1)} %collective-permute-done.14.refs_2_, ...), custom_call_target="tpu_custom_call" | custom-call | flops 2000000000 | bytes 583168 | tf_op jit(solution)/shard_map/steps/pallas_call | solution.py:594
  (40 shorter events, 0.8 us)
Async XLA Ops:
  0.6 9.2 %copy-start.5 = (f32[3,256]{1,0:T(4,128)S(1)}, f32[3,256]{1,0:T(4,128)}, u32[]{:S(2)}) copy-start(f32[3,256]{1,0:T(4,128)} %refs_1_.1) | copy-start | bytes 9220
  0.6 9.1 %copy-start = (bf16[256,128]{1,0:T(8,128)(2,1)S(1)}, bf16[256,128]{1,0:T(8,128)(2,1)}, u32[]{:S(2)}) copy-start(bf16[256,128]{1,0:T(8,128)(2,1)} %refs_0_.1) | copy-start | bytes 196612
  0.7 9.1 %copy-start.2 = (bf16[128,128]{1,0:T(8,128)(2,1)S(1)}, bf16[128,128]{1,0:T(8,128)(2,1)}, u32[]{:S(2)}) copy-start(bf16[128,128]{1,0:T(8,128)(2,1)} %refs_7_.3) | copy-start | bytes 98308
  0.7 9.1 %copy-start.8 = (f32[6,64]{1,0:T(8,128)S(1)}, f32[6,64]{1,0:T(8,128)}, u32[]{:S(2)}) copy-start(f32[6,64]{1,0:T(8,128)} %refs_9_.2) | copy-start | bytes 4612
  0.7 9.1 %copy-start.4 = (bf16[128,64]{0,1:T(8,128)(2,1)S(1)}, bf16[128,64]{0,1:T(8,128)(2,1)}, u32[]{:S(2)}) copy-start(bf16[128,64]{0,1:T(8,128)(2,1)} %param.22) | copy-start | bytes 49156
  0.7 9.1 %copy-start.7 = (bf16[16,128]{1,0:T(8,128)(2,1)S(1)}, bf16[16,128]{1,0:T(8,128)(2,1)}, u32[]{:S(2)}) copy-start(bf16[16,128]{1,0:T(8,128)(2,1)} %refs_6_.1) | copy-start | bytes 12292
  0.7 9.1 %copy-start.6 = (f32[3,256]{1,0:T(4,128)S(1)}, f32[3,256]{1,0:T(4,128)}, u32[]{:S(2)}) copy-start(f32[3,256]{1,0:T(4,128)} %refs_2_.3) | copy-start | bytes 9220
  0.7 9.1 %copy-start.10 = (s32[256]{0:T(256)S(1)}, s32[256]{0:T(256)}, u32[]{:S(2)}) copy-start(s32[256]{0:T(256)} %param.17) | copy-start | bytes 3076
  0.7 9.1 %copy-start.9 = (s32[256]{0:T(256)S(1)}, s32[256]{0:T(256)}, u32[]{:S(2)}) copy-start(s32[256]{0:T(256)} %param.15) | copy-start | bytes 3076
  0.7 9.1 %copy-start.1 = (s32[256,64]{0,1:T(8,128)S(1)}, s32[256,64]{0,1:T(8,128)}, u32[]{:S(2)}) copy-start(s32[256,64]{0,1:T(8,128)} %param.14) | copy-start | bytes 196612
  2.3 9.9 %collective-permute-start.1 = (bf16[288,128]{1,0:T(8,128)(2,1)}, bf16[288,128]{1,0:T(8,128)(2,1)S(1)}, u32[]{:S(2)}, u32[]{:S(2)}) collective-permute-start(bf16[288,128]{1,0:T(8,128)(2,1)} %pack.1), channel_id=1, source_target_pairs={{0,2},{2,0},{4,6},{6,4},{8,10},{10,8},{12,14},{14,12},{16,18},{18,... | collective-permute-start | bytes 221192 | tf_op jit(solution)/shard_map/ppermute | solution.py:610
  5.3 9.5 %collective-permute-start = (bf16[288,128]{1,0:T(8,128)(2,1)}, bf16[288,128]{1,0:T(8,128)(2,1)S(1)}, u32[]{:S(2)}, u32[]{:S(2)}) collective-permute-start(bf16[288,128]{1,0:T(8,128)(2,1)} %pack.1), channel_id=1, source_target_pairs={{0,30},{2,4},{4,2},{6,8},{8,6},{10,12},{12,10},{14,16},{16,14},{18... | collective-permute-start | bytes 221192 | tf_op jit(solution)/shard_map/ppermute | solution.py:660
  14.8 13.0 %copy-start.3 = (s32[3,1024]{1,0:T(4,128)S(1)}, s32[3,1024]{1,0:T(4,128)}, u32[]{:S(2)}) copy-start(s32[3,1024]{1,0:T(4,128)} %refs_10_.1) | copy-start | bytes 36868
  17.7 6.5 %collective-permute-start.4 = (bf16[1,80,256]{2,1,0:T(8,128)(2,1)S(1)}, bf16[1,80,256]{2,1,0:T(8,128)(2,1)S(1)}, u32[]{:S(2)}, u32[]{:S(2)}) collective-permute-start(bf16[1,80,256]{2,1,0:T(8,128)(2,1)S(1)} %get-tuple-element.40), channel_id=1, source_target_pairs={{0,24},{2,26},{4,28},{6,30},{8,16},{10,18},{12,20},{14,22},{16,8},... | collective-permute-start | bytes 122888 | tf_op jit(solution)/shard_map/ppermute | solution.py:610
  18.2 5.9 %collective-permute-start.3 = (bf16[1,80,256]{2,1,0:T(8,128)(2,1)S(1)}, bf16[1,80,256]{2,1,0:T(8,128)(2,1)S(1)}, u32[]{:S(2)}, u32[]{:S(2)}) collective-permute-start(bf16[1,80,256]{2,1,0:T(8,128)(2,1)S(1)} %get-tuple-element.40), channel_id=1, source_target_pairs={{0,16},{2,18},{4,20},{6,22},{8,24},{10,26},{12,28},{14,30},{16,0},... | collective-permute-start | bytes 122888 | tf_op jit(solution)/shard_map/ppermute | solution.py:610
  18.2 5.9 %collective-permute-start.2 = (bf16[1,80,256]{2,1,0:T(8,128)(2,1)S(1)}, bf16[1,80,256]{2,1,0:T(8,128)(2,1)S(1)}, u32[]{:S(2)}, u32[]{:S(2)}) collective-permute-start(bf16[1,80,256]{2,1,0:T(8,128)(2,1)S(1)} %get-tuple-element.40), channel_id=1, source_target_pairs={{0,8},{2,10},{4,12},{6,14},{8,0},{10,2},{12,4},{14,6},{16,24},{18,... | collective-permute-start | bytes 122888 | tf_op jit(solution)/shard_map/ppermute | solution.py:610
  24.2 6.9 %collective-permute-start.7 = (bf16[4,80,256]{2,1,0:T(8,128)(2,1)S(1)}, bf16[4,80,256]{2,1,0:T(8,128)(2,1)S(1)}, u32[]{:S(2)}, u32[]{:S(2)}) collective-permute-start(bf16[4,80,256]{2,1,0:T(8,128)(2,1)S(1)} %constant_dynamic-update-slice_fusion.refs_1_), channel_id=1, source_target_pairs={{0,6},{2,4},{4,2},{6,0},{8,14},{10,12},{12,10},{14,8},{16,22},{18,... | collective-permute-start | bytes 491528 | tf_op jit(solution)/shard_map/ppermute | solution.py:610
  26.5 7.3 %collective-permute-start.6 = (bf16[4,80,256]{2,1,0:T(8,128)(2,1)S(1)}, bf16[4,80,256]{2,1,0:T(8,128)(2,1)S(1)}, u32[]{:S(2)}, u32[]{:S(2)}) collective-permute-start(bf16[4,80,256]{2,1,0:T(8,128)(2,1)S(1)} %constant_dynamic-update-slice_fusion.refs_1_), channel_id=1, source_target_pairs={{0,4},{2,6},{4,0},{6,2},{8,12},{10,14},{12,8},{14,10},{16,20},{18,... | collective-permute-start | bytes 491528 | tf_op jit(solution)/shard_map/ppermute | solution.py:610
  26.5 7.3 %collective-permute-start.5 = (bf16[4,80,256]{2,1,0:T(8,128)(2,1)S(1)}, bf16[4,80,256]{2,1,0:T(8,128)(2,1)S(1)}, u32[]{:S(2)}, u32[]{:S(2)}) collective-permute-start(bf16[4,80,256]{2,1,0:T(8,128)(2,1)S(1)} %constant_dynamic-update-slice_fusion.refs_1_), channel_id=1, source_target_pairs={{0,2},{2,0},{4,6},{6,4},{8,10},{10,8},{12,14},{14,12},{16,18},{18,... | collective-permute-start | bytes 491528 | tf_op jit(solution)/shard_map/ppermute | solution.py:610
  40.6 3.9 %collective-permute-start.8 = (bf16[3,16,256]{2,1,0:T(8,128)(2,1)S(1)}, bf16[3,16,256]{2,1,0:T(8,128)(2,1)S(1)}, u32[]{:S(2)}, u32[]{:S(2)}) collective-permute-start(bf16[3,16,256]{2,1,0:T(8,128)(2,1)S(1)} %get-tuple-element.46), channel_id=1, source_target_pairs={{0,2},{2,0},{4,6},{6,4},{8,10},{10,8},{12,14},{14,12},{16,18},{18,... | collective-permute-start | bytes 73736 | tf_op jit(solution)/shard_map/ppermute | solution.py:610
  48.9 3.9 %collective-permute-start.9 = (bf16[64,256]{1,0:T(8,128)(2,1)S(1)}, bf16[64,256]{1,0:T(8,128)(2,1)S(1)}, u32[]{:S(2)}, u32[]{:S(2)}) collective-permute-start(bf16[64,256]{1,0:T(8,128)(2,1)S(1)} %get-tuple-element.54), channel_id=1, source_target_pairs={{0,2},{2,0},{4,6},{6,4},{8,10},{10,8},{12,14},{14,12},{16,18},{18,... | collective-permute-start | bytes 98312 | tf_op jit(solution)/shard_map/ppermute | solution.py:610
  53.7 6.0 %collective-permute-start.12 = (bf16[224,128]{1,0:T(8,128)(2,1)S(1)}, bf16[224,128]{1,0:T(8,128)(2,1)S(1)}, u32[]{:S(2)}, u32[]{:S(2)}) collective-permute-start(bf16[224,128]{1,0:T(8,128)(2,1)S(1)} %weights.1.refs_0_), channel_id=1, source_target_pairs={{0,24},{2,26},{4,28},{6,30},{8,16},{10,18},{12,20},{14,22},{16,8},... | collective-permute-start | bytes 172040 | tf_op jit(solution)/shard_map/ppermute | solution.py:610
  56.3 5.2 %collective-permute-start.11 = (bf16[224,128]{1,0:T(8,128)(2,1)S(1)}, bf16[224,128]{1,0:T(8,128)(2,1)S(1)}, u32[]{:S(2)}, u32[]{:S(2)}) collective-permute-start(bf16[224,128]{1,0:T(8,128)(2,1)S(1)} %weights.1.refs_0_), channel_id=1, source_target_pairs={{0,16},{2,18},{4,20},{6,22},{8,24},{10,26},{12,28},{14,30},{16,0},... | collective-permute-start | bytes 172040 | tf_op jit(solution)/shard_map/ppermute | solution.py:610
  56.8 4.8 %collective-permute-start.10 = (bf16[224,128]{1,0:T(8,128)(2,1)S(1)}, bf16[224,128]{1,0:T(8,128)(2,1)S(1)}, u32[]{:S(2)}, u32[]{:S(2)}) collective-permute-start(bf16[224,128]{1,0:T(8,128)(2,1)S(1)} %weights.1.refs_0_), channel_id=1, source_target_pairs={{0,8},{2,10},{4,12},{6,14},{8,0},{10,2},{12,4},{14,6},{16,24},{18,... | collective-permute-start | bytes 172040 | tf_op jit(solution)/shard_map/ppermute | solution.py:610
  61.6 5.5 %collective-permute-start.15 = (bf16[352,128]{1,0:T(8,128)(2,1)S(1)}, bf16[352,128]{1,0:T(8,128)(2,1)S(1)}, u32[]{:S(2)}, u32[]{:S(2)}) collective-permute-start(bf16[352,128]{1,0:T(8,128)(2,1)S(1)} %column.1.refs_0_), channel_id=1, source_target_pairs={{0,6},{2,4},{4,2},{6,0},{8,14},{10,12},{12,10},{14,8},{16,22},{18,... | collective-permute-start | bytes 270344 | tf_op jit(solution)/shard_map/ppermute | solution.py:610
  63.2 4.9 %collective-permute-start.14 = (bf16[352,128]{1,0:T(8,128)(2,1)S(1)}, bf16[352,128]{1,0:T(8,128)(2,1)S(1)}, u32[]{:S(2)}, u32[]{:S(2)}) collective-permute-start(bf16[352,128]{1,0:T(8,128)(2,1)S(1)} %column.1.refs_0_), channel_id=1, source_target_pairs={{0,4},{2,6},{4,0},{6,2},{8,12},{10,14},{12,8},{14,10},{16,20},{18,... | collective-permute-start | bytes 270344 | tf_op jit(solution)/shard_map/ppermute | solution.py:610
  63.4 4.7 %collective-permute-start.13 = (bf16[352,128]{1,0:T(8,128)(2,1)S(1)}, bf16[352,128]{1,0:T(8,128)(2,1)S(1)}, u32[]{:S(2)}, u32[]{:S(2)}) collective-permute-start(bf16[352,128]{1,0:T(8,128)(2,1)S(1)} %column.1.refs_0_), channel_id=1, source_target_pairs={{0,2},{2,0},{4,6},{6,4},{8,10},{10,8},{12,14},{14,12},{16,18},{18,... | collective-permute-start | bytes 270344 | tf_op jit(solution)/shard_map/ppermute | solution.py:610
